TPU v7x, 32 devices: a whole 2x2x4 slice. The times are simulated.
32 devices in a mesh: dp: 16 (over z, y, core), tensor: 2 (over x).
Axes of the slice: x: 2, y: 2, z: 4, core: 2. Of those that a mesh axis runs over, the one named last changes fastest.
Arguments:
- block_input: bfloat16 [16384, 1024], P(('dp', 'tensor')), may hold values from -6 to 6
- segment_ids: int32 [16384], P('dp'), may hold values from 0 to 2, as said below
- ln1_gain: float32 [1024], replicated, may hold values from 0.1 to 1.9
- ln1_bias: float32 [1024], replicated, may hold values from -4 to 4
- w_query: bfloat16 [1024, 1024], P('dp', 'tensor'), may hold values from -0.1875 to 0.1875
- w_key: bfloat16 [1024, 1024], P('dp', 'tensor'), may hold values from -0.1875 to 0.1875
- w_value: bfloat16 [1024, 1024], P('dp', 'tensor'), may hold values from -0.1875 to 0.1875
- b_query: float32 [1024], replicated, may hold values from -6 to 6
- b_value: float32 [1024], replicated, may hold values from -6 to 6
- w_out: bfloat16 [1024, 1024], P('dp', 'tensor'), may hold values from -1 to 1
- b_out: float32 [1024], replicated, may hold values from -4 to 4
- ln2_gain: float32 [1024], replicated, may hold values from 0.1 to 1.9
- ln2_bias: float32 [1024], replicated, may hold values from -4 to 4
- w_up: bfloat16 [1024, 4096], P('dp', 'tensor'), may hold values from -0.1875 to 0.1875
- b_up: float32 [4096], replicated, may hold values from -6 to 6
- w_down: bfloat16 [1024, 4096], P('dp', 'tensor'), may hold values from -0.125 to 0.125
- b_down: float32 [1024], replicated, may hold values from -4 to 4
- out_grad: bfloat16 [16384, 1024], P(('dp', 'tensor')), may hold values from -6 to 6
Outputs:
- block_output: bfloat16 [16384, 1024], P(('dp', 'tensor'))
- grad_input: bfloat16 [16384, 1024], P(('dp', 'tensor'))
- grad_ln1_gain: float32 [1024], replicated
- grad_ln1_bias: float32 [1024], replicated
- grad_w_query: float32 [1024, 1024], P('dp', 'tensor')
- grad_w_key: float32 [1024, 1024], P('dp', 'tensor')
- grad_w_value: float32 [1024, 1024], P('dp', 'tensor')
- grad_b_query: float32 [1024], replicated
- grad_b_value: float32 [1024], replicated
- grad_w_out: float32 [1024, 1024], P('dp', 'tensor')
- grad_b_out: float32 [1024], replicated
- grad_ln2_gain: float32 [1024], replicated
- grad_ln2_bias: float32 [1024], replicated
- grad_w_up: float32 [1024, 4096], P('dp', 'tensor')
- grad_b_up: float32 [4096], replicated
- grad_w_down: float32 [1024, 4096], P('dp', 'tensor')
- grad_b_down: float32 [1024], replicated
Inputs may be any that keep to these rules, and one draw needn't show every extreme that they name: `segment_ids`: within each data group of 1024 consecutive tokens the ids are 0, 1 and 2, each present, never falling; the block's attention never reaches across data groups.
All inputs are finite; a program needn't handle non-finite values.
Results may differ from a plain program's by a relative error of at most 0.018.
Values may be sent and summed in bfloat16 or wider, within the bound.
No kernel may reach another device: no remote copies, remote signals or barrier semaphores. Data moves between devices by JAX's collectives and lax.ppermute only.
A program may use at most 192 MiB of HBM per device.

v0:
```python
import functools

import jax
import jax.numpy as jnp
from jax import lax
from jax.experimental import pallas as pl
from jax.experimental.pallas import tpu as pltpu
from jax.sharding import Mesh
from jax.sharding import PartitionSpec as P

HEAD_DIM = 64
LANES = 128
TILE = 512
MASKED = -1e30
VMEM_BYTES = 60 * 1024 * 1024
F32 = jnp.float32
BF16 = jnp.bfloat16
TP = ("l", "c")
SWAP = ("c", "h", "l")
ALL = ("a", "c", "h", "l")


def normalize(values):
    center = values - jnp.mean(values, axis=-1, keepdims=True)
    spread = jnp.mean(center * center, axis=-1, keepdims=True)
    inverse = lax.rsqrt(spread + 1e-05)
    return center * inverse, inverse


def norm_back(grad_in, scaled, inverse, gain_vec):
    local_grad = grad_in * gain_vec
    return inverse * (
        local_grad
        - jnp.mean(local_grad, axis=-1, keepdims=True)
        - scaled * jnp.mean(local_grad * scaled, axis=-1, keepdims=True)
    )


def dot_nn(left, right):
    return lax.dot_general(left, right, (((1,), (0,)), ((), ())), preferred_element_type=F32)


def dot_nt(left, right):
    return lax.dot_general(left, right, (((1,), (1,)), ((), ())), preferred_element_type=F32)


def dot_tn(left, right):
    return lax.dot_general(left, right, (((0,), (0,)), ((), ())), preferred_element_type=F32)


def fill_bias(bias, seg_col, seg_row):
    length = bias.shape[0]
    block = min(256, length)
    for first in range(0, length, block):
        keys = lax.broadcasted_iota(jnp.int32, (block, length), 0) + first
        places = lax.broadcasted_iota(jnp.int32, (block, length), 1)
        same = seg_col[first : first + block, :] == seg_row[...]
        bias[first : first + block, :] = jnp.where(same & (keys <= places), 0.0, MASKED)


def head_lanes(values, head):
    lane = lax.broadcasted_iota(jnp.int32, values.shape, 1)
    inside = (lane >= head * HEAD_DIM) & (lane < (head + 1) * HEAD_DIM)
    return jnp.where(inside, values, jnp.zeros_like(values))


def attn_forward_kernel(seg_col, seg_row, q_ref, k_ref, v_ref, mixed_ref, lse_ref, bias, v_t, block):
    length = q_ref.shape[0]
    heads = LANES // HEAD_DIM

    @pl.when(pl.program_id(0) == 0)
    def _():
        fill_bias(bias, seg_col, seg_row)

    v_t[...] = v_ref[...].T
    for place in range(length // block):
        rows = slice(place * block, (place + 1) * block)
        outs = []
        for head in range(heads):
            query = head_lanes(q_ref[rows, :], head)
            scores = []
            peak = None
            for other in range(place + 1):
                keys = slice(other * block, (other + 1) * block)
                part = dot_nt(k_ref[keys, :], query) + bias[keys, rows]
                top = jnp.max(part, axis=0, keepdims=True)
                peak = top if peak is None else jnp.maximum(peak, top)
                scores.append(part)
            total = None
            acc = None
            for other in range(place + 1):
                keys = slice(other * block, (other + 1) * block)
                weight = jnp.exp(scores[other] - peak)
                part_sum = jnp.sum(weight, axis=0, keepdims=True)
                total = part_sum if total is None else total + part_sum
                part_out = dot_nn(
                    v_t[head * HEAD_DIM : (head + 1) * HEAD_DIM, keys], weight.astype(BF16)
                )
                acc = part_out if acc is None else acc + part_out
            outs.append(acc / total)
            lse_ref[0, head : head + 1, rows] = peak + jnp.log(total)
        mixed_ref[rows, :] = jnp.concatenate(outs, axis=0).T.astype(BF16)


def attn_backward_kernel(
    seg_col, seg_row, q_ref, k_ref, v_ref, mixed_ref, lse_ref, g_ref, grads_ref, bias, k_t, delta, dq_t, block
):
    length = q_ref.shape[0]
    heads = LANES // HEAD_DIM
    count = length // block

    @pl.when(pl.program_id(0) == 0)
    def _():
        fill_bias(bias, seg_col, seg_row)

    k_t[...] = k_ref[...].T
    product = (g_ref[...].astype(F32) * mixed_ref[...].astype(F32)).T
    for head in range(heads):
        delta[head : head + 1, :] = jnp.sum(
            product[head * HEAD_DIM : (head + 1) * HEAD_DIM, :], axis=0, keepdims=True
        )
    for other in range(count):
        keys = slice(other * block, (other + 1) * block)
        key_sum = None
        value_sum = None
        for head in range(heads):
            lanes = slice(head * HEAD_DIM, (head + 1) * HEAD_DIM)
            for place in range(other, count):
                rows = slice(place * block, (place + 1) * block)
                query = head_lanes(q_ref[rows, :], head)
                grad = head_lanes(g_ref[rows, :], head)
                scores = dot_nt(k_ref[keys, :], query) + bias[keys, rows]
                probs = jnp.exp(scores - lse_ref[0, head : head + 1, rows])
                grad_probs = dot_nt(v_ref[keys, :], grad)
                grad_scores = (probs * (grad_probs - delta[head : head + 1, rows])).astype(BF16)
                value_part = dot_nn(probs.astype(BF16), grad)
                key_part = dot_nn(grad_scores, query)
                query_part = dot_nn(k_t[lanes, keys], grad_scores)
                value_sum = value_part if value_sum is None else value_sum + value_part
                key_sum = key_part if key_sum is None else key_sum + key_part
                if other == 0:
                    dq_t[lanes, rows] = query_part
                else:
                    dq_t[lanes, rows] += query_part
        grads_ref[1, keys, :] = key_sum.astype(BF16)
        grads_ref[2, keys, :] = value_sum.astype(BF16)
    grads_ref[0] = (dq_t[...].T * HEAD_DIM ** (-0.5)).astype(BF16)


def attn_forward(segments, qkv, width):
    length = qkv.shape[0]
    pairs = width // LANES
    block = min(256, length)
    column = lambda first: pl.BlockSpec((length, LANES), lambda p: (0, first * pairs + p))
    whole = lambda shape: pl.BlockSpec(shape, lambda p: (0, 0))
    return pl.pallas_call(
        functools.partial(attn_forward_kernel, block=block),
        grid=(pairs,),
        in_specs=[whole((length, 1)), whole((1, length)), column(0), column(1), column(2)],
        out_specs=[
            pl.BlockSpec((length, LANES), lambda p: (0, p)),
            pl.BlockSpec((1, 8, length), lambda p: (p, 0, 0)),
        ],
        out_shape=[
            jax.ShapeDtypeStruct((length, width), BF16),
            jax.ShapeDtypeStruct((pairs, 8, length), F32),
        ],
        scratch_shapes=[pltpu.VMEM((length, length), F32), pltpu.VMEM((LANES, length), BF16)],
        compiler_params=pltpu.CompilerParams(vmem_limit_bytes=VMEM_BYTES),
        cost_estimate=pl.CostEstimate(
            flops=4 * length * length * width,
            bytes_accessed=8 * length * width,
            transcendentals=length * length * width // (2 * HEAD_DIM),
        ),
        name="attn_forward",
    )(segments.reshape(length, 1), segments.reshape(1, length), qkv, qkv, qkv)


def attn_backward(segments, qkv, mixed, lse, grad_mixed, width, after):
    length = qkv.shape[0]
    pairs = width // LANES
    block = min(256, length)
    column = lambda first: pl.BlockSpec((length, LANES), lambda p: (0, first * pairs + p))
    whole = lambda shape: pl.BlockSpec(shape, lambda p: (0, 0))
    return pl.pallas_call(
        without(functools.partial(attn_backward_kernel, block=block), 8),
        grid=(pairs,),
        in_specs=[
            whole((length, 1)),
            whole((1, length)),
            column(0),
            column(1),
            column(2),
            pl.BlockSpec((length, LANES), lambda p: (0, p)),
            pl.BlockSpec((1, 8, length), lambda p: (p, 0, 0)),
            pl.BlockSpec((length, LANES), lambda p: (0, p)),
            pl.BlockSpec(memory_space=pl.ANY),
        ],
        out_specs=pl.BlockSpec((3, length, LANES), lambda p: (0, 0, p)),
        out_shape=jax.ShapeDtypeStruct((3, length, width), BF16),
        scratch_shapes=[
            pltpu.VMEM((length, length), F32),
            pltpu.VMEM((LANES, length), BF16),
            pltpu.VMEM((8, length), F32),
            pltpu.VMEM((LANES, length), F32),
        ],
        compiler_params=pltpu.CompilerParams(vmem_limit_bytes=VMEM_BYTES),
        cost_estimate=pl.CostEstimate(
            flops=10 * length * length * width,
            bytes_accessed=16 * length * width,
            transcendentals=length * length * width // (2 * HEAD_DIM),
        ),
        name="attn_backward",
    )(segments.reshape(length, 1), segments.reshape(1, length), qkv, qkv, qkv, mixed, lse, grad_mixed, after)


def piece_blocks(count):
    far = count // 4
    half = far // 2
    near, by_y, by_x, both = (list(range(i * far, (i + 1) * far)) for i in range(4))
    return [
        both[:half] + by_x[:half],
        both[half:] + by_y[half:],
        by_y[:half],
        by_x[half:],
        near,
    ]


def store_pieces(order, grad, piece_refs, columns):
    count = order.shape[0]
    rows = grad.shape[0] // count
    for blocks, ref in zip(piece_blocks(count), piece_refs):
        for place, block in enumerate(blocks):
            first = pl.multiple_of(order[block] * rows, rows)
            ref[place * rows : (place + 1) * rows, columns] = grad[pl.ds(first, rows), :]


def piece_shapes(count, rows, columns):
    return [
        jax.ShapeDtypeStruct((len(blocks) * rows, columns), BF16) for blocks in piece_blocks(count)
    ]


def whole_spec(shape, **options):
    return pl.BlockSpec(shape, lambda step: (0,) * len(shape), **options)


def norm_kernel(*refs, residual):
    if residual:
        x_ref, own_ref, other_ref, shift_ref, gain_ref, bias_ref, n_ref, nt_ref, hidden_ref = refs
        values = (
            x_ref[...].astype(F32)
            + (own_ref[...].astype(F32) + other_ref[...].astype(F32))
            + shift_ref[...]
        )
        hidden_ref[...] = values
    else:
        x_ref, gain_ref, bias_ref, n_ref, nt_ref = refs
        values = x_ref[...].astype(F32)
    scaled, _ = normalize(values)
    normed = (scaled * gain_ref[...] + bias_ref[...]).astype(BF16)
    n_ref[...] = normed
    nt_ref[...] = normed.T


def norm_rows(x, gain, bias, partials=None, shift=None):
    length, width = x.shape
    block = min(256, length)
    row = pl.BlockSpec((block, width), lambda step: (step, 0))
    vector = whole_spec((1, width))
    residual = partials is not None
    operands = [x] + (list(partials) + [shift.reshape(1, width)] if residual else [])
    operands += [gain.reshape(1, width), bias.reshape(1, width)]
    return pl.pallas_call(
        functools.partial(norm_kernel, residual=residual),
        grid=(length // block,),
        in_specs=[row] + ([row, row, vector] if residual else []) + [vector, vector],
        out_specs=[row, pl.BlockSpec((width, block), lambda step: (0, step))]
        + ([row] if residual else []),
        out_shape=[
            jax.ShapeDtypeStruct((length, width), BF16),
            jax.ShapeDtypeStruct((width, length), BF16),
        ]
        + ([jax.ShapeDtypeStruct((length, width), F32)] if residual else []),
        compiler_params=pltpu.CompilerParams(vmem_limit_bytes=VMEM_BYTES),
        cost_estimate=pl.CostEstimate(
            flops=20 * length * width, bytes_accessed=14 * length * width, transcendentals=length
        ),
        name="norm_two" if residual else "norm_one",
    )(*operands)


def norm_back_kernel(hidden_ref, g_ref, own_ref, other_ref, gain_ref, grad_ref, low_ref, low_t_ref, sums_ref):
    scaled, inverse = normalize(hidden_ref[...])
    incoming = own_ref[...].astype(F32) + other_ref[...].astype(F32)
    grad = g_ref[...].astype(F32) + norm_back(incoming, scaled, inverse, gain_ref[...])
    grad_ref[...] = grad
    low_ref[...] = grad.astype(BF16)
    low_t_ref[...] = grad.astype(BF16).T

    @pl.when(pl.program_id(0) == 0)
    def _():
        sums_ref[...] = jnp.zeros_like(sums_ref)

    sums_ref[0:1, :] += jnp.sum(grad, axis=0, keepdims=True)
    sums_ref[1:2, :] += jnp.sum(incoming * scaled, axis=0, keepdims=True)
    sums_ref[2:3, :] += jnp.sum(incoming, axis=0, keepdims=True)


def norm_back_rows(hidden, grad, partials, gain):
    length, width = hidden.shape
    block = min(256, length)
    row = pl.BlockSpec((block, width), lambda step: (step, 0))
    return pl.pallas_call(
        norm_back_kernel,
        grid=(length // block,),
        in_specs=[row, row, row, row, whole_spec((1, width))],
        out_specs=[
            row,
            row,
            pl.BlockSpec((width, block), lambda step: (0, step)),
            whole_spec((8, width)),
        ],
        out_shape=[
            jax.ShapeDtypeStruct((length, width), F32),
            jax.ShapeDtypeStruct((length, width), BF16),
            jax.ShapeDtypeStruct((width, length), BF16),
            jax.ShapeDtypeStruct((8, width), F32),
        ],
        compiler_params=pltpu.CompilerParams(vmem_limit_bytes=VMEM_BYTES),
        cost_estimate=pl.CostEstimate(
            flops=30 * length * width, bytes_accessed=16 * length * width, transcendentals=length
        ),
        name="norm_two_back",
    )(hidden, grad, *partials, gain.reshape(1, width))


def load_pieces(order, pieces, w_ref):
    rows = w_ref.shape[0] // order.shape[0]
    block = 0
    for ref in pieces:
        for place in range(ref.shape[0] // rows):
            first = pl.multiple_of(order[block] * rows, rows)
            w_ref[pl.ds(first, rows), :] = ref[place * rows : (place + 1) * rows, :]
            block += 1


def mlp_kernel(order, n_ref, g_ref, nt_ref, gt_ref, b_ref, *refs, block, with_previous, cube, in_pieces):
    if in_pieces:
        pieces, refs = refs[:5], refs[5:]
        w_ref, refs = refs[-1], refs[:-1]
        load_pieces(order, pieces, w_ref)
    else:
        w_ref, refs = refs[0], refs[1:]
    if with_previous:
        (before_out, before_gn), refs = refs[:2], refs[2:]
    count = 5 if cube else 1
    (out_ref, gn_ref), grad_refs, refs = refs[:2], refs[2 : 2 + count], refs[2 + count :]
    gb_ref, out_acc, gn_acc, act, gpre, grad_up, grad_down = refs
    step = pl.program_id(0)
    length = n_ref.shape[0]
    tile = w_ref.shape[1] // 2
    ups, downs = slice(0, tile), slice(tile, 2 * tile)

    @pl.when(step == 0)
    def _():
        if with_previous:
            out_acc[...] = before_out[...].astype(F32)
            gn_acc[...] = before_gn[...].astype(F32)
        else:
            out_acc[...] = jnp.zeros_like(out_acc)
            gn_acc[...] = jnp.zeros_like(gn_acc)

    bias_sum = jnp.zeros(gb_ref.shape, F32)
    for first in range(0, length, block):
        rows = slice(first, first + block)
        unit = dot_nn(n_ref[rows, :], w_ref[:, ups]) + b_ref[...]
        grad = dot_nn(g_ref[rows, :], w_ref[:, downs])
        square = unit * unit
        curve = jnp.tanh(0.7978845608028654 * (unit + 0.044715 * (square * unit)))
        half = 0.5 + 0.5 * curve
        slope = half + (0.5 * unit) * (1.0 - curve * curve) * (
            0.7978845608028654 + (3 * 0.044715 * 0.7978845608028654) * square
        )
        active = (unit * half).astype(BF16)
        grad_pre = (grad * slope).astype(BF16)
        act[rows, :] = active
        gpre[rows, :] = grad_pre
        bias_sum = bias_sum + jnp.sum(grad_pre.astype(F32), axis=0, keepdims=True)
        out_acc[rows, :] += dot_nt(active, w_ref[:, downs])
        gn_acc[rows, :] += dot_nt(grad_pre, w_ref[:, ups])
    gb_ref[...] = bias_sum
    if cube:
        grad_up[...] = dot_nn(nt_ref[...], gpre[...]).astype(BF16)
        grad_down[...] = dot_nn(gt_ref[...], act[...]).astype(BF16)
        store_pieces(order, grad_up, grad_refs, ups)
        store_pieces(order, grad_down, grad_refs, downs)
    else:
        grad_refs[0][:, ups] = dot_nn(nt_ref[...], gpre[...]).astype(BF16)
        grad_refs[0][:, downs] = dot_nn(gt_ref[...], act[...]).astype(BF16)

    @pl.when(step == pl.num_programs(0) - 1)
    def _():
        out_ref[...] = out_acc[...].astype(BF16)
        gn_ref[...] = gn_acc[...].astype(BF16)


def mlp(order, normed, grad, normed_t, grad_t, weights, bias, previous, cube):
    length, width = normed.shape
    units = weights[0].shape[1] // 2
    in_pieces = len(weights) > 1
    tile = min(TILE, units)
    once = pl.Buffered(1)
    fixed = lambda shape, **options: pl.BlockSpec(shape, lambda u, o: (0, 0), **options)
    at_tile = lambda rows, columns: pl.BlockSpec((rows, columns), lambda u, o: (0, u))
    count, rows = order.shape[0], width // order.shape[0]
    if cube:
        grad_shapes = piece_shapes(count, rows, 2 * units)
    else:
        grad_shapes = [jax.ShapeDtypeStruct((width, 2 * units), BF16)]
    results = pl.pallas_call(
        functools.partial(
            mlp_kernel, block=min(256, length), with_previous=bool(previous), cube=cube,
            in_pieces=in_pieces,
        ),
        grid_spec=pltpu.PrefetchScalarGridSpec(
            num_scalar_prefetch=1,
            grid=(units // tile,),
            in_specs=[
                fixed((length, width), pipeline_mode=once),
                fixed((length, width), pipeline_mode=once),
                fixed((width, length), pipeline_mode=once),
                fixed((width, length), pipeline_mode=once),
                at_tile(1, tile),
            ]
            + [at_tile(piece.shape[0], 2 * tile) for piece in weights]
            + [fixed((length, width), pipeline_mode=once) for _ in previous],
            out_specs=[fixed((length, width)), fixed((length, width))]
            + [at_tile(shape.shape[0], 2 * tile) for shape in grad_shapes]
            + [at_tile(1, tile)],
            scratch_shapes=[
                pltpu.VMEM((length, width), F32),
                pltpu.VMEM((length, width), F32),
                pltpu.VMEM((length, tile), BF16),
                pltpu.VMEM((length, tile), BF16),
                pltpu.VMEM((width, tile), BF16),
                pltpu.VMEM((width, tile), BF16),
            ]
            + ([pltpu.VMEM((width, 2 * tile), BF16)] if in_pieces else []),
        ),
        out_shape=[jax.ShapeDtypeStruct((length, width), BF16)] * 2
        + grad_shapes
        + [jax.ShapeDtypeStruct((1, units), F32)],
        compiler_params=pltpu.CompilerParams(vmem_limit_bytes=VMEM_BYTES),
        cost_estimate=pl.CostEstimate(
            flops=12 * length * width * units,
            bytes_accessed=12 * length * width + 8 * width * units,
            transcendentals=length * units,
        ),
        name="mlp_second" if previous else "mlp_first",
    )(order, normed, grad, normed_t, grad_t, bias.reshape(1, units), *weights, *previous)
    return results[0], results[1], results[2:-1], results[-1]


def qkv_kernel(order, n_ref, b_ref, near, by_y, by_x, low, high, out_ref, w_ref):
    load_pieces(order, (near, by_y, by_x, low, high), w_ref)
    scale = jnp.where(pl.program_id(0) == 0, HEAD_DIM ** (-0.5), 1.0)
    length = n_ref.shape[0]
    step = min(256, length)
    for first in range(0, length, step):
        span = slice(first, first + step)
        out_ref[span, :] = ((dot_nn(n_ref[span, :], w_ref[...]) + b_ref[...]) * scale).astype(BF16)


def qkv_project(order, normed, pieces, bias):
    length, width = normed.shape
    columns = pieces[0].shape[1] // 3
    at_tile = lambda rows: pl.BlockSpec((rows, columns), lambda k, o: (0, k))
    return pl.pallas_call(
        qkv_kernel,
        grid_spec=pltpu.PrefetchScalarGridSpec(
            num_scalar_prefetch=1,
            grid=(3,),
            in_specs=[
                pl.BlockSpec((length, width), lambda k, o: (0, 0), pipeline_mode=pl.Buffered(1)),
                at_tile(1),
            ]
            + [at_tile(piece.shape[0]) for piece in pieces],
            out_specs=[at_tile(length), at_tile(width)],
        ),
        out_shape=[
            jax.ShapeDtypeStruct((length, 3 * columns), BF16),
            jax.ShapeDtypeStruct((width, 3 * columns), BF16),
        ],
        compiler_params=pltpu.CompilerParams(vmem_limit_bytes=VMEM_BYTES),
        cost_estimate=pl.CostEstimate(
            flops=6 * length * width * columns,
            bytes_accessed=2 * length * width + 12 * width * columns + 6 * length * columns,
            transcendentals=0,
        ),
        name="qkv_project",
    )(order, normed, bias.reshape(1, 3 * columns), *pieces)


def weight_kernel(order, nt_ref, grads_ref, *refs):
    piece_refs, grad = refs[:5], refs[5]
    grad[...] = dot_nn(nt_ref[...], grads_ref[0]).astype(BF16)
    store_pieces(order, grad, piece_refs, slice(None))


def without(kernel, place):
    return lambda *refs: kernel(*refs[:place], *refs[place + 1 :])


ORDER_ONLY = pl.BlockSpec(memory_space=pl.ANY)


def weight_grads(order, normed_t, grads, after):
    width, length = normed_t.shape
    columns = grads.shape[2]
    tile = min(TILE, columns)
    tiles = columns // tile
    parts = grads.shape[0]
    shapes = piece_shapes(order.shape[0], width // order.shape[0], parts * columns)
    return pl.pallas_call(
        without(weight_kernel, 3),
        grid_spec=pltpu.PrefetchScalarGridSpec(
            num_scalar_prefetch=1,
            grid=(parts, tiles),
            in_specs=[
                pl.BlockSpec((width, length), lambda k, u, o: (0, 0), pipeline_mode=pl.Buffered(1)),
                pl.BlockSpec((1, length, tile), lambda k, u, o: (k, 0, u)),
                ORDER_ONLY,
            ],
            out_specs=[
                pl.BlockSpec((shape.shape[0], tile), lambda k, u, o: (0, k * tiles + u))
                for shape in shapes
            ],
            scratch_shapes=[pltpu.VMEM((width, tile), BF16)],
        ),
        out_shape=shapes,
        compiler_params=pltpu.CompilerParams(vmem_limit_bytes=VMEM_BYTES),
        cost_estimate=pl.CostEstimate(
            flops=2 * parts * length * width * columns,
            bytes_accessed=2 * length * width + 4 * parts * width * columns,
            transcendentals=0,
        ),
        name="weight_grads",
    )(order, normed_t, grads, after)


def qkv_back_kernel(grads_ref, w_ref, out_ref):
    columns = grads_ref.shape[2]
    total = None
    for k in range(3):
        part = dot_nt(grads_ref[k], w_ref[:, k * columns : (k + 1) * columns])
        total = part if total is None else total + part
    out_ref[...] = total.astype(BF16)


def qkv_back(grads, weights, after):
    _, length, columns = grads.shape
    width = weights.shape[0]
    block = min(256, length)
    return pl.pallas_call(
        without(qkv_back_kernel, 2),
        grid=(length // block,),
        in_specs=[
            pl.BlockSpec((3, block, columns), lambda i: (0, i, 0)),
            pl.BlockSpec((width, 3 * columns), lambda i: (0, 0), pipeline_mode=pl.Buffered(1)),
            ORDER_ONLY,
        ],
        out_specs=pl.BlockSpec((block, width), lambda i: (i, 0)),
        out_shape=jax.ShapeDtypeStruct((length, width), BF16),
        compiler_params=pltpu.CompilerParams(vmem_limit_bytes=VMEM_BYTES),
        cost_estimate=pl.CostEstimate(
            flops=6 * length * width * columns,
            bytes_accessed=2 * length * width + 6 * width * columns + 6 * length * columns,
            transcendentals=0,
        ),
        name="qkv_back",
    )(grads, weights, after)


def added(*terms):
    total = terms[0].astype(F32)
    for term in terms[1:]:
        total = total + term.astype(F32)
    return total.astype(BF16)


def first_sums_kernel(*refs, spans):
    refs, (y_ref, x_ref) = refs[:-2], refs[-2:]
    half = y_ref.shape[0]
    for index, columns in enumerate(spans):
        from_x, from_y, keep_y, keep_x = (ref[...] for ref in refs[4 * index : 4 * index + 4])
        y_ref[:, columns] = added(keep_y, from_x[:half])
        x_ref[:, columns] = added(keep_x, from_y[:half])


def second_sums_kernel(*refs, spans, far):
    outs, refs = refs[-far:], refs[:-far]
    (from_y2, from_x2), refs = refs[-2:], refs[:-2]
    half = from_y2.shape[0]
    rows = half * 2 // far
    for index, columns in enumerate(spans):
        from_x, from_y, near = refs[3 * index : 3 * index + 3]
        for i in range(far):
            first, second, place = (from_x, from_y2, i) if i < far // 2 else (from_y, from_x2, i - far // 2)
            span = slice(place * rows, (place + 1) * rows)
            outs[i][:, columns] = added(
                near[i * rows : (i + 1) * rows, :],
                first[half + place * rows : half + (place + 1) * rows, :],
                second[span, columns],
            )


def last_sums_kernel(*refs, far, half_tile, head_width):
    parts, other, (up_ref, down_ref, out_ref) = refs[:far], refs[far], refs[far + 1 :]
    total = parts[0][...].astype(F32)
    for part in parts[1:]:
        total = total + part[...].astype(F32)
    units = up_ref.shape[1] // 2
    for first in range(0, units, half_tile):
        here, there = slice(first, first + half_tile), slice(units + first, units + first + half_tile)
        up, down = slice(2 * first, 2 * first + half_tile), slice(2 * first + half_tile, 2 * first + 2 * half_tile)
        up_ref[:, here] = other[:, up].astype(F32)
        down_ref[:, here] = other[:, down].astype(F32)
        up_ref[:, there] = total[:, up]
        down_ref[:, there] = total[:, down]
    out_ref[...] = total[:, 2 * units : 2 * units + head_width]


def qkv_last_kernel(*refs):
    parts, outs = refs[:-3], refs[-3:]
    total = parts[0][...].astype(F32)
    for part in parts[1:]:
        total = total + part[...].astype(F32)
    columns = outs[0].shape[1]
    for k, out in enumerate(outs):
        out[...] = total[:, k * columns : (k + 1) * columns]


def shards_kernel(w_out, w_up, w_down, out_ref, first_ref, second_ref, *, tile):
    out_ref[...] = w_out[...]
    units = first_ref.shape[1] // 2
    for index, ref in enumerate((first_ref, second_ref)):
        for first in range(0, units, tile):
            columns = slice(index * units + first, index * units + first + tile)
            ref[:, 2 * first : 2 * first + tile] = w_up[:, columns]
            ref[:, 2 * first + tile : 2 * first + 2 * tile] = w_down[:, columns]


def copy_kernel(source, target):
    target[...] = source[...]


def column_spans(widths):
    spans, first = [], 0
    for width in widths:
        spans.append(slice(first, first + width))
        first += width
    return spans


def sums_call(kernel, operands, shapes, after, name):
    body = kernel if after is None else without(kernel, 0)
    vmem = pl.BlockSpec(memory_space=pltpu.VMEM)
    return pl.pallas_call(
        body,
        in_specs=([pl.BlockSpec(memory_space=pl.ANY)] if after is not None else [])
        + [vmem] * len(operands),
        out_specs=[vmem] * len(shapes),
        out_shape=shapes,
        compiler_params=pltpu.CompilerParams(vmem_limit_bytes=VMEM_BYTES),
        name=name,
    )(*([after] if after is not None else []), *operands)


def flipped(sizes):
    return 1 if sizes["h"] * sizes["l"] == 2 else 0


def moves(sizes):
    groups, ranks, inner = sizes["a"], sizes["h"] * sizes["l"], sizes["l"]
    far = groups // 2
    flip = flipped(sizes)
    swap_to = {}
    for group in range(2):
        for part in range(ranks):
            place = (part % 2 ^ flip) * ranks + group * (ranks // 2) + part // 2
            swap_to[group * ranks + part] = place

    def swap(values, inverse=False):
        pairs = [(to, frm) if inverse else (frm, to) for frm, to in swap_to.items()]
        return lax.ppermute(values, SWAP, pairs)

    def swap_hop(values, a_mask, inverse=False):
        pairs = []
        for a in range(groups):
            for frm, to in swap_to.items():
                one, two = a * 2 * ranks + frm, (a ^ a_mask) * 2 * ranks + to
                pairs.append((two, one) if inverse else (one, two))
        return lax.ppermute(values, ALL, pairs)

    def hop(values, a_mask, h_mask):
        pairs = []
        for a in range(groups):
            for c in range(2):
                for h in range(2):
                    pairs.append(((a * 2 + c) * 2 + h, ((a ^ a_mask) * 2 + c) * 2 + (h ^ h_mask)))
        return lax.ppermute(values, ("a", "c", "h"), pairs)

    def gather(shard):
        near = jnp.concatenate([swap_hop(shard, 2 * i) for i in range(far)], axis=0)
        half = near.shape[0] // 2
        by_y = hop(near, 1, 0)
        by_x = hop(near, 0, 1)
        return [near, by_y, by_x, hop(by_y[:half], 0, 1), hop(by_x[half:], 1, 0)]

    def first_sends(pieces):
        return hop(pieces[0], 0, 1), hop(pieces[1], 1, 0)

    def finish(chunks, received, after, after_two, name):
        spans = column_spans([pieces[0].shape[1] for pieces in chunks])
        total = spans[-1].stop
        half, rows = chunks[0][2].shape[0], chunks[0][4].shape[0] // far
        operands = []
        for pieces, (from_x, from_y) in zip(chunks, received):
            operands += [from_x, from_y, pieces[2], pieces[3]]
        y_sum, x_sum = sums_call(
            functools.partial(first_sums_kernel, spans=spans),
            operands,
            [jax.ShapeDtypeStruct((half, total), BF16)] * 2,
            after,
            name + "_sums_one",
        )
        from_y2, from_x2 = hop(y_sum, 1, 0), hop(x_sum, 0, 1)
        operands = []
        for pieces, (from_x, from_y) in zip(chunks, received):
            operands += [from_x, from_y, pieces[4]]
        sums = sums_call(
            functools.partial(second_sums_kernel, spans=spans, far=far),
            operands + [from_y2, from_x2],
            [jax.ShapeDtypeStruct((rows, total), BF16)] * far,
            after_two(y_sum),
            name + "_sums_two",
        )
        return sums[0], [swap_hop(sums[i], 2 * i, inverse=True) for i in range(far)]

    def sum_all(values):
        values = values + lax.ppermute(values, "c", [(0, 1), (1, 0)])
        values = values + hop(values, 0, 1)
        for mask in range(groups.bit_length() - 1):
            values = values + hop(values, 1 << mask, 0)
        return lax.psum(values, "l") if inner > 1 else values

    a, h = lax.axis_index("a"), lax.axis_index("h")
    order = []
    for a_low, h_mask in ((0, 0), (1, 0), (0, 1), (1, 1)):
        for i in range(far):
            order.append((a ^ (2 * i + a_low)) * 2 + (h ^ h_mask))
    return swap, gather, first_sends, finish, sum_all, jnp.stack(order).astype(jnp.int32)


def per_device(sizes, *arguments):
    (
        block_input, segment_ids, ln1_gain, ln1_bias, w_query, w_key, w_value, b_query, b_value,
        w_out, b_out, ln2_gain, ln2_bias, w_up, b_up, w_down, b_down, out_grad,
    ) = arguments
    ranks = sizes["h"] * sizes["l"]
    rank = lax.axis_index("l") * 2 + (lax.axis_index("c") ^ flipped(sizes))
    own_rows, width = block_input.shape
    head_width = w_query.shape[1]
    unit_width = w_up.shape[1]
    half_units = unit_width // 2
    tile = min(TILE, half_units)
    swap, gather, first_sends, finish, sum_all, order = moves(sizes)

    def partner(values):
        return lax.ppermute(values, "c", [(0, 1), (1, 0)])

    def tp_gather(values):
        if ranks != 2:
            return lax.all_gather(values, TP, axis=0, tiled=True)
        theirs = partner(values)
        return jnp.where(
            rank == 0,
            jnp.concatenate([values, theirs], axis=0),
            jnp.concatenate([theirs, values], axis=0),
        )

    def tp_terms(values):
        if ranks != 2:
            others = lax.psum(values.astype(F32), TP) - values.astype(F32)
            return values, others.astype(BF16)
        return values, partner(values)

    def own(values):
        return lax.dynamic_slice_in_dim(values, rank * own_rows, own_rows)

    def tp_scatter(values):
        if ranks != 2:
            return lax.psum_scatter(values, TP, scatter_dimension=0, tiled=True).astype(F32)
        theirs = lax.dynamic_slice_in_dim(values, (1 - rank) * own_rows, own_rows)
        return own(values).astype(F32) + partner(theirs).astype(F32)

    pieces_qkv = gather(jnp.concatenate([w_query, w_key, w_value], axis=1))
    shard_out, shard_first, shard_second = sums_call(
        functools.partial(shards_kernel, tile=tile),
        [w_out, w_up, w_down],
        [
            jax.ShapeDtypeStruct(w_out.shape, BF16),
            jax.ShapeDtypeStruct(w_up.shape, BF16),
            jax.ShapeDtypeStruct(w_up.shape, BF16),
        ],
        pieces_qkv[0],
        "mlp_shards",
    )
    full_out = lax.all_gather(swap(shard_out), ("a", "h"), axis=0, tiled=True)
    full_second = lax.all_gather(swap(shard_second), ("a", "h"), axis=0, tiled=True)
    pieces_first = gather(shard_first)
    own_input = swap(block_input)
    segments = swap(segment_ids)
    own_grad = swap(out_grad)
    bias_query = lax.dynamic_slice_in_dim(b_query, rank * head_width, head_width)
    bias_value = lax.dynamic_slice_in_dim(b_value, rank * head_width, head_width)
    bias_up = lax.dynamic_slice_in_dim(b_up, rank * unit_width, unit_width)

    rows_in = tp_gather(own_input)
    grad_rows = tp_gather(own_grad)
    grad_rows_t = grad_rows.T
    normed, normed_t = norm_rows(rows_in, ln1_gain, ln1_bias)
    biases = jnp.concatenate([bias_query, jnp.zeros((head_width,), F32), bias_value])
    qkv, full_qkv = qkv_project(order, normed, pieces_qkv, biases)
    mixed, lse = attn_forward(segments, qkv, head_width)
    attended = tp_terms(dot_nt(mixed, full_out).astype(BF16))
    normed_two, normed_two_t, hidden = norm_rows(rows_in, ln2_gain, ln2_bias, attended, b_out)

    out_part, gn_part, first_grads, bias_first = mlp(
        order, normed_two, grad_rows, normed_two_t, grad_rows_t, pieces_first,
        bias_up[:half_units], (), False,
    )
    first_mlp = lax.psum_scatter(
        swap(first_grads[0], inverse=True), ("a", "c"), scatter_dimension=0, tiled=True
    )
    out_part, gn_part, second_grads, bias_second = mlp(
        order, normed_two, grad_rows, normed_two_t, grad_rows_t, [full_second],
        bias_up[half_units:], (out_part, gn_part), True,
    )
    second_received = first_sends(second_grads)
    own_output = (own(hidden) + tp_scatter(out_part) + b_down).astype(BF16)
    output = swap(own_output, inverse=True)

    grad_hidden, grad_attended, grad_attended_t, sums_two = norm_back_rows(
        hidden, grad_rows, tp_terms(gn_part), ln2_gain
    )
    grad_mixed = dot_nn(grad_attended, full_out).astype(BF16)
    out_grads = weight_grads(order, grad_attended_t, mixed[None], grad_mixed)
    out_received = first_sends(out_grads)

    grads = attn_backward(segments, qkv, mixed, lse, grad_mixed, head_width, out_grads[0])
    grad_normed_part = []

    def after_unit_sums(y_sum):
        pieces = weight_grads(order, normed_t, grads, y_sum)
        grad_normed_part.append((pieces, qkv_back(grads, full_qkv, pieces[0])))
        return grad_normed_part[0][1]

    _, unit_parts = finish(
        [second_grads, out_grads], [second_received, out_received], grads, after_unit_sums, "unit"
    )
    qkv_grads, grad_normed_part = grad_normed_part[0]
    qkv_done, qkv_parts = finish(
        [qkv_grads], [first_sends(qkv_grads)], None, lambda y_sum: None, "qkv"
    )
    shard = lambda columns: jax.ShapeDtypeStruct((w_query.shape[0], columns), F32)
    grad_w_up, grad_w_down, grad_w_out = sums_call(
        functools.partial(
            last_sums_kernel, far=len(unit_parts), half_tile=tile, head_width=head_width
        ),
        unit_parts + [first_mlp],
        [shard(unit_width), shard(unit_width), shard(head_width)],
        None,
        "unit_sums_last",
    )
    late = sums_call(qkv_last_kernel, qkv_parts, [shard(head_width)] * 3, None, "qkv_sums_last")
    grad_normed = tp_scatter(grad_normed_part)
    own_scaled, own_inverse = normalize(own_input.astype(F32))
    grad_own = own(grad_hidden) + norm_back(grad_normed, own_scaled, own_inverse, ln1_gain)
    grad_input = swap(grad_own.astype(BF16), inverse=True)

    def place_part(values, full):
        return lax.dynamic_update_slice_in_dim(
            jnp.zeros((full,), F32), values, rank * values.shape[0], 0
        )

    sums = jnp.concatenate(
        [
            jnp.sum(grad_normed * own_scaled, axis=0),
            jnp.sum(grad_normed, axis=0),
            place_part(jnp.sum(grads[0].astype(F32), axis=0), width),
            place_part(jnp.sum(grads[2].astype(F32), axis=0), width),
            (sums_two[:3] * (1.0 / ranks)).reshape(-1),
            jnp.sum(own_grad.astype(F32), axis=0),
            place_part(jnp.concatenate([bias_first[0], bias_second[0]]), b_up.shape[0]),
        ]
    ).reshape(-1, LANES)
    (sums,) = sums_call(
        copy_kernel, [sums], [jax.ShapeDtypeStruct(sums.shape, F32)], qkv_done, "small_sums"
    )
    sums = sum_all(sums).reshape(-1)
    small = [sums[i * width : (i + 1) * width] for i in range(8)]
    return (
        output, grad_input, small[0], small[1],
        late[0], late[1], late[2], small[2], small[3], grad_w_out, small[4], small[5], small[6],
        grad_w_up, sums[8 * width :], grad_w_down, small[7],
    )


def solution(mesh):
    groups, ranks = mesh.shape["dp"], mesh.shape["tensor"]
    sizes = {"a": groups // 2, "c": 2, "h": 2, "l": ranks // 2}
    fine = Mesh(mesh.devices.reshape(tuple(sizes.values())), tuple(sizes))
    rows = P(("a", "c", "h", "l"), None)
    block = P(("a", "c"), ("h", "l"))
    return jax.shard_map(
        functools.partial(per_device, sizes),
        mesh=fine,
        in_specs=(
            rows, P(("a", "c")), P(), P(), block, block, block, P(), P(), block, P(), P(), P(),
            block, P(), block, P(), rows,
        ),
        out_specs=(
            rows, rows, P(), P(), block, block, block, P(), P(), block, P(), P(), P(), block, P(),
            block, P(),
        ),
        check_vma=False,
    )
```

profile of v0, /device:TPU:17, one launch (start us, length us, event | category | flops | bytes accessed | tf_op | source)
XLA Modules:
  0.0 494.8 jit_solution(12742868190071701443)
XLA Ops:
  11.6 3.6 collective-permute-start.5
  15.2 11.4 %collective-permute-done.4 = bf16[64,1536]{1,0:T(8,128)(2,1)S(1)} collective-permute-done((bf16[64,1536]{1,0:T(8,128)(2,1)S(1)}, bf16[64,1536]{1,0:T(8,128)(2,1)S(1)}, u32[]{:S(2)}, u32[]{:S(2)}) %collective-permute-start.4) | collective-permute-done | bytes 196640 | tf_op jit(solution)/shard_map/ppermute | solution.py:705
  36.8 14.9 %collective-permute-done.15 = bf16[64,2048]{1,0:T(8,128)(2,1)S(1)} collective-permute-done((bf16[64,2048]{1,0:T(8,128)(2,1)}, bf16[64,2048]{1,0:T(8,128)(2,1)S(1)}, u32[]{:S(2)}, u32[]{:S(2)}) %collective-permute-start.15) | collective-permute-done | bytes 262176 | tf_op jit(solution)/shard_map/ppermute | solution.py:697
  52.5 4.0 collective-permute-start.1
  61.3 17.5 %collective-permute-done.2 = s32[1024]{0:T(1024)S(1)} collective-permute-done((s32[1024]{0:T(1024)S(1)}, s32[1024]{0:T(1024)S(1)}, u32[]{:S(2)}, u32[]{:S(2)}) %collective-permute-start.2) | collective-permute-done | bytes 4128 | tf_op jit(solution)/shard_map/ppermute | solution.py:697
  86.2 2.7 collective-permute-start.9
  90.5 4.2 collective-permute-start.18
  97.0 5.0 %norm_one.1 = (bf16[1024,1024]{1,0:T(8,128)(2,1)}, bf16[1024,1024]{1,0:T(8,128)(2,1)}) custom-call(bf16[1024,1024]{1,0:T(8,128)(2,1)} %maximum_select_fusion.refs_0_, f32[1,1024]{1,0:T(1,128)} %bitcast.55, f32[1,1024]{1,0:T(1,128)} %bitcast.61), custom_call_target="tpu_custom_call" | custom-call | flops 20971520 | bytes 14680064 | tf_op jit(solution)/shard_map/norm_one/pallas_call | solution.py:275
  102.0 11.2 %collective-permute-done.9.low = bf16[128,1536]{1,0:T(8,128)(2,1)} collective-permute-done((bf16[128,1536]{1,0:T(8,128)(2,1)S(1)}, bf16[128,1536]{1,0:T(8,128)(2,1)}, u32[]{:S(2)}, u32[]{:S(2)}) %collective-permute-start.9) | collective-permute-done | bytes 393248 | tf_op jit(solution)/shard_map/ppermute | solution.py:713
  113.2 8.5 %qkv_project.1 = (bf16[1024,1536]{1,0:T(8,128)(2,1)}, bf16[1024,1536]{1,0:T(8,128)(2,1)}) custom-call(s32[16]{0:T(128)} %stack.67.order.refs_0_, bf16[1024,1024]{1,0:T(8,128)(2,1)} %get-tuple-element.73.n_ref, f32[1,1536]{1,0:T(1,128)} %reshape.111.b_ref, bf16[256,1536]{1,0:T(8,128)(2,1)} %copy-done.7, bf16[256,1536]{1,0:T(8,128)(2,1)} %collective-permute-done.7.by_y, ...), custom_call_target="tpu_custom_call" | custom-call | flops 3221225472 | bytes 11534336 | tf_op jit(solution)/shard_map/qkv_project/pallas_call | solution.py:480
  121.7 16.4 %attn_forward.1 = (bf16[1024,512]{1,0:T(8,128)(2,1)}, f32[4,8,1024]{2,1,0:T(8,128)}) custom-call(s32[1024,1]{1,0:T(8,128)} %copy.37.seg_col.refs_0_, s32[1,1024]{1,0:T(1,128)} %bitcast.57, bf16[1024,1536]{1,0:T(8,128)(2,1)} %get-tuple-element.74.q_ref.k_ref.v_ref.refs_2_.refs_3_.refs_4_, ...), custom_call_target="tpu_custom_call" | custom-call | flops 2147483648 | bytes 4194304 | tf_op jit(solution)/shard_map/attn_forward/pallas_call | solution.py:156
  138.1 4.2 convolution_convert_fusion.refs_1_
  142.4 3.4 collective-permute-start.12
  149.4 37.1 %collective-permute-done.21.refs_2_ = bf16[256,2048]{1,0:T(8,128)(2,1)S(1)} collective-permute-done((bf16[256,2048]{1,0:T(8,128)(2,1)S(1)}, bf16[256,2048]{1,0:T(8,128)(2,1)S(1)}, u32[]{:S(2)}, u32[]{:S(2)}) %collective-permute-start.21) | collective-permute-done | bytes 1048608 | tf_op jit(solution)/shard_map/ppermute | solution.py:713
  192.1 3.4 maximum_select_fusion.1.g_ref
  195.4 2.7 copy.39.gt_ref
  198.1 7.3 %norm_two.1 = (bf16[1024,1024]{1,0:T(8,128)(2,1)}, bf16[1024,1024]{1,0:T(8,128)(2,1)}, f32[1024,1024]{1,0:T(8,128)}) custom-call(bf16[1024,1024]{1,0:T(8,128)(2,1)} %maximum_select_fusion.refs_0_, bf16[1024,1024]{1,0:T(8,128)(2,1)} %convolution_convert_fusion.refs_1_, bf16[1024,1024]{1,0:T(8,128)(2,1)} %collective-permute-done.12.refs_2_, ...), custom_call_target="tpu_custom_call" | custom-call | flops 20971520 | bytes 14680064 | tf_op jit(solution)/shard_map/norm_two/pallas_call | solution.py:275
  205.4 24.3 %mlp_first.1 = (bf16[1024,1024]{1,0:T(8,128)(2,1)}, bf16[1024,1024]{1,0:T(8,128)(2,1)}, bf16[1024,2048]{1,0:T(8,128)(2,1)}, f32[1,1024]{1,0:T(1,128)}) custom-call(s32[16]{0:T(128)} %stack.67.order.refs_0_, bf16[1024,1024]{1,0:T(8,128)(2,1)} %get-tuple-element.78.n_ref, bf16[1024,1024]{1,0:T(8,128)(2,1)} %copy-done, ...), custom_call_target="tpu_custom_call" | custom-call | flops 12884901888 | bytes 20971520 | tf_op jit(solution)/shard_map/mlp_first/pallas_call | solution.py:422
  231.3 25.4 %mlp_second.1 = (bf16[1024,1024]{1,0:T(8,128)(2,1)}, bf16[1024,1024]{1,0:T(8,128)(2,1)}, bf16[256,2048]{1,0:T(8,128)(2,1)}, bf16[256,2048]{1,0:T(8,128)(2,1)}, b...) custom-call(s32[16]{0:T(128)} %stack.67.order.refs_0_, ...), custom_call_target="tpu_custom_call" | custom-call | flops 12884901888 | bytes 20971520 | tf_op jit(solution)/shard_map/mlp_second/pallas_call | solution.py:422
  258.9 18.5 %collective-permute-done.52 = bf16[1024,2048]{1,0:T(8,128)(2,1)} collective-permute-done((bf16[1024,2048]{1,0:T(8,128)(2,1)}, bf16[1024,2048]{1,0:T(8,128)(2,1)}, u32[]{:S(2)}, u32[]{:S(2)}) %collective-permute-start.52) | collective-permute-done | bytes 4194336 | tf_op jit(solution)/shard_map/ppermute | solution.py:697
  280.7 5.3 %collective-permute-start.24 = (bf16[512,1024]{1,0:T(8,128)(2,1)}, bf16[512,1024]{1,0:T(8,128)(2,1)}, u32[]{:S(2)}, u32[]{:S(2)}) collective-permute-start(bf16[512,1024]{1,0:T(8,128)(2,1)} %constant_dynamic-slice_fusion), channel_id=1, source_target_pairs={{0,2},{2,0},{1,3},{3,1},{4,6},{6,4},{5,7},{7,5},{8,10},{10,8},{9,1... | collective-permute-start | bytes 3145736 | tf_op jit(solution)/shard_map/ppermute | solution.py:782
  286.0 9.4 %norm_two_back.1 = (f32[1024,1024]{1,0:T(8,128)}, bf16[1024,1024]{1,0:T(8,128)(2,1)}, bf16[1024,1024]{1,0:T(8,128)(2,1)}, f32[8,1024]{1,0:T(8,128)}) custom-call(f32[1024,1024]{1,0:T(8,128)} %get-tuple-element.77.hidden_ref, bf16[1024,1024]{1,0:T(8,128)(2,1)} %copy-done, bf16[1024,1024]{1,0:T(8,128)(2,1)} %get-tuple-element.85.own_ref, ...), custom_call_target="tpu_custom_call" | custom-call | flops 31457280 | bytes 16777216 | tf_op jit(solution)/shard_map/norm_two_back/pallas_call | solution.py:315
  295.4 4.3 convolution_convert_fusion.1.refs_3_.refs_7_
  299.6 4.9 weight_grads.2
  305.8 24.2 %attn_backward.1.refs_0_.refs_2_ = bf16[3,1024,512]{2,1,0:T(8,128)(2,1)} custom-call(s32[1024,1]{1,0:T(8,128)} %copy.37.seg_col.refs_0_, s32[1,1024]{1,0:T(1,128)} %bitcast.58, bf16[1024,1536]{1,0:T(8,128)(2,1)} %get-tuple-element.74.q_ref.k_ref.v_ref.refs_2_.refs_3_.refs_4_, bf16[1024,1536]{1,0:T(8,128)(2,1)} %get-tuple-element.74.q_ref.k_ref.v_ref.refs_2_.refs_3_.refs_4_, ...), custom_call_target="tpu_custom_call" | custom-call | flops 5368709120 | bytes 8388608 | tf_op jit(solution)/shard_map/attn_backward/pallas_call | solution.py:185
  331.5 3.4 unit_sums_one.1
  334.9 7.8 %weight_grads.3 = (bf16[256,1536]{1,0:T(8,128)(2,1)}, bf16[256,1536]{1,0:T(8,128)(2,1)}, bf16[128,1536]{1,0:T(8,128)(2,1)}, bf16[128,1536]{1,0:T(8,128)(2,1)}, bf16[256,1536]{1,0:T(8,128)(2,1)}) custom-call(s32[16]{0:T(128)} %stack.67.order.refs_0_, bf16[1024,1024]{1,0:T(8,128)(2,1)} %get-tuple-element.92.refs_1_, ...), custom_call_target="tpu_custom_call" | custom-call | flops 3221225472 | bytes 8388608 | tf_op jit(solution)/shard_map/weight_grads/pallas_call | solution.py:526
  342.7 7.4 %qkv_back.1.refs_0_ = bf16[1024,1024]{1,0:T(8,128)(2,1)} custom-call(bf16[3,1024,512]{2,1,0:T(8,128)(2,1)} %attn_backward.1.refs_0_.refs_2_, bf16[1024,1536]{1,0:T(8,128)(2,1)} %get-tuple-element.91.refs_1_, bf16[256,1536]{1,0:T(8,128)(2,1)} %get-tuple-element.101.refs_2_), custom_call_target="tpu_custom_call" | custom-call | flops 3221225472 | bytes 8388608 | tf_op jit(solution)/shard_map/qkv_back/pallas_call | solution.py:566
  350.1 2.4 constant_dynamic-slice_fusion.1
  356.3 3.5 add_convert_fusion
  365.5 9.7 %collective-permute-done.34.refs_1_ = bf16[256,1536]{1,0:T(8,128)(2,1)} collective-permute-done((bf16[256,1536]{1,0:T(8,128)(2,1)}, bf16[256,1536]{1,0:T(8,128)(2,1)}, u32[]{:S(2)}, u32[]{:S(2)}) %collective-permute-start.34) | collective-permute-done | bytes 786464 | tf_op jit(solution)/shard_map/ppermute | solution.py:713
  375.3 2.6 qkv_sums_one.1
  379.6 2.4 fusion.10
  382.1 3.7 fusion.9
  385.9 11.7 %collective-permute-done.35.refs_3_ = bf16[128,1536]{1,0:T(8,128)(2,1)S(1)} collective-permute-done((bf16[128,1536]{1,0:T(8,128)(2,1)}, bf16[128,1536]{1,0:T(8,128)(2,1)S(1)}, u32[]{:S(2)}, u32[]{:S(2)}) %collective-permute-start.35) | collective-permute-done | bytes 393248 | tf_op jit(solution)/shard_map/ppermute | solution.py:713
  398.7 9.1 %collective-permute-done.36.refs_4_ = bf16[128,1536]{1,0:T(8,128)(2,1)S(1)} collective-permute-done((bf16[128,1536]{1,0:T(8,128)(2,1)}, bf16[128,1536]{1,0:T(8,128)(2,1)S(1)}, u32[]{:S(2)}, u32[]{:S(2)}) %collective-permute-start.36) | collective-permute-done | bytes 393248 | tf_op jit(solution)/shard_map/ppermute | solution.py:713
  408.5 2.9 qkv_sums_two.1
  416.8 3.2 collective-permute-done.38
  420.3 2.7 collective-permute-done.39
  431.1 5.0 %collective-permute-start.41 = (f32[96,128]{1,0:T(8,128)S(1)}, f32[96,128]{1,0:T(8,128)S(1)}, u32[]{:S(2)}, u32[]{:S(2)}) collective-permute-start(f32[96,128]{1,0:T(8,128)S(1)} %add.145), channel_id=1, source_target_pairs={{0,16},{1,17},{2,18},{3,19},{4,20},{5,21},{6,22},{7,23},{8,24},{9,... | collective-permute-start | bytes 147464 | tf_op jit(solution)/shard_map/ppermute | solution.py:713
  436.1 3.8 unit_sums_two.1
  440.0 3.4 collective-permute-start.48
  443.4 4.8 collective-permute-done.45.refs_3_
  448.3 3.7 collective-permute-start.50
  455.2 4.6 collective-permute-done.49.refs_1_
  459.8 14.1 %collective-permute-done.50.refs_2_ = bf16[64,2560]{1,0:T(8,128)(2,1)S(1)} collective-permute-done((bf16[64,2560]{1,0:T(8,128)(2,1)}, bf16[64,2560]{1,0:T(8,128)(2,1)S(1)}, u32[]{:S(2)}, u32[]{:S(2)}) %collective-permute-start.50) | collective-permute-done | bytes 327712 | tf_op jit(solution)/shard_map/ppermute | solution.py:705
  473.9 7.7 %collective-permute-done.51.refs_3_ = bf16[64,2560]{1,0:T(8,128)(2,1)S(1)} collective-permute-done((bf16[64,2560]{1,0:T(8,128)(2,1)}, bf16[64,2560]{1,0:T(8,128)(2,1)S(1)}, u32[]{:S(2)}, u32[]{:S(2)}) %collective-permute-start.51) | collective-permute-done | bytes 327712 | tf_op jit(solution)/shard_map/ppermute | solution.py:705
  482.4 2.4 unit_sums_last.1
  (242 shorter events, 84.4 us)
Async XLA Ops:
  7.2 130.9 %all-gather.3.cloned.1.call-start = ((), (), s32[]{:S(2)}) async-start(), calls=%async_computation.1 | async-start | bytes 1114112 | tf_op jit(solution)/shard_map/all_gather | solution.py:821
  11.0 17.8 %collective-permute-start.6 = (bf16[64,1536]{1,0:T(8,128)(2,1)S(1)}, bf16[64,1536]{1,0:T(8,128)(2,1)S(1)}, u32[]{:S(2)}, u32[]{:S(2)}) collective-permute-start(bf16[64,1536]{1,0:T(8,128)(2,1)S(1)} %constant_dynamic-update-slice_fusion), channel_id=1, source_target_pairs={{0,26},{1,24},{2,27},{3,25},{4,30},{5,28},{6,31},{7,29},{8,18},{9,... | collective-permute-start | bytes 589832 | tf_op jit(solution)/shard_map/ppermute | solution.py:705
  11.6 17.2 %collective-permute-start.5 = (bf16[64,1536]{1,0:T(8,128)(2,1)S(1)}, bf16[64,1536]{1,0:T(8,128)(2,1)S(1)}, u32[]{:S(2)}, u32[]{:S(2)}) collective-permute-start(bf16[64,1536]{1,0:T(8,128)(2,1)S(1)} %constant_dynamic-update-slice_fusion), channel_id=1, source_target_pairs={{0,18},{1,16},{2,19},{3,17},{4,22},{5,20},{6,23},{7,21},{8,26},{9,... | collective-permute-start | bytes 589832 | tf_op jit(solution)/shard_map/ppermute | solution.py:705
  34.6 196.7 %all-gather.5.cloned.1.call-start = ((), (), s32[]{:S(2)}) async-start(), calls=%async_computation.2 | async-start | bytes 4456448 | tf_op jit(solution)/shard_map/all_gather | solution.py:822
  34.7 17.8 %collective-permute-start = (bf16[512,1024]{1,0:T(8,128)(2,1)}, bf16[512,1024]{1,0:T(8,128)(2,1)S(1)}, u32[]{:S(2)}, u32[]{:S(2)}) collective-permute-start(bf16[512,1024]{1,0:T(8,128)(2,1)} %param.18), channel_id=1, source_target_pairs={{0,2},{1,0},{2,3},{3,1},{4,6},{5,4},{6,7},{7,5},{8,10},{9,8},{10,1... | collective-permute-start | bytes 3145736 | tf_op jit(solution)/shard_map/ppermute | solution.py:697
  36.4 15.4 %collective-permute-start.15 = (bf16[64,2048]{1,0:T(8,128)(2,1)}, bf16[64,2048]{1,0:T(8,128)(2,1)S(1)}, u32[]{:S(2)}, u32[]{:S(2)}) collective-permute-start(bf16[64,2048]{1,0:T(8,128)(2,1)} %get-tuple-element.80), channel_id=1, source_target_pairs={{0,2},{1,0},{2,3},{3,1},{4,6},{5,4},{6,7},{7,5},{8,10},{9,8},{10,1... | collective-permute-start | bytes 786440 | tf_op jit(solution)/shard_map/ppermute | solution.py:697
  52.4 429.2 %reduce-scatter.2.cloned.1.call-start = ((), (), s32[]{:S(2)}) async-start(), calls=%async_computation.3 | async-start | bytes 4456448 | tf_op jit(solution)/shard_map/reduce_scatter | solution.py:845
  52.5 38.0 %collective-permute-start.1 = (bf16[512,1024]{1,0:T(8,128)(2,1)S(1)}, bf16[512,1024]{1,0:T(8,128)(2,1)S(1)}, u32[]{:S(2)}, u32[]{:S(2)}) collective-permute-start(bf16[512,1024]{1,0:T(8,128)(2,1)S(1)} %collective-permute-done), channel_id=1, source_target_pairs={{0,2},{2,0},{1,3},{3,1},{4,6},{6,4},{5,7},{7,5},{8,10},{10,8},{9,1... | collective-permute-start | bytes 3145736 | tf_op jit(solution)/shard_map/ppermute | solution.py:782
  56.5 25.3 %collective-permute-start.8 = (bf16[256,1536]{1,0:T(8,128)(2,1)}, bf16[256,1536]{1,0:T(8,128)(2,1)}, u32[]{:S(2)}, u32[]{:S(2)}) collective-permute-start(bf16[256,1536]{1,0:T(8,128)(2,1)} %copy-done.7), channel_id=1, source_target_pairs={{0,1},{1,0},{2,3},{3,2},{4,5},{5,4},{6,7},{7,6},{8,9},{9,8},{10,11... | collective-permute-start | bytes 2359304 | tf_op jit(solution)/shard_map/ppermute | solution.py:713
  56.5 27.3 %collective-permute-start.7 = (bf16[256,1536]{1,0:T(8,128)(2,1)}, bf16[256,1536]{1,0:T(8,128)(2,1)}, u32[]{:S(2)}, u32[]{:S(2)}) collective-permute-start(bf16[256,1536]{1,0:T(8,128)(2,1)} %copy-done.7), channel_id=1, source_target_pairs={{0,4},{1,5},{2,6},{3,7},{4,0},{5,1},{6,2},{7,3},{8,12},{9,13},{10,... | collective-permute-start | bytes 2359304 | tf_op jit(solution)/shard_map/ppermute | solution.py:713
  57.7 28.4 %collective-permute-start.16 = (bf16[64,2048]{1,0:T(8,128)(2,1)}, bf16[64,2048]{1,0:T(8,128)(2,1)}, u32[]{:S(2)}, u32[]{:S(2)}) collective-permute-start(bf16[64,2048]{1,0:T(8,128)(2,1)} %get-tuple-element.81), channel_id=1, source_target_pairs={{0,2},{1,0},{2,3},{3,1},{4,6},{5,4},{6,7},{7,5},{8,10},{9,8},{10,1... | collective-permute-start | bytes 786440 | tf_op jit(solution)/shard_map/ppermute | solution.py:705
  59.2 19.6 %collective-permute-start.2 = (s32[1024]{0:T(1024)S(1)}, s32[1024]{0:T(1024)S(1)}, u32[]{:S(2)}, u32[]{:S(2)}) collective-permute-start(s32[1024]{0:T(1024)S(1)} %copy-done.45), channel_id=1, source_target_pairs={{0,2},{1,0},{2,3},{3,1},{4,6},{5,4},{6,7},{7,5},{8,10},{9,8},{10,1... | collective-permute-start | bytes 12296 | tf_op jit(solution)/shard_map/ppermute | solution.py:697
  78.8 70.3 %collective-permute-start.13 = (bf16[512,1024]{1,0:T(8,128)(2,1)}, bf16[512,1024]{1,0:T(8,128)(2,1)S(1)}, u32[]{:S(2)}, u32[]{:S(2)}) collective-permute-start(bf16[512,1024]{1,0:T(8,128)(2,1)} %param.35), channel_id=1, source_target_pairs={{0,2},{1,0},{2,3},{3,1},{4,6},{5,4},{6,7},{7,5},{8,10},{9,8},{10,1... | collective-permute-start | bytes 3145736 | tf_op jit(solution)/shard_map/ppermute | solution.py:697
  81.8 65.0 %collective-permute-start.19 = (bf16[64,2048]{1,0:T(8,128)(2,1)}, bf16[64,2048]{1,0:T(8,128)(2,1)}, u32[]{:S(2)}, u32[]{:S(2)}) collective-permute-start(bf16[64,2048]{1,0:T(8,128)(2,1)} %get-tuple-element.81), channel_id=1, source_target_pairs={{0,26},{1,24},{2,27},{3,25},{4,30},{5,28},{6,31},{7,29},{8,18},{9,... | collective-permute-start | bytes 786440 | tf_op jit(solution)/shard_map/ppermute | solution.py:705
  83.8 18.2 %collective-permute-start.10 = (bf16[128,1536]{1,0:T(8,128)(2,1)S(1)}, bf16[128,1536]{1,0:T(8,128)(2,1)}, u32[]{:S(2)}, u32[]{:S(2)}) collective-permute-start(bf16[128,1536]{1,0:T(8,128)(2,1)S(1)} %slice.109), channel_id=1, source_target_pairs={{0,4},{1,5},{2,6},{3,7},{4,0},{5,1},{6,2},{7,3},{8,12},{9,13},{10,... | collective-permute-start | bytes 1179656 | tf_op jit(solution)/shard_map/ppermute | solution.py:713
  86.2 27.1 %collective-permute-start.9 = (bf16[128,1536]{1,0:T(8,128)(2,1)S(1)}, bf16[128,1536]{1,0:T(8,128)(2,1)}, u32[]{:S(2)}, u32[]{:S(2)}) collective-permute-start(bf16[128,1536]{1,0:T(8,128)(2,1)S(1)} %slice.108), channel_id=1, source_target_pairs={{0,1},{1,0},{2,3},{3,2},{4,5},{5,4},{6,7},{7,6},{8,9},{9,8},{10,11... | collective-permute-start | bytes 1179656 | tf_op jit(solution)/shard_map/ppermute | solution.py:713
  90.5 55.3 %collective-permute-start.18 = (bf16[64,2048]{1,0:T(8,128)(2,1)}, bf16[64,2048]{1,0:T(8,128)(2,1)}, u32[]{:S(2)}, u32[]{:S(2)}) collective-permute-start(bf16[64,2048]{1,0:T(8,128)(2,1)} %get-tuple-element.81), channel_id=1, source_target_pairs={{0,18},{1,16},{2,19},{3,17},{4,22},{5,20},{6,23},{7,21},{8,26},{9,... | collective-permute-start | bytes 786440 | tf_op jit(solution)/shard_map/ppermute | solution.py:705
  102.0 43.8 %collective-permute-start.17 = (bf16[64,2048]{1,0:T(8,128)(2,1)}, bf16[64,2048]{1,0:T(8,128)(2,1)S(1)}, u32[]{:S(2)}, u32[]{:S(2)}) collective-permute-start(bf16[64,2048]{1,0:T(8,128)(2,1)} %get-tuple-element.81), channel_id=1, source_target_pairs={{0,10},{1,8},{2,11},{3,9},{4,14},{5,12},{6,15},{7,13},{8,2},{9,0},... | collective-permute-start | bytes 786440 | tf_op jit(solution)/shard_map/ppermute | solution.py:705
  142.4 55.8 %collective-permute-start.12 = (bf16[1024,1024]{1,0:T(8,128)(2,1)}, bf16[1024,1024]{1,0:T(8,128)(2,1)}, u32[]{:S(2)}, u32[]{:S(2)}) collective-permute-start(bf16[1024,1024]{1,0:T(8,128)(2,1)} %convolution_convert_fusion.refs_1_), channel_id=1, source_target_pairs={{0,2},{2,0},{1,3},{3,1},{4,6},{6,4},{5,7},{7,5},{8,10},{10,8},{9,1... | collective-permute-start | bytes 6291464 | tf_op jit(solution)/shard_map/ppermute | solution.py:782
  147.8 38.8 %collective-permute-start.21 = (bf16[256,2048]{1,0:T(8,128)(2,1)S(1)}, bf16[256,2048]{1,0:T(8,128)(2,1)S(1)}, u32[]{:S(2)}, u32[]{:S(2)}) collective-permute-start(bf16[256,2048]{1,0:T(8,128)(2,1)S(1)} %constant_dynamic-update-slice_fusion.7.refs_0_), channel_id=1, source_target_pairs={{0,1},{1,0},{2,3},{3,2},{4,5},{5,4},{6,7},{7,6},{8,9},{9,8},{10,11... | collective-permute-start | bytes 3145736 | tf_op jit(solution)/shard_map/ppermute | solution.py:713
  147.9 41.7 %collective-permute-start.20 = (bf16[256,2048]{1,0:T(8,128)(2,1)S(1)}, bf16[256,2048]{1,0:T(8,128)(2,1)S(1)}, u32[]{:S(2)}, u32[]{:S(2)}) collective-permute-start(bf16[256,2048]{1,0:T(8,128)(2,1)S(1)} %constant_dynamic-update-slice_fusion.7.refs_0_), channel_id=1, source_target_pairs={{0,4},{1,5},{2,6},{3,7},{4,0},{5,1},{6,2},{7,3},{8,12},{9,13},{10,... | collective-permute-start | bytes 3145736 | tf_op jit(solution)/shard_map/ppermute | solution.py:713
  149.1 42.9 %collective-permute-start.14 = (bf16[512,1024]{1,0:T(8,128)(2,1)S(1)}, bf16[512,1024]{1,0:T(8,128)(2,1)}, u32[]{:S(2)}, u32[]{:S(2)}) collective-permute-start(bf16[512,1024]{1,0:T(8,128)(2,1)S(1)} %collective-permute-done.13), channel_id=1, source_target_pairs={{0,2},{2,0},{1,3},{3,1},{4,6},{6,4},{5,7},{7,5},{8,10},{10,8},{9,1... | collective-permute-start | bytes 3145736 | tf_op jit(solution)/shard_map/ppermute | solution.py:782
  188.3 17.1 %collective-permute-start.23 = (bf16[128,2048]{1,0:T(8,128)(2,1)}, bf16[128,2048]{1,0:T(8,128)(2,1)}, u32[]{:S(2)}, u32[]{:S(2)}) collective-permute-start(bf16[128,2048]{1,0:T(8,128)(2,1)} %slice.111), channel_id=1, source_target_pairs={{0,4},{1,5},{2,6},{3,7},{4,0},{5,1},{6,2},{7,3},{8,12},{9,13},{10,... | collective-permute-start | bytes 1572872 | tf_op jit(solution)/shard_map/ppermute | solution.py:713
  191.3 14.1 %collective-permute-start.22 = (bf16[128,2048]{1,0:T(8,128)(2,1)}, bf16[128,2048]{1,0:T(8,128)(2,1)}, u32[]{:S(2)}, u32[]{:S(2)}) collective-permute-start(bf16[128,2048]{1,0:T(8,128)(2,1)} %slice.110), channel_id=1, source_target_pairs={{0,1},{1,0},{2,3},{3,2},{4,5},{5,4},{6,7},{7,6},{8,9},{9,8},{10,11... | collective-permute-start | bytes 1572872 | tf_op jit(solution)/shard_map/ppermute | solution.py:713
  229.7 47.7 %collective-permute-start.52 = (bf16[1024,2048]{1,0:T(8,128)(2,1)}, bf16[1024,2048]{1,0:T(8,128)(2,1)}, u32[]{:S(2)}, u32[]{:S(2)}) collective-permute-start(bf16[1024,2048]{1,0:T(8,128)(2,1)} %get-tuple-element.125), channel_id=1, source_target_pairs={{2,0},{0,1},{3,2},{1,3},{6,4},{4,5},{7,6},{5,7},{10,8},{8,9},{11,1... | collective-permute-start | bytes 12582920 | tf_op jit(solution)/shard_map/ppermute | solution.py:697
  256.8 29.2 %collective-permute-start.26 = (bf16[1024,1024]{1,0:T(8,128)(2,1)}, bf16[1024,1024]{1,0:T(8,128)(2,1)}, u32[]{:S(2)}, u32[]{:S(2)}) collective-permute-start(bf16[1024,1024]{1,0:T(8,128)(2,1)} %get-tuple-element.85.own_ref), channel_id=1, source_target_pairs={{0,2},{2,0},{1,3},{3,1},{4,6},{6,4},{5,7},{7,5},{8,10},{10,8},{9,1... | collective-permute-start | bytes 6291464 | tf_op jit(solution)/shard_map/ppermute | solution.py:782
  278.1 51.9 %collective-permute-start.27 = (bf16[256,2048]{1,0:T(8,128)(2,1)}, bf16[256,2048]{1,0:T(8,128)(2,1)S(1)}, u32[]{:S(2)}, u32[]{:S(2)}) collective-permute-start(bf16[256,2048]{1,0:T(8,128)(2,1)} %get-tuple-element.93), channel_id=1, source_target_pairs={{0,1},{1,0},{2,3},{3,2},{4,5},{5,4},{6,7},{7,6},{8,9},{9,8},{10,11... | collective-permute-start | bytes 3145736 | tf_op jit(solution)/shard_map/ppermute | solution.py:713
  278.2 51.8 %collective-permute-start.28 = (bf16[256,2048]{1,0:T(8,128)(2,1)}, bf16[256,2048]{1,0:T(8,128)(2,1)S(1)}, u32[]{:S(2)}, u32[]{:S(2)}) collective-permute-start(bf16[256,2048]{1,0:T(8,128)(2,1)} %get-tuple-element.94), channel_id=1, source_target_pairs={{0,4},{1,5},{2,6},{3,7},{4,0},{5,1},{6,2},{7,3},{8,12},{9,13},{10,... | collective-permute-start | bytes 3145736 | tf_op jit(solution)/shard_map/ppermute | solution.py:713
  280.7 75.5 %collective-permute-start.24 = (bf16[512,1024]{1,0:T(8,128)(2,1)}, bf16[512,1024]{1,0:T(8,128)(2,1)}, u32[]{:S(2)}, u32[]{:S(2)}) collective-permute-start(bf16[512,1024]{1,0:T(8,128)(2,1)} %constant_dynamic-slice_fusion), channel_id=1, source_target_pairs={{0,2},{2,0},{1,3},{3,1},{4,6},{6,4},{5,7},{7,5},{8,10},{10,8},{9,1... | collective-permute-start | bytes 3145736 | tf_op jit(solution)/shard_map/ppermute | solution.py:782
  304.5 25.5 %collective-permute-start.30 = (bf16[256,512]{1,0:T(8,128)(2,1)}, bf16[256,512]{1,0:T(8,128)(2,1)S(1)}, u32[]{:S(2)}, u32[]{:S(2)}) collective-permute-start(bf16[256,512]{1,0:T(8,128)(2,1)} %get-tuple-element.97), channel_id=1, source_target_pairs={{0,4},{1,5},{2,6},{3,7},{4,0},{5,1},{6,2},{7,3},{8,12},{9,13},{10,... | collective-permute-start | bytes 786440 | tf_op jit(solution)/shard_map/ppermute | solution.py:713
  305.7 24.3 %collective-permute-start.29 = (bf16[256,512]{1,0:T(8,128)(2,1)}, bf16[256,512]{1,0:T(8,128)(2,1)S(1)}, u32[]{:S(2)}, u32[]{:S(2)}) collective-permute-start(bf16[256,512]{1,0:T(8,128)(2,1)} %get-tuple-element.90.refs_8_), channel_id=1, source_target_pairs={{0,1},{1,0},{2,3},{3,2},{4,5},{5,4},{6,7},{7,6},{8,9},{9,8},{10,11... | collective-permute-start | bytes 786440 | tf_op jit(solution)/shard_map/ppermute | solution.py:713
  352.5 25.7 %collective-permute-start.31 = (bf16[512,1024]{1,0:T(8,128)(2,1)}, bf16[512,1024]{1,0:T(8,128)(2,1)}, u32[]{:S(2)}, u32[]{:S(2)}) collective-permute-start(bf16[512,1024]{1,0:T(8,128)(2,1)} %constant_dynamic-slice_fusion.1), channel_id=1, source_target_pairs={{0,2},{2,0},{1,3},{3,1},{4,6},{6,4},{5,7},{7,5},{8,10},{10,8},{9,1... | collective-permute-start | bytes 3145736 | tf_op jit(solution)/shard_map/ppermute | solution.py:782
  354.3 21.1 %collective-permute-start.33 = (bf16[256,1536]{1,0:T(8,128)(2,1)}, bf16[256,1536]{1,0:T(8,128)(2,1)}, u32[]{:S(2)}, u32[]{:S(2)}) collective-permute-start(bf16[256,1536]{1,0:T(8,128)(2,1)} %get-tuple-element.101.refs_2_), channel_id=1, source_target_pairs={{0,1},{1,0},{2,3},{3,2},{4,5},{5,4},{6,7},{7,6},{8,9},{9,8},{10,11... | collective-permute-start | bytes 2359304 | tf_op jit(solution)/shard_map/ppermute | solution.py:713
  356.0 19.2 %collective-permute-start.34 = (bf16[256,1536]{1,0:T(8,128)(2,1)}, bf16[256,1536]{1,0:T(8,128)(2,1)}, u32[]{:S(2)}, u32[]{:S(2)}) collective-permute-start(bf16[256,1536]{1,0:T(8,128)(2,1)} %get-tuple-element.102), channel_id=1, source_target_pairs={{0,4},{1,5},{2,6},{3,7},{4,0},{5,1},{6,2},{7,3},{8,12},{9,13},{10,... | collective-permute-start | bytes 2359304 | tf_op jit(solution)/shard_map/ppermute | solution.py:713
  359.8 64.6 %collective-permute-start.25 = (bf16[512,1024]{1,0:T(8,128)(2,1)}, bf16[512,1024]{1,0:T(8,128)(2,1)}, u32[]{:S(2)}, u32[]{:S(2)}) collective-permute-start(bf16[512,1024]{1,0:T(8,128)(2,1)} %add_convert_fusion), channel_id=1, source_target_pairs={{2,0},{0,1},{3,2},{1,3},{6,4},{4,5},{7,6},{5,7},{10,8},{8,9},{11,1... | collective-permute-start | bytes 3145736 | tf_op jit(solution)/shard_map/ppermute | solution.py:697
  364.2 63.7 %collective-permute-start.46 = (bf16[128,2560]{1,0:T(8,128)(2,1)}, bf16[128,2560]{1,0:T(8,128)(2,1)}, u32[]{:S(2)}, u32[]{:S(2)}) collective-permute-start(bf16[128,2560]{1,0:T(8,128)(2,1)} %get-tuple-element.100.refs_3_), channel_id=1, source_target_pairs={{0,4},{1,5},{2,6},{3,7},{4,0},{5,1},{6,2},{7,3},{8,12},{9,13},{10,... | collective-permute-start | bytes 1966088 | tf_op jit(solution)/shard_map/ppermute | solution.py:713
  375.2 50.8 %collective-permute-start.47 = (bf16[128,2560]{1,0:T(8,128)(2,1)}, bf16[128,2560]{1,0:T(8,128)(2,1)}, u32[]{:S(2)}, u32[]{:S(2)}) collective-permute-start(bf16[128,2560]{1,0:T(8,128)(2,1)} %get-tuple-element.120), channel_id=1, source_target_pairs={{0,1},{1,0},{2,3},{3,2},{4,5},{5,4},{6,7},{7,6},{8,9},{9,8},{10,11... | collective-permute-start | bytes 1966088 | tf_op jit(solution)/shard_map/ppermute | solution.py:713
  378.0 19.6 %collective-permute-start.35 = (bf16[128,1536]{1,0:T(8,128)(2,1)}, bf16[128,1536]{1,0:T(8,128)(2,1)S(1)}, u32[]{:S(2)}, u32[]{:S(2)}) collective-permute-start(bf16[128,1536]{1,0:T(8,128)(2,1)} %get-tuple-element.106), channel_id=1, source_target_pairs={{0,4},{1,5},{2,6},{3,7},{4,0},{5,1},{6,2},{7,3},{8,12},{9,13},{10,... | collective-permute-start | bytes 1179656 | tf_op jit(solution)/shard_map/ppermute | solution.py:713
  378.3 29.4 %collective-permute-start.36 = (bf16[128,1536]{1,0:T(8,128)(2,1)}, bf16[128,1536]{1,0:T(8,128)(2,1)S(1)}, u32[]{:S(2)}, u32[]{:S(2)}) collective-permute-start(bf16[128,1536]{1,0:T(8,128)(2,1)} %get-tuple-element.107), channel_id=1, source_target_pairs={{0,1},{1,0},{2,3},{3,2},{4,5},{5,4},{6,7},{7,6},{8,9},{9,8},{10,11... | collective-permute-start | bytes 1179656 | tf_op jit(solution)/shard_map/ppermute | solution.py:713
  397.5 57.7 %collective-permute-start.32 = (bf16[512,1024]{1,0:T(8,128)(2,1)}, bf16[512,1024]{1,0:T(8,128)(2,1)S(1)}, u32[]{:S(2)}, u32[]{:S(2)}) collective-permute-start(bf16[512,1024]{1,0:T(8,128)(2,1)} %fusion.9), channel_id=1, source_target_pairs={{2,0},{0,1},{3,2},{1,3},{6,4},{4,5},{7,6},{5,7},{10,8},{8,9},{11,1... | collective-permute-start | bytes 3145736 | tf_op jit(solution)/shard_map/ppermute | solution.py:697
  426.0 14.0 %collective-permute-start.44 = (bf16[64,1536]{1,0:T(8,128)(2,1)}, bf16[64,1536]{1,0:T(8,128)(2,1)S(1)}, u32[]{:S(2)}, u32[]{:S(2)}) collective-permute-start(bf16[64,1536]{1,0:T(8,128)(2,1)} %get-tuple-element.113), channel_id=1, source_target_pairs={{18,0},{16,1},{19,2},{17,3},{22,4},{20,5},{23,6},{21,7},{26,8},{24... | collective-permute-start | bytes 589832 | tf_op jit(solution)/shard_map/ppermute | solution.py:705
  427.9 20.3 %collective-permute-start.45 = (bf16[64,1536]{1,0:T(8,128)(2,1)}, bf16[64,1536]{1,0:T(8,128)(2,1)S(1)}, u32[]{:S(2)}, u32[]{:S(2)}) collective-permute-start(bf16[64,1536]{1,0:T(8,128)(2,1)} %get-tuple-element.114), channel_id=1, source_target_pairs={{26,0},{24,1},{27,2},{25,3},{30,4},{28,5},{31,6},{29,7},{18,8},{16... | collective-permute-start | bytes 589832 | tf_op jit(solution)/shard_map/ppermute | solution.py:705
  429.3 19.0 %collective-permute-start.42 = (bf16[64,1536]{1,0:T(8,128)(2,1)}, bf16[64,1536]{1,0:T(8,128)(2,1)S(1)}, u32[]{:S(2)}, u32[]{:S(2)}) collective-permute-start(bf16[64,1536]{1,0:T(8,128)(2,1)} %get-tuple-element.108.refs_0_), channel_id=1, source_target_pairs={{2,0},{0,1},{3,2},{1,3},{6,4},{4,5},{7,6},{5,7},{10,8},{8,9},{11,1... | collective-permute-start | bytes 589832 | tf_op jit(solution)/shard_map/ppermute | solution.py:705
  431.1 22.9 %collective-permute-start.41 = (f32[96,128]{1,0:T(8,128)S(1)}, f32[96,128]{1,0:T(8,128)S(1)}, u32[]{:S(2)}, u32[]{:S(2)}) collective-permute-start(f32[96,128]{1,0:T(8,128)S(1)} %add.145), channel_id=1, source_target_pairs={{0,16},{1,17},{2,18},{3,19},{4,20},{5,21},{6,22},{7,23},{8,24},{9,... | collective-permute-start | bytes 147464 | tf_op jit(solution)/shard_map/ppermute | solution.py:713
  440.0 15.2 %collective-permute-start.48 = (bf16[64,2560]{1,0:T(8,128)(2,1)}, bf16[64,2560]{1,0:T(8,128)(2,1)S(1)}, u32[]{:S(2)}, u32[]{:S(2)}) collective-permute-start(bf16[64,2560]{1,0:T(8,128)(2,1)} %get-tuple-element.121), channel_id=1, source_target_pairs={{2,0},{0,1},{3,2},{1,3},{6,4},{4,5},{7,6},{5,7},{10,8},{8,9},{11,1... | collective-permute-start | bytes 983048 | tf_op jit(solution)/shard_map/ppermute | solution.py:705
  448.2 11.6 %collective-permute-start.49 = (bf16[64,2560]{1,0:T(8,128)(2,1)}, bf16[64,2560]{1,0:T(8,128)(2,1)S(1)}, u32[]{:S(2)}, u32[]{:S(2)}) collective-permute-start(bf16[64,2560]{1,0:T(8,128)(2,1)} %get-tuple-element.122), channel_id=1, source_target_pairs={{10,0},{8,1},{11,2},{9,3},{14,4},{12,5},{15,6},{13,7},{2,8},{0,9},... | collective-permute-start | bytes 983048 | tf_op jit(solution)/shard_map/ppermute | solution.py:705
  448.3 25.7 %collective-permute-start.50 = (bf16[64,2560]{1,0:T(8,128)(2,1)}, bf16[64,2560]{1,0:T(8,128)(2,1)S(1)}, u32[]{:S(2)}, u32[]{:S(2)}) collective-permute-start(bf16[64,2560]{1,0:T(8,128)(2,1)} %get-tuple-element.123), channel_id=1, source_target_pairs={{18,0},{16,1},{19,2},{17,3},{22,4},{20,5},{23,6},{21,7},{26,8},{24... | collective-permute-start | bytes 983048 | tf_op jit(solution)/shard_map/ppermute | solution.py:705
  454.0 27.7 %collective-permute-start.51 = (bf16[64,2560]{1,0:T(8,128)(2,1)}, bf16[64,2560]{1,0:T(8,128)(2,1)S(1)}, u32[]{:S(2)}, u32[]{:S(2)}) collective-permute-start(bf16[64,2560]{1,0:T(8,128)(2,1)} %get-tuple-element.124), channel_id=1, source_target_pairs={{26,0},{24,1},{27,2},{25,3},{30,4},{28,5},{31,6},{29,7},{18,8},{16... | collective-permute-start | bytes 983048 | tf_op jit(solution)/shard_map/ppermute | solution.py:705
  (54 other events, 586.6 us)
Sparse Core Ops, SparseCore 0:
  34.8 68.2 all-gather.2
  105.8 92.8 all-gather.4
  277.5 74.2 reduce-scatter.1
where the time goes:
time: 505 us; the launch traced here: 495 us
  waiting for transfers between devices  185 us (37%)
  Pallas kernels  161 us (32%)
  starting transfers between devices  71.4 us (14%)
  local copies, waits for them, and re-layouts  33.9 us (7%)
  other arithmetic  20.1 us (4%)
  between operations  14.6 us (3%)
  matrix products  8.5 us (2%)
    ppermute x22, waiting for transfers between devices, hop(): return lax.ppermute(values, ('a', 'c', 'h'), pairs)  84.7 us
    ppermute x8, waiting for transfers between devices, swap(): return lax.ppermute(values, SWAP, pairs)  52.6 us
    pallas_call x2, Pallas kernels, mlp(): pl.pallas_call(functools.partial(mlp_kernel, block=min(256, length), with...  49.7 us
    ppermute x16, waiting for transfers between devices, swap_hop(): return lax.ppermute(values, ALL, pairs)  46.6 us
    pallas_call x1, Pallas kernels, attn_backward(): pl.pallas_call(without(functools.partial(attn_backward_kernel, block=bloc...  24.2 us
    ppermute x16, starting transfers between devices, swap_hop(): return lax.ppermute(values, ALL, pairs)  24 us
    ppermute x22, starting transfers between devices, hop(): return lax.ppermute(values, ('a', 'c', 'h'), pairs)  23 us
    pallas_call x8, Pallas kernels, sums_call(): pl.pallas_call(body, in_specs=([pl.BlockSpec(memory_space=pl.ANY)] if aft...  20.5 us
  transfers between devices with their start and end apart: 56, of which 19 were waited for; matrix products, arithmetic and copies ran while one was open for 10% of the time, Pallas kernels for 32%

commit v1 on v0

--- a/solution.py
+++ b/solution.py
@@ -18,6 +18,12 @@
 TP = ("l", "c")
 SWAP = ("c", "h", "l")
 ALL = ("a", "c", "h", "l")
+
+
+def small_cost(flops, bytes_accessed, transcendentals):
+    return pl.CostEstimate(
+        flops=flops // 4, bytes_accessed=bytes_accessed // 4, transcendentals=transcendentals // 4
+    )
 
 
 def normalize(values):
@@ -167,7 +173,7 @@
         ],
         scratch_shapes=[pltpu.VMEM((length, length), F32), pltpu.VMEM((LANES, length), BF16)],
         compiler_params=pltpu.CompilerParams(vmem_limit_bytes=VMEM_BYTES),
-        cost_estimate=pl.CostEstimate(
+        cost_estimate=small_cost(
             flops=4 * length * length * width,
             bytes_accessed=8 * length * width,
             transcendentals=length * length * width // (2 * HEAD_DIM),
@@ -205,7 +211,7 @@
             pltpu.VMEM((LANES, length), F32),
         ],
         compiler_params=pltpu.CompilerParams(vmem_limit_bytes=VMEM_BYTES),
-        cost_estimate=pl.CostEstimate(
+        cost_estimate=small_cost(
             flops=10 * length * length * width,
             bytes_accessed=16 * length * width,
             transcendentals=length * length * width // (2 * HEAD_DIM),
@@ -284,7 +290,7 @@
         ]
         + ([jax.ShapeDtypeStruct((length, width), F32)] if residual else []),
         compiler_params=pltpu.CompilerParams(vmem_limit_bytes=VMEM_BYTES),
-        cost_estimate=pl.CostEstimate(
+        cost_estimate=small_cost(
             flops=20 * length * width, bytes_accessed=14 * length * width, transcendentals=length
         ),
         name="norm_two" if residual else "norm_one",
@@ -329,7 +335,7 @@
             jax.ShapeDtypeStruct((8, width), F32),
         ],
         compiler_params=pltpu.CompilerParams(vmem_limit_bytes=VMEM_BYTES),
-        cost_estimate=pl.CostEstimate(
+        cost_estimate=small_cost(
             flops=30 * length * width, bytes_accessed=16 * length * width, transcendentals=length
         ),
         name="norm_two_back",
@@ -453,7 +459,7 @@
         + grad_shapes
         + [jax.ShapeDtypeStruct((1, units), F32)],
         compiler_params=pltpu.CompilerParams(vmem_limit_bytes=VMEM_BYTES),
-        cost_estimate=pl.CostEstimate(
+        cost_estimate=small_cost(
             flops=12 * length * width * units,
             bytes_accessed=12 * length * width + 8 * width * units,
             transcendentals=length * units,
@@ -465,38 +471,45 @@
 
 def qkv_kernel(order, n_ref, b_ref, near, by_y, by_x, low, high, out_ref, w_ref):
     load_pieces(order, (near, by_y, by_x, low, high), w_ref)
-    scale = jnp.where(pl.program_id(0) == 0, HEAD_DIM ** (-0.5), 1.0)
-    length = n_ref.shape[0]
-    step = min(256, length)
-    for first in range(0, length, step):
-        span = slice(first, first + step)
-        out_ref[span, :] = ((dot_nn(n_ref[span, :], w_ref[...]) + b_ref[...]) * scale).astype(BF16)
+    part = pl.program_id(0)
+
+    @pl.when(part < 3)
+    def _():
+        scale = jnp.where(part == 0, HEAD_DIM ** (-0.5), 1.0)
+        length = n_ref.shape[0]
+        step = min(256, length)
+        for first in range(0, length, step):
+            span = slice(first, first + step)
+            out_ref[span, :] = (
+                (dot_nn(n_ref[span, :], w_ref[...]) + b_ref[...]) * scale
+            ).astype(BF16)
 
 
 def qkv_project(order, normed, pieces, bias):
     length, width = normed.shape
-    columns = pieces[0].shape[1] // 3
+    columns = pieces[0].shape[1] // 4
     at_tile = lambda rows: pl.BlockSpec((rows, columns), lambda k, o: (0, k))
+    first_three = lambda rows: pl.BlockSpec((rows, columns), lambda k, o: (0, jnp.minimum(k, 2)))
     return pl.pallas_call(
         qkv_kernel,
         grid_spec=pltpu.PrefetchScalarGridSpec(
             num_scalar_prefetch=1,
-            grid=(3,),
+            grid=(4,),
             in_specs=[
                 pl.BlockSpec((length, width), lambda k, o: (0, 0), pipeline_mode=pl.Buffered(1)),
-                at_tile(1),
+                first_three(1),
             ]
             + [at_tile(piece.shape[0]) for piece in pieces],
-            out_specs=[at_tile(length), at_tile(width)],
+            out_specs=[first_three(length), at_tile(width)],
         ),
         out_shape=[
             jax.ShapeDtypeStruct((length, 3 * columns), BF16),
-            jax.ShapeDtypeStruct((width, 3 * columns), BF16),
+            jax.ShapeDtypeStruct((width, 4 * columns), BF16),
         ],
         compiler_params=pltpu.CompilerParams(vmem_limit_bytes=VMEM_BYTES),
-        cost_estimate=pl.CostEstimate(
+        cost_estimate=small_cost(
             flops=6 * length * width * columns,
-            bytes_accessed=2 * length * width + 12 * width * columns + 6 * length * columns,
+            bytes_accessed=2 * length * width + 16 * width * columns + 6 * length * columns,
             transcendentals=0,
         ),
         name="qkv_project",
@@ -541,7 +554,7 @@
         ),
         out_shape=shapes,
         compiler_params=pltpu.CompilerParams(vmem_limit_bytes=VMEM_BYTES),
-        cost_estimate=pl.CostEstimate(
+        cost_estimate=small_cost(
             flops=2 * parts * length * width * columns,
             bytes_accessed=2 * length * width + 4 * parts * width * columns,
             transcendentals=0,
@@ -568,13 +581,13 @@
         grid=(length // block,),
         in_specs=[
             pl.BlockSpec((3, block, columns), lambda i: (0, i, 0)),
-            pl.BlockSpec((width, 3 * columns), lambda i: (0, 0), pipeline_mode=pl.Buffered(1)),
+            pl.BlockSpec((width, 4 * columns), lambda i: (0, 0), pipeline_mode=pl.Buffered(1)),
             ORDER_ONLY,
         ],
         out_specs=pl.BlockSpec((block, width), lambda i: (i, 0)),
         out_shape=jax.ShapeDtypeStruct((length, width), BF16),
         compiler_params=pltpu.CompilerParams(vmem_limit_bytes=VMEM_BYTES),
-        cost_estimate=pl.CostEstimate(
+        cost_estimate=small_cost(
             flops=6 * length * width * columns,
             bytes_accessed=2 * length * width + 6 * width * columns + 6 * length * columns,
             transcendentals=0,
@@ -616,8 +629,8 @@
             )
 
 
-def last_sums_kernel(*refs, far, half_tile, head_width):
-    parts, other, (up_ref, down_ref, out_ref) = refs[:far], refs[far], refs[far + 1 :]
+def last_sums_kernel(*refs, far, half_tile):
+    parts, other, (up_ref, down_ref) = refs[:far], refs[far], refs[far + 1 :]
     total = parts[0][...].astype(F32)
     for part in parts[1:]:
         total = total + part[...].astype(F32)
@@ -625,15 +638,14 @@
     for first in range(0, units, half_tile):
         here, there = slice(first, first + half_tile), slice(units + first, units + first + half_tile)
         up, down = slice(2 * first, 2 * first + half_tile), slice(2 * first + half_tile, 2 * first + 2 * half_tile)
-        up_ref[:, here] = other[:, up].astype(F32)
-        down_ref[:, here] = other[:, down].astype(F32)
-        up_ref[:, there] = total[:, up]
-        down_ref[:, there] = total[:, down]
-    out_ref[...] = total[:, 2 * units : 2 * units + head_width]
+        up_ref[:, here] = total[:, up]
+        down_ref[:, here] = total[:, down]
+        up_ref[:, there] = other[:, up].astype(F32)
+        down_ref[:, there] = other[:, down].astype(F32)
 
 
 def qkv_last_kernel(*refs):
-    parts, outs = refs[:-3], refs[-3:]
+    parts, outs = refs[:-4], refs[-4:]
     total = parts[0][...].astype(F32)
     for part in parts[1:]:
         total = total + part[...].astype(F32)
@@ -642,14 +654,20 @@
         out[...] = total[:, k * columns : (k + 1) * columns]
 
 
-def shards_kernel(w_out, w_up, w_down, out_ref, first_ref, second_ref, *, tile):
-    out_ref[...] = w_out[...]
+def shards_kernel(w_up, w_down, first_ref, second_ref, *, tile):
     units = first_ref.shape[1] // 2
     for index, ref in enumerate((first_ref, second_ref)):
         for first in range(0, units, tile):
             columns = slice(index * units + first, index * units + first + tile)
             ref[:, 2 * first : 2 * first + tile] = w_up[:, columns]
             ref[:, 2 * first + tile : 2 * first + 2 * tile] = w_down[:, columns]
+
+
+def concat_kernel(*refs):
+    parts, target = refs[:-1], refs[-1]
+    rows = parts[0].shape[0]
+    for i, part in enumerate(parts):
+        target[i * rows : (i + 1) * rows, :] = part[...]
 
 
 def copy_kernel(source, target):
@@ -712,8 +730,15 @@
                     pairs.append(((a * 2 + c) * 2 + h, ((a ^ a_mask) * 2 + c) * 2 + (h ^ h_mask)))
         return lax.ppermute(values, ("a", "c", "h"), pairs)
 
-    def gather(shard):
-        near = jnp.concatenate([swap_hop(shard, 2 * i) for i in range(far)], axis=0)
+    def gather(shard, after):
+        parts = [swap_hop(shard, 2 * i) for i in range(far)]
+        (near,) = sums_call(
+            concat_kernel,
+            parts,
+            [jax.ShapeDtypeStruct((far * shard.shape[0], shard.shape[1]), BF16)],
+            after,
+            "near_rows",
+        )
         half = near.shape[0] // 2
         by_y = hop(near, 1, 0)
         by_x = hop(near, 0, 1)
@@ -744,7 +769,7 @@
             functools.partial(second_sums_kernel, spans=spans, far=far),
             operands + [from_y2, from_x2],
             [jax.ShapeDtypeStruct((rows, total), BF16)] * far,
-            after_two(y_sum),
+            after_two,
             name + "_sums_two",
         )
         return sums[0], [swap_hop(sums[i], 2 * i, inverse=True) for i in range(far)]
@@ -806,23 +831,18 @@
         theirs = lax.dynamic_slice_in_dim(values, (1 - rank) * own_rows, own_rows)
         return own(values).astype(F32) + partner(theirs).astype(F32)
 
-    pieces_qkv = gather(jnp.concatenate([w_query, w_key, w_value], axis=1))
-    shard_out, shard_first, shard_second = sums_call(
-        functools.partial(shards_kernel, tile=tile),
-        [w_out, w_up, w_down],
-        [
-            jax.ShapeDtypeStruct(w_out.shape, BF16),
-            jax.ShapeDtypeStruct(w_up.shape, BF16),
-            jax.ShapeDtypeStruct(w_up.shape, BF16),
-        ],
-        pieces_qkv[0],
-        "mlp_shards",
-    )
-    full_out = lax.all_gather(swap(shard_out), ("a", "h"), axis=0, tiled=True)
-    full_second = lax.all_gather(swap(shard_second), ("a", "h"), axis=0, tiled=True)
-    pieces_first = gather(shard_first)
     own_input = swap(block_input)
     segments = swap(segment_ids)
+    shard_first, shard_second = sums_call(
+        functools.partial(shards_kernel, tile=tile),
+        [w_up, w_down],
+        [jax.ShapeDtypeStruct(w_up.shape, BF16)] * 2,
+        None,
+        "mlp_shards",
+    )
+    full_first = lax.all_gather(swap(shard_first), ("a", "h"), axis=0, tiled=True)
+    full_second = lax.all_gather(swap(shard_second), ("a", "h"), axis=0, tiled=True)
+    pieces_attn = gather(jnp.concatenate([w_query, w_key, w_value, w_out], axis=1), own_input)
     own_grad = swap(out_grad)
     bias_query = lax.dynamic_slice_in_dim(b_query, rank * head_width, head_width)
     bias_value = lax.dynamic_slice_in_dim(b_value, rank * head_width, head_width)
@@ -833,23 +853,22 @@
     grad_rows_t = grad_rows.T
     normed, normed_t = norm_rows(rows_in, ln1_gain, ln1_bias)
     biases = jnp.concatenate([bias_query, jnp.zeros((head_width,), F32), bias_value])
-    qkv, full_qkv = qkv_project(order, normed, pieces_qkv, biases)
+    qkv, full_attn = qkv_project(order, normed, pieces_attn, biases)
+    full_out = full_attn[:, 3 * head_width :]
     mixed, lse = attn_forward(segments, qkv, head_width)
     attended = tp_terms(dot_nt(mixed, full_out).astype(BF16))
     normed_two, normed_two_t, hidden = norm_rows(rows_in, ln2_gain, ln2_bias, attended, b_out)
 
     out_part, gn_part, first_grads, bias_first = mlp(
-        order, normed_two, grad_rows, normed_two_t, grad_rows_t, pieces_first,
-        bias_up[:half_units], (), False,
-    )
-    first_mlp = lax.psum_scatter(
-        swap(first_grads[0], inverse=True), ("a", "c"), scatter_dimension=0, tiled=True
-    )
+        order, normed_two, grad_rows, normed_two_t, grad_rows_t, [full_first],
+        bias_up[:half_units], (), True,
+    )
+    first_received = first_sends(first_grads)
     out_part, gn_part, second_grads, bias_second = mlp(
         order, normed_two, grad_rows, normed_two_t, grad_rows_t, [full_second],
-        bias_up[half_units:], (out_part, gn_part), True,
-    )
-    second_received = first_sends(second_grads)
+        bias_up[half_units:], (out_part, gn_part), False,
+    )
+    second_grads = swap(second_grads[0], inverse=True)
     own_output = (own(hidden) + tp_scatter(out_part) + b_down).astype(BF16)
     output = swap(own_output, inverse=True)
 
@@ -859,33 +878,25 @@
     grad_mixed = dot_nn(grad_attended, full_out).astype(BF16)
     out_grads = weight_grads(order, grad_attended_t, mixed[None], grad_mixed)
     out_received = first_sends(out_grads)
-
-    grads = attn_backward(segments, qkv, mixed, lse, grad_mixed, head_width, out_grads[0])
-    grad_normed_part = []
-
-    def after_unit_sums(y_sum):
-        pieces = weight_grads(order, normed_t, grads, y_sum)
-        grad_normed_part.append((pieces, qkv_back(grads, full_qkv, pieces[0])))
-        return grad_normed_part[0][1]
-
-    _, unit_parts = finish(
-        [second_grads, out_grads], [second_received, out_received], grads, after_unit_sums, "unit"
-    )
-    qkv_grads, grad_normed_part = grad_normed_part[0]
+    unit_done, unit_parts = finish([first_grads], [first_received], gn_part, out_grads[0], "unit")
+
+    grads = attn_backward(segments, qkv, mixed, lse, grad_mixed, head_width, unit_done)
+    second_grads, grads = lax.optimization_barrier((second_grads, grads))
+    second_mlp = lax.psum_scatter(second_grads, ("a", "c"), scatter_dimension=0, tiled=True)
+    qkv_grads = weight_grads(order, normed_t, grads, grads)
+    grad_normed_part = qkv_back(grads, full_attn, qkv_grads[0])
     qkv_done, qkv_parts = finish(
-        [qkv_grads], [first_sends(qkv_grads)], None, lambda y_sum: None, "qkv"
+        [qkv_grads, out_grads], [first_sends(qkv_grads), out_received], grad_normed_part, None, "qkv"
     )
     shard = lambda columns: jax.ShapeDtypeStruct((w_query.shape[0], columns), F32)
-    grad_w_up, grad_w_down, grad_w_out = sums_call(
-        functools.partial(
-            last_sums_kernel, far=len(unit_parts), half_tile=tile, head_width=head_width
-        ),
-        unit_parts + [first_mlp],
-        [shard(unit_width), shard(unit_width), shard(head_width)],
+    grad_w_up, grad_w_down = sums_call(
+        functools.partial(last_sums_kernel, far=len(unit_parts), half_tile=tile),
+        unit_parts + [second_mlp],
+        [shard(unit_width), shard(unit_width)],
         None,
         "unit_sums_last",
     )
-    late = sums_call(qkv_last_kernel, qkv_parts, [shard(head_width)] * 3, None, "qkv_sums_last")
+    late = sums_call(qkv_last_kernel, qkv_parts, [shard(head_width)] * 4, None, "qkv_sums_last")
     grad_normed = tp_scatter(grad_normed_part)
     own_scaled, own_inverse = normalize(own_input.astype(F32))
     grad_own = own(grad_hidden) + norm_back(grad_normed, own_scaled, own_inverse, ln1_gain)
@@ -914,7 +925,7 @@
     small = [sums[i * width : (i + 1) * width] for i in range(8)]
     return (
         output, grad_input, small[0], small[1],
-        late[0], late[1], late[2], small[2], small[3], grad_w_out, small[4], small[5], small[6],
+        late[0], late[1], late[2], small[2], small[3], late[3], small[4], small[5], small[6],
         grad_w_up, sums[8 * width :], grad_w_down, small[7],
     )
 

time: 505 us -> 527 us (1.044)
  the two profiles are of different devices: /device:TPU:17 before, /device:TPU:10 now
where the time goes in v1:
time: 527 us; the launch traced here: 518 us
  waiting for transfers between devices  250 us (47%)
  Pallas kernels  164 us (31%)
  starting transfers between devices  34 us (6%)
  local copies, waits for them, and re-layouts  28.4 us (5%)
  other arithmetic  19.2 us (4%)
  between operations  14.5 us (3%)
  matrix products  8.21 us (2%)
    ppermute x18, waiting for transfers between devices, hop(): return lax.ppermute(values, ('a', 'c', 'h'), pairs)  157 us
    ppermute x12, waiting for transfers between devices, swap_hop(): return lax.ppermute(values, ALL, pairs)  66.7 us
    pallas_call x2, Pallas kernels, mlp(): pl.pallas_call(functools.partial(mlp_kernel, block=min(256, length), with...  49.2 us
    pallas_call x1, Pallas kernels, attn_backward(): pl.pallas_call(without(functools.partial(attn_backward_kernel, block=bloc...  24.2 us
    pallas_call x9, Pallas kernels, sums_call(): pl.pallas_call(body, in_specs=([pl.BlockSpec(memory_space=pl.ANY)] if aft...  22.6 us
    ppermute x8, waiting for transfers between devices, swap(): return lax.ppermute(values, SWAP, pairs)  20.4 us
    ppermute x18, starting transfers between devices, hop(): return lax.ppermute(values, ('a', 'c', 'h'), pairs)  19.3 us
    pallas_call x1, Pallas kernels, attn_forward(): pl.pallas_call(functools.partial(attn_forward_kernel, block=block), grid=...  16.4 us
  transfers between devices with their start and end apart: 48, of which 22 were waited for; matrix products, arithmetic and copies ran while one was open for 8% of the time, Pallas kernels for 26%

profile of v1, /device:TPU:10, one launch (start us, length us, event | category | flops | bytes accessed | tf_op | source)
XLA Modules:
  0.0 518.2 jit_solution(13815117821082784944)
XLA Ops:
  9.6 4.2 collective-permute-done.15
  14.6 2.4 collective-permute-start.14
  17.0 4.2 collective-permute-done.14
  22.0 2.4 collective-permute-start
  32.2 19.1 %collective-permute-done.6.refs_4_ = bf16[64,2048]{1,0:T(8,128)(2,1)S(1)} collective-permute-done((bf16[64,2048]{1,0:T(8,128)(2,1)S(1)}, bf16[64,2048]{1,0:T(8,128)(2,1)S(1)}, u32[]{:S(2)}, u32[]{:S(2)}) %collective-permute-start.6) | collective-permute-done | bytes 262176 | tf_op jit(solution)/shard_map/ppermute | solution.py:723
  51.4 4.8 collective-permute-done.5.refs_3_
  61.7 31.7 %collective-permute-done.8.by_x = bf16[256,2048]{1,0:T(8,128)(2,1)S(1)} collective-permute-done((bf16[256,2048]{1,0:T(8,128)(2,1)}, bf16[256,2048]{1,0:T(8,128)(2,1)S(1)}, u32[]{:S(2)}, u32[]{:S(2)}) %collective-permute-start.8) | collective-permute-done | bytes 1048608 | tf_op jit(solution)/shard_map/ppermute | solution.py:731
  100.1 12.0 %collective-permute-done.2 = s32[1024]{0:T(1024)S(1)} collective-permute-done((s32[1024]{0:T(1024)S(1)}, s32[1024]{0:T(1024)S(1)}, u32[]{:S(2)}, u32[]{:S(2)}) %collective-permute-start.2) | collective-permute-done | bytes 4128 | tf_op jit(solution)/shard_map/ppermute | solution.py:715
  113.2 3.9 maximum_select_fusion.refs_0_
  117.1 5.1 norm_one.1
  122.2 9.2 %qkv_project.1 = (bf16[1024,1536]{1,0:T(8,128)(2,1)}, bf16[1024,2048]{1,0:T(8,128)(2,1)}) custom-call(s32[16]{0:T(128)} %stack.67.order.refs_0_, bf16[1024,1024]{1,0:T(8,128)(2,1)} %get-tuple-element.74.n_ref, f32[1,1536]{1,0:T(1,128)} %reshape.111.b_ref, bf16[256,2048]{1,0:T(8,128)(2,1)} %near_rows.1.near, bf16[256,2048]{1,0:T(8,128)(2,1)} %copy-done.11, ...), custom_call_target="tpu_custom_call" | custom-call | flops 805306368 | bytes 3407872 | tf_op jit(solution)/shard_map/qkv_project/pallas_call | solution.py:493
  131.4 16.4 %attn_forward.1 = (bf16[1024,512]{1,0:T(8,128)(2,1)}, f32[4,8,1024]{2,1,0:T(8,128)}) custom-call(s32[1024,1]{1,0:T(8,128)} %copy.37.seg_col.refs_0_, s32[1,1024]{1,0:T(1,128)} %bitcast.54, bf16[1024,1536]{1,0:T(8,128)(2,1)} %get-tuple-element.75.q_ref.k_ref.v_ref.refs_2_.refs_3_.refs_4_, ...), custom_call_target="tpu_custom_call" | custom-call | flops 536870912 | bytes 1048576 | tf_op jit(solution)/shard_map/attn_forward/pallas_call | solution.py:162
  147.7 4.1 convolution_convert_fusion.refs_1_
  153.4 4.3 collective-permute-done.13
  157.7 3.6 maximum_select_fusion.1.g_ref
  161.3 2.7 copy.39.gt_ref
  164.0 7.5 %norm_two.1 = (bf16[1024,1024]{1,0:T(8,128)(2,1)}, bf16[1024,1024]{1,0:T(8,128)(2,1)}, f32[1024,1024]{1,0:T(8,128)}) custom-call(bf16[1024,1024]{1,0:T(8,128)(2,1)} %maximum_select_fusion.refs_0_, bf16[1024,1024]{1,0:T(8,128)(2,1)} %convolution_convert_fusion.refs_1_, bf16[1024,1024]{1,0:T(8,128)(2,1)} %collective-permute-done.11.refs_2_, ...), custom_call_target="tpu_custom_call" | custom-call | flops 5242880 | bytes 3670016 | tf_op jit(solution)/shard_map/norm_two/pallas_call | solution.py:281
  171.5 24.1 %mlp_first.1 = (bf16[1024,1024]{1,0:T(8,128)(2,1)}, bf16[1024,1024]{1,0:T(8,128)(2,1)}, bf16[256,2048]{1,0:T(8,128)(2,1)}, bf16[256,2048]{1,0:T(8,128)(2,1)}, bf...) custom-call(s32[16]{0:T(128)} %stack.67.order.refs_0_, ...), custom_call_target="tpu_custom_call" | custom-call | flops 3221225472 | bytes 5242880 | tf_op jit(solution)/shard_map/mlp_first/pallas_call | solution.py:428
  196.2 25.1 %mlp_second.1 = (bf16[1024,1024]{1,0:T(8,128)(2,1)}, bf16[1024,1024]{1,0:T(8,128)(2,1)}, bf16[1024,2048]{1,0:T(8,128)(2,1)}, f32[1,1024]{1,0:T(1,128)}) custom-call(s32[16]{0:T(128)} %stack.67.order.refs_0_, bf16[1024,1024]{1,0:T(8,128)(2,1)} %get-tuple-element.79.n_ref, bf16[1024,1024]{1,0:T(8,128)(2,1)} %copy-done.1, ...), custom_call_target="tpu_custom_call" | custom-call | flops 3221225472 | bytes 5242880 | tf_op jit(solution)/shard_map/mlp_second/pallas_call | solution.py:428
  224.6 68.0 %collective-permute-done.20.refs_1_ = bf16[256,2048]{1,0:T(8,128)(2,1)S(1)} collective-permute-done((bf16[256,2048]{1,0:T(8,128)(2,1)}, bf16[256,2048]{1,0:T(8,128)(2,1)S(1)}, u32[]{:S(2)}, u32[]{:S(2)}) %collective-permute-start.20) | collective-permute-done | bytes 1048608 | tf_op jit(solution)/shard_map/ppermute | solution.py:731
  293.9 2.9 unit_sums_one.1
  297.7 9.1 %norm_two_back.1 = (f32[1024,1024]{1,0:T(8,128)}, bf16[1024,1024]{1,0:T(8,128)(2,1)}, bf16[1024,1024]{1,0:T(8,128)(2,1)}, f32[8,1024]{1,0:T(8,128)}) custom-call(f32[1024,1024]{1,0:T(8,128)} %get-tuple-element.78.hidden_ref, bf16[1024,1024]{1,0:T(8,128)(2,1)} %copy-done.1, bf16[1024,1024]{1,0:T(8,128)(2,1)} %get-tuple-element.86.own_ref.refs_0_, ...), custom_call_target="tpu_custom_call" | custom-call | flops 7864320 | bytes 4194304 | tf_op jit(solution)/shard_map/norm_two_back/pallas_call | solution.py:321
  306.8 4.1 convolution_convert_fusion.1.refs_3_.refs_7_
  310.9 4.8 weight_grads.2
  316.6 3.2 unit_sums_two.1
  319.8 24.2 %attn_backward.1.refs_2_.refs_3_.refs_0_ = bf16[3,1024,512]{2,1,0:T(8,128)(2,1)} custom-call(s32[1024,1]{1,0:T(8,128)} %copy.37.seg_col.refs_0_, s32[1,1024]{1,0:T(1,128)} %bitcast.55, bf16[1024,1536]{1,0:T(8,128)(2,1)} %get-tuple-element.75.q_ref.k_ref.v_ref.refs_2_.refs_3_.refs_4_, ...), custom_call_target="tpu_custom_call" | custom-call | flops 1342177280 | bytes 2097152 | tf_op jit(solution)/shard_map/attn_backward/pallas_call | solution.py:191
  347.6 7.9 %weight_grads.3 = (bf16[256,1536]{1,0:T(8,128)(2,1)}, bf16[256,1536]{1,0:T(8,128)(2,1)}, bf16[128,1536]{1,0:T(8,128)(2,1)}, bf16[128,1536]{1,0:T(8,128)(2,1)}, bf16[256,1536]{1,0:T(8,128)(2,1)}) custom-call(s32[16]{0:T(128)} %stack.67.order.refs_0_, bf16[1024,1024]{1,0:T(8,128)(2,1)} %get-tuple-element.102.refs_1_, ...), custom_call_target="tpu_custom_call" | custom-call | flops 805306368 | bytes 2097152 | tf_op jit(solution)/shard_map/weight_grads/pallas_call | solution.py:539
  355.5 8.0 %qkv_back.1.refs_0_ = bf16[1024,1024]{1,0:T(8,128)(2,1)} custom-call(bf16[3,1024,512]{2,1,0:T(8,128)(2,1)} %attn_backward.1.refs_2_.refs_3_.refs_0_, bf16[1024,2048]{1,0:T(8,128)(2,1)} %get-tuple-element.77.refs_1_, bf16[256,1536]{1,0:T(8,128)(2,1)} %get-tuple-element.103.refs_2_), custom_call_target="tpu_custom_call" | custom-call | flops 805306368 | bytes 2097152 | tf_op jit(solution)/shard_map/qkv_back/pallas_call | solution.py:579
  363.4 2.5 constant_dynamic-slice_fusion.1
  369.6 3.6 add_convert_fusion
  375.2 29.6 %collective-permute-done.29.refs_6_.refs_4_ = bf16[256,512]{1,0:T(8,128)(2,1)} collective-permute-done((bf16[256,512]{1,0:T(8,128)(2,1)}, bf16[256,512]{1,0:T(8,128)(2,1)}, u32[]{:S(2)}, u32[]{:S(2)}) %collective-permute-start.29) | collective-permute-done | bytes 262176 | tf_op jit(solution)/shard_map/ppermute | solution.py:731
  405.5 3.2 qkv_sums_one.1
  411.8 2.3 fusion.10
  414.1 3.8 fusion.9
  418.0 6.8 %collective-permute-done.30.refs_6_ = bf16[128,2048]{1,0:T(8,128)(2,1)S(1)} collective-permute-done((bf16[128,2048]{1,0:T(8,128)(2,1)}, bf16[128,2048]{1,0:T(8,128)(2,1)S(1)}, u32[]{:S(2)}, u32[]{:S(2)}) %collective-permute-start.30) | collective-permute-done | bytes 524320 | tf_op jit(solution)/shard_map/ppermute | solution.py:731
  424.8 6.3 %collective-permute-done.31.refs_7_ = bf16[128,2048]{1,0:T(8,128)(2,1)} collective-permute-done((bf16[128,2048]{1,0:T(8,128)(2,1)}, bf16[128,2048]{1,0:T(8,128)(2,1)}, u32[]{:S(2)}, u32[]{:S(2)}) %collective-permute-start.31) | collective-permute-done | bytes 524320 | tf_op jit(solution)/shard_map/ppermute | solution.py:731
  431.1 3.4 qkv_sums_two.1
  438.2 5.1 collective-permute-done.33
  444.4 3.0 collective-permute-done.34
  448.2 3.4 collective-permute-done.35
  451.6 3.0 collective-permute-start.36
  455.7 2.7 collective-permute-done.36
  458.8 6.2 %collective-permute-done.38.refs_1_ = bf16[64,2048]{1,0:T(8,128)(2,1)S(1)} collective-permute-done((bf16[64,2048]{1,0:T(8,128)(2,1)}, bf16[64,2048]{1,0:T(8,128)(2,1)S(1)}, u32[]{:S(2)}, u32[]{:S(2)}) %collective-permute-start.38) | collective-permute-done | bytes 262176 | tf_op jit(solution)/shard_map/ppermute | solution.py:723
  465.1 9.0 %collective-permute-done.39.refs_2_ = bf16[64,2048]{1,0:T(8,128)(2,1)S(1)} collective-permute-done((bf16[64,2048]{1,0:T(8,128)(2,1)}, bf16[64,2048]{1,0:T(8,128)(2,1)S(1)}, u32[]{:S(2)}, u32[]{:S(2)}) %collective-permute-start.39) | collective-permute-done | bytes 262176 | tf_op jit(solution)/shard_map/ppermute | solution.py:723
  474.1 7.0 %collective-permute-done.40.refs_3_ = bf16[64,2048]{1,0:T(8,128)(2,1)S(1)} collective-permute-done((bf16[64,2048]{1,0:T(8,128)(2,1)}, bf16[64,2048]{1,0:T(8,128)(2,1)S(1)}, u32[]{:S(2)}, u32[]{:S(2)}) %collective-permute-start.40) | collective-permute-done | bytes 262176 | tf_op jit(solution)/shard_map/ppermute | solution.py:723
  484.5 14.1 %collective-permute-done.43.refs_2_ = bf16[64,2048]{1,0:T(8,128)(2,1)S(1)} collective-permute-done((bf16[64,2048]{1,0:T(8,128)(2,1)}, bf16[64,2048]{1,0:T(8,128)(2,1)S(1)}, u32[]{:S(2)}, u32[]{:S(2)}) %collective-permute-start.43) | collective-permute-done | bytes 262176 | tf_op jit(solution)/shard_map/ppermute | solution.py:723
  498.7 6.4 %collective-permute-done.44.refs_3_ = bf16[64,2048]{1,0:T(8,128)(2,1)S(1)} collective-permute-done((bf16[64,2048]{1,0:T(8,128)(2,1)S(1)}, bf16[64,2048]{1,0:T(8,128)(2,1)S(1)}, u32[]{:S(2)}, u32[]{:S(2)}) %collective-permute-start.44) | collective-permute-done | bytes 262176 | tf_op jit(solution)/shard_map/ppermute | solution.py:723
  505.9 2.4 unit_sums_last.1
  (216 shorter events, 61.1 us)
Async XLA Ops:
  7.2 164.3 %all-gather.5.cloned.1.call-start = ((), (), s32[]{:S(2)}) async-start(), calls=%async_computation.2 | async-start | bytes 4456448 | tf_op jit(solution)/shard_map/all_gather | solution.py:843
  9.1 4.7 collective-permute-start.15
  14.5 181.7 %all-gather.3.cloned.1.call-start = ((), (), s32[]{:S(2)}) async-start(), calls=%async_computation.1 | async-start | bytes 4456448 | tf_op jit(solution)/shard_map/all_gather | solution.py:844
  14.6 6.6 %collective-permute-start.14 = (bf16[64,2048]{1,0:T(8,128)(2,1)}, bf16[64,2048]{1,0:T(8,128)(2,1)S(1)}, u32[]{:S(2)}, u32[]{:S(2)}) collective-permute-start(bf16[64,2048]{1,0:T(8,128)(2,1)} %get-tuple-element.81), channel_id=1, source_target_pairs={{0,2},{1,0},{2,3},{3,1},{4,6},{5,4},{6,7},{7,5},{8,10},{9,8},{10,1... | collective-permute-start | bytes 786440 | tf_op jit(solution)/shard_map/ppermute | solution.py:715
  21.9 483.2 %reduce-scatter.2.cloned.1.call-start = ((), (), s32[]{:S(2)}) async-start(), calls=%async_computation.3 | async-start | bytes 4456448 | tf_op jit(solution)/shard_map/reduce_scatter | solution.py:885
  22.0 34.2 %collective-permute-start = (bf16[512,1024]{1,0:T(8,128)(2,1)}, bf16[512,1024]{1,0:T(8,128)(2,1)S(1)}, u32[]{:S(2)}, u32[]{:S(2)}) collective-permute-start(bf16[512,1024]{1,0:T(8,128)(2,1)} %param.18), channel_id=1, source_target_pairs={{0,2},{1,0},{2,3},{3,1},{4,6},{5,4},{6,7},{7,5},{8,10},{9,8},{10,1... | collective-permute-start | bytes 3145736 | tf_op jit(solution)/shard_map/ppermute | solution.py:715
  27.8 23.6 %collective-permute-start.6 = (bf16[64,2048]{1,0:T(8,128)(2,1)S(1)}, bf16[64,2048]{1,0:T(8,128)(2,1)S(1)}, u32[]{:S(2)}, u32[]{:S(2)}) collective-permute-start(bf16[64,2048]{1,0:T(8,128)(2,1)S(1)} %constant_dynamic-update-slice_fusion), channel_id=1, source_target_pairs={{0,26},{1,24},{2,27},{3,25},{4,30},{5,28},{6,31},{7,29},{8,18},{9,... | collective-permute-start | bytes 786440 | tf_op jit(solution)/shard_map/ppermute | solution.py:723
  28.8 27.3 %collective-permute-start.5 = (bf16[64,2048]{1,0:T(8,128)(2,1)S(1)}, bf16[64,2048]{1,0:T(8,128)(2,1)S(1)}, u32[]{:S(2)}, u32[]{:S(2)}) collective-permute-start(bf16[64,2048]{1,0:T(8,128)(2,1)S(1)} %constant_dynamic-update-slice_fusion), channel_id=1, source_target_pairs={{0,18},{1,16},{2,19},{3,17},{4,22},{5,20},{6,23},{7,21},{8,26},{9,... | collective-permute-start | bytes 786440 | tf_op jit(solution)/shard_map/ppermute | solution.py:723
  29.9 26.2 %collective-permute-start.4 = (bf16[64,2048]{1,0:T(8,128)(2,1)S(1)}, bf16[64,2048]{1,0:T(8,128)(2,1)S(1)}, u32[]{:S(2)}, u32[]{:S(2)}) collective-permute-start(bf16[64,2048]{1,0:T(8,128)(2,1)S(1)} %constant_dynamic-update-slice_fusion), channel_id=1, source_target_pairs={{0,10},{1,8},{2,11},{3,9},{4,14},{5,12},{6,15},{7,13},{8,2},{9,0},... | collective-permute-start | bytes 786440 | tf_op jit(solution)/shard_map/ppermute | solution.py:723
  29.9 26.2 %collective-permute-start.3 = (bf16[64,2048]{1,0:T(8,128)(2,1)S(1)}, bf16[64,2048]{1,0:T(8,128)(2,1)S(1)}, u32[]{:S(2)}, u32[]{:S(2)}) collective-permute-start(bf16[64,2048]{1,0:T(8,128)(2,1)S(1)} %constant_dynamic-update-slice_fusion), channel_id=1, source_target_pairs={{0,2},{1,0},{2,3},{3,1},{4,6},{5,4},{6,7},{7,5},{8,10},{9,8},{10,1... | collective-permute-start | bytes 786440 | tf_op jit(solution)/shard_map/ppermute | solution.py:723
  60.2 33.2 %collective-permute-start.8 = (bf16[256,2048]{1,0:T(8,128)(2,1)}, bf16[256,2048]{1,0:T(8,128)(2,1)S(1)}, u32[]{:S(2)}, u32[]{:S(2)}) collective-permute-start(bf16[256,2048]{1,0:T(8,128)(2,1)} %near_rows.1.near), channel_id=1, source_target_pairs={{0,1},{1,0},{2,3},{3,2},{4,5},{5,4},{6,7},{7,6},{8,9},{9,8},{10,11... | collective-permute-start | bytes 3145736 | tf_op jit(solution)/shard_map/ppermute | solution.py:731
  60.2 35.6 %collective-permute-start.7 = (bf16[256,2048]{1,0:T(8,128)(2,1)}, bf16[256,2048]{1,0:T(8,128)(2,1)S(1)}, u32[]{:S(2)}, u32[]{:S(2)}) collective-permute-start(bf16[256,2048]{1,0:T(8,128)(2,1)} %near_rows.1.near), channel_id=1, source_target_pairs={{0,4},{1,5},{2,6},{3,7},{4,0},{5,1},{6,2},{7,3},{8,12},{9,13},{10,... | collective-permute-start | bytes 3145736 | tf_op jit(solution)/shard_map/ppermute | solution.py:731
  61.7 51.5 %collective-permute-start.1 = (bf16[512,1024]{1,0:T(8,128)(2,1)}, bf16[512,1024]{1,0:T(8,128)(2,1)}, u32[]{:S(2)}, u32[]{:S(2)}) collective-permute-start(bf16[512,1024]{1,0:T(8,128)(2,1)} %copy-done.2), channel_id=1, source_target_pairs={{0,2},{2,0},{1,3},{3,1},{4,6},{6,4},{5,7},{7,5},{8,10},{10,8},{9,1... | collective-permute-start | bytes 3145736 | tf_op jit(solution)/shard_map/ppermute | solution.py:807
  94.3 27.9 %collective-permute-start.10 = (bf16[128,2048]{1,0:T(8,128)(2,1)}, bf16[128,2048]{1,0:T(8,128)(2,1)}, u32[]{:S(2)}, u32[]{:S(2)}) collective-permute-start(bf16[128,2048]{1,0:T(8,128)(2,1)} %slice.105), channel_id=1, source_target_pairs={{0,4},{1,5},{2,6},{3,7},{4,0},{5,1},{6,2},{7,3},{8,12},{9,13},{10,... | collective-permute-start | bytes 1572872 | tf_op jit(solution)/shard_map/ppermute | solution.py:731
  96.7 25.5 %collective-permute-start.9 = (bf16[128,2048]{1,0:T(8,128)(2,1)}, bf16[128,2048]{1,0:T(8,128)(2,1)}, u32[]{:S(2)}, u32[]{:S(2)}) collective-permute-start(bf16[128,2048]{1,0:T(8,128)(2,1)} %slice.104), channel_id=1, source_target_pairs={{0,1},{1,0},{2,3},{3,2},{4,5},{5,4},{6,7},{7,6},{8,9},{9,8},{10,11... | collective-permute-start | bytes 1572872 | tf_op jit(solution)/shard_map/ppermute | solution.py:731
  98.1 14.1 %collective-permute-start.2 = (s32[1024]{0:T(1024)S(1)}, s32[1024]{0:T(1024)S(1)}, u32[]{:S(2)}, u32[]{:S(2)}) collective-permute-start(s32[1024]{0:T(1024)S(1)} %copy-done.44), channel_id=1, source_target_pairs={{0,2},{1,0},{2,3},{3,1},{4,6},{5,4},{6,7},{7,5},{8,10},{9,8},{10,1... | collective-permute-start | bytes 12296 | tf_op jit(solution)/shard_map/ppermute | solution.py:715
  98.7 53.7 %collective-permute-start.12 = (bf16[512,1024]{1,0:T(8,128)(2,1)}, bf16[512,1024]{1,0:T(8,128)(2,1)S(1)}, u32[]{:S(2)}, u32[]{:S(2)}) collective-permute-start(bf16[512,1024]{1,0:T(8,128)(2,1)} %param.35), channel_id=1, source_target_pairs={{0,2},{1,0},{2,3},{3,1},{4,6},{5,4},{6,7},{7,5},{8,10},{9,8},{10,1... | collective-permute-start | bytes 3145736 | tf_op jit(solution)/shard_map/ppermute | solution.py:715
  151.9 12.1 %collective-permute-start.11 = (bf16[1024,1024]{1,0:T(8,128)(2,1)}, bf16[1024,1024]{1,0:T(8,128)(2,1)}, u32[]{:S(2)}, u32[]{:S(2)}) collective-permute-start(bf16[1024,1024]{1,0:T(8,128)(2,1)} %convolution_convert_fusion.refs_1_), channel_id=1, source_target_pairs={{0,2},{2,0},{1,3},{3,1},{4,6},{6,4},{5,7},{7,5},{8,10},{10,8},{9,1... | collective-permute-start | bytes 6291464 | tf_op jit(solution)/shard_map/ppermute | solution.py:807
  152.4 5.3 %collective-permute-start.13 = (bf16[512,1024]{1,0:T(8,128)(2,1)S(1)}, bf16[512,1024]{1,0:T(8,128)(2,1)}, u32[]{:S(2)}, u32[]{:S(2)}) collective-permute-start(bf16[512,1024]{1,0:T(8,128)(2,1)S(1)} %collective-permute-done.12), channel_id=1, source_target_pairs={{0,2},{2,0},{1,3},{3,1},{4,6},{6,4},{5,7},{7,5},{8,10},{10,8},{9,1... | collective-permute-start | bytes 3145736 | tf_op jit(solution)/shard_map/ppermute | solution.py:807
  221.3 122.8 %collective-permute-start.19 = (bf16[1024,2048]{1,0:T(8,128)(2,1)}, bf16[1024,2048]{1,0:T(8,128)(2,1)}, u32[]{:S(2)}, u32[]{:S(2)}) collective-permute-start(bf16[1024,2048]{1,0:T(8,128)(2,1)} %get-tuple-element.88), channel_id=1, source_target_pairs={{2,0},{0,1},{3,2},{1,3},{6,4},{4,5},{7,6},{5,7},{10,8},{8,9},{11,1... | collective-permute-start | bytes 12582920 | tf_op jit(solution)/shard_map/ppermute | solution.py:715
  221.4 76.4 %collective-permute-start.18 = (bf16[1024,1024]{1,0:T(8,128)(2,1)}, bf16[1024,1024]{1,0:T(8,128)(2,1)}, u32[]{:S(2)}, u32[]{:S(2)}) collective-permute-start(bf16[1024,1024]{1,0:T(8,128)(2,1)} %get-tuple-element.86.own_ref.refs_0_), channel_id=1, source_target_pairs={{0,2},{2,0},{1,3},{3,1},{4,6},{6,4},{5,7},{7,5},{8,10},{10,8},{9,1... | collective-permute-start | bytes 6291464 | tf_op jit(solution)/shard_map/ppermute | solution.py:807
  222.7 69.8 %collective-permute-start.20 = (bf16[256,2048]{1,0:T(8,128)(2,1)}, bf16[256,2048]{1,0:T(8,128)(2,1)S(1)}, u32[]{:S(2)}, u32[]{:S(2)}) collective-permute-start(bf16[256,2048]{1,0:T(8,128)(2,1)} %get-tuple-element.93), channel_id=1, source_target_pairs={{0,1},{1,0},{2,3},{3,2},{4,5},{5,4},{6,7},{7,6},{8,9},{9,8},{10,11... | collective-permute-start | bytes 3145736 | tf_op jit(solution)/shard_map/ppermute | solution.py:731
  223.4 69.2 %collective-permute-start.21 = (bf16[256,2048]{1,0:T(8,128)(2,1)}, bf16[256,2048]{1,0:T(8,128)(2,1)S(1)}, u32[]{:S(2)}, u32[]{:S(2)}) collective-permute-start(bf16[256,2048]{1,0:T(8,128)(2,1)} %get-tuple-element.94), channel_id=1, source_target_pairs={{0,4},{1,5},{2,6},{3,7},{4,0},{5,1},{6,2},{7,3},{8,12},{9,13},{10,... | collective-permute-start | bytes 3145736 | tf_op jit(solution)/shard_map/ppermute | solution.py:731
  296.8 18.8 %collective-permute-start.22 = (bf16[128,2048]{1,0:T(8,128)(2,1)}, bf16[128,2048]{1,0:T(8,128)(2,1)S(1)}, u32[]{:S(2)}, u32[]{:S(2)}) collective-permute-start(bf16[128,2048]{1,0:T(8,128)(2,1)} %get-tuple-element.98), channel_id=1, source_target_pairs={{0,4},{1,5},{2,6},{3,7},{4,0},{5,1},{6,2},{7,3},{8,12},{9,13},{10,... | collective-permute-start | bytes 1572872 | tf_op jit(solution)/shard_map/ppermute | solution.py:731
  297.7 17.9 %collective-permute-start.23 = (bf16[128,2048]{1,0:T(8,128)(2,1)}, bf16[128,2048]{1,0:T(8,128)(2,1)S(1)}, u32[]{:S(2)}, u32[]{:S(2)}) collective-permute-start(bf16[128,2048]{1,0:T(8,128)(2,1)} %get-tuple-element.99), channel_id=1, source_target_pairs={{0,1},{1,0},{2,3},{3,2},{4,5},{5,4},{6,7},{7,6},{8,9},{9,8},{10,11... | collective-permute-start | bytes 1572872 | tf_op jit(solution)/shard_map/ppermute | solution.py:731
  346.7 22.8 %collective-permute-start.16 = (bf16[512,1024]{1,0:T(8,128)(2,1)}, bf16[512,1024]{1,0:T(8,128)(2,1)}, u32[]{:S(2)}, u32[]{:S(2)}) collective-permute-start(bf16[512,1024]{1,0:T(8,128)(2,1)} %constant_dynamic-slice_fusion), channel_id=1, source_target_pairs={{0,2},{2,0},{1,3},{3,1},{4,6},{6,4},{5,7},{7,5},{8,10},{10,8},{9,1... | collective-permute-start | bytes 3145736 | tf_op jit(solution)/shard_map/ppermute | solution.py:807
  365.9 45.8 %collective-permute-start.24 = (bf16[512,1024]{1,0:T(8,128)(2,1)}, bf16[512,1024]{1,0:T(8,128)(2,1)}, u32[]{:S(2)}, u32[]{:S(2)}) collective-permute-start(bf16[512,1024]{1,0:T(8,128)(2,1)} %constant_dynamic-slice_fusion.1), channel_id=1, source_target_pairs={{0,2},{2,0},{1,3},{3,1},{4,6},{6,4},{5,7},{7,5},{8,10},{10,8},{9,1... | collective-permute-start | bytes 3145736 | tf_op jit(solution)/shard_map/ppermute | solution.py:807
  366.2 38.6 %collective-permute-start.26 = (bf16[256,1536]{1,0:T(8,128)(2,1)}, bf16[256,1536]{1,0:T(8,128)(2,1)}, u32[]{:S(2)}, u32[]{:S(2)}) collective-permute-start(bf16[256,1536]{1,0:T(8,128)(2,1)} %get-tuple-element.103.refs_2_), channel_id=1, source_target_pairs={{0,1},{1,0},{2,3},{3,2},{4,5},{5,4},{6,7},{7,6},{8,9},{9,8},{10,11... | collective-permute-start | bytes 2359304 | tf_op jit(solution)/shard_map/ppermute | solution.py:731
  368.4 36.4 %collective-permute-start.27 = (bf16[256,1536]{1,0:T(8,128)(2,1)}, bf16[256,1536]{1,0:T(8,128)(2,1)}, u32[]{:S(2)}, u32[]{:S(2)}) collective-permute-start(bf16[256,1536]{1,0:T(8,128)(2,1)} %get-tuple-element.104), channel_id=1, source_target_pairs={{0,4},{1,5},{2,6},{3,7},{4,0},{5,1},{6,2},{7,3},{8,12},{9,13},{10,... | collective-permute-start | bytes 2359304 | tf_op jit(solution)/shard_map/ppermute | solution.py:731
  373.2 31.6 %collective-permute-start.28 = (bf16[256,512]{1,0:T(8,128)(2,1)}, bf16[256,512]{1,0:T(8,128)(2,1)S(1)}, u32[]{:S(2)}, u32[]{:S(2)}) collective-permute-start(bf16[256,512]{1,0:T(8,128)(2,1)} %get-tuple-element.92.refs_0_), channel_id=1, source_target_pairs={{0,1},{1,0},{2,3},{3,2},{4,5},{5,4},{6,7},{7,6},{8,9},{9,8},{10,11... | collective-permute-start | bytes 786440 | tf_op jit(solution)/shard_map/ppermute | solution.py:731
  373.3 31.5 %collective-permute-start.29 = (bf16[256,512]{1,0:T(8,128)(2,1)}, bf16[256,512]{1,0:T(8,128)(2,1)}, u32[]{:S(2)}, u32[]{:S(2)}) collective-permute-start(bf16[256,512]{1,0:T(8,128)(2,1)} %get-tuple-element.106), channel_id=1, source_target_pairs={{0,4},{1,5},{2,6},{3,7},{4,0},{5,1},{6,2},{7,3},{8,12},{9,13},{10,... | collective-permute-start | bytes 786440 | tf_op jit(solution)/shard_map/ppermute | solution.py:731
  404.8 49.8 %collective-permute-start.17 = (bf16[512,1024]{1,0:T(8,128)(2,1)}, bf16[512,1024]{1,0:T(8,128)(2,1)}, u32[]{:S(2)}, u32[]{:S(2)}) collective-permute-start(bf16[512,1024]{1,0:T(8,128)(2,1)} %add_convert_fusion), channel_id=1, source_target_pairs={{2,0},{0,1},{3,2},{1,3},{6,4},{4,5},{7,6},{5,7},{10,8},{8,9},{11,1... | collective-permute-start | bytes 3145736 | tf_op jit(solution)/shard_map/ppermute | solution.py:715
  408.7 16.1 %collective-permute-start.30 = (bf16[128,2048]{1,0:T(8,128)(2,1)}, bf16[128,2048]{1,0:T(8,128)(2,1)S(1)}, u32[]{:S(2)}, u32[]{:S(2)}) collective-permute-start(bf16[128,2048]{1,0:T(8,128)(2,1)} %get-tuple-element.112), channel_id=1, source_target_pairs={{0,4},{1,5},{2,6},{3,7},{4,0},{5,1},{6,2},{7,3},{8,12},{9,13},{10,... | collective-permute-start | bytes 1572872 | tf_op jit(solution)/shard_map/ppermute | solution.py:731
  409.7 21.4 %collective-permute-start.31 = (bf16[128,2048]{1,0:T(8,128)(2,1)}, bf16[128,2048]{1,0:T(8,128)(2,1)}, u32[]{:S(2)}, u32[]{:S(2)}) collective-permute-start(bf16[128,2048]{1,0:T(8,128)(2,1)} %get-tuple-element.113), channel_id=1, source_target_pairs={{0,1},{1,0},{2,3},{3,2},{4,5},{5,4},{6,7},{7,6},{8,9},{9,8},{10,11... | collective-permute-start | bytes 1572872 | tf_op jit(solution)/shard_map/ppermute | solution.py:731
  417.9 66.6 %collective-permute-start.25 = (bf16[512,1024]{1,0:T(8,128)(2,1)}, bf16[512,1024]{1,0:T(8,128)(2,1)S(1)}, u32[]{:S(2)}, u32[]{:S(2)}) collective-permute-start(bf16[512,1024]{1,0:T(8,128)(2,1)} %fusion.9), channel_id=1, source_target_pairs={{2,0},{0,1},{3,2},{1,3},{6,4},{4,5},{7,6},{5,7},{10,8},{8,9},{11,1... | collective-permute-start | bytes 3145736 | tf_op jit(solution)/shard_map/ppermute | solution.py:715
  436.0 1.4 collective-permute-start.32
  438.2 5.1 collective-permute-start.33
  443.3 4.2 collective-permute-start.34
  447.5 4.2 collective-permute-start.35
  451.6 6.8 %collective-permute-start.36 = (f32[96,128]{1,0:T(8,128)S(1)}, f32[96,128]{1,0:T(8,128)S(1)}, u32[]{:S(2)}, u32[]{:S(2)}) collective-permute-start(f32[96,128]{1,0:T(8,128)S(1)} %add.145), channel_id=1, source_target_pairs={{0,16},{1,17},{2,18},{3,19},{4,20},{5,21},{6,22},{7,23},{8,24},{9,... | collective-permute-start | bytes 147464 | tf_op jit(solution)/shard_map/ppermute | solution.py:731
  454.6 10.5 %collective-permute-start.38 = (bf16[64,2048]{1,0:T(8,128)(2,1)}, bf16[64,2048]{1,0:T(8,128)(2,1)S(1)}, u32[]{:S(2)}, u32[]{:S(2)}) collective-permute-start(bf16[64,2048]{1,0:T(8,128)(2,1)} %get-tuple-element.118), channel_id=1, source_target_pairs={{10,0},{8,1},{11,2},{9,3},{14,4},{12,5},{15,6},{13,7},{2,8},{0,9},... | collective-permute-start | bytes 786440 | tf_op jit(solution)/shard_map/ppermute | solution.py:723
  454.6 19.5 %collective-permute-start.39 = (bf16[64,2048]{1,0:T(8,128)(2,1)}, bf16[64,2048]{1,0:T(8,128)(2,1)S(1)}, u32[]{:S(2)}, u32[]{:S(2)}) collective-permute-start(bf16[64,2048]{1,0:T(8,128)(2,1)} %get-tuple-element.119), channel_id=1, source_target_pairs={{18,0},{16,1},{19,2},{17,3},{22,4},{20,5},{23,6},{21,7},{26,8},{24... | collective-permute-start | bytes 786440 | tf_op jit(solution)/shard_map/ppermute | solution.py:723
  454.6 26.5 %collective-permute-start.40 = (bf16[64,2048]{1,0:T(8,128)(2,1)}, bf16[64,2048]{1,0:T(8,128)(2,1)S(1)}, u32[]{:S(2)}, u32[]{:S(2)}) collective-permute-start(bf16[64,2048]{1,0:T(8,128)(2,1)} %get-tuple-element.120), channel_id=1, source_target_pairs={{26,0},{24,1},{27,2},{25,3},{30,4},{28,5},{31,6},{29,7},{18,8},{16... | collective-permute-start | bytes 786440 | tf_op jit(solution)/shard_map/ppermute | solution.py:723
  458.4 22.7 %collective-permute-start.37 = (bf16[64,2048]{1,0:T(8,128)(2,1)}, bf16[64,2048]{1,0:T(8,128)(2,1)S(1)}, u32[]{:S(2)}, u32[]{:S(2)}) collective-permute-start(bf16[64,2048]{1,0:T(8,128)(2,1)} %get-tuple-element.114.refs_0_), channel_id=1, source_target_pairs={{2,0},{0,1},{3,2},{1,3},{6,4},{4,5},{7,6},{5,7},{10,8},{8,9},{11,1... | collective-permute-start | bytes 786440 | tf_op jit(solution)/shard_map/ppermute | solution.py:723
  465.1 40.0 %collective-permute-start.41 = (bf16[64,2048]{1,0:T(8,128)(2,1)S(1)}, bf16[64,2048]{1,0:T(8,128)(2,1)S(1)}, u32[]{:S(2)}, u32[]{:S(2)}) collective-permute-start(bf16[64,2048]{1,0:T(8,128)(2,1)S(1)} %copy-done.18), channel_id=1, source_target_pairs={{2,0},{0,1},{3,2},{1,3},{6,4},{4,5},{7,6},{5,7},{10,8},{8,9},{11,1... | collective-permute-start | bytes 786440 | tf_op jit(solution)/shard_map/ppermute | solution.py:723
  474.1 10.4 %collective-permute-start.42 = (bf16[64,2048]{1,0:T(8,128)(2,1)}, bf16[64,2048]{1,0:T(8,128)(2,1)S(1)}, u32[]{:S(2)}, u32[]{:S(2)}) collective-permute-start(bf16[64,2048]{1,0:T(8,128)(2,1)} %get-tuple-element.125), channel_id=1, source_target_pairs={{10,0},{8,1},{11,2},{9,3},{14,4},{12,5},{15,6},{13,7},{2,8},{0,9},... | collective-permute-start | bytes 786440 | tf_op jit(solution)/shard_map/ppermute | solution.py:723
  481.1 17.6 %collective-permute-start.43 = (bf16[64,2048]{1,0:T(8,128)(2,1)}, bf16[64,2048]{1,0:T(8,128)(2,1)S(1)}, u32[]{:S(2)}, u32[]{:S(2)}) collective-permute-start(bf16[64,2048]{1,0:T(8,128)(2,1)} %get-tuple-element.126), channel_id=1, source_target_pairs={{18,0},{16,1},{19,2},{17,3},{22,4},{20,5},{23,6},{21,7},{26,8},{24... | collective-permute-start | bytes 786440 | tf_op jit(solution)/shard_map/ppermute | solution.py:723
  481.1 23.9 %collective-permute-start.44 = (bf16[64,2048]{1,0:T(8,128)(2,1)S(1)}, bf16[64,2048]{1,0:T(8,128)(2,1)S(1)}, u32[]{:S(2)}, u32[]{:S(2)}) collective-permute-start(bf16[64,2048]{1,0:T(8,128)(2,1)S(1)} %copy-done.43), channel_id=1, source_target_pairs={{26,0},{24,1},{27,2},{25,3},{30,4},{28,5},{31,6},{29,7},{18,8},{16... | collective-permute-start | bytes 786440 | tf_op jit(solution)/shard_map/ppermute | solution.py:723
  (45 other events, 539.8 us)
Sparse Core Ops, SparseCore 0:
  14.7 102.9 all-gather.4
  120.4 75.7 all-gather.2
  344.2 86.2 reduce-scatter.1

commit v2 on v0

--- a/solution.py
+++ b/solution.py
@@ -336,28 +336,11 @@
     )(hidden, grad, *partials, gain.reshape(1, width))
 
 
-def load_pieces(order, pieces, w_ref):
-    rows = w_ref.shape[0] // order.shape[0]
-    block = 0
-    for ref in pieces:
-        for place in range(ref.shape[0] // rows):
-            first = pl.multiple_of(order[block] * rows, rows)
-            w_ref[pl.ds(first, rows), :] = ref[place * rows : (place + 1) * rows, :]
-            block += 1
-
-
-def mlp_kernel(order, n_ref, g_ref, nt_ref, gt_ref, b_ref, *refs, block, with_previous, cube, in_pieces):
-    if in_pieces:
-        pieces, refs = refs[:5], refs[5:]
-        w_ref, refs = refs[-1], refs[:-1]
-        load_pieces(order, pieces, w_ref)
-    else:
-        w_ref, refs = refs[0], refs[1:]
+def mlp_kernel(n_ref, g_ref, nt_ref, gt_ref, b_ref, w_ref, *refs, block, with_previous):
     if with_previous:
         (before_out, before_gn), refs = refs[:2], refs[2:]
-    count = 5 if cube else 1
-    (out_ref, gn_ref), grad_refs, refs = refs[:2], refs[2 : 2 + count], refs[2 + count :]
-    gb_ref, out_acc, gn_acc, act, gpre, grad_up, grad_down = refs
+    (out_ref, gn_ref, grad_ref), refs = refs[:3], refs[3:]
+    gb_ref, out_acc, gn_acc, act, gpre = refs
     step = pl.program_id(0)
     length = n_ref.shape[0]
     tile = w_ref.shape[1] // 2
@@ -391,14 +374,8 @@
         out_acc[rows, :] += dot_nt(active, w_ref[:, downs])
         gn_acc[rows, :] += dot_nt(grad_pre, w_ref[:, ups])
     gb_ref[...] = bias_sum
-    if cube:
-        grad_up[...] = dot_nn(nt_ref[...], gpre[...]).astype(BF16)
-        grad_down[...] = dot_nn(gt_ref[...], act[...]).astype(BF16)
-        store_pieces(order, grad_up, grad_refs, ups)
-        store_pieces(order, grad_down, grad_refs, downs)
-    else:
-        grad_refs[0][:, ups] = dot_nn(nt_ref[...], gpre[...]).astype(BF16)
-        grad_refs[0][:, downs] = dot_nn(gt_ref[...], act[...]).astype(BF16)
+    grad_ref[:, ups] = dot_nn(nt_ref[...], gpre[...]).astype(BF16)
+    grad_ref[:, downs] = dot_nn(gt_ref[...], act[...]).astype(BF16)
 
     @pl.when(step == pl.num_programs(0) - 1)
     def _():
@@ -406,52 +383,42 @@
         gn_ref[...] = gn_acc[...].astype(BF16)
 
 
-def mlp(order, normed, grad, normed_t, grad_t, weights, bias, previous, cube):
+def mlp(normed, grad, normed_t, grad_t, weights, bias, previous):
     length, width = normed.shape
-    units = weights[0].shape[1] // 2
-    in_pieces = len(weights) > 1
+    units = weights.shape[1] // 2
     tile = min(TILE, units)
     once = pl.Buffered(1)
-    fixed = lambda shape, **options: pl.BlockSpec(shape, lambda u, o: (0, 0), **options)
-    at_tile = lambda rows, columns: pl.BlockSpec((rows, columns), lambda u, o: (0, u))
-    count, rows = order.shape[0], width // order.shape[0]
-    if cube:
-        grad_shapes = piece_shapes(count, rows, 2 * units)
-    else:
-        grad_shapes = [jax.ShapeDtypeStruct((width, 2 * units), BF16)]
-    results = pl.pallas_call(
-        functools.partial(
-            mlp_kernel, block=min(256, length), with_previous=bool(previous), cube=cube,
-            in_pieces=in_pieces,
-        ),
-        grid_spec=pltpu.PrefetchScalarGridSpec(
-            num_scalar_prefetch=1,
-            grid=(units // tile,),
-            in_specs=[
-                fixed((length, width), pipeline_mode=once),
-                fixed((length, width), pipeline_mode=once),
-                fixed((width, length), pipeline_mode=once),
-                fixed((width, length), pipeline_mode=once),
-                at_tile(1, tile),
-            ]
-            + [at_tile(piece.shape[0], 2 * tile) for piece in weights]
-            + [fixed((length, width), pipeline_mode=once) for _ in previous],
-            out_specs=[fixed((length, width)), fixed((length, width))]
-            + [at_tile(shape.shape[0], 2 * tile) for shape in grad_shapes]
-            + [at_tile(1, tile)],
-            scratch_shapes=[
-                pltpu.VMEM((length, width), F32),
-                pltpu.VMEM((length, width), F32),
-                pltpu.VMEM((length, tile), BF16),
-                pltpu.VMEM((length, tile), BF16),
-                pltpu.VMEM((width, tile), BF16),
-                pltpu.VMEM((width, tile), BF16),
-            ]
-            + ([pltpu.VMEM((width, 2 * tile), BF16)] if in_pieces else []),
-        ),
-        out_shape=[jax.ShapeDtypeStruct((length, width), BF16)] * 2
-        + grad_shapes
-        + [jax.ShapeDtypeStruct((1, units), F32)],
+    at_tile = lambda rows, columns: pl.BlockSpec((rows, columns), lambda u: (0, u))
+    return pl.pallas_call(
+        functools.partial(mlp_kernel, block=min(256, length), with_previous=bool(previous)),
+        grid=(units // tile,),
+        in_specs=[
+            whole_spec((length, width), pipeline_mode=once),
+            whole_spec((length, width), pipeline_mode=once),
+            whole_spec((width, length), pipeline_mode=once),
+            whole_spec((width, length), pipeline_mode=once),
+            at_tile(1, tile),
+            at_tile(width, 2 * tile),
+        ]
+        + [whole_spec((length, width), pipeline_mode=once) for _ in previous],
+        out_specs=[
+            whole_spec((length, width)),
+            whole_spec((length, width)),
+            at_tile(width, 2 * tile),
+            at_tile(1, tile),
+        ],
+        out_shape=[
+            jax.ShapeDtypeStruct((length, width), BF16),
+            jax.ShapeDtypeStruct((length, width), BF16),
+            jax.ShapeDtypeStruct((width, 2 * units), BF16),
+            jax.ShapeDtypeStruct((1, units), F32),
+        ],
+        scratch_shapes=[
+            pltpu.VMEM((length, width), F32),
+            pltpu.VMEM((length, width), F32),
+            pltpu.VMEM((length, tile), BF16),
+            pltpu.VMEM((length, tile), BF16),
+        ],
         compiler_params=pltpu.CompilerParams(vmem_limit_bytes=VMEM_BYTES),
         cost_estimate=pl.CostEstimate(
             flops=12 * length * width * units,
@@ -459,12 +426,10 @@
             transcendentals=length * units,
         ),
         name="mlp_second" if previous else "mlp_first",
-    )(order, normed, grad, normed_t, grad_t, bias.reshape(1, units), *weights, *previous)
-    return results[0], results[1], results[2:-1], results[-1]
-
-
-def qkv_kernel(order, n_ref, b_ref, near, by_y, by_x, low, high, out_ref, w_ref):
-    load_pieces(order, (near, by_y, by_x, low, high), w_ref)
+    )(normed, grad, normed_t, grad_t, bias.reshape(1, units), weights, *previous)
+
+
+def qkv_kernel(n_ref, b_ref, w_ref, out_ref):
     scale = jnp.where(pl.program_id(0) == 0, HEAD_DIM ** (-0.5), 1.0)
     length = n_ref.shape[0]
     step = min(256, length)
@@ -473,39 +438,40 @@
         out_ref[span, :] = ((dot_nn(n_ref[span, :], w_ref[...]) + b_ref[...]) * scale).astype(BF16)
 
 
-def qkv_project(order, normed, pieces, bias):
+def qkv_project(normed, weights, bias):
     length, width = normed.shape
-    columns = pieces[0].shape[1] // 3
-    at_tile = lambda rows: pl.BlockSpec((rows, columns), lambda k, o: (0, k))
+    columns = weights.shape[1] // 4
+    at_tile = lambda rows: pl.BlockSpec((rows, columns), lambda k: (0, k))
     return pl.pallas_call(
         qkv_kernel,
-        grid_spec=pltpu.PrefetchScalarGridSpec(
-            num_scalar_prefetch=1,
-            grid=(3,),
-            in_specs=[
-                pl.BlockSpec((length, width), lambda k, o: (0, 0), pipeline_mode=pl.Buffered(1)),
-                at_tile(1),
-            ]
-            + [at_tile(piece.shape[0]) for piece in pieces],
-            out_specs=[at_tile(length), at_tile(width)],
-        ),
-        out_shape=[
-            jax.ShapeDtypeStruct((length, 3 * columns), BF16),
-            jax.ShapeDtypeStruct((width, 3 * columns), BF16),
-        ],
+        grid=(3,),
+        in_specs=[
+            whole_spec((length, width), pipeline_mode=pl.Buffered(1)), at_tile(1), at_tile(width)
+        ],
+        out_specs=at_tile(length),
+        out_shape=jax.ShapeDtypeStruct((length, 3 * columns), BF16),
         compiler_params=pltpu.CompilerParams(vmem_limit_bytes=VMEM_BYTES),
         cost_estimate=pl.CostEstimate(
             flops=6 * length * width * columns,
-            bytes_accessed=2 * length * width + 12 * width * columns + 6 * length * columns,
+            bytes_accessed=2 * length * width + 6 * width * columns + 6 * length * columns,
             transcendentals=0,
         ),
         name="qkv_project",
-    )(order, normed, bias.reshape(1, 3 * columns), *pieces)
-
-
-def weight_kernel(order, nt_ref, grads_ref, *refs):
+    )(normed, bias.reshape(1, 3 * columns), weights)
+
+
+def weight_kernel(order, nt_ref, grads_ref, gt_ref, mixed_ref, *refs):
     piece_refs, grad = refs[:5], refs[5]
-    grad[...] = dot_nn(nt_ref[...], grads_ref[0]).astype(BF16)
+    part = pl.program_id(0)
+
+    @pl.when(part < 3)
+    def _():
+        grad[...] = dot_nn(nt_ref[...], grads_ref[0]).astype(BF16)
+
+    @pl.when(part == 3)
+    def _():
+        grad[...] = dot_nn(gt_ref[...], mixed_ref[...]).astype(BF16)
+
     store_pieces(order, grad, piece_refs, slice(None))
 
 
@@ -516,38 +482,36 @@
 ORDER_ONLY = pl.BlockSpec(memory_space=pl.ANY)
 
 
-def weight_grads(order, normed_t, grads, after):
+def weight_grads(order, normed_t, grads, grad_t, mixed):
     width, length = normed_t.shape
     columns = grads.shape[2]
-    tile = min(TILE, columns)
-    tiles = columns // tile
-    parts = grads.shape[0]
-    shapes = piece_shapes(order.shape[0], width // order.shape[0], parts * columns)
+    shapes = piece_shapes(order.shape[0], width // order.shape[0], 4 * columns)
+    fixed = lambda shape: pl.BlockSpec(shape, lambda k, o: (0, 0), pipeline_mode=pl.Buffered(1))
     return pl.pallas_call(
-        without(weight_kernel, 3),
+        weight_kernel,
         grid_spec=pltpu.PrefetchScalarGridSpec(
             num_scalar_prefetch=1,
-            grid=(parts, tiles),
+            grid=(4,),
             in_specs=[
-                pl.BlockSpec((width, length), lambda k, u, o: (0, 0), pipeline_mode=pl.Buffered(1)),
-                pl.BlockSpec((1, length, tile), lambda k, u, o: (k, 0, u)),
-                ORDER_ONLY,
+                fixed((width, length)),
+                pl.BlockSpec((1, length, columns), lambda k, o: (jnp.minimum(k, 2), 0, 0)),
+                fixed((width, length)),
+                fixed((length, columns)),
             ],
             out_specs=[
-                pl.BlockSpec((shape.shape[0], tile), lambda k, u, o: (0, k * tiles + u))
-                for shape in shapes
+                pl.BlockSpec((shape.shape[0], columns), lambda k, o: (0, k)) for shape in shapes
             ],
-            scratch_shapes=[pltpu.VMEM((width, tile), BF16)],
+            scratch_shapes=[pltpu.VMEM((width, columns), BF16)],
         ),
         out_shape=shapes,
         compiler_params=pltpu.CompilerParams(vmem_limit_bytes=VMEM_BYTES),
         cost_estimate=pl.CostEstimate(
-            flops=2 * parts * length * width * columns,
-            bytes_accessed=2 * length * width + 4 * parts * width * columns,
+            flops=8 * length * width * columns,
+            bytes_accessed=4 * length * width + 16 * width * columns,
             transcendentals=0,
         ),
         name="weight_grads",
-    )(order, normed_t, grads, after)
+    )(order, normed_t, grads, grad_t, mixed)
 
 
 def qkv_back_kernel(grads_ref, w_ref, out_ref):
@@ -568,7 +532,7 @@
         grid=(length // block,),
         in_specs=[
             pl.BlockSpec((3, block, columns), lambda i: (0, i, 0)),
-            pl.BlockSpec((width, 3 * columns), lambda i: (0, 0), pipeline_mode=pl.Buffered(1)),
+            pl.BlockSpec((width, 4 * columns), lambda i: (0, 0), pipeline_mode=pl.Buffered(1)),
             ORDER_ONLY,
         ],
         out_specs=pl.BlockSpec((block, width), lambda i: (i, 0)),
@@ -590,78 +554,57 @@
     return total.astype(BF16)
 
 
-def first_sums_kernel(*refs, spans):
-    refs, (y_ref, x_ref) = refs[:-2], refs[-2:]
+def first_sums_kernel(from_x, from_y, keep_y, keep_x, y_ref, x_ref):
     half = y_ref.shape[0]
-    for index, columns in enumerate(spans):
-        from_x, from_y, keep_y, keep_x = (ref[...] for ref in refs[4 * index : 4 * index + 4])
-        y_ref[:, columns] = added(keep_y, from_x[:half])
-        x_ref[:, columns] = added(keep_x, from_y[:half])
-
-
-def second_sums_kernel(*refs, spans, far):
-    outs, refs = refs[-far:], refs[:-far]
-    (from_y2, from_x2), refs = refs[-2:], refs[:-2]
+    y_ref[...] = added(keep_y[...], from_x[:half, :])
+    x_ref[...] = added(keep_x[...], from_y[:half, :])
+
+
+def second_sums_kernel(from_x, from_y, near, from_y2, from_x2, small, *outs):
+    far = len(outs)
     half = from_y2.shape[0]
     rows = half * 2 // far
-    for index, columns in enumerate(spans):
-        from_x, from_y, near = refs[3 * index : 3 * index + 3]
-        for i in range(far):
-            first, second, place = (from_x, from_y2, i) if i < far // 2 else (from_y, from_x2, i - far // 2)
-            span = slice(place * rows, (place + 1) * rows)
-            outs[i][:, columns] = added(
-                near[i * rows : (i + 1) * rows, :],
-                first[half + place * rows : half + (place + 1) * rows, :],
-                second[span, columns],
-            )
-
-
-def last_sums_kernel(*refs, far, half_tile, head_width):
-    parts, other, (up_ref, down_ref, out_ref) = refs[:far], refs[far], refs[far + 1 :]
+    values = small[...]
+    high = values.astype(BF16).astype(F32)
+    extra = jnp.concatenate([high, values - high], axis=0).astype(BF16)
+    for i, out in enumerate(outs):
+        first, second, place = (from_x, from_y2, i) if i < far // 2 else (from_y, from_x2, i - far // 2)
+        out[:rows, :] = added(
+            near[i * rows : (i + 1) * rows, :],
+            first[half + place * rows : half + (place + 1) * rows, :],
+            second[place * rows : (place + 1) * rows, :],
+        )
+        out[rows:, :] = extra
+
+
+def weights_last_kernel(*refs):
+    parts, outs, small = refs[:-5], refs[-5:-1], refs[-1]
     total = parts[0][...].astype(F32)
     for part in parts[1:]:
         total = total + part[...].astype(F32)
+    rows, columns = outs[0].shape
+    for k, out in enumerate(outs):
+        out[...] = total[:rows, k * columns : (k + 1) * columns]
+    extra = small.shape[0]
+    small[...] = total[rows : rows + extra, :] + total[rows + extra :, :]
+
+
+def units_last_kernel(first_ref, second_ref, up_ref, down_ref, *, tile):
     units = up_ref.shape[1] // 2
-    for first in range(0, units, half_tile):
-        here, there = slice(first, first + half_tile), slice(units + first, units + first + half_tile)
-        up, down = slice(2 * first, 2 * first + half_tile), slice(2 * first + half_tile, 2 * first + 2 * half_tile)
-        up_ref[:, here] = other[:, up].astype(F32)
-        down_ref[:, here] = other[:, down].astype(F32)
-        up_ref[:, there] = total[:, up]
-        down_ref[:, there] = total[:, down]
-    out_ref[...] = total[:, 2 * units : 2 * units + head_width]
-
-
-def qkv_last_kernel(*refs):
-    parts, outs = refs[:-3], refs[-3:]
-    total = parts[0][...].astype(F32)
-    for part in parts[1:]:
-        total = total + part[...].astype(F32)
-    columns = outs[0].shape[1]
-    for k, out in enumerate(outs):
-        out[...] = total[:, k * columns : (k + 1) * columns]
-
-
-def shards_kernel(w_out, w_up, w_down, out_ref, first_ref, second_ref, *, tile):
-    out_ref[...] = w_out[...]
+    for index, ref in enumerate((first_ref, second_ref)):
+        for first in range(0, units, tile):
+            columns = slice(index * units + first, index * units + first + tile)
+            up_ref[:, columns] = ref[:, 2 * first : 2 * first + tile].astype(F32)
+            down_ref[:, columns] = ref[:, 2 * first + tile : 2 * first + 2 * tile].astype(F32)
+
+
+def shards_kernel(w_up, w_down, first_ref, second_ref, *, tile):
     units = first_ref.shape[1] // 2
     for index, ref in enumerate((first_ref, second_ref)):
         for first in range(0, units, tile):
             columns = slice(index * units + first, index * units + first + tile)
             ref[:, 2 * first : 2 * first + tile] = w_up[:, columns]
             ref[:, 2 * first + tile : 2 * first + 2 * tile] = w_down[:, columns]
-
-
-def copy_kernel(source, target):
-    target[...] = source[...]
-
-
-def column_spans(widths):
-    spans, first = [], 0
-    for width in widths:
-        spans.append(slice(first, first + width))
-        first += width
-    return spans
 
 
 def sums_call(kernel, operands, shapes, after, name):
@@ -674,6 +617,7 @@
         out_specs=[vmem] * len(shapes),
         out_shape=shapes,
         compiler_params=pltpu.CompilerParams(vmem_limit_bytes=VMEM_BYTES),
+        cost_estimate=pl.CostEstimate(flops=0, bytes_accessed=32 * 1024 * 1024, transcendentals=0),
         name=name,
     )(*([after] if after is not None else []), *operands)
 
@@ -712,48 +656,45 @@
                     pairs.append(((a * 2 + c) * 2 + h, ((a ^ a_mask) * 2 + c) * 2 + (h ^ h_mask)))
         return lax.ppermute(values, ("a", "c", "h"), pairs)
 
-    def gather(shard):
-        near = jnp.concatenate([swap_hop(shard, 2 * i) for i in range(far)], axis=0)
-        half = near.shape[0] // 2
-        by_y = hop(near, 1, 0)
-        by_x = hop(near, 0, 1)
-        return [near, by_y, by_x, hop(by_y[:half], 0, 1), hop(by_x[half:], 1, 0)]
-
-    def first_sends(pieces):
-        return hop(pieces[0], 0, 1), hop(pieces[1], 1, 0)
-
-    def finish(chunks, received, after, after_two, name):
-        spans = column_spans([pieces[0].shape[1] for pieces in chunks])
-        total = spans[-1].stop
-        half, rows = chunks[0][2].shape[0], chunks[0][4].shape[0] // far
-        operands = []
-        for pieces, (from_x, from_y) in zip(chunks, received):
-            operands += [from_x, from_y, pieces[2], pieces[3]]
+    def scatter_near(pieces, after):
+        from_x, from_y = hop(pieces[0], 0, 1), hop(pieces[1], 1, 0)
+        half, columns = pieces[2].shape
         y_sum, x_sum = sums_call(
-            functools.partial(first_sums_kernel, spans=spans),
-            operands,
-            [jax.ShapeDtypeStruct((half, total), BF16)] * 2,
+            first_sums_kernel,
+            [from_x, from_y, pieces[2], pieces[3]],
+            [jax.ShapeDtypeStruct((half, columns), BF16)] * 2,
             after,
-            name + "_sums_one",
+            "sums_one",
         )
+        return from_x, from_y, pieces[4], y_sum, x_sum
+
+    def scatter_far(state, small):
+        from_x, from_y, near, y_sum, x_sum = state
+        columns = near.shape[1]
         from_y2, from_x2 = hop(y_sum, 1, 0), hop(x_sum, 0, 1)
-        operands = []
-        for pieces, (from_x, from_y) in zip(chunks, received):
-            operands += [from_x, from_y, pieces[4]]
+        rows, extra = near.shape[0] // far, 2 * small.shape[0]
         sums = sums_call(
-            functools.partial(second_sums_kernel, spans=spans, far=far),
-            operands + [from_y2, from_x2],
-            [jax.ShapeDtypeStruct((rows, total), BF16)] * far,
-            after_two(y_sum),
-            name + "_sums_two",
+            second_sums_kernel,
+            [from_x, from_y, near, from_y2, from_x2, small],
+            [jax.ShapeDtypeStruct((rows + extra, columns), BF16)] * far,
+            None,
+            "sums_two",
         )
-        return sums[0], [swap_hop(sums[i], 2 * i, inverse=True) for i in range(far)]
-
-    def sum_all(values):
+        parts = [swap_hop(sums[i], 2 * i, inverse=True) for i in range(far)]
+        outs = sums_call(
+            weights_last_kernel,
+            parts,
+            [jax.ShapeDtypeStruct((rows, columns // 4), F32)] * 4
+            + [jax.ShapeDtypeStruct(small.shape, F32)],
+            None,
+            "sums_last",
+        )
+        return outs[:4], outs[4]
+
+    def near_sum(values):
         values = values + lax.ppermute(values, "c", [(0, 1), (1, 0)])
         values = values + hop(values, 0, 1)
-        for mask in range(groups.bit_length() - 1):
-            values = values + hop(values, 1 << mask, 0)
+        values = values + hop(values, 1, 0)
         return lax.psum(values, "l") if inner > 1 else values
 
     a, h = lax.axis_index("a"), lax.axis_index("h")
@@ -761,7 +702,7 @@
     for a_low, h_mask in ((0, 0), (1, 0), (0, 1), (1, 1)):
         for i in range(far):
             order.append((a ^ (2 * i + a_low)) * 2 + (h ^ h_mask))
-    return swap, gather, first_sends, finish, sum_all, jnp.stack(order).astype(jnp.int32)
+    return swap, scatter_near, scatter_far, near_sum, jnp.stack(order).astype(jnp.int32)
 
 
 def per_device(sizes, *arguments):
@@ -776,7 +717,7 @@
     unit_width = w_up.shape[1]
     half_units = unit_width // 2
     tile = min(TILE, half_units)
-    swap, gather, first_sends, finish, sum_all, order = moves(sizes)
+    swap, scatter_near, scatter_far, near_sum, order = moves(sizes)
 
     def partner(values):
         return lax.ppermute(values, "c", [(0, 1), (1, 0)])
@@ -806,23 +747,22 @@
         theirs = lax.dynamic_slice_in_dim(values, (1 - rank) * own_rows, own_rows)
         return own(values).astype(F32) + partner(theirs).astype(F32)
 
-    pieces_qkv = gather(jnp.concatenate([w_query, w_key, w_value], axis=1))
-    shard_out, shard_first, shard_second = sums_call(
+    own_input = swap(block_input)
+    segments = swap(segment_ids)
+    shard_first, shard_second = sums_call(
         functools.partial(shards_kernel, tile=tile),
-        [w_out, w_up, w_down],
-        [
-            jax.ShapeDtypeStruct(w_out.shape, BF16),
-            jax.ShapeDtypeStruct(w_up.shape, BF16),
-            jax.ShapeDtypeStruct(w_up.shape, BF16),
-        ],
-        pieces_qkv[0],
+        [w_up, w_down],
+        [jax.ShapeDtypeStruct(w_up.shape, BF16)] * 2,
+        own_input,
         "mlp_shards",
     )
-    full_out = lax.all_gather(swap(shard_out), ("a", "h"), axis=0, tiled=True)
-    full_second = lax.all_gather(swap(shard_second), ("a", "h"), axis=0, tiled=True)
-    pieces_first = gather(shard_first)
-    own_input = swap(block_input)
-    segments = swap(segment_ids)
+
+    def gather(shard):
+        return swap(lax.all_gather(shard, ("a", "c"), axis=0, tiled=True))
+
+    full_attn = gather(jnp.concatenate([w_query, w_key, w_value, w_out], axis=1))
+    full_first = gather(shard_first)
+    late_second = lax.all_gather(shard_second, ("a", "c"), axis=0, tiled=True)
     own_grad = swap(out_grad)
     bias_query = lax.dynamic_slice_in_dim(b_query, rank * head_width, head_width)
     bias_value = lax.dynamic_slice_in_dim(b_value, rank * head_width, head_width)
@@ -833,59 +773,39 @@
     grad_rows_t = grad_rows.T
     normed, normed_t = norm_rows(rows_in, ln1_gain, ln1_bias)
     biases = jnp.concatenate([bias_query, jnp.zeros((head_width,), F32), bias_value])
-    qkv, full_qkv = qkv_project(order, normed, pieces_qkv, biases)
+    qkv = qkv_project(normed, full_attn, biases)
+    full_out = full_attn[:, 3 * head_width :]
     mixed, lse = attn_forward(segments, qkv, head_width)
+    late_second, mixed = lax.optimization_barrier((late_second, mixed))
+    full_second = swap(late_second)
     attended = tp_terms(dot_nt(mixed, full_out).astype(BF16))
     normed_two, normed_two_t, hidden = norm_rows(rows_in, ln2_gain, ln2_bias, attended, b_out)
 
     out_part, gn_part, first_grads, bias_first = mlp(
-        order, normed_two, grad_rows, normed_two_t, grad_rows_t, pieces_first,
-        bias_up[:half_units], (), False,
+        normed_two, grad_rows, normed_two_t, grad_rows_t, full_first, bias_up[:half_units], ()
     )
-    first_mlp = lax.psum_scatter(
-        swap(first_grads[0], inverse=True), ("a", "c"), scatter_dimension=0, tiled=True
+    first_grads = swap(first_grads, inverse=True)
+    out_part, gn_part, second_grads, bias_second = mlp(
+        normed_two, grad_rows, normed_two_t, grad_rows_t, full_second, bias_up[half_units:],
+        (out_part, gn_part),
     )
-    out_part, gn_part, second_grads, bias_second = mlp(
-        order, normed_two, grad_rows, normed_two_t, grad_rows_t, [full_second],
-        bias_up[half_units:], (out_part, gn_part), True,
-    )
-    second_received = first_sends(second_grads)
+    second_grads = swap(second_grads, inverse=True)
     own_output = (own(hidden) + tp_scatter(out_part) + b_down).astype(BF16)
     output = swap(own_output, inverse=True)
 
     grad_hidden, grad_attended, grad_attended_t, sums_two = norm_back_rows(
         hidden, grad_rows, tp_terms(gn_part), ln2_gain
     )
+    first_grads, grad_attended = lax.optimization_barrier((first_grads, grad_attended))
+    first_mlp = lax.psum_scatter(first_grads, ("a", "c"), scatter_dimension=0, tiled=True)
     grad_mixed = dot_nn(grad_attended, full_out).astype(BF16)
-    out_grads = weight_grads(order, grad_attended_t, mixed[None], grad_mixed)
-    out_received = first_sends(out_grads)
-
-    grads = attn_backward(segments, qkv, mixed, lse, grad_mixed, head_width, out_grads[0])
-    grad_normed_part = []
-
-    def after_unit_sums(y_sum):
-        pieces = weight_grads(order, normed_t, grads, y_sum)
-        grad_normed_part.append((pieces, qkv_back(grads, full_qkv, pieces[0])))
-        return grad_normed_part[0][1]
-
-    _, unit_parts = finish(
-        [second_grads, out_grads], [second_received, out_received], grads, after_unit_sums, "unit"
-    )
-    qkv_grads, grad_normed_part = grad_normed_part[0]
-    qkv_done, qkv_parts = finish(
-        [qkv_grads], [first_sends(qkv_grads)], None, lambda y_sum: None, "qkv"
-    )
-    shard = lambda columns: jax.ShapeDtypeStruct((w_query.shape[0], columns), F32)
-    grad_w_up, grad_w_down, grad_w_out = sums_call(
-        functools.partial(
-            last_sums_kernel, far=len(unit_parts), half_tile=tile, head_width=head_width
-        ),
-        unit_parts + [first_mlp],
-        [shard(unit_width), shard(unit_width), shard(head_width)],
-        None,
-        "unit_sums_last",
-    )
-    late = sums_call(qkv_last_kernel, qkv_parts, [shard(head_width)] * 3, None, "qkv_sums_last")
+    grads = attn_backward(segments, qkv, mixed, lse, grad_mixed, head_width, grad_mixed)
+    second_grads, first_mlp = lax.optimization_barrier((second_grads, first_mlp))
+    second_mlp = lax.psum_scatter(second_grads, ("a", "c"), scatter_dimension=0, tiled=True)
+    pieces = weight_grads(order, normed_t, grads, grad_attended_t, mixed)
+    grad_normed_part = qkv_back(grads, full_attn, pieces[0])
+    state = scatter_near(pieces, grad_normed_part)
+    grad_normed_part, state = lax.optimization_barrier((grad_normed_part, state))
     grad_normed = tp_scatter(grad_normed_part)
     own_scaled, own_inverse = normalize(own_input.astype(F32))
     grad_own = own(grad_hidden) + norm_back(grad_normed, own_scaled, own_inverse, ln1_gain)
@@ -906,16 +826,25 @@
             jnp.sum(own_grad.astype(F32), axis=0),
             place_part(jnp.concatenate([bias_first[0], bias_second[0]]), b_up.shape[0]),
         ]
-    ).reshape(-1, LANES)
-    (sums,) = sums_call(
-        copy_kernel, [sums], [jax.ShapeDtypeStruct(sums.shape, F32)], qkv_done, "small_sums"
     )
-    sums = sum_all(sums).reshape(-1)
+    columns = pieces[0].shape[1]
+    filled = sums.shape[0]
+    sums = jnp.pad(sums, (0, -filled % (8 * columns))).reshape(-1, columns)
+    late, sums = scatter_far(state, near_sum(sums))
+    sums = sums.reshape(-1)
+    shard = jax.ShapeDtypeStruct((w_query.shape[0], unit_width), F32)
+    grad_w_up, grad_w_down = sums_call(
+        functools.partial(units_last_kernel, tile=tile),
+        [first_mlp, second_mlp],
+        [shard, shard],
+        None,
+        "units_last",
+    )
     small = [sums[i * width : (i + 1) * width] for i in range(8)]
     return (
         output, grad_input, small[0], small[1],
-        late[0], late[1], late[2], small[2], small[3], grad_w_out, small[4], small[5], small[6],
-        grad_w_up, sums[8 * width :], grad_w_down, small[7],
+        late[0], late[1], late[2], small[2], small[3], late[3], small[4], small[5], small[6],
+        grad_w_up, sums[8 * width : filled], grad_w_down, small[7],
     )
 
 

time: 505 us -> 548 us (1.085)
  the two profiles are of different devices: /device:TPU:17 before, /device:TPU:10 now
where the time goes in v2:
time: 548 us; the launch traced here: 540 us
  waiting for transfers between devices  310 us (57%)
  Pallas kernels  147 us (27%)
  local copies, waits for them, and re-layouts  21.5 us (4%)
  other arithmetic  21.2 us (4%)
  starting transfers between devices  18 us (3%)
  between operations  14.7 us (3%)
  matrix products  7.59 us (1%)
    ppermute x10, waiting for transfers between devices, swap(): return lax.ppermute(values, SWAP, pairs)  114 us
    all_gather x2, waiting for transfers between devices, gather(): return swap(lax.all_gather(shard, ('a', 'c'), axis=0, tiled=True))  87.9 us
    pallas_call x2, Pallas kernels, mlp(): pl.pallas_call(functools.partial(mlp_kernel, block=min(256, length), with...  47.3 us
    ppermute x6, waiting for transfers between devices, hop(): return lax.ppermute(values, ('a', 'c', 'h'), pairs)  45.8 us
    ppermute x4, waiting for transfers between devices, swap_hop(): return lax.ppermute(values, ALL, pairs)  29.4 us
    pallas_call x1, Pallas kernels, attn_backward(): pl.pallas_call(without(functools.partial(attn_backward_kernel, block=bloc...  24.3 us
    reduce_scatter x1, waiting for transfers between devices, per_device(): lax.psum_scatter(first_grads, ('a', 'c'), scatter_dimension=0, tiled=True)  21.8 us
    pallas_call x1, Pallas kernels, attn_forward(): pl.pallas_call(functools.partial(attn_forward_kernel, block=block), grid=...  16.4 us
  transfers between devices with their start and end apart: 32, of which 18 were waited for; matrix products, arithmetic and copies ran while one was open for 7% of the time, Pallas kernels for 27%

profile of v2, /device:TPU:10, one launch (start us, length us, event | category | flops | bytes accessed | tf_op | source)
XLA Modules:
  0.0 540.3 jit_solution(17150146710532692262)
XLA Ops:
  7.3 1.7 pad_maximum_fusion
  9.6 12.6 %collective-permute-done.refs_0_ = bf16[512,1024]{1,0:T(8,128)(2,1)S(1)} collective-permute-done((bf16[512,1024]{1,0:T(8,128)(2,1)}, bf16[512,1024]{1,0:T(8,128)(2,1)S(1)}, u32[]{:S(2)}, u32[]{:S(2)}) %collective-permute-start) | collective-permute-done | bytes 1048608 | tf_op jit(solution)/shard_map/ppermute | solution.py:641
  23.2 1.9 mlp_shards.1
  25.9 36.6 %all-gather.6.cloned.1.call-done = bf16[1024,2048]{1,0:T(8,128)(2,1)} async-done(((bf16[64,2048]{1,0:T(8,128)(2,1)}), bf16[1024,2048]{1,0:T(8,128)(2,1)}) %all-gather.6.cloned.1.call-update) | async-done | bytes 4194320 | tf_op jit(solution)/shard_map/all_gather | solution.py:761
  63.1 51.3 %all-gather.8.cloned.1.call-done = bf16[1024,2048]{1,0:T(8,128)(2,1)} async-done(((bf16[64,2048]{1,0:T(8,128)(2,1)}), bf16[1024,2048]{1,0:T(8,128)(2,1)}) %all-gather.8.cloned.1.call-update) | async-done | bytes 4194320 | tf_op jit(solution)/shard_map/all_gather | solution.py:761
  117.1 44.1 %collective-permute-done.2 = s32[1024]{0:T(1024)S(1)} collective-permute-done((s32[1024]{0:T(1024)S(1)}, s32[1024]{0:T(1024)S(1)}, u32[]{:S(2)}, u32[]{:S(2)}) %collective-permute-start.2) | collective-permute-done | bytes 4128 | tf_op jit(solution)/shard_map/ppermute | solution.py:641
  162.3 4.0 maximum_select_fusion.refs_0_
  166.3 4.9 norm_one.1
  171.2 7.1 %qkv_project.1.q_ref.k_ref.v_ref.refs_2_.refs_3_.refs_4_ = bf16[1024,1536]{1,0:T(8,128)(2,1)} custom-call(bf16[1024,1024]{1,0:T(8,128)(2,1)} %get-tuple-element.69.n_ref, f32[1,1536]{1,0:T(1,128)} %reshape.105.b_ref, bf16[1024,2048]{1,0:T(8,128)(2,1)} %collective-permute-done.3.w_ref.refs_1_), custom_call_target="tpu_custom_call" | custom-call | flops 3221225472 | bytes 8388608 | tf_op jit(solution)/shard_map/qkv_project/pallas_call | solution.py:445
  178.3 16.4 %attn_forward.1 = (bf16[1024,512]{1,0:T(8,128)(2,1)}, f32[4,8,1024]{2,1,0:T(8,128)}) custom-call(s32[1024,1]{1,0:T(8,128)} %copy.37.seg_col.refs_0_, s32[1,1024]{1,0:T(1,128)} %bitcast.40, bf16[1024,1536]{1,0:T(8,128)(2,1)} %qkv_project.1.q_ref.k_ref.v_ref.refs_2_.refs_3_.refs_4_, bf16[1024,1536]{1,0:T(8,128)(2,1)} %qkv_project.1.q_ref.k_ref.v_ref.refs_2_.refs_3_.refs_4_, ...), custom_call_target="tpu_custom_call" | custom-call | flops 2147483648 | bytes 4194304 | tf_op jit(solution)/shard_map/attn_forward/pallas_call | solution.py:156
  194.7 2.6 collective-permute-start.7
  197.3 4.1 convolution_convert_fusion.refs_1_
  202.5 4.3 collective-permute-done.6
  206.8 2.5 maximum_select_fusion.1.g_ref
  209.4 2.7 copy.39.gt_ref
  212.1 7.2 %norm_two.1 = (bf16[1024,1024]{1,0:T(8,128)(2,1)}, bf16[1024,1024]{1,0:T(8,128)(2,1)}, f32[1024,1024]{1,0:T(8,128)}) custom-call(bf16[1024,1024]{1,0:T(8,128)(2,1)} %maximum_select_fusion.refs_0_, bf16[1024,1024]{1,0:T(8,128)(2,1)} %convolution_convert_fusion.refs_1_, bf16[1024,1024]{1,0:T(8,128)(2,1)} %collective-permute-done.4.refs_2_, ...), custom_call_target="tpu_custom_call" | custom-call | flops 20971520 | bytes 14680064 | tf_op jit(solution)/shard_map/norm_two/pallas_call | solution.py:275
  219.3 23.1 %mlp_first.1 = (bf16[1024,1024]{1,0:T(8,128)(2,1)}, bf16[1024,1024]{1,0:T(8,128)(2,1)}, bf16[1024,2048]{1,0:T(8,128)(2,1)}, f32[1,1024]{1,0:T(1,128)}) custom-call(bf16[1024,1024]{1,0:T(8,128)(2,1)} %get-tuple-element.73.n_ref, bf16[1024,1024]{1,0:T(8,128)(2,1)} %copy-done.2, bf16[1024,1024]{1,0:T(8,128)(2,1)} %get-tuple-element.74.nt_ref, ...), custom_call_target="tpu_custom_call" | custom-call | flops 12884901888 | bytes 20971520 | tf_op jit(solution)/shard_map/mlp_first/pallas_call | solution.py:392
  243.7 24.2 %mlp_second.1 = (bf16[1024,1024]{1,0:T(8,128)(2,1)}, bf16[1024,1024]{1,0:T(8,128)(2,1)}, bf16[1024,2048]{1,0:T(8,128)(2,1)}, f32[1,1024]{1,0:T(1,128)}) custom-call(bf16[1024,1024]{1,0:T(8,128)(2,1)} %get-tuple-element.73.n_ref, bf16[1024,1024]{1,0:T(8,128)(2,1)} %copy-done.2, bf16[1024,1024]{1,0:T(8,128)(2,1)} %get-tuple-element.74.nt_ref, ...), custom_call_target="tpu_custom_call" | custom-call | flops 12884901888 | bytes 20971520 | tf_op jit(solution)/shard_map/mlp_second/pallas_call | solution.py:392
  268.1 4.2 collective-permute-done.11.other_ref
  273.7 9.1 %norm_two_back.1 = (f32[1024,1024]{1,0:T(8,128)}, bf16[1024,1024]{1,0:T(8,128)(2,1)}, bf16[1024,1024]{1,0:T(8,128)(2,1)}, f32[8,1024]{1,0:T(8,128)}) custom-call(f32[1024,1024]{1,0:T(8,128)} %get-tuple-element.72.hidden_ref, bf16[1024,1024]{1,0:T(8,128)(2,1)} %copy-done.2, bf16[1024,1024]{1,0:T(8,128)(2,1)} %get-tuple-element.80.own_ref, ...), custom_call_target="tpu_custom_call" | custom-call | flops 31457280 | bytes 16777216 | tf_op jit(solution)/shard_map/norm_two_back/pallas_call | solution.py:315
  282.7 8.4 %collective-permute-done.12 = bf16[1024,2048]{1,0:T(8,128)(2,1)} collective-permute-done((bf16[1024,2048]{1,0:T(8,128)(2,1)}, bf16[1024,2048]{1,0:T(8,128)(2,1)}, u32[]{:S(2)}, u32[]{:S(2)}) %collective-permute-start.12) | collective-permute-done | bytes 4194336 | tf_op jit(solution)/shard_map/ppermute | solution.py:641
  292.0 48.1 %collective-permute-done.26 = bf16[1024,2048]{1,0:T(8,128)(2,1)} collective-permute-done((bf16[1024,2048]{1,0:T(8,128)(2,1)}, bf16[1024,2048]{1,0:T(8,128)(2,1)}, u32[]{:S(2)}, u32[]{:S(2)}) %collective-permute-start.26) | collective-permute-done | bytes 4194336 | tf_op jit(solution)/shard_map/ppermute | solution.py:641
  340.1 21.8 %reduce-scatter.3.cloned.1.call-done.first_ref = bf16[64,2048]{1,0:T(8,128)(2,1)} async-done(((bf16[1024,2048]{1,0:T(8,128)(2,1)}), bf16[64,2048]{1,0:T(8,128)(2,1)}) %reduce-scatter.3.cloned.1.call-update) | async-done | bytes 262160 | tf_op jit(solution)/shard_map/reduce_scatter | solution.py:800
  361.9 3.5 convolution_convert_fusion.1.refs_7_.refs_8_
  365.4 24.3 %attn_backward.1.grads_ref.refs_0_ = bf16[3,1024,512]{2,1,0:T(8,128)(2,1)} custom-call(s32[1024,1]{1,0:T(8,128)} %copy.37.seg_col.refs_0_, s32[1,1024]{1,0:T(1,128)} %bitcast.41, bf16[1024,1536]{1,0:T(8,128)(2,1)} %qkv_project.1.q_ref.k_ref.v_ref.refs_2_.refs_3_.refs_4_, bf16[1024,1536]{1,0:T(8,128)(2,1)} %qkv_project.1.q_ref.k_ref.v_ref.refs_2_.refs_3_.refs_4_, ...), custom_call_target="tpu_custom_call" | custom-call | flops 5368709120 | bytes 8388608 | tf_op jit(solution)/shard_map/attn_backward/pallas_call | solution.py:185
  389.6 10.4 %weight_grads.1 = (bf16[256,2048]{1,0:T(8,128)(2,1)}, bf16[256,2048]{1,0:T(8,128)(2,1)}, bf16[128,2048]{1,0:T(8,128)(2,1)}, bf16[128,2048]{1,0:T(8,128)(2,1)}, bf16[256,2048]{1,0:T(8,128)(2,1)}) custom-call(s32[16]{0:T(128)} %stack.67.order, bf16[1024,1024]{1,0:T(8,128)(2,1)} %get-tuple-element.86.nt_ref, ...), custom_call_target="tpu_custom_call" | custom-call | flops 4294967296 | bytes 12582912 | tf_op jit(solution)/shard_map/weight_grads/pallas_call | solution.py:490
  402.4 2.3 constant_dynamic-slice_fusion
  405.1 7.7 %qkv_back.1.refs_0_ = bf16[1024,1024]{1,0:T(8,128)(2,1)} custom-call(bf16[3,1024,512]{2,1,0:T(8,128)(2,1)} %attn_backward.1.grads_ref.refs_0_, bf16[1024,2048]{1,0:T(8,128)(2,1)} %collective-permute-done.3.w_ref.refs_1_, bf16[256,2048]{1,0:T(8,128)(2,1)} %get-tuple-element.88.refs_2_), custom_call_target="tpu_custom_call" | custom-call | flops 3221225472 | bytes 8388608 | tf_op jit(solution)/shard_map/qkv_back/pallas_call | solution.py:530
  412.8 18.2 %collective-permute-done.14.refs_2_.from_y = bf16[256,2048]{1,0:T(8,128)(2,1)S(1)} collective-permute-done((bf16[256,2048]{1,0:T(8,128)(2,1)}, bf16[256,2048]{1,0:T(8,128)(2,1)S(1)}, u32[]{:S(2)}, u32[]{:S(2)}) %collective-permute-start.14) | collective-permute-done | bytes 1048608 | tf_op jit(solution)/shard_map/ppermute | solution.py:657
  432.3 3.1 sums_one.1
  437.8 3.5 add_convert_fusion
  441.3 1.9 convert_reduce_fusion.2
  444.6 2.0 collective-permute-start.18
  446.6 2.4 fusion.10
  449.0 3.8 fusion.9
  452.9 2.2 collective-permute-done.19
  456.3 23.9 %collective-permute-done.20 = f32[8,2048]{1,0:T(8,128)S(1)} collective-permute-done((f32[8,2048]{1,0:T(8,128)S(1)}, f32[8,2048]{1,0:T(8,128)S(1)}, u32[]{:S(2)}, u32[]{:S(2)}) %collective-permute-start.20) | collective-permute-done | bytes 65568 | tf_op jit(solution)/shard_map/ppermute | solution.py:657
  480.8 3.7 collective-permute-done.21
  485.1 3.3 sums_two.1
  488.5 1.8 collective-permute-start.24
  490.3 2.6 collective-permute-start.25
  492.9 5.5 %collective-permute-done.22.refs_0_ = bf16[80,2048]{1,0:T(8,128)(2,1)S(1)} collective-permute-done((bf16[80,2048]{1,0:T(8,128)(2,1)}, bf16[80,2048]{1,0:T(8,128)(2,1)S(1)}, u32[]{:S(2)}, u32[]{:S(2)}) %collective-permute-start.22) | collective-permute-done | bytes 327712 | tf_op jit(solution)/shard_map/ppermute | solution.py:649
  498.4 3.3 collective-permute-done.23.refs_1_
  501.7 6.6 %collective-permute-done.24.refs_2_ = bf16[80,2048]{1,0:T(8,128)(2,1)S(1)} collective-permute-done((bf16[80,2048]{1,0:T(8,128)(2,1)}, bf16[80,2048]{1,0:T(8,128)(2,1)S(1)}, u32[]{:S(2)}, u32[]{:S(2)}) %collective-permute-start.24) | collective-permute-done | bytes 327712 | tf_op jit(solution)/shard_map/ppermute | solution.py:649
  508.3 14.0 %collective-permute-done.25.refs_3_ = bf16[80,2048]{1,0:T(8,128)(2,1)S(1)} collective-permute-done((bf16[80,2048]{1,0:T(8,128)(2,1)}, bf16[80,2048]{1,0:T(8,128)(2,1)S(1)}, u32[]{:S(2)}, u32[]{:S(2)}) %collective-permute-start.25) | collective-permute-done | bytes 327712 | tf_op jit(solution)/shard_map/ppermute | solution.py:649
  523.0 2.1 sums_last.1
  528.0 2.1 units_last.1
  530.1 2.3 copy.55
  (140 shorter events, 26.5 us)
Async XLA Ops:
  7.2 107.7 %copy-start.25 = (s32[1024]{0:T(1024)S(1)}, s32[1024]{0:T(1024)}, u32[]{:S(2)}) copy-start(s32[1024]{0:T(1024)} %param.19) | copy-start | bytes 12292
  7.2 108.0 %copy-start.24 = (bf16[512,1024]{1,0:T(8,128)(2,1)S(1)}, bf16[512,1024]{1,0:T(8,128)(2,1)}, u32[]{:S(2)}) copy-start(bf16[512,1024]{1,0:T(8,128)(2,1)} %param.35) | copy-start | bytes 3145732
  7.2 109.2 %copy-start.21 = (f32[1024]{0:T(1024)S(1)}, f32[1024]{0:T(1024)}, u32[]{:S(2)}) copy-start(f32[1024]{0:T(1024)} %param.25) | copy-start | bytes 12292
  7.2 109.2 %copy-start.22 = (f32[1024]{0:T(1024)S(1)}, f32[1024]{0:T(1024)}, u32[]{:S(2)}) copy-start(f32[1024]{0:T(1024)} %param.26) | copy-start | bytes 12292
  7.2 55.3 %all-gather.6.cloned.1.call-start = ((), (), s32[]{:S(2)}) async-start(), calls=%async_computation.3 | async-start | bytes 4456448 | tf_op jit(solution)/shard_map/all_gather | solution.py:761
  9.0 105.3 %all-gather.8.cloned.1.call-start = ((), (), s32[]{:S(2)}) async-start(), calls=%async_computation.4 | async-start | bytes 4456448 | tf_op jit(solution)/shard_map/all_gather | solution.py:761
  9.1 13.2 %collective-permute-start = (bf16[512,1024]{1,0:T(8,128)(2,1)}, bf16[512,1024]{1,0:T(8,128)(2,1)S(1)}, u32[]{:S(2)}, u32[]{:S(2)}) collective-permute-start(bf16[512,1024]{1,0:T(8,128)(2,1)} %param.18), channel_id=1, source_target_pairs={{0,2},{1,0},{2,3},{3,1},{4,6},{5,4},{6,7},{7,5},{8,10},{9,8},{10,1... | collective-permute-start | bytes 3145736 | tf_op jit(solution)/shard_map/ppermute | solution.py:641
  25.1 169.6 %all-gather.4.cloned.1.call-start = ((), (), s32[]{:S(2)}) async-start(), calls=%async_computation.2 | async-start | bytes 4456448 | tf_op jit(solution)/shard_map/all_gather | solution.py:765
  25.9 336.0 %reduce-scatter.3.cloned.1.call-start = ((), (), s32[]{:S(2)}) async-start(), calls=%async_computation.5 | async-start | bytes 4456448 | tf_op jit(solution)/shard_map/reduce_scatter | solution.py:800
  62.5 108.7 %collective-permute-start.3 = (bf16[1024,2048]{1,0:T(8,128)(2,1)}, bf16[1024,2048]{1,0:T(8,128)(2,1)}, u32[]{:S(2)}, u32[]{:S(2)}) collective-permute-start(bf16[1024,2048]{1,0:T(8,128)(2,1)} %all-gather.6.cloned.1.call-done), channel_id=1, source_target_pairs={{0,2},{1,0},{2,3},{3,1},{4,6},{5,4},{6,7},{7,5},{8,10},{9,8},{10,1... | collective-permute-start | bytes 12582920 | tf_op jit(solution)/shard_map/ppermute | solution.py:641
  63.1 99.2 %collective-permute-start.1 = (bf16[512,1024]{1,0:T(8,128)(2,1)}, bf16[512,1024]{1,0:T(8,128)(2,1)S(1)}, u32[]{:S(2)}, u32[]{:S(2)}) collective-permute-start(bf16[512,1024]{1,0:T(8,128)(2,1)} %copy-done), channel_id=1, source_target_pairs={{0,2},{2,0},{1,3},{3,1},{4,6},{6,4},{5,7},{7,5},{8,10},{10,8},{9,1... | collective-permute-start | bytes 3145736 | tf_op jit(solution)/shard_map/ppermute | solution.py:723
  114.4 104.9 %collective-permute-start.8 = (bf16[1024,2048]{1,0:T(8,128)(2,1)}, bf16[1024,2048]{1,0:T(8,128)(2,1)}, u32[]{:S(2)}, u32[]{:S(2)}) collective-permute-start(bf16[1024,2048]{1,0:T(8,128)(2,1)} %all-gather.8.cloned.1.call-done), channel_id=1, source_target_pairs={{0,2},{1,0},{2,3},{3,1},{4,6},{5,4},{6,7},{7,5},{8,10},{9,8},{10,1... | collective-permute-start | bytes 12582920 | tf_op jit(solution)/shard_map/ppermute | solution.py:641
  114.9 46.3 %collective-permute-start.2 = (s32[1024]{0:T(1024)S(1)}, s32[1024]{0:T(1024)S(1)}, u32[]{:S(2)}, u32[]{:S(2)}) collective-permute-start(s32[1024]{0:T(1024)S(1)} %copy-done.25), channel_id=1, source_target_pairs={{0,2},{1,0},{2,3},{3,1},{4,6},{5,4},{6,7},{7,5},{8,10},{9,8},{10,1... | collective-permute-start | bytes 12296 | tf_op jit(solution)/shard_map/ppermute | solution.py:641
  115.2 86.2 %collective-permute-start.5 = (bf16[512,1024]{1,0:T(8,128)(2,1)S(1)}, bf16[512,1024]{1,0:T(8,128)(2,1)S(1)}, u32[]{:S(2)}, u32[]{:S(2)}) collective-permute-start(bf16[512,1024]{1,0:T(8,128)(2,1)S(1)} %copy-done.24), channel_id=1, source_target_pairs={{0,2},{1,0},{2,3},{3,1},{4,6},{5,4},{6,7},{7,5},{8,10},{9,8},{10,1... | collective-permute-start | bytes 3145736 | tf_op jit(solution)/shard_map/ppermute | solution.py:641
  161.3 5.0 copy-start.15
  194.7 7.2 %copy-start.18 = (f32[4096]{0:T(1024)S(1)}, f32[4096]{0:T(1024)}, u32[]{:S(2)}) copy-start(f32[4096]{0:T(1024)} %param.32) | copy-start | bytes 49156
  194.7 48.9 %collective-permute-start.7 = (bf16[1024,2048]{1,0:T(8,128)(2,1)}, bf16[1024,2048]{1,0:T(8,128)(2,1)}, u32[]{:S(2)}, u32[]{:S(2)}) collective-permute-start(bf16[1024,2048]{1,0:T(8,128)(2,1)} %all-gather.4.cloned.1.call-done), channel_id=1, source_target_pairs={{0,2},{1,0},{2,3},{3,1},{4,6},{5,4},{6,7},{7,5},{8,10},{9,8},{10,1... | collective-permute-start | bytes 12582920 | tf_op jit(solution)/shard_map/ppermute | solution.py:641
  201.4 10.7 %collective-permute-start.4 = (bf16[1024,1024]{1,0:T(8,128)(2,1)}, bf16[1024,1024]{1,0:T(8,128)(2,1)}, u32[]{:S(2)}, u32[]{:S(2)}) collective-permute-start(bf16[1024,1024]{1,0:T(8,128)(2,1)} %convolution_convert_fusion.refs_1_), channel_id=1, source_target_pairs={{0,2},{2,0},{1,3},{3,1},{4,6},{6,4},{5,7},{7,5},{8,10},{10,8},{9,1... | collective-permute-start | bytes 6291464 | tf_op jit(solution)/shard_map/ppermute | solution.py:723
  201.4 8.0 %copy-start.4 = (bf16[512,1024]{1,0:T(8,128)(2,1)}, bf16[512,1024]{1,0:T(8,128)(2,1)S(1)}, u32[]{:S(2)}) copy-start(bf16[512,1024]{1,0:T(8,128)(2,1)S(1)} %collective-permute-done.5) | copy-start | bytes 3145732
  201.4 5.4 %collective-permute-start.6 = (bf16[512,1024]{1,0:T(8,128)(2,1)S(1)}, bf16[512,1024]{1,0:T(8,128)(2,1)}, u32[]{:S(2)}, u32[]{:S(2)}) collective-permute-start(bf16[512,1024]{1,0:T(8,128)(2,1)S(1)} %collective-permute-done.5), channel_id=1, source_target_pairs={{0,2},{2,0},{1,3},{3,1},{4,6},{6,4},{5,7},{7,5},{8,10},{10,8},{9,1... | collective-permute-start | bytes 3145736 | tf_op jit(solution)/shard_map/ppermute | solution.py:723
  209.4 2.7 copy-start.2
  242.3 48.8 %collective-permute-start.12 = (bf16[1024,2048]{1,0:T(8,128)(2,1)}, bf16[1024,2048]{1,0:T(8,128)(2,1)}, u32[]{:S(2)}, u32[]{:S(2)}) collective-permute-start(bf16[1024,2048]{1,0:T(8,128)(2,1)} %get-tuple-element.83), channel_id=1, source_target_pairs={{2,0},{0,1},{3,2},{1,3},{6,4},{4,5},{7,6},{5,7},{10,8},{8,9},{11,1... | collective-permute-start | bytes 12582920 | tf_op jit(solution)/shard_map/ppermute | solution.py:641
  267.9 4.4 collective-permute-start.11
  291.2 236.8 %reduce-scatter.5.cloned.1.call-start = ((), (), s32[]{:S(2)}) async-start(), calls=%async_computation.6 | async-start | bytes 4456448 | tf_op jit(solution)/shard_map/reduce_scatter | solution.py:804
  291.2 48.8 %collective-permute-start.26 = (bf16[1024,2048]{1,0:T(8,128)(2,1)}, bf16[1024,2048]{1,0:T(8,128)(2,1)}, u32[]{:S(2)}, u32[]{:S(2)}) collective-permute-start(bf16[1024,2048]{1,0:T(8,128)(2,1)} %get-tuple-element.113), channel_id=1, source_target_pairs={{2,0},{0,1},{3,2},{1,3},{6,4},{4,5},{7,6},{5,7},{10,8},{8,9},{11,1... | collective-permute-start | bytes 12582920 | tf_op jit(solution)/shard_map/ppermute | solution.py:641
  340.1 21.8 %copy-start.23 = (bf16[1024,1024]{1,0:T(8,128)(2,1)S(1)}, bf16[1024,1024]{1,0:T(8,128)(2,1)}, u32[]{:S(2)}) copy-start(bf16[1024,1024]{1,0:T(8,128)(2,1)} %get-tuple-element.85) | copy-start | bytes 6291460
  389.6 12.5 %copy-start.1 = (bf16[512,1024]{1,0:T(8,128)(2,1)S(1)}, bf16[512,1024]{1,0:T(8,128)(2,1)}, u32[]{:S(2)}) copy-start(bf16[512,1024]{1,0:T(8,128)(2,1)} %copy-done) | copy-start | bytes 3145732
  400.1 30.9 %collective-permute-start.14 = (bf16[256,2048]{1,0:T(8,128)(2,1)}, bf16[256,2048]{1,0:T(8,128)(2,1)S(1)}, u32[]{:S(2)}, u32[]{:S(2)}) collective-permute-start(bf16[256,2048]{1,0:T(8,128)(2,1)} %get-tuple-element.89), channel_id=1, source_target_pairs={{0,4},{1,5},{2,6},{3,7},{4,0},{5,1},{6,2},{7,3},{8,12},{9,13},{10,... | collective-permute-start | bytes 3145736 | tf_op jit(solution)/shard_map/ppermute | solution.py:657
  401.6 29.4 %collective-permute-start.13 = (bf16[256,2048]{1,0:T(8,128)(2,1)}, bf16[256,2048]{1,0:T(8,128)(2,1)S(1)}, u32[]{:S(2)}, u32[]{:S(2)}) collective-permute-start(bf16[256,2048]{1,0:T(8,128)(2,1)} %get-tuple-element.88.refs_2_), channel_id=1, source_target_pairs={{0,1},{1,0},{2,3},{3,2},{4,5},{5,4},{6,7},{7,6},{8,9},{9,8},{10,11... | collective-permute-start | bytes 3145736 | tf_op jit(solution)/shard_map/ppermute | solution.py:657
  404.7 32.6 %collective-permute-start.9 = (bf16[512,1024]{1,0:T(8,128)(2,1)}, bf16[512,1024]{1,0:T(8,128)(2,1)}, u32[]{:S(2)}, u32[]{:S(2)}) collective-permute-start(bf16[512,1024]{1,0:T(8,128)(2,1)} %constant_dynamic-slice_fusion), channel_id=1, source_target_pairs={{0,2},{2,0},{1,3},{3,1},{4,6},{6,4},{5,7},{7,5},{8,10},{10,8},{9,1... | collective-permute-start | bytes 3145736 | tf_op jit(solution)/shard_map/ppermute | solution.py:723
  432.3 3.1 copy-start.3
  436.5 10.1 %collective-permute-start.15 = (bf16[512,1024]{1,0:T(8,128)(2,1)}, bf16[512,1024]{1,0:T(8,128)(2,1)}, u32[]{:S(2)}, u32[]{:S(2)}) collective-permute-start(bf16[512,1024]{1,0:T(8,128)(2,1)} %constant_dynamic-slice_fusion.1), channel_id=1, source_target_pairs={{0,2},{2,0},{1,3},{3,1},{4,6},{6,4},{5,7},{7,5},{8,10},{10,8},{9,1... | collective-permute-start | bytes 3145736 | tf_op jit(solution)/shard_map/ppermute | solution.py:723
  437.3 4.0 copy-start.16
  441.3 5.3 copy-start.14
  441.3 49.0 %collective-permute-start.10 = (bf16[512,1024]{1,0:T(8,128)(2,1)}, bf16[512,1024]{1,0:T(8,128)(2,1)}, u32[]{:S(2)}, u32[]{:S(2)}) collective-permute-start(bf16[512,1024]{1,0:T(8,128)(2,1)} %add_convert_fusion), channel_id=1, source_target_pairs={{2,0},{0,1},{3,2},{1,3},{6,4},{4,5},{7,6},{5,7},{10,8},{8,9},{11,1... | collective-permute-start | bytes 3145736 | tf_op jit(solution)/shard_map/ppermute | solution.py:641
  443.9 41.2 %collective-permute-start.17 = (bf16[128,2048]{1,0:T(8,128)(2,1)}, bf16[128,2048]{1,0:T(8,128)(2,1)}, u32[]{:S(2)}, u32[]{:S(2)}) collective-permute-start(bf16[128,2048]{1,0:T(8,128)(2,1)} %get-tuple-element.99), channel_id=1, source_target_pairs={{0,4},{1,5},{2,6},{3,7},{4,0},{5,1},{6,2},{7,3},{8,12},{9,13},{10,... | collective-permute-start | bytes 1572872 | tf_op jit(solution)/shard_map/ppermute | solution.py:657
  444.6 40.6 %collective-permute-start.18 = (bf16[128,2048]{1,0:T(8,128)(2,1)}, bf16[128,2048]{1,0:T(8,128)(2,1)}, u32[]{:S(2)}, u32[]{:S(2)}) collective-permute-start(bf16[128,2048]{1,0:T(8,128)(2,1)} %get-tuple-element.100), channel_id=1, source_target_pairs={{0,1},{1,0},{2,3},{3,2},{4,5},{5,4},{6,7},{7,6},{8,9},{9,8},{10,11... | collective-permute-start | bytes 1572872 | tf_op jit(solution)/shard_map/ppermute | solution.py:657
  452.7 75.3 %collective-permute-start.16 = (bf16[512,1024]{1,0:T(8,128)(2,1)}, bf16[512,1024]{1,0:T(8,128)(2,1)S(1)}, u32[]{:S(2)}, u32[]{:S(2)}) collective-permute-start(bf16[512,1024]{1,0:T(8,128)(2,1)} %fusion.9), channel_id=1, source_target_pairs={{2,0},{0,1},{3,2},{1,3},{6,4},{4,5},{7,6},{5,7},{10,8},{8,9},{11,1... | collective-permute-start | bytes 3145736 | tf_op jit(solution)/shard_map/ppermute | solution.py:641
  452.8 2.3 collective-permute-start.19
  455.1 25.0 %collective-permute-start.20 = (f32[8,2048]{1,0:T(8,128)S(1)}, f32[8,2048]{1,0:T(8,128)S(1)}, u32[]{:S(2)}, u32[]{:S(2)}) collective-permute-start(f32[8,2048]{1,0:T(8,128)S(1)} %add.140), channel_id=1, source_target_pairs={{0,1},{1,0},{2,3},{3,2},{4,5},{5,4},{6,7},{7,6},{8,9},{9,8},{10,11... | collective-permute-start | bytes 196616 | tf_op jit(solution)/shard_map/ppermute | solution.py:657
  480.2 4.3 collective-permute-start.21
  488.5 9.9 %collective-permute-start.22 = (bf16[80,2048]{1,0:T(8,128)(2,1)}, bf16[80,2048]{1,0:T(8,128)(2,1)S(1)}, u32[]{:S(2)}, u32[]{:S(2)}) collective-permute-start(bf16[80,2048]{1,0:T(8,128)(2,1)} %get-tuple-element.104), channel_id=1, source_target_pairs={{2,0},{0,1},{3,2},{1,3},{6,4},{4,5},{7,6},{5,7},{10,8},{8,9},{11,1... | collective-permute-start | bytes 983048 | tf_op jit(solution)/shard_map/ppermute | solution.py:649
  488.5 13.2 %collective-permute-start.23 = (bf16[80,2048]{1,0:T(8,128)(2,1)}, bf16[80,2048]{1,0:T(8,128)(2,1)S(1)}, u32[]{:S(2)}, u32[]{:S(2)}) collective-permute-start(bf16[80,2048]{1,0:T(8,128)(2,1)} %get-tuple-element.105), channel_id=1, source_target_pairs={{10,0},{8,1},{11,2},{9,3},{14,4},{12,5},{15,6},{13,7},{2,8},{0,9},... | collective-permute-start | bytes 983048 | tf_op jit(solution)/shard_map/ppermute | solution.py:649
  488.5 19.8 %collective-permute-start.24 = (bf16[80,2048]{1,0:T(8,128)(2,1)}, bf16[80,2048]{1,0:T(8,128)(2,1)S(1)}, u32[]{:S(2)}, u32[]{:S(2)}) collective-permute-start(bf16[80,2048]{1,0:T(8,128)(2,1)} %get-tuple-element.106), channel_id=1, source_target_pairs={{18,0},{16,1},{19,2},{17,3},{22,4},{20,5},{23,6},{21,7},{26,8},{24... | collective-permute-start | bytes 983048 | tf_op jit(solution)/shard_map/ppermute | solution.py:649
  490.3 32.0 %collective-permute-start.25 = (bf16[80,2048]{1,0:T(8,128)(2,1)}, bf16[80,2048]{1,0:T(8,128)(2,1)S(1)}, u32[]{:S(2)}, u32[]{:S(2)}) collective-permute-start(bf16[80,2048]{1,0:T(8,128)(2,1)} %get-tuple-element.107), channel_id=1, source_target_pairs={{26,0},{24,1},{27,2},{25,3},{30,4},{28,5},{31,6},{29,7},{18,8},{16... | collective-permute-start | bytes 983048 | tf_op jit(solution)/shard_map/ppermute | solution.py:649
  498.4 23.9 %copy-start.10 = (bf16[80,2048]{1,0:T(8,128)(2,1)}, bf16[80,2048]{1,0:T(8,128)(2,1)S(1)}, u32[]{:S(2)}) copy-start(bf16[80,2048]{1,0:T(8,128)(2,1)S(1)} %collective-permute-done.22.refs_0_) | copy-start | bytes 983044
  501.7 20.5 %copy-start.11 = (bf16[80,2048]{1,0:T(8,128)(2,1)}, bf16[80,2048]{1,0:T(8,128)(2,1)S(1)}, u32[]{:S(2)}) copy-start(bf16[80,2048]{1,0:T(8,128)(2,1)S(1)} %collective-permute-done.23.refs_1_) | copy-start | bytes 983044
  508.3 14.0 %copy-start.12 = (bf16[80,2048]{1,0:T(8,128)(2,1)}, bf16[80,2048]{1,0:T(8,128)(2,1)S(1)}, u32[]{:S(2)}) copy-start(bf16[80,2048]{1,0:T(8,128)(2,1)S(1)} %collective-permute-done.24.refs_2_) | copy-start | bytes 983044
  (10 other events, 15.3 us)
Sparse Core Ops, SparseCore 0:
  10.8 51.6 all-gather.5
  65.3 49.0 all-gather.7
  116.5 49.0 all-gather.3
  291.3 70.5 reduce-scatter.2
  366.1 78.5 reduce-scatter.4

commit v3 on v2

--- a/solution.py
+++ b/solution.py
@@ -336,11 +336,11 @@
     )(hidden, grad, *partials, gain.reshape(1, width))
 
 
-def mlp_kernel(n_ref, g_ref, nt_ref, gt_ref, b_ref, w_ref, *refs, block, with_previous):
+def mlp_kernel(order, n_ref, g_ref, nt_ref, gt_ref, b_ref, w_ref, *refs, block, with_previous, cube):
     if with_previous:
         (before_out, before_gn), refs = refs[:2], refs[2:]
-    (out_ref, gn_ref, grad_ref), refs = refs[:3], refs[3:]
-    gb_ref, out_acc, gn_acc, act, gpre = refs
+    (out_ref, gn_ref), refs = refs[:2], refs[2:]
+    grad_refs, (gb_ref, out_acc, gn_acc, act, gpre, grad_w) = refs[:-6], refs[-6:]
     step = pl.program_id(0)
     length = n_ref.shape[0]
     tile = w_ref.shape[1] // 2
@@ -374,8 +374,12 @@
         out_acc[rows, :] += dot_nt(active, w_ref[:, downs])
         gn_acc[rows, :] += dot_nt(grad_pre, w_ref[:, ups])
     gb_ref[...] = bias_sum
-    grad_ref[:, ups] = dot_nn(nt_ref[...], gpre[...]).astype(BF16)
-    grad_ref[:, downs] = dot_nn(gt_ref[...], act[...]).astype(BF16)
+    for columns, left, right in ((ups, nt_ref, gpre), (downs, gt_ref, act)):
+        if cube:
+            grad_w[...] = dot_nn(left[...], right[...]).astype(BF16)
+            store_pieces(order, grad_w, grad_refs, columns)
+        else:
+            grad_refs[0][:, columns] = dot_nn(left[...], right[...]).astype(BF16)
 
     @pl.when(step == pl.num_programs(0) - 1)
     def _():
@@ -383,42 +387,48 @@
         gn_ref[...] = gn_acc[...].astype(BF16)
 
 
-def mlp(normed, grad, normed_t, grad_t, weights, bias, previous):
+def mlp(order, normed, grad, normed_t, grad_t, weights, bias, previous, cube):
     length, width = normed.shape
     units = weights.shape[1] // 2
     tile = min(TILE, units)
-    once = pl.Buffered(1)
-    at_tile = lambda rows, columns: pl.BlockSpec((rows, columns), lambda u: (0, u))
-    return pl.pallas_call(
-        functools.partial(mlp_kernel, block=min(256, length), with_previous=bool(previous)),
-        grid=(units // tile,),
-        in_specs=[
-            whole_spec((length, width), pipeline_mode=once),
-            whole_spec((length, width), pipeline_mode=once),
-            whole_spec((width, length), pipeline_mode=once),
-            whole_spec((width, length), pipeline_mode=once),
-            at_tile(1, tile),
-            at_tile(width, 2 * tile),
-        ]
-        + [whole_spec((length, width), pipeline_mode=once) for _ in previous],
-        out_specs=[
-            whole_spec((length, width)),
-            whole_spec((length, width)),
-            at_tile(width, 2 * tile),
-            at_tile(1, tile),
-        ],
-        out_shape=[
-            jax.ShapeDtypeStruct((length, width), BF16),
-            jax.ShapeDtypeStruct((length, width), BF16),
-            jax.ShapeDtypeStruct((width, 2 * units), BF16),
-            jax.ShapeDtypeStruct((1, units), F32),
-        ],
-        scratch_shapes=[
-            pltpu.VMEM((length, width), F32),
-            pltpu.VMEM((length, width), F32),
-            pltpu.VMEM((length, tile), BF16),
-            pltpu.VMEM((length, tile), BF16),
-        ],
+    at_tile = lambda rows, columns: pl.BlockSpec((rows, columns), lambda u, o: (0, u))
+    fixed = lambda shape: pl.BlockSpec(shape, lambda u, o: (0, 0))
+    once = lambda shape: pl.BlockSpec(shape, lambda u, o: (0, 0), pipeline_mode=pl.Buffered(1))
+    if cube:
+        count = order.shape[0]
+        grad_shapes = piece_shapes(count, width // count, 2 * units)
+    else:
+        grad_shapes = [jax.ShapeDtypeStruct((width, 2 * units), BF16)]
+    results = pl.pallas_call(
+        functools.partial(
+            mlp_kernel, block=min(256, length), with_previous=bool(previous), cube=cube
+        ),
+        grid_spec=pltpu.PrefetchScalarGridSpec(
+            num_scalar_prefetch=1,
+            grid=(units // tile,),
+            in_specs=[
+                once((length, width)),
+                once((length, width)),
+                once((width, length)),
+                once((width, length)),
+                at_tile(1, tile),
+                at_tile(width, 2 * tile),
+            ]
+            + [once((length, width)) for _ in previous],
+            out_specs=[fixed((length, width)), fixed((length, width))]
+            + [at_tile(shape.shape[0], 2 * tile) for shape in grad_shapes]
+            + [at_tile(1, tile)],
+            scratch_shapes=[
+                pltpu.VMEM((length, width), F32),
+                pltpu.VMEM((length, width), F32),
+                pltpu.VMEM((length, tile), BF16),
+                pltpu.VMEM((length, tile), BF16),
+                pltpu.VMEM((width, tile), BF16),
+            ],
+        ),
+        out_shape=[jax.ShapeDtypeStruct((length, width), BF16)] * 2
+        + grad_shapes
+        + [jax.ShapeDtypeStruct((1, units), F32)],
         compiler_params=pltpu.CompilerParams(vmem_limit_bytes=VMEM_BYTES),
         cost_estimate=pl.CostEstimate(
             flops=12 * length * width * units,
@@ -426,7 +436,8 @@
             transcendentals=length * units,
         ),
         name="mlp_second" if previous else "mlp_first",
-    )(normed, grad, normed_t, grad_t, bias.reshape(1, units), weights, *previous)
+    )(order, normed, grad, normed_t, grad_t, bias.reshape(1, units), weights, *previous)
+    return results[0], results[1], results[2:-1], results[-1]
 
 
 def qkv_kernel(n_ref, b_ref, w_ref, out_ref):
@@ -460,7 +471,7 @@
     )(normed, bias.reshape(1, 3 * columns), weights)
 
 
-def weight_kernel(order, nt_ref, grads_ref, gt_ref, mixed_ref, *refs):
+def weight_kernel(order, nt_ref, grads_ref, gt_ref, mixed_ref, order_only, *refs):
     piece_refs, grad = refs[:5], refs[5]
     part = pl.program_id(0)
 
@@ -482,7 +493,7 @@
 ORDER_ONLY = pl.BlockSpec(memory_space=pl.ANY)
 
 
-def weight_grads(order, normed_t, grads, grad_t, mixed):
+def weight_grads(order, normed_t, grads, grad_t, mixed, after):
     width, length = normed_t.shape
     columns = grads.shape[2]
     shapes = piece_shapes(order.shape[0], width // order.shape[0], 4 * columns)
@@ -497,6 +508,7 @@
                 pl.BlockSpec((1, length, columns), lambda k, o: (jnp.minimum(k, 2), 0, 0)),
                 fixed((width, length)),
                 fixed((length, columns)),
+                ORDER_ONLY,
             ],
             out_specs=[
                 pl.BlockSpec((shape.shape[0], columns), lambda k, o: (0, k)) for shape in shapes
@@ -511,7 +523,7 @@
             transcendentals=0,
         ),
         name="weight_grads",
-    )(order, normed_t, grads, grad_t, mixed)
+    )(order, normed_t, grads, grad_t, mixed, after)
 
 
 def qkv_back_kernel(grads_ref, w_ref, out_ref):
@@ -560,13 +572,16 @@
     x_ref[...] = added(keep_x[...], from_y[:half, :])
 
 
-def second_sums_kernel(from_x, from_y, near, from_y2, from_x2, small, *outs):
+def second_sums_kernel(from_x, from_y, near, from_y2, from_x2, *outs, with_small):
+    if with_small:
+        small, outs = outs[0], outs[1:]
     far = len(outs)
     half = from_y2.shape[0]
     rows = half * 2 // far
-    values = small[...]
-    high = values.astype(BF16).astype(F32)
-    extra = jnp.concatenate([high, values - high], axis=0).astype(BF16)
+    if with_small:
+        values = small[...]
+        high = values.astype(BF16).astype(F32)
+        extra = jnp.concatenate([high, values - high], axis=0).astype(BF16)
     for i, out in enumerate(outs):
         first, second, place = (from_x, from_y2, i) if i < far // 2 else (from_y, from_x2, i - far // 2)
         out[:rows, :] = added(
@@ -574,7 +589,16 @@
             first[half + place * rows : half + (place + 1) * rows, :],
             second[place * rows : (place + 1) * rows, :],
         )
-        out[rows:, :] = extra
+        if with_small:
+            out[rows:, :] = extra
+
+
+def total_kernel(*refs):
+    parts, out = refs[:-1], refs[-1]
+    total = parts[0][...].astype(F32)
+    for part in parts[1:]:
+        total = total + part[...].astype(F32)
+    out[...] = total
 
 
 def weights_last_kernel(*refs):
@@ -617,7 +641,7 @@
         out_specs=[vmem] * len(shapes),
         out_shape=shapes,
         compiler_params=pltpu.CompilerParams(vmem_limit_bytes=VMEM_BYTES),
-        cost_estimate=pl.CostEstimate(flops=0, bytes_accessed=32 * 1024 * 1024, transcendentals=0),
+        cost_estimate=pl.CostEstimate(flops=0, bytes_accessed=1024 * 1024, transcendentals=0),
         name=name,
     )(*([after] if after is not None else []), *operands)
 
@@ -668,28 +692,21 @@
         )
         return from_x, from_y, pieces[4], y_sum, x_sum
 
-    def scatter_far(state, small):
+    def far_sums(state, small, after):
         from_x, from_y, near, y_sum, x_sum = state
         columns = near.shape[1]
         from_y2, from_x2 = hop(y_sum, 1, 0), hop(x_sum, 0, 1)
-        rows, extra = near.shape[0] // far, 2 * small.shape[0]
-        sums = sums_call(
-            second_sums_kernel,
-            [from_x, from_y, near, from_y2, from_x2, small],
-            [jax.ShapeDtypeStruct((rows + extra, columns), BF16)] * far,
-            None,
+        rows = near.shape[0] // far + sum(2 * values.shape[0] for values in small)
+        return sums_call(
+            functools.partial(second_sums_kernel, with_small=bool(small)),
+            [from_x, from_y, near, from_y2, from_x2] + small,
+            [jax.ShapeDtypeStruct((rows, columns), BF16)] * far,
+            after,
             "sums_two",
         )
-        parts = [swap_hop(sums[i], 2 * i, inverse=True) for i in range(far)]
-        outs = sums_call(
-            weights_last_kernel,
-            parts,
-            [jax.ShapeDtypeStruct((rows, columns // 4), F32)] * 4
-            + [jax.ShapeDtypeStruct(small.shape, F32)],
-            None,
-            "sums_last",
-        )
-        return outs[:4], outs[4]
+
+    def far_parts(sums):
+        return [swap_hop(sums[i], 2 * i, inverse=True) for i in range(far)]
 
     def near_sum(values):
         values = values + lax.ppermute(values, "c", [(0, 1), (1, 0)])
@@ -702,7 +719,7 @@
     for a_low, h_mask in ((0, 0), (1, 0), (0, 1), (1, 1)):
         for i in range(far):
             order.append((a ^ (2 * i + a_low)) * 2 + (h ^ h_mask))
-    return swap, scatter_near, scatter_far, near_sum, jnp.stack(order).astype(jnp.int32)
+    return swap, scatter_near, far_sums, far_parts, near_sum, jnp.stack(order).astype(jnp.int32)
 
 
 def per_device(sizes, *arguments):
@@ -717,7 +734,7 @@
     unit_width = w_up.shape[1]
     half_units = unit_width // 2
     tile = min(TILE, half_units)
-    swap, scatter_near, scatter_far, near_sum, order = moves(sizes)
+    swap, scatter_near, far_sums, far_parts, near_sum, order = moves(sizes)
 
     def partner(values):
         return lax.ppermute(values, "c", [(0, 1), (1, 0)])
@@ -749,21 +766,19 @@
 
     own_input = swap(block_input)
     segments = swap(segment_ids)
+    own_grad = swap(out_grad)
     shard_first, shard_second = sums_call(
         functools.partial(shards_kernel, tile=tile),
         [w_up, w_down],
         [jax.ShapeDtypeStruct(w_up.shape, BF16)] * 2,
-        own_input,
+        None,
         "mlp_shards",
     )
-
-    def gather(shard):
-        return swap(lax.all_gather(shard, ("a", "c"), axis=0, tiled=True))
-
-    full_attn = gather(jnp.concatenate([w_query, w_key, w_value, w_out], axis=1))
-    full_first = gather(shard_first)
-    late_second = lax.all_gather(shard_second, ("a", "c"), axis=0, tiled=True)
-    own_grad = swap(out_grad)
+    early_attn = lax.all_gather(
+        jnp.concatenate([w_query, w_key, w_value, w_out], axis=1), ("a", "c"), axis=0, tiled=True
+    )
+    early_first = lax.all_gather(shard_first, ("a", "c"), axis=0, tiled=True)
+    shard_second = swap(shard_second)
     bias_query = lax.dynamic_slice_in_dim(b_query, rank * head_width, head_width)
     bias_value = lax.dynamic_slice_in_dim(b_value, rank * head_width, head_width)
     bias_up = lax.dynamic_slice_in_dim(b_up, rank * unit_width, unit_width)
@@ -772,22 +787,32 @@
     grad_rows = tp_gather(own_grad)
     grad_rows_t = grad_rows.T
     normed, normed_t = norm_rows(rows_in, ln1_gain, ln1_bias)
+    early_attn, normed, segments, grad_rows, grad_rows_t, shard_second = lax.optimization_barrier(
+        (early_attn, normed, segments, grad_rows, grad_rows_t, shard_second)
+    )
+    full_second = lax.all_gather(shard_second, ("a", "h"), axis=0, tiled=True)
+    full_attn = swap(early_attn)
     biases = jnp.concatenate([bias_query, jnp.zeros((head_width,), F32), bias_value])
     qkv = qkv_project(normed, full_attn, biases)
     full_out = full_attn[:, 3 * head_width :]
+    early_first, qkv = lax.optimization_barrier((early_first, qkv))
+    full_first = swap(early_first)
     mixed, lse = attn_forward(segments, qkv, head_width)
-    late_second, mixed = lax.optimization_barrier((late_second, mixed))
-    full_second = swap(late_second)
     attended = tp_terms(dot_nt(mixed, full_out).astype(BF16))
     normed_two, normed_two_t, hidden = norm_rows(rows_in, ln2_gain, ln2_bias, attended, b_out)
 
     out_part, gn_part, first_grads, bias_first = mlp(
-        normed_two, grad_rows, normed_two_t, grad_rows_t, full_first, bias_up[:half_units], ()
-    )
-    first_grads = swap(first_grads, inverse=True)
+        order, normed_two, grad_rows, normed_two_t, grad_rows_t, full_first,
+        bias_up[:half_units], (), True,
+    )
+    full_second, gn_part = lax.optimization_barrier((full_second, gn_part))
     out_part, gn_part, second_grads, bias_second = mlp(
-        normed_two, grad_rows, normed_two_t, grad_rows_t, full_second, bias_up[half_units:],
-        (out_part, gn_part),
+        order, normed_two, grad_rows, normed_two_t, grad_rows_t, full_second,
+        bias_up[half_units:], (out_part, gn_part), False,
+    )
+    first_state = scatter_near(first_grads, gn_part)
+    gn_part, second_grads, first_state = lax.optimization_barrier(
+        (gn_part, second_grads[0], first_state)
     )
     second_grads = swap(second_grads, inverse=True)
     own_output = (own(hidden) + tp_scatter(out_part) + b_down).astype(BF16)
@@ -796,13 +821,20 @@
     grad_hidden, grad_attended, grad_attended_t, sums_two = norm_back_rows(
         hidden, grad_rows, tp_terms(gn_part), ln2_gain
     )
-    first_grads, grad_attended = lax.optimization_barrier((first_grads, grad_attended))
-    first_mlp = lax.psum_scatter(first_grads, ("a", "c"), scatter_dimension=0, tiled=True)
     grad_mixed = dot_nn(grad_attended, full_out).astype(BF16)
-    grads = attn_backward(segments, qkv, mixed, lse, grad_mixed, head_width, grad_mixed)
-    second_grads, first_mlp = lax.optimization_barrier((second_grads, first_mlp))
+    first_sums = far_sums(first_state, [], grad_mixed)
+    grads = attn_backward(segments, qkv, mixed, lse, grad_mixed, head_width, first_sums[0])
+    block_rows = w_query.shape[0]
+    (first_mlp,) = sums_call(
+        total_kernel,
+        far_parts(first_sums),
+        [jax.ShapeDtypeStruct((block_rows, unit_width), F32)],
+        grads,
+        "units_first",
+    )
+    second_grads, grads = lax.optimization_barrier((second_grads, grads))
     second_mlp = lax.psum_scatter(second_grads, ("a", "c"), scatter_dimension=0, tiled=True)
-    pieces = weight_grads(order, normed_t, grads, grad_attended_t, mixed)
+    pieces = weight_grads(order, normed_t, grads, grad_attended_t, mixed, first_mlp)
     grad_normed_part = qkv_back(grads, full_attn, pieces[0])
     state = scatter_near(pieces, grad_normed_part)
     grad_normed_part, state = lax.optimization_barrier((grad_normed_part, state))
@@ -830,9 +862,8 @@
     columns = pieces[0].shape[1]
     filled = sums.shape[0]
     sums = jnp.pad(sums, (0, -filled % (8 * columns))).reshape(-1, columns)
-    late, sums = scatter_far(state, near_sum(sums))
-    sums = sums.reshape(-1)
-    shard = jax.ShapeDtypeStruct((w_query.shape[0], unit_width), F32)
+    sums = near_sum(sums)
+    shard = jax.ShapeDtypeStruct((block_rows, unit_width), F32)
     grad_w_up, grad_w_down = sums_call(
         functools.partial(units_last_kernel, tile=tile),
         [first_mlp, second_mlp],
@@ -840,6 +871,15 @@
         None,
         "units_last",
     )
+    *late, sums = sums_call(
+        weights_last_kernel,
+        far_parts(far_sums(state, [sums], None)),
+        [jax.ShapeDtypeStruct((block_rows, head_width), F32)] * 4
+        + [jax.ShapeDtypeStruct(sums.shape, F32)],
+        grad_w_up,
+        "sums_last",
+    )
+    sums = sums.reshape(-1)
     small = [sums[i * width : (i + 1) * width] for i in range(8)]
     return (
         output, grad_input, small[0], small[1],

time: 548 us -> 514 us (0.938)
  waiting for transfers between devices: 310 us -> 246 us
  starting transfers between devices: 18 us -> 34.4 us
  Pallas kernels: 147 us -> 158 us
    all_gather x3, waiting for transfers between devices: 87.9 us -> 13.1 us  [the longest x1 13.1 us: per_device(): lax.all_gather(jnp.concatenate([w_query, w_key, w_value, w_out], axis=1),...]
    ppermute x6 -> x10, waiting for transfers between devices: 45.8 us -> 73.2 us  [hop(): return lax.ppermute(values, ('a', 'c', 'h'), pairs)]
    reduce_scatter x1 -> x0, waiting for transfers between devices: 21.8 us -> none  [per_device(): lax.psum_scatter(first_grads, ('a', 'c'), scatter_dimension=0, tiled=True)]
    ppermute x4 -> x8, waiting for transfers between devices: 29.4 us -> 49 us  [swap_hop(): return lax.ppermute(values, ALL, pairs)]
    ppermute x6 -> x10, starting transfers between devices: 6.5 us -> 17.7 us  [hop(): return lax.ppermute(values, ('a', 'c', 'h'), pairs)]
    ppermute x10 -> x9, waiting for transfers between devices: 114 us -> 104 us  [swap(): return lax.ppermute(values, SWAP, pairs)]
    pallas_call x5 -> x8, Pallas kernels: 12.4 us -> 21.2 us  [sums_call(): pl.pallas_call(body, in_specs=([pl.BlockSpec(memory_space=pl.ANY)] if aft...]
    unnamed x63 -> x79, local copies, waits for them, and re-layouts: 11 us -> 13.5 us
  transfers between devices with their start and end apart: 32 -> 38, of which waited for: 18 -> 20; matrix products, arithmetic and copies ran while one was open for 7% -> 7% of each run, Pallas kernels for 27% -> 30%
where the time goes in v3:
time: 514 us; the launch traced here: 505 us
  waiting for transfers between devices  246 us (48%)
  Pallas kernels  158 us (31%)
  starting transfers between devices  34.4 us (7%)
  local copies, waits for them, and re-layouts  23.5 us (5%)
  other arithmetic  20.4 us (4%)
  between operations  14.6 us (3%)
  matrix products  8.28 us (2%)
    ppermute x9, waiting for transfers between devices, swap(): return lax.ppermute(values, SWAP, pairs)  104 us
    ppermute x10, waiting for transfers between devices, hop(): return lax.ppermute(values, ('a', 'c', 'h'), pairs)  73.2 us
    pallas_call x2, Pallas kernels, mlp(): pl.pallas_call(functools.partial(mlp_kernel, block=min(256, length), with...  49.1 us
    ppermute x8, waiting for transfers between devices, swap_hop(): return lax.ppermute(values, ALL, pairs)  49 us
    pallas_call x1, Pallas kernels, attn_backward(): pl.pallas_call(without(functools.partial(attn_backward_kernel, block=bloc...  24.3 us
    pallas_call x8, Pallas kernels, sums_call(): pl.pallas_call(body, in_specs=([pl.BlockSpec(memory_space=pl.ANY)] if aft...  21.2 us
    ppermute x10, starting transfers between devices, hop(): return lax.ppermute(values, ('a', 'c', 'h'), pairs)  17.7 us
    pallas_call x1, Pallas kernels, attn_forward(): pl.pallas_call(functools.partial(attn_forward_kernel, block=block), grid=...  16.4 us
  transfers between devices with their start and end apart: 38, of which 20 were waited for; matrix products, arithmetic and copies ran while one was open for 7% of the time, Pallas kernels for 30%

profile of v3, /device:TPU:10, one launch (start us, length us, event | category | flops | bytes accessed | tf_op | source)
XLA Modules:
  0.0 504.6 jit_solution(802595732024326581)
XLA Ops:
  11.5 12.6 %collective-permute-done = bf16[512,1024]{1,0:T(8,128)(2,1)S(1)} collective-permute-done((bf16[512,1024]{1,0:T(8,128)(2,1)}, bf16[512,1024]{1,0:T(8,128)(2,1)S(1)}, u32[]{:S(2)}, u32[]{:S(2)}) %collective-permute-start) | collective-permute-done | bytes 1048608 | tf_op jit(solution)/shard_map/ppermute | solution.py:665
  25.0 10.3 %collective-permute-done.3 = bf16[512,1024]{1,0:T(8,128)(2,1)S(1)} collective-permute-done((bf16[512,1024]{1,0:T(8,128)(2,1)}, bf16[512,1024]{1,0:T(8,128)(2,1)S(1)}, u32[]{:S(2)}, u32[]{:S(2)}) %collective-permute-start.3) | collective-permute-done | bytes 1048608 | tf_op jit(solution)/shard_map/ppermute | solution.py:665
  38.2 2.3 maximum_select_fusion.refs_0_
  40.5 3.4 maximum_select_fusion.1.g_ref
  43.9 5.5 %norm_one.1 = (bf16[1024,1024]{1,0:T(8,128)(2,1)}, bf16[1024,1024]{1,0:T(8,128)(2,1)}) custom-call(bf16[1024,1024]{1,0:T(8,128)(2,1)} %maximum_select_fusion.refs_0_, f32[1,1024]{1,0:T(1,128)} %bitcast.38, f32[1,1024]{1,0:T(1,128)} %bitcast.45), custom_call_target="tpu_custom_call" | custom-call | flops 20971520 | bytes 14680064 | tf_op jit(solution)/shard_map/norm_one/pallas_call | solution.py:275
  49.4 13.1 %all-gather.4.cloned.1.call-done = bf16[1024,2048]{1,0:T(8,128)(2,1)} async-done(((bf16[64,2048]{1,0:T(8,128)(2,1)}), bf16[1024,2048]{1,0:T(8,128)(2,1)}) %all-gather.4.cloned.1.call-update) | async-done | bytes 4194320 | tf_op jit(solution)/shard_map/all_gather | solution.py:777
  63.9 45.5 %collective-permute-done.6.w_ref.refs_1_ = bf16[1024,2048]{1,0:T(8,128)(2,1)} collective-permute-done((bf16[1024,2048]{1,0:T(8,128)(2,1)}, bf16[1024,2048]{1,0:T(8,128)(2,1)}, u32[]{:S(2)}, u32[]{:S(2)}) %collective-permute-start.6) | collective-permute-done | bytes 4194336 | tf_op jit(solution)/shard_map/ppermute | solution.py:665
  109.4 7.1 %qkv_project.1.q_ref.k_ref.v_ref.refs_2_.refs_3_.refs_4_ = bf16[1024,1536]{1,0:T(8,128)(2,1)} custom-call(bf16[1024,1024]{1,0:T(8,128)(2,1)} %get-tuple-element.95.n_ref, f32[1,1536]{1,0:T(1,128)} %reshape.105.b_ref, bf16[1024,2048]{1,0:T(8,128)(2,1)} %collective-permute-done.6.w_ref.refs_1_), custom_call_target="tpu_custom_call" | custom-call | flops 3221225472 | bytes 8388608 | tf_op jit(solution)/shard_map/qkv_project/pallas_call | solution.py:456
  116.5 2.5 collective-permute-start.8
  120.0 16.4 %attn_forward.1 = (bf16[1024,512]{1,0:T(8,128)(2,1)}, f32[4,8,1024]{2,1,0:T(8,128)}) custom-call(s32[1024,1]{1,0:T(8,128)} %copy.37.seg_col.refs_0_, s32[1,1024]{1,0:T(1,128)} %bitcast.40, bf16[1024,1536]{1,0:T(8,128)(2,1)} %qkv_project.1.q_ref.k_ref.v_ref.refs_2_.refs_3_.refs_4_, bf16[1024,1536]{1,0:T(8,128)(2,1)} %qkv_project.1.q_ref.k_ref.v_ref.refs_2_.refs_3_.refs_4_, ...), custom_call_target="tpu_custom_call" | custom-call | flops 2147483648 | bytes 4194304 | tf_op jit(solution)/shard_map/attn_forward/pallas_call | solution.py:156
  136.4 4.2 convolution_convert_fusion.refs_1_
  141.9 2.5 copy.39.gt_ref
  145.1 7.3 %norm_two.1 = (bf16[1024,1024]{1,0:T(8,128)(2,1)}, bf16[1024,1024]{1,0:T(8,128)(2,1)}, f32[1024,1024]{1,0:T(8,128)}) custom-call(bf16[1024,1024]{1,0:T(8,128)(2,1)} %maximum_select_fusion.refs_0_, bf16[1024,1024]{1,0:T(8,128)(2,1)} %convolution_convert_fusion.refs_1_, bf16[1024,1024]{1,0:T(8,128)(2,1)} %collective-permute-done.7.refs_2_, ...), custom_call_target="tpu_custom_call" | custom-call | flops 20971520 | bytes 14680064 | tf_op jit(solution)/shard_map/norm_two/pallas_call | solution.py:275
  152.4 35.9 %collective-permute-done.8.w_ref = bf16[1024,2048]{1,0:T(8,128)(2,1)} collective-permute-done((bf16[1024,2048]{1,0:T(8,128)(2,1)}, bf16[1024,2048]{1,0:T(8,128)(2,1)}, u32[]{:S(2)}, u32[]{:S(2)}) %collective-permute-start.8) | collective-permute-done | bytes 4194336 | tf_op jit(solution)/shard_map/ppermute | solution.py:665
  188.2 24.1 %mlp_first.1 = (bf16[1024,1024]{1,0:T(8,128)(2,1)}, bf16[1024,1024]{1,0:T(8,128)(2,1)}, bf16[256,2048]{1,0:T(8,128)(2,1)}, bf16[256,2048]{1,0:T(8,128)(2,1)}, bf...) custom-call(s32[16]{0:T(128)} %stack.67.order, ...), custom_call_target="tpu_custom_call" | custom-call | flops 12884901888 | bytes 20971520 | tf_op jit(solution)/shard_map/mlp_first/pallas_call | solution.py:402
  212.4 2.6 collective-permute-start.11
  215.0 24.9 %mlp_second.1 = (bf16[1024,1024]{1,0:T(8,128)(2,1)}, bf16[1024,1024]{1,0:T(8,128)(2,1)}, bf16[1024,2048]{1,0:T(8,128)(2,1)}, f32[1,1024]{1,0:T(1,128)}) custom-call(s32[16]{0:T(128)} %stack.67.order, bf16[1024,1024]{1,0:T(8,128)(2,1)} %get-tuple-element.100.n_ref, bf16[1024,1024]{1,0:T(8,128)(2,1)} %copy-done, bf16[1024,1024]{1,0:T(8,128)(2,1)} %get-tuple-element.102.nt_ref, ...), custom_call_target="tpu_custom_call" | custom-call | flops 12884901888 | bytes 20971520 | tf_op jit(solution)/shard_map/mlp_second/pallas_call | solution.py:402
  241.2 3.1 sums_one.2
  248.4 3.4 collective-permute-done.13.other_ref
  253.1 9.1 %norm_two_back.1 = (f32[1024,1024]{1,0:T(8,128)}, bf16[1024,1024]{1,0:T(8,128)(2,1)}, bf16[1024,1024]{1,0:T(8,128)(2,1)}, f32[8,1024]{1,0:T(8,128)}) custom-call(f32[1024,1024]{1,0:T(8,128)} %get-tuple-element.99.hidden_ref, bf16[1024,1024]{1,0:T(8,128)(2,1)} %copy-done, bf16[1024,1024]{1,0:T(8,128)(2,1)} %get-tuple-element.120.refs_0_.own_ref, ...), custom_call_target="tpu_custom_call" | custom-call | flops 31457280 | bytes 16777216 | tf_op jit(solution)/shard_map/norm_two_back/pallas_call | solution.py:315
  262.2 4.1 convolution_convert_fusion.1.refs_0_.refs_7_
  266.3 38.1 %collective-permute-done.16.refs_5_ = bf16[128,2048]{1,0:T(8,128)(2,1)} collective-permute-done((bf16[128,2048]{1,0:T(8,128)(2,1)}, bf16[128,2048]{1,0:T(8,128)(2,1)}, u32[]{:S(2)}, u32[]{:S(2)}) %collective-permute-start.16) | collective-permute-done | bytes 524320 | tf_op jit(solution)/shard_map/ppermute | solution.py:681
  304.4 3.2 sums_two.2
  307.6 24.3 %attn_backward.1.refs_0_.grads_ref = bf16[3,1024,512]{2,1,0:T(8,128)(2,1)} custom-call(s32[1024,1]{1,0:T(8,128)} %copy.37.seg_col.refs_0_, s32[1,1024]{1,0:T(1,128)} %bitcast.41, bf16[1024,1536]{1,0:T(8,128)(2,1)} %qkv_project.1.q_ref.k_ref.v_ref.refs_2_.refs_3_.refs_4_, bf16[1024,1536]{1,0:T(8,128)(2,1)} %qkv_project.1.q_ref.k_ref.v_ref.refs_2_.refs_3_.refs_4_, ...), custom_call_target="tpu_custom_call" | custom-call | flops 5368709120 | bytes 8388608 | tf_op jit(solution)/shard_map/attn_backward/pallas_call | solution.py:185
  334.9 2.3 collective-permute-start.17
  337.2 6.0 %collective-permute-done.18.refs_2_ = bf16[64,2048]{1,0:T(8,128)(2,1)S(1)} collective-permute-done((bf16[64,2048]{1,0:T(8,128)(2,1)S(1)}, bf16[64,2048]{1,0:T(8,128)(2,1)S(1)}, u32[]{:S(2)}, u32[]{:S(2)}) %collective-permute-start.18) | collective-permute-done | bytes 262176 | tf_op jit(solution)/shard_map/ppermute | solution.py:673
  343.1 7.2 %collective-permute-done.19.refs_3_ = bf16[64,2048]{1,0:T(8,128)(2,1)S(1)} collective-permute-done((bf16[64,2048]{1,0:T(8,128)(2,1)S(1)}, bf16[64,2048]{1,0:T(8,128)(2,1)S(1)}, u32[]{:S(2)}, u32[]{:S(2)}) %collective-permute-start.19) | collective-permute-done | bytes 262176 | tf_op jit(solution)/shard_map/ppermute | solution.py:673
  350.4 8.7 %collective-permute-done.20.refs_4_ = bf16[64,2048]{1,0:T(8,128)(2,1)S(1)} collective-permute-done((bf16[64,2048]{1,0:T(8,128)(2,1)S(1)}, bf16[64,2048]{1,0:T(8,128)(2,1)S(1)}, u32[]{:S(2)}, u32[]{:S(2)}) %collective-permute-start.20) | collective-permute-done | bytes 262176 | tf_op jit(solution)/shard_map/ppermute | solution.py:673
  360.4 2.3 units_first.1.order_only.first_ref
  362.7 10.1 %weight_grads.1 = (bf16[256,2048]{1,0:T(8,128)(2,1)}, bf16[256,2048]{1,0:T(8,128)(2,1)}, bf16[128,2048]{1,0:T(8,128)(2,1)}, bf16[128,2048]{1,0:T(8,128)(2,1)}, bf16[256,2048]{1,0:T(8,128)(2,1)}) custom-call(s32[16]{0:T(128)} %stack.67.order, bf16[1024,1024]{1,0:T(8,128)(2,1)} %get-tuple-element.132.nt_ref, ...), custom_call_target="tpu_custom_call" | custom-call | flops 4294967296 | bytes 12582912 | tf_op jit(solution)/shard_map/weight_grads/pallas_call | solution.py:501
  376.2 2.3 constant_dynamic-slice_fusion
  378.9 7.8 %qkv_back.1.refs_0_ = bf16[1024,1024]{1,0:T(8,128)(2,1)} custom-call(bf16[3,1024,512]{2,1,0:T(8,128)(2,1)} %attn_backward.1.refs_0_.grads_ref, bf16[1024,2048]{1,0:T(8,128)(2,1)} %collective-permute-done.6.w_ref.refs_1_, bf16[256,2048]{1,0:T(8,128)(2,1)} %get-tuple-element.137.refs_2_), custom_call_target="tpu_custom_call" | custom-call | flops 3221225472 | bytes 8388608 | tf_op jit(solution)/shard_map/qkv_back/pallas_call | solution.py:542
  386.6 10.2 %collective-permute-done.22.refs_2_.from_y = bf16[256,2048]{1,0:T(8,128)(2,1)S(1)} collective-permute-done((bf16[256,2048]{1,0:T(8,128)(2,1)}, bf16[256,2048]{1,0:T(8,128)(2,1)S(1)}, u32[]{:S(2)}, u32[]{:S(2)}) %collective-permute-start.22) | collective-permute-done | bytes 1048608 | tf_op jit(solution)/shard_map/ppermute | solution.py:681
  398.2 3.1 sums_one.3
  403.6 3.5 add_convert_fusion
  410.1 4.0 collective-permute-start.26
  414.1 2.4 fusion.10
  416.5 3.8 fusion.9
  423.7 22.4 %collective-permute-done.28 = f32[8,2048]{1,0:T(8,128)S(1)} collective-permute-done((f32[8,2048]{1,0:T(8,128)S(1)}, f32[8,2048]{1,0:T(8,128)S(1)}, u32[]{:S(2)}, u32[]{:S(2)}) %collective-permute-start.28) | collective-permute-done | bytes 65568 | tf_op jit(solution)/shard_map/ppermute | solution.py:681
  446.2 2.4 collective-permute-start.29
  448.6 2.2 collective-permute-done.29
  451.5 3.4 sums_two.3
  454.9 3.0 collective-permute-start.32
  461.4 3.4 collective-permute-done.30.refs_1_
  464.8 4.1 collective-permute-done.31.refs_2_
  468.9 10.3 %collective-permute-done.32.refs_3_ = bf16[80,2048]{1,0:T(8,128)(2,1)S(1)} collective-permute-done((bf16[80,2048]{1,0:T(8,128)(2,1)}, bf16[80,2048]{1,0:T(8,128)(2,1)S(1)}, u32[]{:S(2)}, u32[]{:S(2)}) %collective-permute-start.32) | collective-permute-done | bytes 327712 | tf_op jit(solution)/shard_map/ppermute | solution.py:673
  479.2 9.4 %collective-permute-done.33.refs_4_ = bf16[80,2048]{1,0:T(8,128)(2,1)S(1)} collective-permute-done((bf16[80,2048]{1,0:T(8,128)(2,1)}, bf16[80,2048]{1,0:T(8,128)(2,1)S(1)}, u32[]{:S(2)}, u32[]{:S(2)}) %collective-permute-start.33) | collective-permute-done | bytes 327712 | tf_op jit(solution)/shard_map/ppermute | solution.py:673
  494.4 2.3 copy.55
  (170 shorter events, 48.0 us)
Async XLA Ops:
  7.2 55.3 %all-gather.4.cloned.1.call-start = ((), (), s32[]{:S(2)}) async-start(), calls=%async_computation.1 | async-start | bytes 4456448 | tf_op jit(solution)/shard_map/all_gather | solution.py:777
  8.9 107.6 %all-gather.6.cloned.1.call-start = ((), (), s32[]{:S(2)}) async-start(), calls=%async_computation.2 | async-start | bytes 4456448 | tf_op jit(solution)/shard_map/all_gather | solution.py:780
  10.8 201.6 %all-gather.8.cloned.1.call-start = ((), (), s32[]{:S(2)}) async-start(), calls=%async_computation.3 | async-start | bytes 4456448 | tf_op jit(solution)/shard_map/all_gather | solution.py:793
  10.9 13.2 %collective-permute-start = (bf16[512,1024]{1,0:T(8,128)(2,1)}, bf16[512,1024]{1,0:T(8,128)(2,1)S(1)}, u32[]{:S(2)}, u32[]{:S(2)}) collective-permute-start(bf16[512,1024]{1,0:T(8,128)(2,1)} %param.18), channel_id=1, source_target_pairs={{0,2},{1,0},{2,3},{3,1},{4,6},{5,4},{6,7},{7,5},{8,10},{9,8},{10,1... | collective-permute-start | bytes 3145736 | tf_op jit(solution)/shard_map/ppermute | solution.py:665
  11.4 23.9 %collective-permute-start.3 = (bf16[512,1024]{1,0:T(8,128)(2,1)}, bf16[512,1024]{1,0:T(8,128)(2,1)S(1)}, u32[]{:S(2)}, u32[]{:S(2)}) collective-permute-start(bf16[512,1024]{1,0:T(8,128)(2,1)} %param.35), channel_id=1, source_target_pairs={{0,2},{1,0},{2,3},{3,1},{4,6},{5,4},{6,7},{7,5},{8,10},{9,8},{10,1... | collective-permute-start | bytes 3145736 | tf_op jit(solution)/shard_map/ppermute | solution.py:665
  24.1 14.1 %collective-permute-start.1 = (bf16[512,1024]{1,0:T(8,128)(2,1)S(1)}, bf16[512,1024]{1,0:T(8,128)(2,1)S(1)}, u32[]{:S(2)}, u32[]{:S(2)}) collective-permute-start(bf16[512,1024]{1,0:T(8,128)(2,1)S(1)} %collective-permute-done), channel_id=1, source_target_pairs={{0,2},{2,0},{1,3},{3,1},{4,6},{6,4},{5,7},{7,5},{8,10},{10,8},{9,1... | collective-permute-start | bytes 3145736 | tf_op jit(solution)/shard_map/ppermute | solution.py:740
  35.3 5.2 %collective-permute-start.4 = (bf16[512,1024]{1,0:T(8,128)(2,1)S(1)}, bf16[512,1024]{1,0:T(8,128)(2,1)}, u32[]{:S(2)}, u32[]{:S(2)}) collective-permute-start(bf16[512,1024]{1,0:T(8,128)(2,1)S(1)} %collective-permute-done.3), channel_id=1, source_target_pairs={{0,2},{2,0},{1,3},{3,1},{4,6},{6,4},{5,7},{7,5},{8,10},{10,8},{9,1... | collective-permute-start | bytes 3145736 | tf_op jit(solution)/shard_map/ppermute | solution.py:740
  35.8 13.6 %collective-permute-start.2 = (s32[1024]{0:T(1024)}, s32[1024]{0:T(1024)S(1)}, u32[]{:S(2)}, u32[]{:S(2)}) collective-permute-start(s32[1024]{0:T(1024)} %param.19), channel_id=1, source_target_pairs={{0,2},{1,0},{2,3},{3,1},{4,6},{5,4},{6,7},{7,5},{8,10},{9,8},{10,1... | collective-permute-start | bytes 12296 | tf_op jit(solution)/shard_map/ppermute | solution.py:665
  37.7 11.7 %collective-permute-start.5 = (bf16[64,2048]{1,0:T(8,128)(2,1)}, bf16[64,2048]{1,0:T(8,128)(2,1)S(1)}, u32[]{:S(2)}, u32[]{:S(2)}) collective-permute-start(bf16[64,2048]{1,0:T(8,128)(2,1)} %get-tuple-element.92), channel_id=1, source_target_pairs={{0,2},{1,0},{2,3},{3,1},{4,6},{5,4},{6,7},{7,5},{8,10},{9,8},{10,1... | collective-permute-start | bytes 786440 | tf_op jit(solution)/shard_map/ppermute | solution.py:665
  43.9 98.0 %copy-start = (bf16[1024,1024]{1,0:T(8,128)(2,1)}, bf16[1024,1024]{1,0:T(8,128)(2,1)S(1)}, u32[]{:S(2)}) copy-start(bf16[1024,1024]{1,0:T(8,128)(2,1)S(1)} %maximum_select_fusion.1.g_ref) | copy-start | bytes 6291460
  43.9 19.3 %copy-start.28 = (f32[1024]{0:T(1024)S(1)}, f32[1024]{0:T(1024)}, u32[]{:S(2)}) copy-start(f32[1024]{0:T(1024)} %param.25) | copy-start | bytes 12292
  43.9 19.3 %copy-start.29 = (f32[1024]{0:T(1024)S(1)}, f32[1024]{0:T(1024)}, u32[]{:S(2)}) copy-start(f32[1024]{0:T(1024)} %param.26) | copy-start | bytes 12292
  49.4 69.6 %copy-start.22 = (s32[1024]{0:T(1024)}, s32[1024]{0:T(1024)S(1)}, u32[]{:S(2)}) copy-start(s32[1024]{0:T(1024)S(1)} %collective-permute-done.2) | copy-start | bytes 12292
  49.4 13.6 %copy-start.20 = (bf16[64,2048]{1,0:T(8,128)(2,1)}, bf16[64,2048]{1,0:T(8,128)(2,1)S(1)}, u32[]{:S(2)}) copy-start(bf16[64,2048]{1,0:T(8,128)(2,1)S(1)} %collective-permute-done.5) | copy-start | bytes 786436
  62.5 46.9 %collective-permute-start.6 = (bf16[1024,2048]{1,0:T(8,128)(2,1)}, bf16[1024,2048]{1,0:T(8,128)(2,1)}, u32[]{:S(2)}, u32[]{:S(2)}) collective-permute-start(bf16[1024,2048]{1,0:T(8,128)(2,1)} %all-gather.4.cloned.1.call-done), channel_id=1, source_target_pairs={{0,2},{1,0},{2,3},{3,1},{4,6},{5,4},{6,7},{7,5},{8,10},{9,8},{10,1... | collective-permute-start | bytes 12582920 | tf_op jit(solution)/shard_map/ppermute | solution.py:665
  63.1 396.2 %reduce-scatter.2.cloned.1.call-start = ((), (), s32[]{:S(2)}) async-start(), calls=%async_computation.4 | async-start | bytes 4456448 | tf_op jit(solution)/shard_map/reduce_scatter | solution.py:836
  116.5 71.7 %collective-permute-start.8 = (bf16[1024,2048]{1,0:T(8,128)(2,1)}, bf16[1024,2048]{1,0:T(8,128)(2,1)}, u32[]{:S(2)}, u32[]{:S(2)}) collective-permute-start(bf16[1024,2048]{1,0:T(8,128)(2,1)} %all-gather.6.cloned.1.call-done), channel_id=1, source_target_pairs={{0,2},{1,0},{2,3},{3,1},{4,6},{5,4},{6,7},{7,5},{8,10},{9,8},{10,1... | collective-permute-start | bytes 12582920 | tf_op jit(solution)/shard_map/ppermute | solution.py:665
  140.6 4.5 collective-permute-start.7
  212.4 27.5 %collective-permute-start.11 = (bf16[256,2048]{1,0:T(8,128)(2,1)}, bf16[256,2048]{1,0:T(8,128)(2,1)S(1)}, u32[]{:S(2)}, u32[]{:S(2)}) collective-permute-start(bf16[256,2048]{1,0:T(8,128)(2,1)} %get-tuple-element.113), channel_id=1, source_target_pairs={{0,1},{1,0},{2,3},{3,2},{4,5},{5,4},{6,7},{7,6},{8,9},{9,8},{10,11... | collective-permute-start | bytes 3145736 | tf_op jit(solution)/shard_map/ppermute | solution.py:681
  214.9 25.0 %collective-permute-start.12 = (bf16[256,2048]{1,0:T(8,128)(2,1)}, bf16[256,2048]{1,0:T(8,128)(2,1)S(1)}, u32[]{:S(2)}, u32[]{:S(2)}) collective-permute-start(bf16[256,2048]{1,0:T(8,128)(2,1)} %get-tuple-element.114), channel_id=1, source_target_pairs={{0,4},{1,5},{2,6},{3,7},{4,0},{5,1},{6,2},{7,3},{8,12},{9,13},{10,... | collective-permute-start | bytes 3145736 | tf_op jit(solution)/shard_map/ppermute | solution.py:681
  244.3 87.6 %collective-permute-start.14 = (bf16[1024,2048]{1,0:T(8,128)(2,1)}, bf16[1024,2048]{1,0:T(8,128)(2,1)}, u32[]{:S(2)}, u32[]{:S(2)}) collective-permute-start(bf16[1024,2048]{1,0:T(8,128)(2,1)} %get-tuple-element.122), channel_id=1, source_target_pairs={{2,0},{0,1},{3,2},{1,3},{6,4},{4,5},{7,6},{5,7},{10,8},{8,9},{11,1... | collective-permute-start | bytes 12582920 | tf_op jit(solution)/shard_map/ppermute | solution.py:665
  244.3 7.5 %collective-permute-start.13 = (bf16[1024,1024]{1,0:T(8,128)(2,1)S(1)}, bf16[1024,1024]{1,0:T(8,128)(2,1)S(1)}, u32[]{:S(2)}, u32[]{:S(2)}) collective-permute-start(bf16[1024,1024]{1,0:T(8,128)(2,1)S(1)} %copy-done.2), channel_id=1, source_target_pairs={{0,2},{2,0},{1,3},{3,1},{4,6},{6,4},{5,7},{7,5},{8,10},{10,8},{9,1... | collective-permute-start | bytes 6291464 | tf_op jit(solution)/shard_map/ppermute | solution.py:740
  244.4 21.9 %collective-permute-start.15 = (bf16[128,2048]{1,0:T(8,128)(2,1)}, bf16[128,2048]{1,0:T(8,128)(2,1)S(1)}, u32[]{:S(2)}, u32[]{:S(2)}) collective-permute-start(bf16[128,2048]{1,0:T(8,128)(2,1)} %get-tuple-element.128), channel_id=1, source_target_pairs={{0,4},{1,5},{2,6},{3,7},{4,0},{5,1},{6,2},{7,3},{8,12},{9,13},{10,... | collective-permute-start | bytes 1572872 | tf_op jit(solution)/shard_map/ppermute | solution.py:681
  246.5 57.9 %collective-permute-start.16 = (bf16[128,2048]{1,0:T(8,128)(2,1)}, bf16[128,2048]{1,0:T(8,128)(2,1)}, u32[]{:S(2)}, u32[]{:S(2)}) collective-permute-start(bf16[128,2048]{1,0:T(8,128)(2,1)} %get-tuple-element.129), channel_id=1, source_target_pairs={{0,1},{1,0},{2,3},{3,2},{4,5},{5,4},{6,7},{7,6},{8,9},{9,8},{10,11... | collective-permute-start | bytes 1572872 | tf_op jit(solution)/shard_map/ppermute | solution.py:681
  266.3 38.1 %copy-start.11 = (bf16[128,2048]{1,0:T(8,128)(2,1)}, bf16[128,2048]{1,0:T(8,128)(2,1)S(1)}, u32[]{:S(2)}) copy-start(bf16[128,2048]{1,0:T(8,128)(2,1)S(1)} %collective-permute-done.15.refs_4_) | copy-start | bytes 1572868
  332.9 10.2 %collective-permute-start.18 = (bf16[64,2048]{1,0:T(8,128)(2,1)S(1)}, bf16[64,2048]{1,0:T(8,128)(2,1)S(1)}, u32[]{:S(2)}, u32[]{:S(2)}) collective-permute-start(bf16[64,2048]{1,0:T(8,128)(2,1)S(1)} %copy-done.33), channel_id=1, source_target_pairs={{10,0},{8,1},{11,2},{9,3},{14,4},{12,5},{15,6},{13,7},{2,8},{0,9},... | collective-permute-start | bytes 786440 | tf_op jit(solution)/shard_map/ppermute | solution.py:673
  333.0 17.4 %collective-permute-start.19 = (bf16[64,2048]{1,0:T(8,128)(2,1)S(1)}, bf16[64,2048]{1,0:T(8,128)(2,1)S(1)}, u32[]{:S(2)}, u32[]{:S(2)}) collective-permute-start(bf16[64,2048]{1,0:T(8,128)(2,1)S(1)} %copy-done.32), channel_id=1, source_target_pairs={{18,0},{16,1},{19,2},{17,3},{22,4},{20,5},{23,6},{21,7},{26,8},{24... | collective-permute-start | bytes 786440 | tf_op jit(solution)/shard_map/ppermute | solution.py:673
  333.1 26.0 %collective-permute-start.20 = (bf16[64,2048]{1,0:T(8,128)(2,1)S(1)}, bf16[64,2048]{1,0:T(8,128)(2,1)S(1)}, u32[]{:S(2)}, u32[]{:S(2)}) collective-permute-start(bf16[64,2048]{1,0:T(8,128)(2,1)S(1)} %copy-done.31), channel_id=1, source_target_pairs={{26,0},{24,1},{27,2},{25,3},{30,4},{28,5},{31,6},{29,7},{18,8},{16... | collective-permute-start | bytes 786440 | tf_op jit(solution)/shard_map/ppermute | solution.py:673
  334.9 24.2 %collective-permute-start.17 = (bf16[64,2048]{1,0:T(8,128)(2,1)S(1)}, bf16[64,2048]{1,0:T(8,128)(2,1)S(1)}, u32[]{:S(2)}, u32[]{:S(2)}) collective-permute-start(bf16[64,2048]{1,0:T(8,128)(2,1)S(1)} %copy-done.30), channel_id=1, source_target_pairs={{2,0},{0,1},{3,2},{1,3},{6,4},{4,5},{7,6},{5,7},{10,8},{8,9},{11,1... | collective-permute-start | bytes 786440 | tf_op jit(solution)/shard_map/ppermute | solution.py:673
  343.1 15.9 %copy-start.16 = (bf16[64,2048]{1,0:T(8,128)(2,1)}, bf16[64,2048]{1,0:T(8,128)(2,1)S(1)}, u32[]{:S(2)}) copy-start(bf16[64,2048]{1,0:T(8,128)(2,1)S(1)} %collective-permute-done.18.refs_2_) | copy-start | bytes 786436
  372.8 24.0 %collective-permute-start.22 = (bf16[256,2048]{1,0:T(8,128)(2,1)}, bf16[256,2048]{1,0:T(8,128)(2,1)S(1)}, u32[]{:S(2)}, u32[]{:S(2)}) collective-permute-start(bf16[256,2048]{1,0:T(8,128)(2,1)} %get-tuple-element.138), channel_id=1, source_target_pairs={{0,4},{1,5},{2,6},{3,7},{4,0},{5,1},{6,2},{7,3},{8,12},{9,13},{10,... | collective-permute-start | bytes 3145736 | tf_op jit(solution)/shard_map/ppermute | solution.py:681
  374.8 22.3 %collective-permute-start.21 = (bf16[256,2048]{1,0:T(8,128)(2,1)}, bf16[256,2048]{1,0:T(8,128)(2,1)S(1)}, u32[]{:S(2)}, u32[]{:S(2)}) collective-permute-start(bf16[256,2048]{1,0:T(8,128)(2,1)} %get-tuple-element.137.refs_2_), channel_id=1, source_target_pairs={{0,1},{1,0},{2,3},{3,2},{4,5},{5,4},{6,7},{7,6},{8,9},{9,8},{10,11... | collective-permute-start | bytes 3145736 | tf_op jit(solution)/shard_map/ppermute | solution.py:681
  378.4 24.7 %collective-permute-start.9 = (bf16[512,1024]{1,0:T(8,128)(2,1)}, bf16[512,1024]{1,0:T(8,128)(2,1)}, u32[]{:S(2)}, u32[]{:S(2)}) collective-permute-start(bf16[512,1024]{1,0:T(8,128)(2,1)} %constant_dynamic-slice_fusion), channel_id=1, source_target_pairs={{0,2},{2,0},{1,3},{3,1},{4,6},{6,4},{5,7},{7,5},{8,10},{10,8},{9,1... | collective-permute-start | bytes 3145736 | tf_op jit(solution)/shard_map/ppermute | solution.py:740
  402.4 11.7 %collective-permute-start.23 = (bf16[512,1024]{1,0:T(8,128)(2,1)}, bf16[512,1024]{1,0:T(8,128)(2,1)}, u32[]{:S(2)}, u32[]{:S(2)}) collective-permute-start(bf16[512,1024]{1,0:T(8,128)(2,1)} %constant_dynamic-slice_fusion.1), channel_id=1, source_target_pairs={{0,2},{2,0},{1,3},{3,1},{4,6},{6,4},{5,7},{7,5},{8,10},{10,8},{9,1... | collective-permute-start | bytes 3145736 | tf_op jit(solution)/shard_map/ppermute | solution.py:740
  407.1 50.8 %collective-permute-start.10 = (bf16[512,1024]{1,0:T(8,128)(2,1)}, bf16[512,1024]{1,0:T(8,128)(2,1)}, u32[]{:S(2)}, u32[]{:S(2)}) collective-permute-start(bf16[512,1024]{1,0:T(8,128)(2,1)} %add_convert_fusion), channel_id=1, source_target_pairs={{2,0},{0,1},{3,2},{1,3},{6,4},{4,5},{7,6},{5,7},{10,8},{8,9},{11,1... | collective-permute-start | bytes 3145736 | tf_op jit(solution)/shard_map/ppermute | solution.py:665
  409.5 42.0 %collective-permute-start.25 = (bf16[128,2048]{1,0:T(8,128)(2,1)}, bf16[128,2048]{1,0:T(8,128)(2,1)}, u32[]{:S(2)}, u32[]{:S(2)}) collective-permute-start(bf16[128,2048]{1,0:T(8,128)(2,1)} %get-tuple-element.150), channel_id=1, source_target_pairs={{0,4},{1,5},{2,6},{3,7},{4,0},{5,1},{6,2},{7,3},{8,12},{9,13},{10,... | collective-permute-start | bytes 1572872 | tf_op jit(solution)/shard_map/ppermute | solution.py:681
  410.1 41.4 %collective-permute-start.26 = (bf16[128,2048]{1,0:T(8,128)(2,1)}, bf16[128,2048]{1,0:T(8,128)(2,1)}, u32[]{:S(2)}, u32[]{:S(2)}) collective-permute-start(bf16[128,2048]{1,0:T(8,128)(2,1)} %get-tuple-element.151), channel_id=1, source_target_pairs={{0,1},{1,0},{2,3},{3,2},{4,5},{5,4},{6,7},{7,6},{8,9},{9,8},{10,11... | collective-permute-start | bytes 1572872 | tf_op jit(solution)/shard_map/ppermute | solution.py:681
  420.2 39.1 %collective-permute-start.24 = (bf16[512,1024]{1,0:T(8,128)(2,1)}, bf16[512,1024]{1,0:T(8,128)(2,1)S(1)}, u32[]{:S(2)}, u32[]{:S(2)}) collective-permute-start(bf16[512,1024]{1,0:T(8,128)(2,1)} %fusion.9), channel_id=1, source_target_pairs={{2,0},{0,1},{3,2},{1,3},{6,4},{4,5},{7,6},{5,7},{10,8},{8,9},{11,1... | collective-permute-start | bytes 3145736 | tf_op jit(solution)/shard_map/ppermute | solution.py:665
  420.3 2.3 collective-permute-start.27
  422.6 23.5 %collective-permute-start.28 = (f32[8,2048]{1,0:T(8,128)S(1)}, f32[8,2048]{1,0:T(8,128)S(1)}, u32[]{:S(2)}, u32[]{:S(2)}) collective-permute-start(f32[8,2048]{1,0:T(8,128)S(1)} %add.138), channel_id=1, source_target_pairs={{0,1},{1,0},{2,3},{3,2},{4,5},{5,4},{6,7},{7,6},{8,9},{9,8},{10,11... | collective-permute-start | bytes 196616 | tf_op jit(solution)/shard_map/ppermute | solution.py:681
  446.2 4.7 collective-permute-start.29
  454.9 9.9 %collective-permute-start.30 = (bf16[80,2048]{1,0:T(8,128)(2,1)}, bf16[80,2048]{1,0:T(8,128)(2,1)S(1)}, u32[]{:S(2)}, u32[]{:S(2)}) collective-permute-start(bf16[80,2048]{1,0:T(8,128)(2,1)} %get-tuple-element.155), channel_id=1, source_target_pairs={{2,0},{0,1},{3,2},{1,3},{6,4},{4,5},{7,6},{5,7},{10,8},{8,9},{11,1... | collective-permute-start | bytes 983048 | tf_op jit(solution)/shard_map/ppermute | solution.py:673
  454.9 14.0 %collective-permute-start.31 = (bf16[80,2048]{1,0:T(8,128)(2,1)}, bf16[80,2048]{1,0:T(8,128)(2,1)S(1)}, u32[]{:S(2)}, u32[]{:S(2)}) collective-permute-start(bf16[80,2048]{1,0:T(8,128)(2,1)} %get-tuple-element.156), channel_id=1, source_target_pairs={{10,0},{8,1},{11,2},{9,3},{14,4},{12,5},{15,6},{13,7},{2,8},{0,9},... | collective-permute-start | bytes 983048 | tf_op jit(solution)/shard_map/ppermute | solution.py:673
  454.9 24.2 %collective-permute-start.32 = (bf16[80,2048]{1,0:T(8,128)(2,1)}, bf16[80,2048]{1,0:T(8,128)(2,1)S(1)}, u32[]{:S(2)}, u32[]{:S(2)}) collective-permute-start(bf16[80,2048]{1,0:T(8,128)(2,1)} %get-tuple-element.157), channel_id=1, source_target_pairs={{18,0},{16,1},{19,2},{17,3},{22,4},{20,5},{23,6},{21,7},{26,8},{24... | collective-permute-start | bytes 983048 | tf_op jit(solution)/shard_map/ppermute | solution.py:673
  457.9 30.7 %collective-permute-start.33 = (bf16[80,2048]{1,0:T(8,128)(2,1)}, bf16[80,2048]{1,0:T(8,128)(2,1)S(1)}, u32[]{:S(2)}, u32[]{:S(2)}) collective-permute-start(bf16[80,2048]{1,0:T(8,128)(2,1)} %get-tuple-element.158), channel_id=1, source_target_pairs={{26,0},{24,1},{27,2},{25,3},{30,4},{28,5},{31,6},{29,7},{18,8},{16... | collective-permute-start | bytes 983048 | tf_op jit(solution)/shard_map/ppermute | solution.py:673
  464.8 23.8 %copy-start.12 = (bf16[80,2048]{1,0:T(8,128)(2,1)}, bf16[80,2048]{1,0:T(8,128)(2,1)S(1)}, u32[]{:S(2)}) copy-start(bf16[80,2048]{1,0:T(8,128)(2,1)S(1)} %collective-permute-done.30.refs_1_) | copy-start | bytes 983044
  468.9 19.7 %copy-start.13 = (bf16[80,2048]{1,0:T(8,128)(2,1)}, bf16[80,2048]{1,0:T(8,128)(2,1)S(1)}, u32[]{:S(2)}) copy-start(bf16[80,2048]{1,0:T(8,128)(2,1)S(1)} %collective-permute-done.31.refs_2_) | copy-start | bytes 983044
  479.2 9.4 %copy-start.14 = (bf16[80,2048]{1,0:T(8,128)(2,1)}, bf16[80,2048]{1,0:T(8,128)(2,1)S(1)}, u32[]{:S(2)}) copy-start(bf16[80,2048]{1,0:T(8,128)(2,1)S(1)} %collective-permute-done.32.refs_3_) | copy-start | bytes 983044
  (24 other events, 59.6 us)
Sparse Core Ops, SparseCore 0:
  10.8 51.6 all-gather.3
  65.2 49.0 all-gather.5
  117.1 82.8 all-gather.7
  332.2 76.2 reduce-scatter.1

commit v4 on v3

--- a/solution.py
+++ b/solution.py
@@ -17,7 +17,7 @@
 BF16 = jnp.bfloat16
 TP = ("l", "c")
 SWAP = ("c", "h", "l")
-ALL = ("a", "c", "h", "l")
+ALL = ("z", "y", "c", "h", "l")
 
 
 def normalize(values):
@@ -593,12 +593,17 @@
             out[rows:, :] = extra
 
 
-def total_kernel(*refs):
-    parts, out = refs[:-1], refs[-1]
-    total = parts[0][...].astype(F32)
-    for part in parts[1:]:
-        total = total + part[...].astype(F32)
-    out[...] = total
+def z_sums_kernel(z_ref, from_x, from_y, near, from_y2, from_x2, out, *, far):
+    half = from_y2.shape[0]
+    rows = half * 2 // far
+    for i in range(far):
+        first, second, place = (from_x, from_y2, i) if i < far // 2 else (from_y, from_x2, i - far // 2)
+        target = pl.multiple_of((z_ref[0] ^ i) * rows, rows)
+        out[pl.ds(target, rows), :] = added(
+            near[i * rows : (i + 1) * rows, :],
+            first[half + place * rows : half + (place + 1) * rows, :],
+            second[place * rows : (place + 1) * rows, :],
+        )
 
 
 def weights_last_kernel(*refs):
@@ -678,7 +683,7 @@
             for c in range(2):
                 for h in range(2):
                     pairs.append(((a * 2 + c) * 2 + h, ((a ^ a_mask) * 2 + c) * 2 + (h ^ h_mask)))
-        return lax.ppermute(values, ("a", "c", "h"), pairs)
+        return lax.ppermute(values, ("z", "y", "c", "h"), pairs)
 
     def scatter_near(pieces, after):
         from_x, from_y = hop(pieces[0], 0, 1), hop(pieces[1], 1, 0)
@@ -705,6 +710,19 @@
             "sums_two",
         )
 
+    def z_sums(state, after):
+        from_x, from_y, near, y_sum, x_sum = state
+        from_y2, from_x2 = hop(y_sum, 1, 0), hop(x_sum, 0, 1)
+        vmem = pl.BlockSpec(memory_space=pltpu.VMEM)
+        return pl.pallas_call(
+            without(functools.partial(z_sums_kernel, far=far), 6),
+            in_specs=[pl.BlockSpec(memory_space=pltpu.SMEM)] + [vmem] * 5 + [ORDER_ONLY],
+            out_specs=vmem,
+            out_shape=jax.ShapeDtypeStruct(near.shape, BF16),
+            compiler_params=pltpu.CompilerParams(vmem_limit_bytes=VMEM_BYTES),
+            name="sums_two_z",
+        )(lax.axis_index("z").reshape(1), from_x, from_y, near, from_y2, from_x2, after)
+
     def far_parts(sums):
         return [swap_hop(sums[i], 2 * i, inverse=True) for i in range(far)]
 
@@ -714,12 +732,12 @@
         values = values + hop(values, 1, 0)
         return lax.psum(values, "l") if inner > 1 else values
 
-    a, h = lax.axis_index("a"), lax.axis_index("h")
+    a, h = lax.axis_index(("z", "y")), lax.axis_index("h")
     order = []
     for a_low, h_mask in ((0, 0), (1, 0), (0, 1), (1, 1)):
         for i in range(far):
             order.append((a ^ (2 * i + a_low)) * 2 + (h ^ h_mask))
-    return swap, scatter_near, far_sums, far_parts, near_sum, jnp.stack(order).astype(jnp.int32)
+    return swap, scatter_near, far_sums, z_sums, far_parts, near_sum, jnp.stack(order).astype(jnp.int32)
 
 
 def per_device(sizes, *arguments):
@@ -734,7 +752,7 @@
     unit_width = w_up.shape[1]
     half_units = unit_width // 2
     tile = min(TILE, half_units)
-    swap, scatter_near, far_sums, far_parts, near_sum, order = moves(sizes)
+    swap, scatter_near, far_sums, z_sums, far_parts, near_sum, order = moves(sizes)
 
     def partner(values):
         return lax.ppermute(values, "c", [(0, 1), (1, 0)])
@@ -775,9 +793,9 @@
         "mlp_shards",
     )
     early_attn = lax.all_gather(
-        jnp.concatenate([w_query, w_key, w_value, w_out], axis=1), ("a", "c"), axis=0, tiled=True
-    )
-    early_first = lax.all_gather(shard_first, ("a", "c"), axis=0, tiled=True)
+        jnp.concatenate([w_query, w_key, w_value, w_out], axis=1), ("z", "y", "c"), axis=0, tiled=True
+    )
+    early_first = lax.all_gather(shard_first, ("z", "y", "c"), axis=0, tiled=True)
     shard_second = swap(shard_second)
     bias_query = lax.dynamic_slice_in_dim(b_query, rank * head_width, head_width)
     bias_value = lax.dynamic_slice_in_dim(b_value, rank * head_width, head_width)
@@ -790,7 +808,7 @@
     early_attn, normed, segments, grad_rows, grad_rows_t, shard_second = lax.optimization_barrier(
         (early_attn, normed, segments, grad_rows, grad_rows_t, shard_second)
     )
-    full_second = lax.all_gather(shard_second, ("a", "h"), axis=0, tiled=True)
+    full_second = lax.all_gather(shard_second, ("z", "y", "h"), axis=0, tiled=True)
     full_attn = swap(early_attn)
     biases = jnp.concatenate([bias_query, jnp.zeros((head_width,), F32), bias_value])
     qkv = qkv_project(normed, full_attn, biases)
@@ -814,34 +832,31 @@
     gn_part, second_grads, first_state = lax.optimization_barrier(
         (gn_part, second_grads[0], first_state)
     )
-    second_grads = swap(second_grads, inverse=True)
     own_output = (own(hidden) + tp_scatter(out_part) + b_down).astype(BF16)
-    output = swap(own_output, inverse=True)
 
     grad_hidden, grad_attended, grad_attended_t, sums_two = norm_back_rows(
         hidden, grad_rows, tp_terms(gn_part), ln2_gain
     )
+    first_sums = z_sums(first_state, grad_attended)
+    second_grads, first_sums = lax.optimization_barrier((second_grads, first_sums))
+    second_grads = swap(second_grads, inverse=True)
     grad_mixed = dot_nn(grad_attended, full_out).astype(BF16)
-    first_sums = far_sums(first_state, [], grad_mixed)
-    grads = attn_backward(segments, qkv, mixed, lse, grad_mixed, head_width, first_sums[0])
+    first_mlp = lax.psum_scatter(first_sums, "z", scatter_dimension=0, tiled=True)
+    grads = attn_backward(segments, qkv, mixed, lse, grad_mixed, head_width, first_sums)
     block_rows = w_query.shape[0]
-    (first_mlp,) = sums_call(
-        total_kernel,
-        far_parts(first_sums),
-        [jax.ShapeDtypeStruct((block_rows, unit_width), F32)],
-        grads,
-        "units_first",
-    )
-    second_grads, grads = lax.optimization_barrier((second_grads, grads))
-    second_mlp = lax.psum_scatter(second_grads, ("a", "c"), scatter_dimension=0, tiled=True)
-    pieces = weight_grads(order, normed_t, grads, grad_attended_t, mixed, first_mlp)
+    pieces = weight_grads(order, normed_t, grads, grad_attended_t, mixed, grads)
     grad_normed_part = qkv_back(grads, full_attn, pieces[0])
+    second_grads, first_mlp, grad_normed_part = lax.optimization_barrier(
+        (second_grads, first_mlp, grad_normed_part)
+    )
+    second_mlp = lax.psum_scatter(second_grads, ("z", "y", "c"), scatter_dimension=0, tiled=True)
+    first_mlp = swap(first_mlp, inverse=True)
     state = scatter_near(pieces, grad_normed_part)
     grad_normed_part, state = lax.optimization_barrier((grad_normed_part, state))
     grad_normed = tp_scatter(grad_normed_part)
     own_scaled, own_inverse = normalize(own_input.astype(F32))
     grad_own = own(grad_hidden) + norm_back(grad_normed, own_scaled, own_inverse, ln1_gain)
-    grad_input = swap(grad_own.astype(BF16), inverse=True)
+    grad_own = grad_own.astype(BF16)
 
     def place_part(values, full):
         return lax.dynamic_update_slice_in_dim(
@@ -871,9 +886,13 @@
         None,
         "units_last",
     )
+    last_sums = far_sums(state, [sums], None)
+    own_output, grad_own, *last_sums = lax.optimization_barrier((own_output, grad_own, *last_sums))
+    output = swap(own_output, inverse=True)
+    grad_input = swap(grad_own, inverse=True)
     *late, sums = sums_call(
         weights_last_kernel,
-        far_parts(far_sums(state, [sums], None)),
+        far_parts(last_sums),
         [jax.ShapeDtypeStruct((block_rows, head_width), F32)] * 4
         + [jax.ShapeDtypeStruct(sums.shape, F32)],
         grad_w_up,
@@ -890,15 +909,15 @@
 
 def solution(mesh):
     groups, ranks = mesh.shape["dp"], mesh.shape["tensor"]
-    sizes = {"a": groups // 2, "c": 2, "h": 2, "l": ranks // 2}
-    fine = Mesh(mesh.devices.reshape(tuple(sizes.values())), tuple(sizes))
-    rows = P(("a", "c", "h", "l"), None)
-    block = P(("a", "c"), ("h", "l"))
+    sizes = {"a": groups // 2, "h": 2, "l": ranks // 2}
+    fine = Mesh(mesh.devices.reshape(groups // 4, 2, 2, 2, ranks // 2), ALL)
+    rows = P(ALL, None)
+    block = P(("z", "y", "c"), ("h", "l"))
     return jax.shard_map(
         functools.partial(per_device, sizes),
         mesh=fine,
         in_specs=(
-            rows, P(("a", "c")), P(), P(), block, block, block, P(), P(), block, P(), P(), P(),
+            rows, P(("z", "y", "c")), P(), P(), block, block, block, P(), P(), block, P(), P(), P(),
             block, P(), block, P(), rows,
         ),
         out_specs=(

time: 514 us -> 449 us (0.87)
  waiting for transfers between devices: 246 us -> 200 us
  starting transfers between devices: 34.4 us -> 21.3 us
    ppermute x8 -> x4, waiting for transfers between devices: 49 us -> 0.01 us  [swap_hop(): return lax.ppermute(values, ALL, pairs)]
    ppermute x9 -> x10, waiting for transfers between devices: 104 us -> 148 us  [swap(): return lax.ppermute(values, SWAP, pairs)]
    ppermute x10, waiting for transfers between devices: 73.2 us -> 36.5 us  [hop(): return lax.ppermute(values, ('z', 'y', 'c', 'h'), pairs)]
    ppermute x10, starting transfers between devices: 17.7 us -> 9.88 us  [hop(): return lax.ppermute(values, ('z', 'y', 'c', 'h'), pairs)]
    pallas_call x8 -> x6, Pallas kernels: 21.2 us -> 15.5 us  [sums_call(): pl.pallas_call(body, in_specs=([pl.BlockSpec(memory_space=pl.ANY)] if aft...]
    ppermute x8 -> x4, starting transfers between devices: 8.46 us -> 3.17 us  [swap_hop(): return lax.ppermute(values, ALL, pairs)]
    unnamed x79 -> x73, local copies, waits for them, and re-layouts: 13.5 us -> 11.6 us
  transfers between devices with their start and end apart: 38 -> 36, of which waited for: 20 -> 16; matrix products, arithmetic and copies ran while one was open for 7% -> 8% of each run, Pallas kernels for 30% -> 33%
where the time goes in v4:
time: 449 us; the launch traced here: 441 us
  waiting for transfers between devices  200 us (45%)
  Pallas kernels  156 us (35%)
  starting transfers between devices  21.3 us (5%)
  local copies, waits for them, and re-layouts  20.7 us (5%)
  other arithmetic  20.5 us (5%)
  between operations  14.7 us (3%)
  matrix products  7.61 us (2%)
    ppermute x10, waiting for transfers between devices, swap(): return lax.ppermute(values, SWAP, pairs)  148 us
    pallas_call x2, Pallas kernels, mlp(): pl.pallas_call(functools.partial(mlp_kernel, block=min(256, length), with...  49.1 us
    ppermute x10, waiting for transfers between devices, hop(): return lax.ppermute(values, ('z', 'y', 'c', 'h'), pairs)  36.5 us
    pallas_call x1, Pallas kernels, attn_backward(): pl.pallas_call(without(functools.partial(attn_backward_kernel, block=bloc...  24.3 us
    pallas_call x1, Pallas kernels, attn_forward(): pl.pallas_call(functools.partial(attn_forward_kernel, block=block), grid=...  16.4 us
    pallas_call x6, Pallas kernels, sums_call(): pl.pallas_call(body, in_specs=([pl.BlockSpec(memory_space=pl.ANY)] if aft...  15.5 us
    pallas_call x2, Pallas kernels, norm_rows(): pl.pallas_call(functools.partial(norm_kernel, residual=residual), grid=(l...  12.8 us
    all_gather x1, waiting for transfers between devices, per_device(): lax.all_gather(jnp.concatenate([w_query, w_key, w_value, w_out], axis=1),...  12.8 us
  transfers between devices with their start and end apart: 36, of which 16 were waited for; matrix products, arithmetic and copies ran while one was open for 8% of the time, Pallas kernels for 33%

profile of v4, /device:TPU:10, one launch (start us, length us, event | category | flops | bytes accessed | tf_op | source)
XLA Modules:
  0.0 440.8 jit_solution(14465064643174331187)
XLA Ops:
  7.2 1.7 pad_maximum_fusion
  9.0 1.8 mlp_shards.1
  11.5 12.6 %collective-permute-done = bf16[512,1024]{1,0:T(8,128)(2,1)S(1)} collective-permute-done((bf16[512,1024]{1,0:T(8,128)(2,1)}, bf16[512,1024]{1,0:T(8,128)(2,1)S(1)}, u32[]{:S(2)}, u32[]{:S(2)}) %collective-permute-start) | collective-permute-done | bytes 1048608 | tf_op jit(solution)/shard_map/ppermute | solution.py:670
  25.0 10.3 %collective-permute-done.3 = bf16[512,1024]{1,0:T(8,128)(2,1)S(1)} collective-permute-done((bf16[512,1024]{1,0:T(8,128)(2,1)}, bf16[512,1024]{1,0:T(8,128)(2,1)S(1)}, u32[]{:S(2)}, u32[]{:S(2)}) %collective-permute-start.3) | collective-permute-done | bytes 1048608 | tf_op jit(solution)/shard_map/ppermute | solution.py:670
  35.8 1.9 collective-permute-start.2
  38.2 2.3 maximum_select_fusion.refs_0_
  40.5 3.7 maximum_select_fusion.1.g_ref
  44.2 5.5 %norm_one.1 = (bf16[1024,1024]{1,0:T(8,128)(2,1)}, bf16[1024,1024]{1,0:T(8,128)(2,1)}) custom-call(bf16[1024,1024]{1,0:T(8,128)(2,1)} %maximum_select_fusion.refs_0_, f32[1,1024]{1,0:T(1,128)} %bitcast.39, f32[1,1024]{1,0:T(1,128)} %bitcast.46), custom_call_target="tpu_custom_call" | custom-call | flops 20971520 | bytes 14680064 | tf_op jit(solution)/shard_map/norm_one/pallas_call | solution.py:275
  49.7 12.8 %all-gather.4.cloned.1.call-done = bf16[1024,2048]{1,0:T(8,128)(2,1)} async-done(((bf16[64,2048]{1,0:T(8,128)(2,1)}), bf16[1024,2048]{1,0:T(8,128)(2,1)}) %all-gather.4.cloned.1.call-update) | async-done | bytes 4194320 | tf_op jit(solution)/shard_map/all_gather | solution.py:795
  63.9 45.5 %collective-permute-done.6.w_ref.refs_1_ = bf16[1024,2048]{1,0:T(8,128)(2,1)} collective-permute-done((bf16[1024,2048]{1,0:T(8,128)(2,1)}, bf16[1024,2048]{1,0:T(8,128)(2,1)}, u32[]{:S(2)}, u32[]{:S(2)}) %collective-permute-start.6) | collective-permute-done | bytes 4194336 | tf_op jit(solution)/shard_map/ppermute | solution.py:670
  109.4 7.2 %qkv_project.1.q_ref.k_ref.v_ref.refs_2_.refs_3_.refs_4_ = bf16[1024,1536]{1,0:T(8,128)(2,1)} custom-call(bf16[1024,1024]{1,0:T(8,128)(2,1)} %get-tuple-element.100.n_ref, f32[1,1536]{1,0:T(1,128)} %reshape.108.b_ref, bf16[1024,2048]{1,0:T(8,128)(2,1)} %collective-permute-done.6.w_ref.refs_1_), custom_call_target="tpu_custom_call" | custom-call | flops 3221225472 | bytes 8388608 | tf_op jit(solution)/shard_map/qkv_project/pallas_call | solution.py:456
  116.6 2.5 collective-permute-start.8
  120.1 16.4 %attn_forward.1 = (bf16[1024,512]{1,0:T(8,128)(2,1)}, f32[4,8,1024]{2,1,0:T(8,128)}) custom-call(s32[1024,1]{1,0:T(8,128)} %copy.37.seg_col.refs_0_, s32[1,1024]{1,0:T(1,128)} %bitcast.41, bf16[1024,1536]{1,0:T(8,128)(2,1)} %qkv_project.1.q_ref.k_ref.v_ref.refs_2_.refs_3_.refs_4_, bf16[1024,1536]{1,0:T(8,128)(2,1)} %qkv_project.1.q_ref.k_ref.v_ref.refs_2_.refs_3_.refs_4_, ...), custom_call_target="tpu_custom_call" | custom-call | flops 2147483648 | bytes 4194304 | tf_op jit(solution)/shard_map/attn_forward/pallas_call | solution.py:156
  136.5 4.2 convolution_convert_fusion.refs_1_
  142.0 2.6 copy.39.gt_ref
  145.2 7.3 %norm_two.1 = (bf16[1024,1024]{1,0:T(8,128)(2,1)}, bf16[1024,1024]{1,0:T(8,128)(2,1)}, f32[1024,1024]{1,0:T(8,128)}) custom-call(bf16[1024,1024]{1,0:T(8,128)(2,1)} %maximum_select_fusion.refs_0_, bf16[1024,1024]{1,0:T(8,128)(2,1)} %convolution_convert_fusion.refs_1_, bf16[1024,1024]{1,0:T(8,128)(2,1)} %collective-permute-done.7.refs_2_, ...), custom_call_target="tpu_custom_call" | custom-call | flops 20971520 | bytes 14680064 | tf_op jit(solution)/shard_map/norm_two/pallas_call | solution.py:275
  152.5 36.1 %collective-permute-done.8.w_ref = bf16[1024,2048]{1,0:T(8,128)(2,1)} collective-permute-done((bf16[1024,2048]{1,0:T(8,128)(2,1)}, bf16[1024,2048]{1,0:T(8,128)(2,1)}, u32[]{:S(2)}, u32[]{:S(2)}) %collective-permute-start.8) | collective-permute-done | bytes 4194336 | tf_op jit(solution)/shard_map/ppermute | solution.py:670
  188.6 24.1 %mlp_first.1 = (bf16[1024,1024]{1,0:T(8,128)(2,1)}, bf16[1024,1024]{1,0:T(8,128)(2,1)}, bf16[256,2048]{1,0:T(8,128)(2,1)}, bf16[256,2048]{1,0:T(8,128)(2,1)}, bf...) custom-call(s32[16]{0:T(128)} %stack.67.order, ...), custom_call_target="tpu_custom_call" | custom-call | flops 12884901888 | bytes 20971520 | tf_op jit(solution)/shard_map/mlp_first/pallas_call | solution.py:402
  212.8 2.5 collective-permute-start.10
  215.3 24.9 %mlp_second.1 = (bf16[1024,1024]{1,0:T(8,128)(2,1)}, bf16[1024,1024]{1,0:T(8,128)(2,1)}, bf16[1024,2048]{1,0:T(8,128)(2,1)}, f32[1,1024]{1,0:T(1,128)}) custom-call(s32[16]{0:T(128)} %stack.67.order, bf16[1024,1024]{1,0:T(8,128)(2,1)} %get-tuple-element.105.n_ref, bf16[1024,1024]{1,0:T(8,128)(2,1)} %copy-done, bf16[1024,1024]{1,0:T(8,128)(2,1)} %get-tuple-element.107.nt_ref, ...), custom_call_target="tpu_custom_call" | custom-call | flops 12884901888 | bytes 20971520 | tf_op jit(solution)/shard_map/mlp_second/pallas_call | solution.py:402
  241.7 3.1 sums_one.2
  244.8 2.1 collective-permute-start.13
  246.9 2.0 collective-permute-done.12.other_ref
  250.2 9.2 %norm_two_back.1 = (f32[1024,1024]{1,0:T(8,128)}, bf16[1024,1024]{1,0:T(8,128)(2,1)}, bf16[1024,1024]{1,0:T(8,128)(2,1)}, f32[8,1024]{1,0:T(8,128)}) custom-call(f32[1024,1024]{1,0:T(8,128)} %get-tuple-element.104.hidden_ref, bf16[1024,1024]{1,0:T(8,128)(2,1)} %copy-done, bf16[1024,1024]{1,0:T(8,128)(2,1)} %get-tuple-element.125.refs_0_.own_ref, ...), custom_call_target="tpu_custom_call" | custom-call | flops 31457280 | bytes 16777216 | tf_op jit(solution)/shard_map/norm_two_back/pallas_call | solution.py:315
  259.6 1.6 collective-permute-done.14.refs_5_
  261.2 3.7 sums_two_z.1.refs_8_
  264.9 3.5 convolution_convert_fusion.1.refs_7_
  268.4 24.3 %attn_backward.1.grads_ref.order_only.refs_0_ = bf16[3,1024,512]{2,1,0:T(8,128)(2,1)} custom-call(s32[1024,1]{1,0:T(8,128)} %copy.37.seg_col.refs_0_, s32[1,1024]{1,0:T(1,128)} %bitcast.42, bf16[1024,1536]{1,0:T(8,128)(2,1)} %qkv_project.1.q_ref.k_ref.v_ref.refs_2_.refs_3_.refs_4_, bf16[1024,1536]{1,0:T(8,128)(2,1)} %qkv_project.1.q_ref.k_ref.v_ref.refs_2_.refs_3_.refs_4_, ...), custom_call_target="tpu_custom_call" | custom-call | flops 5368709120 | bytes 8388608 | tf_op jit(solution)/shard_map/attn_backward/pallas_call | solution.py:185
  292.7 10.1 %weight_grads.1 = (bf16[256,2048]{1,0:T(8,128)(2,1)}, bf16[256,2048]{1,0:T(8,128)(2,1)}, bf16[128,2048]{1,0:T(8,128)(2,1)}, bf16[128,2048]{1,0:T(8,128)(2,1)}, bf16[256,2048]{1,0:T(8,128)(2,1)}) custom-call(s32[16]{0:T(128)} %stack.67.order, bf16[1024,1024]{1,0:T(8,128)(2,1)} %get-tuple-element.137.nt_ref, ...), custom_call_target="tpu_custom_call" | custom-call | flops 4294967296 | bytes 12582912 | tf_op jit(solution)/shard_map/weight_grads/pallas_call | solution.py:501
  302.8 7.8 %qkv_back.1.refs_0_ = bf16[1024,1024]{1,0:T(8,128)(2,1)} custom-call(bf16[3,1024,512]{2,1,0:T(8,128)(2,1)} %attn_backward.1.grads_ref.order_only.refs_0_, bf16[1024,2048]{1,0:T(8,128)(2,1)} %collective-permute-done.6.w_ref.refs_1_, bf16[256,2048]{1,0:T(8,128)(2,1)} %get-tuple-element.139.refs_2_), custom_call_target="tpu_custom_call" | custom-call | flops 3221225472 | bytes 8388608 | tf_op jit(solution)/shard_map/qkv_back/pallas_call | solution.py:542
  310.5 3.1 collective-permute-done.15
  315.4 20.1 %collective-permute-done.17.refs_2_.from_y = bf16[256,2048]{1,0:T(8,128)(2,1)S(1)} collective-permute-done((bf16[256,2048]{1,0:T(8,128)(2,1)}, bf16[256,2048]{1,0:T(8,128)(2,1)S(1)}, u32[]{:S(2)}, u32[]{:S(2)}) %collective-permute-start.17) | collective-permute-done | bytes 1048608 | tf_op jit(solution)/shard_map/ppermute | solution.py:686
  335.5 1.8 collective-permute-done.16.refs_1_.from_x
  338.3 3.1 sums_one.3
  345.1 1.9 convert_reduce_fusion.2
  347.7 2.4 fusion.10
  350.8 4.0 add_convert_fusion
  355.1 1.8 collective-permute-start.20
  357.3 12.9 %collective-permute-done.22 = f32[8,2048]{1,0:T(8,128)S(1)} collective-permute-done((f32[8,2048]{1,0:T(8,128)S(1)}, f32[8,2048]{1,0:T(8,128)S(1)}, u32[]{:S(2)}, u32[]{:S(2)}) %collective-permute-start.22) | collective-permute-done | bytes 65568 | tf_op jit(solution)/shard_map/ppermute | solution.py:686
  370.1 1.6 collective-permute-start.23
  371.7 3.1 fusion.9
  376.3 3.3 sums_two.1
  379.6 3.0 collective-permute-start.27
  382.8 19.4 %collective-permute-done.24 = bf16[512,1024]{1,0:T(8,128)(2,1)S(1)} collective-permute-done((bf16[512,1024]{1,0:T(8,128)(2,1)S(1)}, bf16[512,1024]{1,0:T(8,128)(2,1)S(1)}, u32[]{:S(2)}, u32[]{:S(2)}) %collective-permute-start.24) | collective-permute-done | bytes 1048608 | tf_op jit(solution)/shard_map/ppermute | solution.py:670
  402.2 13.5 %collective-permute-done.25 = bf16[512,1024]{1,0:T(8,128)(2,1)S(1)} collective-permute-done((bf16[512,1024]{1,0:T(8,128)(2,1)}, bf16[512,1024]{1,0:T(8,128)(2,1)S(1)}, u32[]{:S(2)}, u32[]{:S(2)}) %collective-permute-start.25) | collective-permute-done | bytes 1048608 | tf_op jit(solution)/shard_map/ppermute | solution.py:670
  415.7 7.6 %collective-permute-done.26.first_ref = bf16[64,2048]{1,0:T(8,128)(2,1)S(1)} collective-permute-done((bf16[64,2048]{1,0:T(8,128)(2,1)}, bf16[64,2048]{1,0:T(8,128)(2,1)S(1)}, u32[]{:S(2)}, u32[]{:S(2)}) %collective-permute-start.26) | collective-permute-done | bytes 262176 | tf_op jit(solution)/shard_map/ppermute | solution.py:670
  423.9 2.1 units_last.1
  426.8 2.1 sums_last.1
  (160 shorter events, 26.6 us)
Async XLA Ops:
  7.2 55.3 %all-gather.4.cloned.1.call-start = ((), (), s32[]{:S(2)}) async-start(), calls=%async_computation.2 | async-start | bytes 4456448 | tf_op jit(solution)/shard_map/all_gather | solution.py:795
  8.9 107.6 %all-gather.6.cloned.1.call-start = ((), (), s32[]{:S(2)}) async-start(), calls=%async_computation.3 | async-start | bytes 4456448 | tf_op jit(solution)/shard_map/all_gather | solution.py:798
  10.8 201.9 %all-gather.8.cloned.1.call-start = ((), (), s32[]{:S(2)}) async-start(), calls=%async_computation.4 | async-start | bytes 4456448 | tf_op jit(solution)/shard_map/all_gather | solution.py:811
  10.9 13.2 %collective-permute-start = (bf16[512,1024]{1,0:T(8,128)(2,1)}, bf16[512,1024]{1,0:T(8,128)(2,1)S(1)}, u32[]{:S(2)}, u32[]{:S(2)}) collective-permute-start(bf16[512,1024]{1,0:T(8,128)(2,1)} %param.18), channel_id=1, source_target_pairs={{0,2},{1,0},{2,3},{3,1},{4,6},{5,4},{6,7},{7,5},{8,10},{9,8},{10,1... | collective-permute-start | bytes 3145736 | tf_op jit(solution)/shard_map/ppermute | solution.py:670
  11.4 23.9 %collective-permute-start.3 = (bf16[512,1024]{1,0:T(8,128)(2,1)}, bf16[512,1024]{1,0:T(8,128)(2,1)S(1)}, u32[]{:S(2)}, u32[]{:S(2)}) collective-permute-start(bf16[512,1024]{1,0:T(8,128)(2,1)} %param.35), channel_id=1, source_target_pairs={{0,2},{1,0},{2,3},{3,1},{4,6},{5,4},{6,7},{7,5},{8,10},{9,8},{10,1... | collective-permute-start | bytes 3145736 | tf_op jit(solution)/shard_map/ppermute | solution.py:670
  24.1 14.1 %collective-permute-start.1 = (bf16[512,1024]{1,0:T(8,128)(2,1)S(1)}, bf16[512,1024]{1,0:T(8,128)(2,1)S(1)}, u32[]{:S(2)}, u32[]{:S(2)}) collective-permute-start(bf16[512,1024]{1,0:T(8,128)(2,1)S(1)} %collective-permute-done), channel_id=1, source_target_pairs={{0,2},{2,0},{1,3},{3,1},{4,6},{6,4},{5,7},{7,5},{8,10},{10,8},{9,1... | collective-permute-start | bytes 3145736 | tf_op jit(solution)/shard_map/ppermute | solution.py:758
  35.3 5.2 %copy-start.3 = (bf16[512,1024]{1,0:T(8,128)(2,1)}, bf16[512,1024]{1,0:T(8,128)(2,1)S(1)}, u32[]{:S(2)}) copy-start(bf16[512,1024]{1,0:T(8,128)(2,1)S(1)} %collective-permute-done.3) | copy-start | bytes 3145732
  35.3 5.2 %collective-permute-start.4 = (bf16[512,1024]{1,0:T(8,128)(2,1)S(1)}, bf16[512,1024]{1,0:T(8,128)(2,1)}, u32[]{:S(2)}, u32[]{:S(2)}) collective-permute-start(bf16[512,1024]{1,0:T(8,128)(2,1)S(1)} %collective-permute-done.3), channel_id=1, source_target_pairs={{0,2},{2,0},{1,3},{3,1},{4,6},{6,4},{5,7},{7,5},{8,10},{10,8},{9,1... | collective-permute-start | bytes 3145736 | tf_op jit(solution)/shard_map/ppermute | solution.py:758
  35.8 13.9 %collective-permute-start.2 = (s32[1024]{0:T(1024)}, s32[1024]{0:T(1024)S(1)}, u32[]{:S(2)}, u32[]{:S(2)}) collective-permute-start(s32[1024]{0:T(1024)} %param.19), channel_id=1, source_target_pairs={{0,2},{1,0},{2,3},{3,1},{4,6},{5,4},{6,7},{7,5},{8,10},{9,8},{10,1... | collective-permute-start | bytes 12296 | tf_op jit(solution)/shard_map/ppermute | solution.py:670
  37.7 12.0 %collective-permute-start.5 = (bf16[64,2048]{1,0:T(8,128)(2,1)}, bf16[64,2048]{1,0:T(8,128)(2,1)S(1)}, u32[]{:S(2)}, u32[]{:S(2)}) collective-permute-start(bf16[64,2048]{1,0:T(8,128)(2,1)} %get-tuple-element.97), channel_id=1, source_target_pairs={{0,2},{1,0},{2,3},{3,1},{4,6},{5,4},{6,7},{7,5},{8,10},{9,8},{10,1... | collective-permute-start | bytes 786440 | tf_op jit(solution)/shard_map/ppermute | solution.py:670
  44.2 97.8 %copy-start = (bf16[1024,1024]{1,0:T(8,128)(2,1)}, bf16[1024,1024]{1,0:T(8,128)(2,1)S(1)}, u32[]{:S(2)}) copy-start(bf16[1024,1024]{1,0:T(8,128)(2,1)S(1)} %maximum_select_fusion.1.g_ref) | copy-start | bytes 6291460
  44.2 19.0 %copy-start.27 = (f32[1024]{0:T(1024)S(1)}, f32[1024]{0:T(1024)}, u32[]{:S(2)}) copy-start(f32[1024]{0:T(1024)} %param.25) | copy-start | bytes 12292
  44.2 19.0 %copy-start.28 = (f32[1024]{0:T(1024)S(1)}, f32[1024]{0:T(1024)}, u32[]{:S(2)}) copy-start(f32[1024]{0:T(1024)} %param.26) | copy-start | bytes 12292
  49.7 69.4 %copy-start.21 = (s32[1024]{0:T(1024)}, s32[1024]{0:T(1024)S(1)}, u32[]{:S(2)}) copy-start(s32[1024]{0:T(1024)S(1)} %collective-permute-done.2) | copy-start | bytes 12292
  49.7 13.4 %copy-start.18 = (bf16[64,2048]{1,0:T(8,128)(2,1)}, bf16[64,2048]{1,0:T(8,128)(2,1)S(1)}, u32[]{:S(2)}) copy-start(bf16[64,2048]{1,0:T(8,128)(2,1)S(1)} %collective-permute-done.5) | copy-start | bytes 786436
  62.5 46.9 %collective-permute-start.6 = (bf16[1024,2048]{1,0:T(8,128)(2,1)}, bf16[1024,2048]{1,0:T(8,128)(2,1)}, u32[]{:S(2)}, u32[]{:S(2)}) collective-permute-start(bf16[1024,2048]{1,0:T(8,128)(2,1)} %all-gather.4.cloned.1.call-done), channel_id=1, source_target_pairs={{0,2},{1,0},{2,3},{3,1},{4,6},{5,4},{6,7},{7,5},{8,10},{9,8},{10,1... | collective-permute-start | bytes 12582920 | tf_op jit(solution)/shard_map/ppermute | solution.py:670
  63.1 247.4 %reduce-scatter.3.cloned.1.call-start = ((), (), s32[]{:S(2)}) async-start(), calls=%async_computation.5 | async-start | bytes 1310720 | tf_op jit(solution)/shard_map/reduce_scatter | solution.py:844
  116.6 72.0 %collective-permute-start.8 = (bf16[1024,2048]{1,0:T(8,128)(2,1)}, bf16[1024,2048]{1,0:T(8,128)(2,1)}, u32[]{:S(2)}, u32[]{:S(2)}) collective-permute-start(bf16[1024,2048]{1,0:T(8,128)(2,1)} %all-gather.6.cloned.1.call-done), channel_id=1, source_target_pairs={{0,2},{1,0},{2,3},{3,1},{4,6},{5,4},{6,7},{7,5},{8,10},{9,8},{10,1... | collective-permute-start | bytes 12582920 | tf_op jit(solution)/shard_map/ppermute | solution.py:670
  136.5 4.9 %copy-start.24 = (f32[4096]{0:T(1024)S(1)}, f32[4096]{0:T(1024)}, u32[]{:S(2)}) copy-start(f32[4096]{0:T(1024)} %param.32) | copy-start | bytes 49156
  140.7 4.5 %collective-permute-start.7 = (bf16[1024,1024]{1,0:T(8,128)(2,1)}, bf16[1024,1024]{1,0:T(8,128)(2,1)}, u32[]{:S(2)}, u32[]{:S(2)}) collective-permute-start(bf16[1024,1024]{1,0:T(8,128)(2,1)} %convolution_convert_fusion.refs_1_), channel_id=1, source_target_pairs={{0,2},{2,0},{1,3},{3,1},{4,6},{6,4},{5,7},{7,5},{8,10},{10,8},{9,1... | collective-permute-start | bytes 6291464 | tf_op jit(solution)/shard_map/ppermute | solution.py:758
  212.8 27.5 %collective-permute-start.10 = (bf16[256,2048]{1,0:T(8,128)(2,1)}, bf16[256,2048]{1,0:T(8,128)(2,1)S(1)}, u32[]{:S(2)}, u32[]{:S(2)}) collective-permute-start(bf16[256,2048]{1,0:T(8,128)(2,1)} %get-tuple-element.118), channel_id=1, source_target_pairs={{0,1},{1,0},{2,3},{3,2},{4,5},{5,4},{6,7},{7,6},{8,9},{9,8},{10,11... | collective-permute-start | bytes 3145736 | tf_op jit(solution)/shard_map/ppermute | solution.py:686
  215.3 25.0 %collective-permute-start.11 = (bf16[256,2048]{1,0:T(8,128)(2,1)}, bf16[256,2048]{1,0:T(8,128)(2,1)S(1)}, u32[]{:S(2)}, u32[]{:S(2)}) collective-permute-start(bf16[256,2048]{1,0:T(8,128)(2,1)} %get-tuple-element.119), channel_id=1, source_target_pairs={{0,4},{1,5},{2,6},{3,7},{4,0},{5,1},{6,2},{7,3},{8,12},{9,13},{10,... | collective-permute-start | bytes 3145736 | tf_op jit(solution)/shard_map/ppermute | solution.py:686
  244.8 4.2 collective-permute-start.12
  244.8 14.8 %collective-permute-start.13 = (bf16[128,2048]{1,0:T(8,128)(2,1)}, bf16[128,2048]{1,0:T(8,128)(2,1)S(1)}, u32[]{:S(2)}, u32[]{:S(2)}) collective-permute-start(bf16[128,2048]{1,0:T(8,128)(2,1)} %get-tuple-element.131), channel_id=1, source_target_pairs={{0,4},{1,5},{2,6},{3,7},{4,0},{5,1},{6,2},{7,3},{8,12},{9,13},{10,... | collective-permute-start | bytes 1572872 | tf_op jit(solution)/shard_map/ppermute | solution.py:686
  246.8 14.3 %collective-permute-start.14 = (bf16[128,2048]{1,0:T(8,128)(2,1)}, bf16[128,2048]{1,0:T(8,128)(2,1)}, u32[]{:S(2)}, u32[]{:S(2)}) collective-permute-start(bf16[128,2048]{1,0:T(8,128)(2,1)} %get-tuple-element.132), channel_id=1, source_target_pairs={{0,1},{1,0},{2,3},{3,2},{4,5},{5,4},{6,7},{7,6},{8,9},{9,8},{10,11... | collective-permute-start | bytes 1572872 | tf_op jit(solution)/shard_map/ppermute | solution.py:686
  264.8 48.8 %collective-permute-start.15 = (bf16[1024,2048]{1,0:T(8,128)(2,1)}, bf16[1024,2048]{1,0:T(8,128)(2,1)}, u32[]{:S(2)}, u32[]{:S(2)}) collective-permute-start(bf16[1024,2048]{1,0:T(8,128)(2,1)} %get-tuple-element.134), channel_id=1, source_target_pairs={{2,0},{0,1},{3,2},{1,3},{6,4},{4,5},{7,6},{5,7},{10,8},{8,9},{11,1... | collective-permute-start | bytes 12582920 | tf_op jit(solution)/shard_map/ppermute | solution.py:670
  264.9 158.4 %reduce-scatter.5.cloned.1.call-start = ((), (), s32[]{:S(2)}) async-start(), calls=%async_computation.6 | async-start | bytes 4456448 | tf_op jit(solution)/shard_map/reduce_scatter | solution.py:852
  313.7 21.9 %collective-permute-start.17 = (bf16[256,2048]{1,0:T(8,128)(2,1)}, bf16[256,2048]{1,0:T(8,128)(2,1)S(1)}, u32[]{:S(2)}, u32[]{:S(2)}) collective-permute-start(bf16[256,2048]{1,0:T(8,128)(2,1)} %get-tuple-element.141), channel_id=1, source_target_pairs={{0,4},{1,5},{2,6},{3,7},{4,0},{5,1},{6,2},{7,3},{8,12},{9,13},{10,... | collective-permute-start | bytes 3145736 | tf_op jit(solution)/shard_map/ppermute | solution.py:686
  314.8 22.5 %collective-permute-start.16 = (bf16[256,2048]{1,0:T(8,128)(2,1)}, bf16[256,2048]{1,0:T(8,128)(2,1)S(1)}, u32[]{:S(2)}, u32[]{:S(2)}) collective-permute-start(bf16[256,2048]{1,0:T(8,128)(2,1)} %get-tuple-element.139.refs_2_), channel_id=1, source_target_pairs={{0,1},{1,0},{2,3},{3,2},{4,5},{5,4},{6,7},{7,6},{8,9},{9,8},{10,11... | collective-permute-start | bytes 3145736 | tf_op jit(solution)/shard_map/ppermute | solution.py:686
  342.5 5.2 %collective-permute-start.18 = (bf16[512,1024]{1,0:T(8,128)(2,1)}, bf16[512,1024]{1,0:T(8,128)(2,1)}, u32[]{:S(2)}, u32[]{:S(2)}) collective-permute-start(bf16[512,1024]{1,0:T(8,128)(2,1)} %constant_dynamic-slice_fusion.1), channel_id=1, source_target_pairs={{0,2},{2,0},{1,3},{3,1},{4,6},{6,4},{5,7},{7,5},{8,10},{10,8},{9,1... | collective-permute-start | bytes 3145736 | tf_op jit(solution)/shard_map/ppermute | solution.py:758
  345.0 5.8 %collective-permute-start.9 = (bf16[512,1024]{1,0:T(8,128)(2,1)}, bf16[512,1024]{1,0:T(8,128)(2,1)}, u32[]{:S(2)}, u32[]{:S(2)}) collective-permute-start(bf16[512,1024]{1,0:T(8,128)(2,1)} %constant_dynamic-slice_fusion), channel_id=1, source_target_pairs={{0,2},{2,0},{1,3},{3,1},{4,6},{6,4},{5,7},{7,5},{8,10},{10,8},{9,1... | collective-permute-start | bytes 3145736 | tf_op jit(solution)/shard_map/ppermute | solution.py:758
  347.0 3.8 copy-start.23
  350.2 4.6 %copy-start.30 = (bf16[128,2048]{1,0:T(8,128)(2,1)S(1)}, bf16[128,2048]{1,0:T(8,128)(2,1)}, u32[]{:S(2)}) copy-start(bf16[128,2048]{1,0:T(8,128)(2,1)} %get-tuple-element.151) | copy-start | bytes 1572868
  350.2 4.9 %copy-start.29 = (bf16[128,2048]{1,0:T(8,128)(2,1)S(1)}, bf16[128,2048]{1,0:T(8,128)(2,1)}, u32[]{:S(2)}) copy-start(bf16[128,2048]{1,0:T(8,128)(2,1)} %get-tuple-element.152) | copy-start | bytes 1572868
  350.2 21.5 %copy-start.12 = (f32[1024,1024]{1,0:T(8,128)S(1)}, f32[1024,1024]{1,0:T(8,128)}, u32[]{:S(2)}) copy-start(f32[1024,1024]{1,0:T(8,128)} %get-tuple-element.126) | copy-start | bytes 12582916
  350.2 6.8 %collective-permute-start.21 = (f32[8,2048]{1,0:T(8,128)S(1)}, f32[8,2048]{1,0:T(8,128)S(1)}, u32[]{:S(2)}, u32[]{:S(2)}) collective-permute-start(f32[8,2048]{1,0:T(8,128)S(1)} %reshape.116), channel_id=1, source_target_pairs={{0,2},{2,0},{1,3},{3,1},{4,6},{6,4},{5,7},{7,5},{8,10},{10,8},{9,1... | collective-permute-start | bytes 196616 | tf_op jit(solution)/shard_map/ppermute | solution.py:730
  354.8 20.7 %collective-permute-start.19 = (bf16[128,2048]{1,0:T(8,128)(2,1)S(1)}, bf16[128,2048]{1,0:T(8,128)(2,1)S(1)}, u32[]{:S(2)}, u32[]{:S(2)}) collective-permute-start(bf16[128,2048]{1,0:T(8,128)(2,1)S(1)} %copy-done.30), channel_id=1, source_target_pairs={{0,4},{1,5},{2,6},{3,7},{4,0},{5,1},{6,2},{7,3},{8,12},{9,13},{10,... | collective-permute-start | bytes 1572872 | tf_op jit(solution)/shard_map/ppermute | solution.py:686
  355.1 20.3 %collective-permute-start.20 = (bf16[128,2048]{1,0:T(8,128)(2,1)S(1)}, bf16[128,2048]{1,0:T(8,128)(2,1)}, u32[]{:S(2)}, u32[]{:S(2)}) collective-permute-start(bf16[128,2048]{1,0:T(8,128)(2,1)S(1)} %copy-done.29), channel_id=1, source_target_pairs={{0,1},{1,0},{2,3},{3,2},{4,5},{5,4},{6,7},{7,6},{8,9},{9,8},{10,11... | collective-permute-start | bytes 1572872 | tf_op jit(solution)/shard_map/ppermute | solution.py:686
  357.0 13.1 %collective-permute-start.22 = (f32[8,2048]{1,0:T(8,128)S(1)}, f32[8,2048]{1,0:T(8,128)S(1)}, u32[]{:S(2)}, u32[]{:S(2)}) collective-permute-start(f32[8,2048]{1,0:T(8,128)S(1)} %add.144), channel_id=1, source_target_pairs={{0,1},{1,0},{2,3},{3,2},{4,5},{5,4},{6,7},{7,6},{8,9},{9,8},{10,11... | collective-permute-start | bytes 196616 | tf_op jit(solution)/shard_map/ppermute | solution.py:686
  370.1 4.7 %collective-permute-start.23 = (f32[8,2048]{1,0:T(8,128)S(1)}, f32[8,2048]{1,0:T(8,128)S(1)}, u32[]{:S(2)}, u32[]{:S(2)}) collective-permute-start(f32[8,2048]{1,0:T(8,128)S(1)} %add.145), channel_id=1, source_target_pairs={{0,4},{1,5},{2,6},{3,7},{4,0},{5,1},{6,2},{7,3},{8,12},{9,13},{10,... | collective-permute-start | bytes 196616 | tf_op jit(solution)/shard_map/ppermute | solution.py:686
  375.5 4.1 copy-start.13
  379.6 22.6 %collective-permute-start.24 = (bf16[512,1024]{1,0:T(8,128)(2,1)S(1)}, bf16[512,1024]{1,0:T(8,128)(2,1)S(1)}, u32[]{:S(2)}, u32[]{:S(2)}) collective-permute-start(bf16[512,1024]{1,0:T(8,128)(2,1)S(1)} %copy-done.13), channel_id=1, source_target_pairs={{2,0},{0,1},{3,2},{1,3},{6,4},{4,5},{7,6},{5,7},{10,8},{8,9},{11,1... | collective-permute-start | bytes 3145736 | tf_op jit(solution)/shard_map/ppermute | solution.py:670
  379.6 36.1 %collective-permute-start.25 = (bf16[512,1024]{1,0:T(8,128)(2,1)}, bf16[512,1024]{1,0:T(8,128)(2,1)S(1)}, u32[]{:S(2)}, u32[]{:S(2)}) collective-permute-start(bf16[512,1024]{1,0:T(8,128)(2,1)} %fusion.9), channel_id=1, source_target_pairs={{2,0},{0,1},{3,2},{1,3},{6,4},{4,5},{7,6},{5,7},{10,8},{8,9},{11,1... | collective-permute-start | bytes 3145736 | tf_op jit(solution)/shard_map/ppermute | solution.py:670
  379.6 46.4 %collective-permute-start.27 = (bf16[80,2048]{1,0:T(8,128)(2,1)}, bf16[80,2048]{1,0:T(8,128)(2,1)S(1)}, u32[]{:S(2)}, u32[]{:S(2)}) collective-permute-start(bf16[80,2048]{1,0:T(8,128)(2,1)} %get-tuple-element.165), channel_id=1, source_target_pairs={{2,0},{0,1},{3,2},{1,3},{6,4},{4,5},{7,6},{5,7},{10,8},{8,9},{11,1... | collective-permute-start | bytes 983048 | tf_op jit(solution)/shard_map/ppermute | solution.py:678
  382.6 43.4 %collective-permute-start.28 = (bf16[80,2048]{1,0:T(8,128)(2,1)}, bf16[80,2048]{1,0:T(8,128)(2,1)}, u32[]{:S(2)}, u32[]{:S(2)}) collective-permute-start(bf16[80,2048]{1,0:T(8,128)(2,1)} %get-tuple-element.166), channel_id=1, source_target_pairs={{10,0},{8,1},{11,2},{9,3},{14,4},{12,5},{15,6},{13,7},{2,8},{0,9},... | collective-permute-start | bytes 983048 | tf_op jit(solution)/shard_map/ppermute | solution.py:678
  382.8 43.2 %collective-permute-start.29 = (bf16[80,2048]{1,0:T(8,128)(2,1)}, bf16[80,2048]{1,0:T(8,128)(2,1)}, u32[]{:S(2)}, u32[]{:S(2)}) collective-permute-start(bf16[80,2048]{1,0:T(8,128)(2,1)} %get-tuple-element.167), channel_id=1, source_target_pairs={{18,0},{16,1},{19,2},{17,3},{22,4},{20,5},{23,6},{21,7},{26,8},{24... | collective-permute-start | bytes 983048 | tf_op jit(solution)/shard_map/ppermute | solution.py:678
  402.2 23.8 %collective-permute-start.30 = (bf16[80,2048]{1,0:T(8,128)(2,1)}, bf16[80,2048]{1,0:T(8,128)(2,1)S(1)}, u32[]{:S(2)}, u32[]{:S(2)}) collective-permute-start(bf16[80,2048]{1,0:T(8,128)(2,1)} %get-tuple-element.168), channel_id=1, source_target_pairs={{26,0},{24,1},{27,2},{25,3},{30,4},{28,5},{31,6},{29,7},{18,8},{16... | collective-permute-start | bytes 983048 | tf_op jit(solution)/shard_map/ppermute | solution.py:678
  415.7 7.6 %collective-permute-start.26 = (bf16[64,2048]{1,0:T(8,128)(2,1)}, bf16[64,2048]{1,0:T(8,128)(2,1)S(1)}, u32[]{:S(2)}, u32[]{:S(2)}) collective-permute-start(bf16[64,2048]{1,0:T(8,128)(2,1)} %reduce-scatter.3.cloned.1.call-done), channel_id=1, source_target_pairs={{2,0},{0,1},{3,2},{1,3},{6,4},{4,5},{7,6},{5,7},{10,8},{8,9},{11,1... | collective-permute-start | bytes 786440 | tf_op jit(solution)/shard_map/ppermute | solution.py:670
  (19 other events, 36.6 us)
Sparse Core Ops, SparseCore 0:
  10.8 51.6 all-gather.3
  65.2 49.0 all-gather.5
  117.1 82.9 all-gather.7
  265.0 24.2 reduce-scatter.2
  313.8 74.5 reduce-scatter.4

commit v5 on v4

--- a/solution.py
+++ b/solution.py
@@ -728,8 +728,8 @@
 
     def near_sum(values):
         values = values + lax.ppermute(values, "c", [(0, 1), (1, 0)])
+        values = values + hop(values, 1, 0)
         values = values + hop(values, 0, 1)
-        values = values + hop(values, 1, 0)
         return lax.psum(values, "l") if inner > 1 else values
 
     a, h = lax.axis_index(("z", "y")), lax.axis_index("h")
@@ -737,7 +737,7 @@
     for a_low, h_mask in ((0, 0), (1, 0), (0, 1), (1, 1)):
         for i in range(far):
             order.append((a ^ (2 * i + a_low)) * 2 + (h ^ h_mask))
-    return swap, scatter_near, far_sums, z_sums, far_parts, near_sum, jnp.stack(order).astype(jnp.int32)
+    return swap, hop, scatter_near, far_sums, z_sums, far_parts, near_sum, jnp.stack(order).astype(jnp.int32)
 
 
 def per_device(sizes, *arguments):
@@ -752,7 +752,7 @@
     unit_width = w_up.shape[1]
     half_units = unit_width // 2
     tile = min(TILE, half_units)
-    swap, scatter_near, far_sums, z_sums, far_parts, near_sum, order = moves(sizes)
+    swap, hop, scatter_near, far_sums, z_sums, far_parts, near_sum, order = moves(sizes)
 
     def partner(values):
         return lax.ppermute(values, "c", [(0, 1), (1, 0)])
@@ -797,6 +797,12 @@
     )
     early_first = lax.all_gather(shard_first, ("z", "y", "c"), axis=0, tiled=True)
     shard_second = swap(shard_second)
+    other_second = hop(shard_second, 0, 1)
+    shard_second = jnp.where(
+        lax.axis_index("h") == 0,
+        jnp.concatenate([shard_second, other_second], axis=0),
+        jnp.concatenate([other_second, shard_second], axis=0),
+    )
     bias_query = lax.dynamic_slice_in_dim(b_query, rank * head_width, head_width)
     bias_value = lax.dynamic_slice_in_dim(b_value, rank * head_width, head_width)
     bias_up = lax.dynamic_slice_in_dim(b_up, rank * unit_width, unit_width)
@@ -808,7 +814,7 @@
     early_attn, normed, segments, grad_rows, grad_rows_t, shard_second = lax.optimization_barrier(
         (early_attn, normed, segments, grad_rows, grad_rows_t, shard_second)
     )
-    full_second = lax.all_gather(shard_second, ("z", "y", "h"), axis=0, tiled=True)
+    full_second = lax.all_gather(shard_second, ("z", "y"), axis=0, tiled=True)
     full_attn = swap(early_attn)
     biases = jnp.concatenate([bias_query, jnp.zeros((head_width,), F32), bias_value])
     qkv = qkv_project(normed, full_attn, biases)
@@ -850,9 +856,7 @@
         (second_grads, first_mlp, grad_normed_part)
     )
     second_mlp = lax.psum_scatter(second_grads, ("z", "y", "c"), scatter_dimension=0, tiled=True)
-    first_mlp = swap(first_mlp, inverse=True)
     state = scatter_near(pieces, grad_normed_part)
-    grad_normed_part, state = lax.optimization_barrier((grad_normed_part, state))
     grad_normed = tp_scatter(grad_normed_part)
     own_scaled, own_inverse = normalize(own_input.astype(F32))
     grad_own = own(grad_hidden) + norm_back(grad_normed, own_scaled, own_inverse, ln1_gain)
@@ -878,6 +882,20 @@
     filled = sums.shape[0]
     sums = jnp.pad(sums, (0, -filled % (8 * columns))).reshape(-1, columns)
     sums = near_sum(sums)
+    last_sums = far_sums(state, [sums], None)
+    own_output, grad_own, *last_sums = lax.optimization_barrier((own_output, grad_own, *last_sums))
+    leaving = jnp.concatenate([own_output, grad_own, first_mlp.reshape(-1, width)], axis=0)
+    leaving = swap(leaving, inverse=True)
+    output, grad_input = leaving[:own_rows], leaving[own_rows : 2 * own_rows]
+    first_mlp = leaving[2 * own_rows :].reshape(block_rows, unit_width)
+    *late, sums = sums_call(
+        weights_last_kernel,
+        far_parts(last_sums),
+        [jax.ShapeDtypeStruct((block_rows, head_width), F32)] * 4
+        + [jax.ShapeDtypeStruct(sums.shape, F32)],
+        None,
+        "sums_last",
+    )
     shard = jax.ShapeDtypeStruct((block_rows, unit_width), F32)
     grad_w_up, grad_w_down = sums_call(
         functools.partial(units_last_kernel, tile=tile),
@@ -885,18 +903,6 @@
         [shard, shard],
         None,
         "units_last",
-    )
-    last_sums = far_sums(state, [sums], None)
-    own_output, grad_own, *last_sums = lax.optimization_barrier((own_output, grad_own, *last_sums))
-    output = swap(own_output, inverse=True)
-    grad_input = swap(grad_own, inverse=True)
-    *late, sums = sums_call(
-        weights_last_kernel,
-        far_parts(last_sums),
-        [jax.ShapeDtypeStruct((block_rows, head_width), F32)] * 4
-        + [jax.ShapeDtypeStruct(sums.shape, F32)],
-        grad_w_up,
-        "sums_last",
     )
     sums = sums.reshape(-1)
     small = [sums[i * width : (i + 1) * width] for i in range(8)]

time: 449 us -> 429 us (0.955)
  the two profiles are of different devices: /device:TPU:10 before, /device:TPU:0 now
where the time goes in v5:
time: 429 us; the launch traced here: 421 us
  waiting for transfers between devices  174 us (41%)
  Pallas kernels  156 us (36%)
  other arithmetic  24.5 us (6%)
  starting transfers between devices  23.7 us (6%)
  local copies, waits for them, and re-layouts  20.8 us (5%)
  between operations  14.8 us (3%)
  matrix products  7.61 us (2%)
    ppermute x8, waiting for transfers between devices, swap(): return lax.ppermute(values, SWAP, pairs)  94.4 us
    pallas_call x2, Pallas kernels, mlp(): pl.pallas_call(functools.partial(mlp_kernel, block=min(256, length), with...  49 us
    ppermute x11, waiting for transfers between devices, hop(): return lax.ppermute(values, ('z', 'y', 'c', 'h'), pairs)  40.8 us
    ppermute x4, waiting for transfers between devices, swap_hop(): return lax.ppermute(values, ALL, pairs)  35.5 us
    pallas_call x1, Pallas kernels, attn_backward(): pl.pallas_call(without(functools.partial(attn_backward_kernel, block=bloc...  24.3 us
    pallas_call x1, Pallas kernels, attn_forward(): pl.pallas_call(functools.partial(attn_forward_kernel, block=block), grid=...  16.4 us
    pallas_call x6, Pallas kernels, sums_call(): pl.pallas_call(body, in_specs=([pl.BlockSpec(memory_space=pl.ANY)] if aft...  15.6 us
    pallas_call x2, Pallas kernels, norm_rows(): pl.pallas_call(functools.partial(norm_kernel, residual=residual), grid=(l...  12.9 us
  transfers between devices with their start and end apart: 35, of which 13 were waited for; matrix products, arithmetic and copies ran while one was open for 11% of the time, Pallas kernels for 35%

profile of v5, /device:TPU:0, one launch (start us, length us, event | category | flops | bytes accessed | tf_op | source)
XLA Modules:
  0.0 420.7 jit_solution(18437000705735129812)
XLA Ops:
  7.2 1.7 pad_maximum_fusion.1
  9.0 1.8 mlp_shards.1
  11.4 2.0 collective-permute-start.3
  13.4 13.4 %collective-permute-done = bf16[512,1024]{1,0:T(8,128)(2,1)S(1)} collective-permute-done((bf16[512,1024]{1,0:T(8,128)(2,1)}, bf16[512,1024]{1,0:T(8,128)(2,1)S(1)}, u32[]{:S(2)}, u32[]{:S(2)}) %collective-permute-start) | collective-permute-done | bytes 1048608 | tf_op jit(solution)/shard_map/ppermute | solution.py:670
  26.8 11.2 %collective-permute-done.3 = bf16[512,1024]{1,0:T(8,128)(2,1)S(1)} collective-permute-done((bf16[512,1024]{1,0:T(8,128)(2,1)}, bf16[512,1024]{1,0:T(8,128)(2,1)S(1)}, u32[]{:S(2)}, u32[]{:S(2)}) %collective-permute-start.3) | collective-permute-done | bytes 1048608 | tf_op jit(solution)/shard_map/ppermute | solution.py:670
  38.6 6.1 %collective-permute-done.5 = bf16[64,2048]{1,0:T(8,128)(2,1)S(1)} collective-permute-done((bf16[64,2048]{1,0:T(8,128)(2,1)}, bf16[64,2048]{1,0:T(8,128)(2,1)S(1)}, u32[]{:S(2)}, u32[]{:S(2)}) %collective-permute-start.5) | collective-permute-done | bytes 262176 | tf_op jit(solution)/shard_map/ppermute | solution.py:670
  44.7 6.6 %collective-permute-done.6 = bf16[64,2048]{1,0:T(8,128)(2,1)} collective-permute-done((bf16[64,2048]{1,0:T(8,128)(2,1)S(1)}, bf16[64,2048]{1,0:T(8,128)(2,1)}, u32[]{:S(2)}, u32[]{:S(2)}) %collective-permute-start.6) | collective-permute-done | bytes 262176 | tf_op jit(solution)/shard_map/ppermute | solution.py:686
  51.3 2.0 maximum_select_fusion.2
  53.3 2.3 maximum_select_fusion.refs_0_
  55.6 3.3 maximum_select_fusion.1.g_ref
  59.0 5.5 %norm_one.1 = (bf16[1024,1024]{1,0:T(8,128)(2,1)}, bf16[1024,1024]{1,0:T(8,128)(2,1)}) custom-call(bf16[1024,1024]{1,0:T(8,128)(2,1)} %maximum_select_fusion.refs_0_, f32[1,1024]{1,0:T(1,128)} %bitcast.39, f32[1,1024]{1,0:T(1,128)} %bitcast.46), custom_call_target="tpu_custom_call" | custom-call | flops 20971520 | bytes 14680064 | tf_op jit(solution)/shard_map/norm_one/pallas_call | solution.py:275
  65.3 47.9 %collective-permute-done.7.w_ref.refs_1_ = bf16[1024,2048]{1,0:T(8,128)(2,1)} collective-permute-done((bf16[1024,2048]{1,0:T(8,128)(2,1)}, bf16[1024,2048]{1,0:T(8,128)(2,1)}, u32[]{:S(2)}, u32[]{:S(2)}) %collective-permute-start.7) | collective-permute-done | bytes 4194336 | tf_op jit(solution)/shard_map/ppermute | solution.py:670
  113.3 7.2 %qkv_project.1.q_ref.k_ref.v_ref.refs_2_.refs_3_.refs_4_ = bf16[1024,1536]{1,0:T(8,128)(2,1)} custom-call(bf16[1024,1024]{1,0:T(8,128)(2,1)} %get-tuple-element.94.n_ref, f32[1,1536]{1,0:T(1,128)} %reshape.114.b_ref, bf16[1024,2048]{1,0:T(8,128)(2,1)} %collective-permute-done.7.w_ref.refs_1_), custom_call_target="tpu_custom_call" | custom-call | flops 3221225472 | bytes 8388608 | tf_op jit(solution)/shard_map/qkv_project/pallas_call | solution.py:456
  121.5 16.4 %attn_forward.1 = (bf16[1024,512]{1,0:T(8,128)(2,1)}, f32[4,8,1024]{2,1,0:T(8,128)}) custom-call(s32[1024,1]{1,0:T(8,128)} %copy.37.seg_col.refs_0_, s32[1,1024]{1,0:T(1,128)} %bitcast.41, bf16[1024,1536]{1,0:T(8,128)(2,1)} %qkv_project.1.q_ref.k_ref.v_ref.refs_2_.refs_3_.refs_4_, bf16[1024,1536]{1,0:T(8,128)(2,1)} %qkv_project.1.q_ref.k_ref.v_ref.refs_2_.refs_3_.refs_4_, ...), custom_call_target="tpu_custom_call" | custom-call | flops 2147483648 | bytes 4194304 | tf_op jit(solution)/shard_map/attn_forward/pallas_call | solution.py:156
  137.9 4.1 convolution_convert_fusion.refs_1_
  143.4 2.6 copy.39.gt_ref
  146.6 7.4 %norm_two.1 = (bf16[1024,1024]{1,0:T(8,128)(2,1)}, bf16[1024,1024]{1,0:T(8,128)(2,1)}, f32[1024,1024]{1,0:T(8,128)}) custom-call(bf16[1024,1024]{1,0:T(8,128)(2,1)} %maximum_select_fusion.refs_0_, bf16[1024,1024]{1,0:T(8,128)(2,1)} %convolution_convert_fusion.refs_1_, bf16[1024,1024]{1,0:T(8,128)(2,1)} %collective-permute-done.8.refs_2_, ...), custom_call_target="tpu_custom_call" | custom-call | flops 20971520 | bytes 14680064 | tf_op jit(solution)/shard_map/norm_two/pallas_call | solution.py:275
  154.0 15.3 %collective-permute-done.9.w_ref = bf16[1024,2048]{1,0:T(8,128)(2,1)} collective-permute-done((bf16[1024,2048]{1,0:T(8,128)(2,1)}, bf16[1024,2048]{1,0:T(8,128)(2,1)}, u32[]{:S(2)}, u32[]{:S(2)}) %collective-permute-start.9) | collective-permute-done | bytes 4194336 | tf_op jit(solution)/shard_map/ppermute | solution.py:670
  169.3 24.1 %mlp_first.1 = (bf16[1024,1024]{1,0:T(8,128)(2,1)}, bf16[1024,1024]{1,0:T(8,128)(2,1)}, bf16[256,2048]{1,0:T(8,128)(2,1)}, bf16[256,2048]{1,0:T(8,128)(2,1)}, bf...) custom-call(s32[16]{0:T(128)} %stack.67.order, ...), custom_call_target="tpu_custom_call" | custom-call | flops 12884901888 | bytes 20971520 | tf_op jit(solution)/shard_map/mlp_first/pallas_call | solution.py:402
  193.5 2.0 collective-permute-start.12
  195.5 25.0 %mlp_second.1 = (bf16[1024,1024]{1,0:T(8,128)(2,1)}, bf16[1024,1024]{1,0:T(8,128)(2,1)}, bf16[1024,2048]{1,0:T(8,128)(2,1)}, f32[1,1024]{1,0:T(1,128)}) custom-call(s32[16]{0:T(128)} %stack.67.order, bf16[1024,1024]{1,0:T(8,128)(2,1)} %get-tuple-element.99.n_ref, bf16[1024,1024]{1,0:T(8,128)(2,1)} %copy-done, bf16[1024,1024]{1,0:T(8,128)(2,1)} %get-tuple-element.101.nt_ref, ...), custom_call_target="tpu_custom_call" | custom-call | flops 12884901888 | bytes 20971520 | tf_op jit(solution)/shard_map/mlp_second/pallas_call | solution.py:402
  221.8 3.1 sums_one.2
  225.1 1.9 collective-permute-start.15
  227.0 2.0 collective-permute-done.13.other_ref
  230.4 9.1 %norm_two_back.1 = (f32[1024,1024]{1,0:T(8,128)}, bf16[1024,1024]{1,0:T(8,128)(2,1)}, bf16[1024,1024]{1,0:T(8,128)(2,1)}, f32[8,1024]{1,0:T(8,128)}) custom-call(f32[1024,1024]{1,0:T(8,128)} %get-tuple-element.98.hidden_ref, bf16[1024,1024]{1,0:T(8,128)(2,1)} %copy-done, bf16[1024,1024]{1,0:T(8,128)(2,1)} %get-tuple-element.119.refs_0_.own_ref, ...), custom_call_target="tpu_custom_call" | custom-call | flops 31457280 | bytes 16777216 | tf_op jit(solution)/shard_map/norm_two_back/pallas_call | solution.py:315
  240.3 3.5 sums_two_z.1.refs_8_
  243.8 2.0 collective-permute-start.16
  246.1 3.5 convolution_convert_fusion.1.refs_7_
  249.5 24.3 %attn_backward.1.grads_ref.order_only.refs_0_ = bf16[3,1024,512]{2,1,0:T(8,128)(2,1)} custom-call(s32[1024,1]{1,0:T(8,128)} %copy.37.seg_col.refs_0_, s32[1,1024]{1,0:T(1,128)} %bitcast.42, bf16[1024,1536]{1,0:T(8,128)(2,1)} %qkv_project.1.q_ref.k_ref.v_ref.refs_2_.refs_3_.refs_4_, bf16[1024,1536]{1,0:T(8,128)(2,1)} %qkv_project.1.q_ref.k_ref.v_ref.refs_2_.refs_3_.refs_4_, ...), custom_call_target="tpu_custom_call" | custom-call | flops 5368709120 | bytes 8388608 | tf_op jit(solution)/shard_map/attn_backward/pallas_call | solution.py:185
  273.8 10.1 %weight_grads.1 = (bf16[256,2048]{1,0:T(8,128)(2,1)}, bf16[256,2048]{1,0:T(8,128)(2,1)}, bf16[128,2048]{1,0:T(8,128)(2,1)}, bf16[128,2048]{1,0:T(8,128)(2,1)}, bf16[256,2048]{1,0:T(8,128)(2,1)}) custom-call(s32[16]{0:T(128)} %stack.67.order, bf16[1024,1024]{1,0:T(8,128)(2,1)} %get-tuple-element.131.nt_ref, ...), custom_call_target="tpu_custom_call" | custom-call | flops 4294967296 | bytes 12582912 | tf_op jit(solution)/shard_map/weight_grads/pallas_call | solution.py:501
  283.9 7.7 %qkv_back.1.refs_0_ = bf16[1024,1024]{1,0:T(8,128)(2,1)} custom-call(bf16[3,1024,512]{2,1,0:T(8,128)(2,1)} %attn_backward.1.grads_ref.order_only.refs_0_, bf16[1024,2048]{1,0:T(8,128)(2,1)} %collective-permute-done.7.w_ref.refs_1_, bf16[256,2048]{1,0:T(8,128)(2,1)} %get-tuple-element.133.refs_2_), custom_call_target="tpu_custom_call" | custom-call | flops 3221225472 | bytes 8388608 | tf_op jit(solution)/shard_map/qkv_back/pallas_call | solution.py:542
  296.5 2.5 collective-permute-start.18
  300.2 2.0 convert_reduce_fusion.2
  303.0 2.4 fusion.10
  305.6 3.9 add_convert_fusion
  309.6 14.7 %collective-permute-done.19.refs_2_.from_y = bf16[256,2048]{1,0:T(8,128)(2,1)} collective-permute-done((bf16[256,2048]{1,0:T(8,128)(2,1)}, bf16[256,2048]{1,0:T(8,128)(2,1)}, u32[]{:S(2)}, u32[]{:S(2)}) %collective-permute-start.19) | collective-permute-done | bytes 1048608 | tf_op jit(solution)/shard_map/ppermute | solution.py:686
  324.3 3.1 sums_one.3
  330.2 19.2 %collective-permute-done.23 = f32[8,2048]{1,0:T(8,128)S(1)} collective-permute-done((f32[8,2048]{1,0:T(8,128)S(1)}, f32[8,2048]{1,0:T(8,128)S(1)}, u32[]{:S(2)}, u32[]{:S(2)}) %collective-permute-start.23) | collective-permute-done | bytes 65568 | tf_op jit(solution)/shard_map/ppermute | solution.py:686
  349.4 1.5 collective-permute-start.24
  351.0 3.8 fusion.9
  356.3 3.5 sums_two.1
  359.8 1.6 pad_maximum_fusion
  362.0 1.3 collective-permute-start.27
  363.4 3.3 collective-permute-start.28
  367.1 35.5 %collective-permute-done.26.refs_0_ = bf16[80,2048]{1,0:T(8,128)(2,1)S(1)} collective-permute-done((bf16[80,2048]{1,0:T(8,128)(2,1)S(1)}, bf16[80,2048]{1,0:T(8,128)(2,1)S(1)}, u32[]{:S(2)}, u32[]{:S(2)}) %collective-permute-start.26) | collective-permute-done | bytes 327712 | tf_op jit(solution)/shard_map/ppermute | solution.py:678
  404.3 2.1 sums_last.1
  410.2 1.5 fusion.17
  411.7 2.1 units_last.1
  (168 shorter events, 26.8 us)
Async XLA Ops:
  7.2 57.3 %all-gather.4.cloned.1.call-start = ((), (), s32[]{:S(2)}) async-start(), calls=%async_computation.2 | async-start | bytes 4456448 | tf_op jit(solution)/shard_map/all_gather | solution.py:795
  8.9 111.6 %all-gather.6.cloned.1.call-start = ((), (), s32[]{:S(2)}) async-start(), calls=%async_computation.3 | async-start | bytes 4456448 | tf_op jit(solution)/shard_map/all_gather | solution.py:798
  10.8 182.6 %all-gather.8.cloned.1.call-start = ((), (), s32[]{:S(2)}) async-start(), calls=%async_computation.4 | async-start | bytes 4718592 | tf_op jit(solution)/shard_map/all_gather | solution.py:817
  10.9 15.9 %collective-permute-start = (bf16[512,1024]{1,0:T(8,128)(2,1)}, bf16[512,1024]{1,0:T(8,128)(2,1)S(1)}, u32[]{:S(2)}, u32[]{:S(2)}) collective-permute-start(bf16[512,1024]{1,0:T(8,128)(2,1)} %param.18), channel_id=1, source_target_pairs={{0,2},{1,0},{2,3},{3,1},{4,6},{5,4},{6,7},{7,5},{8,10},{9,8},{10,1... | collective-permute-start | bytes 3145736 | tf_op jit(solution)/shard_map/ppermute | solution.py:670
  11.4 26.7 %collective-permute-start.3 = (bf16[512,1024]{1,0:T(8,128)(2,1)}, bf16[512,1024]{1,0:T(8,128)(2,1)S(1)}, u32[]{:S(2)}, u32[]{:S(2)}) collective-permute-start(bf16[512,1024]{1,0:T(8,128)(2,1)} %param.35), channel_id=1, source_target_pairs={{0,2},{1,0},{2,3},{3,1},{4,6},{5,4},{6,7},{7,5},{8,10},{9,8},{10,1... | collective-permute-start | bytes 3145736 | tf_op jit(solution)/shard_map/ppermute | solution.py:670
  26.8 26.4 %collective-permute-start.1 = (bf16[512,1024]{1,0:T(8,128)(2,1)S(1)}, bf16[512,1024]{1,0:T(8,128)(2,1)S(1)}, u32[]{:S(2)}, u32[]{:S(2)}) collective-permute-start(bf16[512,1024]{1,0:T(8,128)(2,1)S(1)} %collective-permute-done), channel_id=1, source_target_pairs={{0,2},{2,0},{1,3},{3,1},{4,6},{6,4},{5,7},{7,5},{8,10},{10,8},{9,1... | collective-permute-start | bytes 3145736 | tf_op jit(solution)/shard_map/ppermute | solution.py:758
  38.1 17.5 %copy-start.4 = (bf16[512,1024]{1,0:T(8,128)(2,1)}, bf16[512,1024]{1,0:T(8,128)(2,1)S(1)}, u32[]{:S(2)}) copy-start(bf16[512,1024]{1,0:T(8,128)(2,1)S(1)} %collective-permute-done.3) | copy-start | bytes 3145732
  38.1 17.5 %collective-permute-start.4 = (bf16[512,1024]{1,0:T(8,128)(2,1)S(1)}, bf16[512,1024]{1,0:T(8,128)(2,1)}, u32[]{:S(2)}, u32[]{:S(2)}) collective-permute-start(bf16[512,1024]{1,0:T(8,128)(2,1)S(1)} %collective-permute-done.3), channel_id=1, source_target_pairs={{0,2},{2,0},{1,3},{3,1},{4,6},{6,4},{5,7},{7,5},{8,10},{10,8},{9,1... | collective-permute-start | bytes 3145736 | tf_op jit(solution)/shard_map/ppermute | solution.py:758
  38.1 6.6 %collective-permute-start.5 = (bf16[64,2048]{1,0:T(8,128)(2,1)}, bf16[64,2048]{1,0:T(8,128)(2,1)S(1)}, u32[]{:S(2)}, u32[]{:S(2)}) collective-permute-start(bf16[64,2048]{1,0:T(8,128)(2,1)} %get-tuple-element.91), channel_id=1, source_target_pairs={{0,2},{1,0},{2,3},{3,1},{4,6},{5,4},{6,7},{7,5},{8,10},{9,8},{10,1... | collective-permute-start | bytes 786440 | tf_op jit(solution)/shard_map/ppermute | solution.py:670
  44.7 6.6 %collective-permute-start.6 = (bf16[64,2048]{1,0:T(8,128)(2,1)S(1)}, bf16[64,2048]{1,0:T(8,128)(2,1)}, u32[]{:S(2)}, u32[]{:S(2)}) collective-permute-start(bf16[64,2048]{1,0:T(8,128)(2,1)S(1)} %collective-permute-done.5), channel_id=1, source_target_pairs={{0,1},{1,0},{2,3},{3,2},{4,5},{5,4},{6,7},{7,6},{8,9},{9,8},{10,11... | collective-permute-start | bytes 786440 | tf_op jit(solution)/shard_map/ppermute | solution.py:686
  44.7 19.8 %collective-permute-start.2 = (s32[1024]{0:T(1024)}, s32[1024]{0:T(1024)S(1)}, u32[]{:S(2)}, u32[]{:S(2)}) collective-permute-start(s32[1024]{0:T(1024)} %param.19), channel_id=1, source_target_pairs={{0,2},{1,0},{2,3},{3,1},{4,6},{5,4},{6,7},{7,5},{8,10},{9,8},{10,1... | collective-permute-start | bytes 12296 | tf_op jit(solution)/shard_map/ppermute | solution.py:670
  58.9 84.5 %copy-start = (bf16[1024,1024]{1,0:T(8,128)(2,1)}, bf16[1024,1024]{1,0:T(8,128)(2,1)S(1)}, u32[]{:S(2)}) copy-start(bf16[1024,1024]{1,0:T(8,128)(2,1)S(1)} %maximum_select_fusion.1.g_ref) | copy-start | bytes 6291460
  58.9 5.6 %copy-start.28 = (f32[1024]{0:T(1024)S(1)}, f32[1024]{0:T(1024)}, u32[]{:S(2)}) copy-start(f32[1024]{0:T(1024)} %param.25) | copy-start | bytes 12292
  58.9 5.7 %copy-start.29 = (f32[1024]{0:T(1024)S(1)}, f32[1024]{0:T(1024)}, u32[]{:S(2)}) copy-start(f32[1024]{0:T(1024)} %param.26) | copy-start | bytes 12292
  64.4 56.1 %copy-start.22 = (s32[1024]{0:T(1024)}, s32[1024]{0:T(1024)S(1)}, u32[]{:S(2)}) copy-start(s32[1024]{0:T(1024)S(1)} %collective-permute-done.2) | copy-start | bytes 12292
  64.5 48.8 %collective-permute-start.7 = (bf16[1024,2048]{1,0:T(8,128)(2,1)}, bf16[1024,2048]{1,0:T(8,128)(2,1)}, u32[]{:S(2)}, u32[]{:S(2)}) collective-permute-start(bf16[1024,2048]{1,0:T(8,128)(2,1)} %all-gather.4.cloned.1.call-done), channel_id=1, source_target_pairs={{0,2},{1,0},{2,3},{3,1},{4,6},{5,4},{6,7},{7,5},{8,10},{9,8},{10,1... | collective-permute-start | bytes 12582920 | tf_op jit(solution)/shard_map/ppermute | solution.py:670
  64.5 227.2 %reduce-scatter.3.cloned.1.call-start = ((), (), s32[]{:S(2)}) async-start(), calls=%async_computation.5 | async-start | bytes 1310720 | tf_op jit(solution)/shard_map/reduce_scatter | solution.py:850
  120.5 48.8 %collective-permute-start.9 = (bf16[1024,2048]{1,0:T(8,128)(2,1)}, bf16[1024,2048]{1,0:T(8,128)(2,1)}, u32[]{:S(2)}, u32[]{:S(2)}) collective-permute-start(bf16[1024,2048]{1,0:T(8,128)(2,1)} %all-gather.6.cloned.1.call-done), channel_id=1, source_target_pairs={{0,2},{1,0},{2,3},{3,1},{4,6},{5,4},{6,7},{7,5},{8,10},{9,8},{10,1... | collective-permute-start | bytes 12582920 | tf_op jit(solution)/shard_map/ppermute | solution.py:670
  137.9 4.9 %copy-start.25 = (f32[4096]{0:T(1024)S(1)}, f32[4096]{0:T(1024)}, u32[]{:S(2)}) copy-start(f32[4096]{0:T(1024)} %param.32) | copy-start | bytes 49156
  142.1 4.5 %collective-permute-start.8 = (bf16[1024,1024]{1,0:T(8,128)(2,1)}, bf16[1024,1024]{1,0:T(8,128)(2,1)}, u32[]{:S(2)}, u32[]{:S(2)}) collective-permute-start(bf16[1024,1024]{1,0:T(8,128)(2,1)} %convolution_convert_fusion.refs_1_), channel_id=1, source_target_pairs={{0,2},{2,0},{1,3},{3,1},{4,6},{6,4},{5,7},{7,5},{8,10},{10,8},{9,1... | collective-permute-start | bytes 6291464 | tf_op jit(solution)/shard_map/ppermute | solution.py:758
  193.4 27.0 %collective-permute-start.11 = (bf16[256,2048]{1,0:T(8,128)(2,1)}, bf16[256,2048]{1,0:T(8,128)(2,1)S(1)}, u32[]{:S(2)}, u32[]{:S(2)}) collective-permute-start(bf16[256,2048]{1,0:T(8,128)(2,1)} %get-tuple-element.112), channel_id=1, source_target_pairs={{0,1},{1,0},{2,3},{3,2},{4,5},{5,4},{6,7},{7,6},{8,9},{9,8},{10,11... | collective-permute-start | bytes 3145736 | tf_op jit(solution)/shard_map/ppermute | solution.py:686
  193.5 26.9 %collective-permute-start.12 = (bf16[256,2048]{1,0:T(8,128)(2,1)}, bf16[256,2048]{1,0:T(8,128)(2,1)S(1)}, u32[]{:S(2)}, u32[]{:S(2)}) collective-permute-start(bf16[256,2048]{1,0:T(8,128)(2,1)} %get-tuple-element.113), channel_id=1, source_target_pairs={{0,4},{1,5},{2,6},{3,7},{4,0},{5,1},{6,2},{7,3},{8,12},{9,13},{10,... | collective-permute-start | bytes 3145736 | tf_op jit(solution)/shard_map/ppermute | solution.py:686
  224.9 4.2 collective-permute-start.13
  224.9 14.6 %collective-permute-start.14 = (bf16[128,2048]{1,0:T(8,128)(2,1)}, bf16[128,2048]{1,0:T(8,128)(2,1)S(1)}, u32[]{:S(2)}, u32[]{:S(2)}) collective-permute-start(bf16[128,2048]{1,0:T(8,128)(2,1)} %get-tuple-element.125), channel_id=1, source_target_pairs={{0,4},{1,5},{2,6},{3,7},{4,0},{5,1},{6,2},{7,3},{8,12},{9,13},{10,... | collective-permute-start | bytes 1572872 | tf_op jit(solution)/shard_map/ppermute | solution.py:686
  225.1 14.7 %collective-permute-start.15 = (bf16[128,2048]{1,0:T(8,128)(2,1)}, bf16[128,2048]{1,0:T(8,128)(2,1)}, u32[]{:S(2)}, u32[]{:S(2)}) collective-permute-start(bf16[128,2048]{1,0:T(8,128)(2,1)} %get-tuple-element.126), channel_id=1, source_target_pairs={{0,1},{1,0},{2,3},{3,2},{4,5},{5,4},{6,7},{7,6},{8,9},{9,8},{10,11... | collective-permute-start | bytes 1572872 | tf_op jit(solution)/shard_map/ppermute | solution.py:686
  243.8 48.3 %collective-permute-start.16 = (bf16[1024,2048]{1,0:T(8,128)(2,1)}, bf16[1024,2048]{1,0:T(8,128)(2,1)}, u32[]{:S(2)}, u32[]{:S(2)}) collective-permute-start(bf16[1024,2048]{1,0:T(8,128)(2,1)} %get-tuple-element.128), channel_id=1, source_target_pairs={{2,0},{0,1},{3,2},{1,3},{6,4},{4,5},{7,6},{5,7},{10,8},{8,9},{11,1... | collective-permute-start | bytes 12582920 | tf_op jit(solution)/shard_map/ppermute | solution.py:670
  245.8 165.9 %reduce-scatter.5.cloned.1.call-start = ((), (), s32[]{:S(2)}) async-start(), calls=%async_computation.6 | async-start | bytes 4456448 | tf_op jit(solution)/shard_map/reduce_scatter | solution.py:858
  294.7 4.3 %copy-start.23 = (f32[8,1024]{1,0:T(8,128)S(1)}, f32[8,1024]{1,0:T(8,128)}, u32[]{:S(2)}) copy-start(f32[8,1024]{1,0:T(8,128)} %get-tuple-element.141) | copy-start | bytes 98308
  294.7 8.2 %collective-permute-start.17 = (bf16[512,1024]{1,0:T(8,128)(2,1)}, bf16[512,1024]{1,0:T(8,128)(2,1)}, u32[]{:S(2)}, u32[]{:S(2)}) collective-permute-start(bf16[512,1024]{1,0:T(8,128)(2,1)} %constant_dynamic-slice_fusion.1), channel_id=1, source_target_pairs={{0,2},{2,0},{1,3},{3,1},{4,6},{6,4},{5,7},{7,5},{8,10},{10,8},{9,1... | collective-permute-start | bytes 3145736 | tf_op jit(solution)/shard_map/ppermute | solution.py:758
  295.0 8.0 %copy-start.21 = (f32[1024]{0:T(1024)S(1)}, f32[1024]{0:T(1024)}, u32[]{:S(2)}) copy-start(f32[1024]{0:T(1024)} %param.20) | copy-start | bytes 12292
  296.0 9.6 %collective-permute-start.10 = (bf16[512,1024]{1,0:T(8,128)(2,1)}, bf16[512,1024]{1,0:T(8,128)(2,1)}, u32[]{:S(2)}, u32[]{:S(2)}) collective-permute-start(bf16[512,1024]{1,0:T(8,128)(2,1)} %constant_dynamic-slice_fusion), channel_id=1, source_target_pairs={{0,2},{2,0},{1,3},{3,1},{4,6},{6,4},{5,7},{7,5},{8,10},{10,8},{9,1... | collective-permute-start | bytes 3145736 | tf_op jit(solution)/shard_map/ppermute | solution.py:758
  296.5 27.8 %collective-permute-start.18 = (bf16[256,2048]{1,0:T(8,128)(2,1)}, bf16[256,2048]{1,0:T(8,128)(2,1)}, u32[]{:S(2)}, u32[]{:S(2)}) collective-permute-start(bf16[256,2048]{1,0:T(8,128)(2,1)} %get-tuple-element.133.refs_2_), channel_id=1, source_target_pairs={{0,1},{1,0},{2,3},{3,2},{4,5},{5,4},{6,7},{7,6},{8,9},{9,8},{10,11... | collective-permute-start | bytes 3145736 | tf_op jit(solution)/shard_map/ppermute | solution.py:686
  299.1 25.2 %collective-permute-start.19 = (bf16[256,2048]{1,0:T(8,128)(2,1)}, bf16[256,2048]{1,0:T(8,128)(2,1)}, u32[]{:S(2)}, u32[]{:S(2)}) collective-permute-start(bf16[256,2048]{1,0:T(8,128)(2,1)} %get-tuple-element.135), channel_id=1, source_target_pairs={{0,4},{1,5},{2,6},{3,7},{4,0},{5,1},{6,2},{7,3},{8,12},{9,13},{10,... | collective-permute-start | bytes 3145736 | tf_op jit(solution)/shard_map/ppermute | solution.py:686
  305.5 4.0 copy-start.20
  305.5 23.7 %collective-permute-start.22 = (f32[8,2048]{1,0:T(8,128)S(1)}, f32[8,2048]{1,0:T(8,128)S(1)}, u32[]{:S(2)}, u32[]{:S(2)}) collective-permute-start(f32[8,2048]{1,0:T(8,128)S(1)} %reshape.122), channel_id=1, source_target_pairs={{0,2},{2,0},{1,3},{3,1},{4,6},{6,4},{5,7},{7,5},{8,10},{10,8},{9,1... | collective-permute-start | bytes 196616 | tf_op jit(solution)/shard_map/ppermute | solution.py:730
  324.3 26.7 %copy-start.2 = (bf16[1024,1024]{1,0:T(8,128)(2,1)S(1)}, bf16[1024,1024]{1,0:T(8,128)(2,1)}, u32[]{:S(2)}) copy-start(bf16[1024,1024]{1,0:T(8,128)(2,1)} %qkv_back.1.refs_0_) | copy-start | bytes 6291460
  327.4 28.0 %collective-permute-start.20 = (bf16[128,2048]{1,0:T(8,128)(2,1)}, bf16[128,2048]{1,0:T(8,128)(2,1)S(1)}, u32[]{:S(2)}, u32[]{:S(2)}) collective-permute-start(bf16[128,2048]{1,0:T(8,128)(2,1)} %get-tuple-element.139), channel_id=1, source_target_pairs={{0,4},{1,5},{2,6},{3,7},{4,0},{5,1},{6,2},{7,3},{8,12},{9,13},{10,... | collective-permute-start | bytes 1572872 | tf_op jit(solution)/shard_map/ppermute | solution.py:686
  328.4 26.9 %collective-permute-start.21 = (bf16[128,2048]{1,0:T(8,128)(2,1)}, bf16[128,2048]{1,0:T(8,128)(2,1)S(1)}, u32[]{:S(2)}, u32[]{:S(2)}) collective-permute-start(bf16[128,2048]{1,0:T(8,128)(2,1)} %get-tuple-element.140), channel_id=1, source_target_pairs={{0,1},{1,0},{2,3},{3,2},{4,5},{5,4},{6,7},{7,6},{8,9},{9,8},{10,11... | collective-permute-start | bytes 1572872 | tf_op jit(solution)/shard_map/ppermute | solution.py:686
  329.3 20.1 %collective-permute-start.23 = (f32[8,2048]{1,0:T(8,128)S(1)}, f32[8,2048]{1,0:T(8,128)S(1)}, u32[]{:S(2)}, u32[]{:S(2)}) collective-permute-start(f32[8,2048]{1,0:T(8,128)S(1)} %add.144), channel_id=1, source_target_pairs={{0,4},{1,5},{2,6},{3,7},{4,0},{5,1},{6,2},{7,3},{8,12},{9,13},{10,... | collective-permute-start | bytes 196616 | tf_op jit(solution)/shard_map/ppermute | solution.py:686
  349.4 5.3 %collective-permute-start.24 = (f32[8,2048]{1,0:T(8,128)S(1)}, f32[8,2048]{1,0:T(8,128)S(1)}, u32[]{:S(2)}, u32[]{:S(2)}) collective-permute-start(f32[8,2048]{1,0:T(8,128)S(1)} %add.145), channel_id=1, source_target_pairs={{0,1},{1,0},{2,3},{3,2},{4,5},{5,4},{6,7},{7,6},{8,9},{9,8},{10,11... | collective-permute-start | bytes 196616 | tf_op jit(solution)/shard_map/ppermute | solution.py:686
  356.3 3.5 copy-start.9
  359.8 3.6 copy-start.31
  359.8 6.8 %copy-start.30 = (bf16[80,2048]{1,0:T(8,128)(2,1)S(1)}, bf16[80,2048]{1,0:T(8,128)(2,1)}, u32[]{:S(2)}) copy-start(bf16[80,2048]{1,0:T(8,128)(2,1)} %get-tuple-element.154) | copy-start | bytes 983044
  361.5 47.9 %collective-permute-start.25 = (bf16[1152,1024]{1,0:T(8,128)(2,1)}, bf16[1152,1024]{1,0:T(8,128)(2,1)S(1)}, u32[]{:S(2)}, u32[]{:S(2)}) collective-permute-start(bf16[1152,1024]{1,0:T(8,128)(2,1)} %pad_maximum_fusion), channel_id=1, source_target_pairs={{2,0},{0,1},{3,2},{1,3},{6,4},{4,5},{7,6},{5,7},{10,8},{8,9},{11,1... | collective-permute-start | bytes 7077896 | tf_op jit(solution)/shard_map/ppermute | solution.py:670
  362.0 40.6 %collective-permute-start.26 = (bf16[80,2048]{1,0:T(8,128)(2,1)S(1)}, bf16[80,2048]{1,0:T(8,128)(2,1)S(1)}, u32[]{:S(2)}, u32[]{:S(2)}) collective-permute-start(bf16[80,2048]{1,0:T(8,128)(2,1)S(1)} %copy-done.33), channel_id=1, source_target_pairs={{2,0},{0,1},{3,2},{1,3},{6,4},{4,5},{7,6},{5,7},{10,8},{8,9},{11,1... | collective-permute-start | bytes 983048 | tf_op jit(solution)/shard_map/ppermute | solution.py:678
  362.0 40.6 %collective-permute-start.27 = (bf16[80,2048]{1,0:T(8,128)(2,1)S(1)}, bf16[80,2048]{1,0:T(8,128)(2,1)S(1)}, u32[]{:S(2)}, u32[]{:S(2)}) collective-permute-start(bf16[80,2048]{1,0:T(8,128)(2,1)S(1)} %copy-done.32), channel_id=1, source_target_pairs={{10,0},{8,1},{11,2},{9,3},{14,4},{12,5},{15,6},{13,7},{2,8},{0,9},... | collective-permute-start | bytes 983048 | tf_op jit(solution)/shard_map/ppermute | solution.py:678
  363.4 39.2 %collective-permute-start.28 = (bf16[80,2048]{1,0:T(8,128)(2,1)S(1)}, bf16[80,2048]{1,0:T(8,128)(2,1)S(1)}, u32[]{:S(2)}, u32[]{:S(2)}) collective-permute-start(bf16[80,2048]{1,0:T(8,128)(2,1)S(1)} %copy-done.31), channel_id=1, source_target_pairs={{18,0},{16,1},{19,2},{17,3},{22,4},{20,5},{23,6},{21,7},{26,8},{24... | collective-permute-start | bytes 983048 | tf_op jit(solution)/shard_map/ppermute | solution.py:678
  366.7 36.0 %collective-permute-start.29 = (bf16[80,2048]{1,0:T(8,128)(2,1)S(1)}, bf16[80,2048]{1,0:T(8,128)(2,1)S(1)}, u32[]{:S(2)}, u32[]{:S(2)}) collective-permute-start(bf16[80,2048]{1,0:T(8,128)(2,1)S(1)} %copy-done.30), channel_id=1, source_target_pairs={{26,0},{24,1},{27,2},{25,3},{30,4},{28,5},{31,6},{29,7},{18,8},{16... | collective-permute-start | bytes 983048 | tf_op jit(solution)/shard_map/ppermute | solution.py:678
  (21 other events, 36.7 us)
Sparse Core Ops, SparseCore 0:
  10.8 53.2 all-gather.3
  66.8 49.0 all-gather.5
  118.0 71.8 all-gather.7
  245.9 26.9 reduce-scatter.2
  292.3 89.7 reduce-scatter.4

commit v6 on v5

--- a/solution.py
+++ b/solution.py
@@ -11,6 +11,7 @@
 HEAD_DIM = 64
 LANES = 128
 TILE = 512
+ROWS = 512
 MASKED = -1e30
 VMEM_BYTES = 60 * 1024 * 1024
 F32 = jnp.float32
@@ -401,7 +402,7 @@
         grad_shapes = [jax.ShapeDtypeStruct((width, 2 * units), BF16)]
     results = pl.pallas_call(
         functools.partial(
-            mlp_kernel, block=min(256, length), with_previous=bool(previous), cube=cube
+            mlp_kernel, block=min(ROWS, length), with_previous=bool(previous), cube=cube
         ),
         grid_spec=pltpu.PrefetchScalarGridSpec(
             num_scalar_prefetch=1,
@@ -443,7 +444,7 @@
 def qkv_kernel(n_ref, b_ref, w_ref, out_ref):
     scale = jnp.where(pl.program_id(0) == 0, HEAD_DIM ** (-0.5), 1.0)
     length = n_ref.shape[0]
-    step = min(256, length)
+    step = min(ROWS, length)
     for first in range(0, length, step):
         span = slice(first, first + step)
         out_ref[span, :] = ((dot_nn(n_ref[span, :], w_ref[...]) + b_ref[...]) * scale).astype(BF16)
@@ -538,7 +539,7 @@
 def qkv_back(grads, weights, after):
     _, length, columns = grads.shape
     width = weights.shape[0]
-    block = min(256, length)
+    block = min(ROWS, length)
     return pl.pallas_call(
         without(qkv_back_kernel, 2),
         grid=(length // block,),
@@ -776,11 +777,16 @@
     def own(values):
         return lax.dynamic_slice_in_dim(values, rank * own_rows, own_rows)
 
+    def tp_scatter_terms(values):
+        if ranks != 2:
+            total = lax.psum_scatter(values, TP, scatter_dimension=0, tiled=True)
+            return total, jnp.zeros_like(total)
+        theirs = lax.dynamic_slice_in_dim(values, (1 - rank) * own_rows, own_rows)
+        return own(values), partner(theirs)
+
     def tp_scatter(values):
-        if ranks != 2:
-            return lax.psum_scatter(values, TP, scatter_dimension=0, tiled=True).astype(F32)
-        theirs = lax.dynamic_slice_in_dim(values, (1 - rank) * own_rows, own_rows)
-        return own(values).astype(F32) + partner(theirs).astype(F32)
+        own_part, other_part = tp_scatter_terms(values)
+        return own_part.astype(F32) + other_part.astype(F32)
 
     own_input = swap(block_input)
     segments = swap(segment_ids)
@@ -857,7 +863,12 @@
     )
     second_mlp = lax.psum_scatter(second_grads, ("z", "y", "c"), scatter_dimension=0, tiled=True)
     state = scatter_near(pieces, grad_normed_part)
-    grad_normed = tp_scatter(grad_normed_part)
+    grad_normed_own, grad_normed_other = tp_scatter_terms(grad_normed_part)
+    first_mlp, grad_normed_other, state = lax.optimization_barrier(
+        (first_mlp, grad_normed_other, state)
+    )
+    first_mlp = swap(first_mlp, inverse=True)
+    grad_normed = grad_normed_own.astype(F32) + grad_normed_other.astype(F32)
     own_scaled, own_inverse = normalize(own_input.astype(F32))
     grad_own = own(grad_hidden) + norm_back(grad_normed, own_scaled, own_inverse, ln1_gain)
     grad_own = grad_own.astype(BF16)
@@ -882,20 +893,10 @@
     filled = sums.shape[0]
     sums = jnp.pad(sums, (0, -filled % (8 * columns))).reshape(-1, columns)
     sums = near_sum(sums)
-    last_sums = far_sums(state, [sums], None)
+    last_sums = far_sums(state, [sums], first_mlp)
     own_output, grad_own, *last_sums = lax.optimization_barrier((own_output, grad_own, *last_sums))
-    leaving = jnp.concatenate([own_output, grad_own, first_mlp.reshape(-1, width)], axis=0)
-    leaving = swap(leaving, inverse=True)
-    output, grad_input = leaving[:own_rows], leaving[own_rows : 2 * own_rows]
-    first_mlp = leaving[2 * own_rows :].reshape(block_rows, unit_width)
-    *late, sums = sums_call(
-        weights_last_kernel,
-        far_parts(last_sums),
-        [jax.ShapeDtypeStruct((block_rows, head_width), F32)] * 4
-        + [jax.ShapeDtypeStruct(sums.shape, F32)],
-        None,
-        "sums_last",
-    )
+    leaving = swap(jnp.concatenate([own_output, grad_own], axis=0), inverse=True)
+    output, grad_input = leaving[:own_rows], leaving[own_rows:]
     shard = jax.ShapeDtypeStruct((block_rows, unit_width), F32)
     grad_w_up, grad_w_down = sums_call(
         functools.partial(units_last_kernel, tile=tile),
@@ -903,6 +904,14 @@
         [shard, shard],
         None,
         "units_last",
+    )
+    *late, sums = sums_call(
+        weights_last_kernel,
+        far_parts(last_sums),
+        [jax.ShapeDtypeStruct((block_rows, head_width), F32)] * 4
+        + [jax.ShapeDtypeStruct(sums.shape, F32)],
+        grad_w_up,
+        "sums_last",
     )
     sums = sums.reshape(-1)
     small = [sums[i * width : (i + 1) * width] for i in range(8)]

time: 429 us -> 419 us (0.977)
  waiting for transfers between devices: 174 us -> 167 us
    ppermute x4, waiting for transfers between devices: 35.5 us -> 0.01 us  [swap_hop(): return lax.ppermute(values, ALL, pairs)]
    ppermute x8 -> x9, waiting for transfers between devices: 94.4 us -> 124 us  [swap(): return lax.ppermute(values, SWAP, pairs)]
    unnamed x77 -> x83, local copies, waits for them, and re-layouts: 9.35 us -> 8.71 us
  transfers between devices with their start and end apart: 35 -> 36, of which waited for: 13 -> 13; matrix products, arithmetic and copies ran while one was open for 11% -> 9% of each run, Pallas kernels for 35% -> 36%
where the time goes in v6:
time: 419 us; the launch traced here: 411 us
  waiting for transfers between devices  167 us (40%)
  Pallas kernels  155 us (37%)
  starting transfers between devices  25.4 us (6%)
  other arithmetic  22.2 us (5%)
  local copies, waits for them, and re-layouts  19.2 us (5%)
  between operations  14.9 us (4%)
  matrix products  7.59 us (2%)
    ppermute x9, waiting for transfers between devices, swap(): return lax.ppermute(values, SWAP, pairs)  124 us
    pallas_call x2, Pallas kernels, mlp(): pl.pallas_call(functools.partial(mlp_kernel, block=min(ROWS, length), wit...  48.4 us
    ppermute x11, waiting for transfers between devices, hop(): return lax.ppermute(values, ('z', 'y', 'c', 'h'), pairs)  39.8 us
    pallas_call x1, Pallas kernels, attn_backward(): pl.pallas_call(without(functools.partial(attn_backward_kernel, block=bloc...  24.3 us
    pallas_call x1, Pallas kernels, attn_forward(): pl.pallas_call(functools.partial(attn_forward_kernel, block=block), grid=...  16.4 us
    pallas_call x6, Pallas kernels, sums_call(): pl.pallas_call(body, in_specs=([pl.BlockSpec(memory_space=pl.ANY)] if aft...  15.6 us
    pallas_call x2, Pallas kernels, norm_rows(): pl.pallas_call(functools.partial(norm_kernel, residual=residual), grid=(l...  12.9 us
    ppermute x11, starting transfers between devices, hop(): return lax.ppermute(values, ('z', 'y', 'c', 'h'), pairs)  11.7 us
  transfers between devices with their start and end apart: 36, of which 13 were waited for; matrix products, arithmetic and copies ran while one was open for 9% of the time, Pallas kernels for 36%

profile of v6, /device:TPU:0, one launch (start us, length us, event | category | flops | bytes accessed | tf_op | source)
XLA Modules:
  0.0 410.8 jit_solution(8969776720417720061)
XLA Ops:
  7.2 1.7 pad_maximum_fusion.1
  9.0 1.8 mlp_shards.1
  11.3 2.0 collective-permute-start.3
  13.4 13.4 %collective-permute-done = bf16[512,1024]{1,0:T(8,128)(2,1)S(1)} collective-permute-done((bf16[512,1024]{1,0:T(8,128)(2,1)}, bf16[512,1024]{1,0:T(8,128)(2,1)S(1)}, u32[]{:S(2)}, u32[]{:S(2)}) %collective-permute-start) | collective-permute-done | bytes 1048608 | tf_op jit(solution)/shard_map/ppermute | solution.py:671
  26.8 11.2 %collective-permute-done.3 = bf16[512,1024]{1,0:T(8,128)(2,1)S(1)} collective-permute-done((bf16[512,1024]{1,0:T(8,128)(2,1)}, bf16[512,1024]{1,0:T(8,128)(2,1)S(1)}, u32[]{:S(2)}, u32[]{:S(2)}) %collective-permute-start.3) | collective-permute-done | bytes 1048608 | tf_op jit(solution)/shard_map/ppermute | solution.py:671
  38.6 6.1 %collective-permute-done.5 = bf16[64,2048]{1,0:T(8,128)(2,1)S(1)} collective-permute-done((bf16[64,2048]{1,0:T(8,128)(2,1)}, bf16[64,2048]{1,0:T(8,128)(2,1)S(1)}, u32[]{:S(2)}, u32[]{:S(2)}) %collective-permute-start.5) | collective-permute-done | bytes 262176 | tf_op jit(solution)/shard_map/ppermute | solution.py:671
  44.7 6.6 %collective-permute-done.6 = bf16[64,2048]{1,0:T(8,128)(2,1)} collective-permute-done((bf16[64,2048]{1,0:T(8,128)(2,1)S(1)}, bf16[64,2048]{1,0:T(8,128)(2,1)}, u32[]{:S(2)}, u32[]{:S(2)}) %collective-permute-start.6) | collective-permute-done | bytes 262176 | tf_op jit(solution)/shard_map/ppermute | solution.py:687
  51.3 2.0 maximum_select_fusion.2
  53.2 2.3 maximum_select_fusion.refs_0_
  55.6 3.4 maximum_select_fusion.1.g_ref
  59.0 5.5 %norm_one.1 = (bf16[1024,1024]{1,0:T(8,128)(2,1)}, bf16[1024,1024]{1,0:T(8,128)(2,1)}) custom-call(bf16[1024,1024]{1,0:T(8,128)(2,1)} %maximum_select_fusion.refs_0_, f32[1,1024]{1,0:T(1,128)} %bitcast.39, f32[1,1024]{1,0:T(1,128)} %bitcast.46), custom_call_target="tpu_custom_call" | custom-call | flops 20971520 | bytes 14680064 | tf_op jit(solution)/shard_map/norm_one/pallas_call | solution.py:276
  65.4 47.9 %collective-permute-done.7.w_ref.refs_1_ = bf16[1024,2048]{1,0:T(8,128)(2,1)} collective-permute-done((bf16[1024,2048]{1,0:T(8,128)(2,1)}, bf16[1024,2048]{1,0:T(8,128)(2,1)}, u32[]{:S(2)}, u32[]{:S(2)}) %collective-permute-start.7) | collective-permute-done | bytes 4194336 | tf_op jit(solution)/shard_map/ppermute | solution.py:671
  113.3 7.1 %qkv_project.1.q_ref.k_ref.v_ref.refs_2_.refs_3_.refs_4_ = bf16[1024,1536]{1,0:T(8,128)(2,1)} custom-call(bf16[1024,1024]{1,0:T(8,128)(2,1)} %get-tuple-element.101.n_ref, f32[1,1536]{1,0:T(1,128)} %reshape.108.b_ref, bf16[1024,2048]{1,0:T(8,128)(2,1)} %collective-permute-done.7.w_ref.refs_1_), custom_call_target="tpu_custom_call" | custom-call | flops 3221225472 | bytes 8388608 | tf_op jit(solution)/shard_map/qkv_project/pallas_call | solution.py:457
  121.5 16.4 %attn_forward.1 = (bf16[1024,512]{1,0:T(8,128)(2,1)}, f32[4,8,1024]{2,1,0:T(8,128)}) custom-call(s32[1024,1]{1,0:T(8,128)} %copy.37.seg_col.refs_0_, s32[1,1024]{1,0:T(1,128)} %bitcast.41, bf16[1024,1536]{1,0:T(8,128)(2,1)} %qkv_project.1.q_ref.k_ref.v_ref.refs_2_.refs_3_.refs_4_, bf16[1024,1536]{1,0:T(8,128)(2,1)} %qkv_project.1.q_ref.k_ref.v_ref.refs_2_.refs_3_.refs_4_, ...), custom_call_target="tpu_custom_call" | custom-call | flops 2147483648 | bytes 4194304 | tf_op jit(solution)/shard_map/attn_forward/pallas_call | solution.py:157
  137.9 4.1 %convolution_convert_fusion.refs_1_ = bf16[1024,1024]{1,0:T(8,128)(2,1)} fusion(bf16[1024,512]{1,0:T(8,128)(2,1)} %get-tuple-element.104.refs_5_.mixed_ref, bf16[1024,2048]{1,0:T(8,128)(2,1)} %collective-permute-done.7.w_ref.refs_1_), kind=kOutput, calls=%fused_computation.22 | convolution fusion | flops 1074790400 | bytes 4194304 | tf_op jit(solution)/shard_map/dot_general | solution.py:45
  143.3 2.5 copy.39.gt_ref
  146.5 7.5 %norm_two.1 = (bf16[1024,1024]{1,0:T(8,128)(2,1)}, bf16[1024,1024]{1,0:T(8,128)(2,1)}, f32[1024,1024]{1,0:T(8,128)}) custom-call(bf16[1024,1024]{1,0:T(8,128)(2,1)} %maximum_select_fusion.refs_0_, bf16[1024,1024]{1,0:T(8,128)(2,1)} %convolution_convert_fusion.refs_1_, bf16[1024,1024]{1,0:T(8,128)(2,1)} %collective-permute-done.8.refs_2_, ...), custom_call_target="tpu_custom_call" | custom-call | flops 20971520 | bytes 14680064 | tf_op jit(solution)/shard_map/norm_two/pallas_call | solution.py:276
  154.0 15.3 %collective-permute-done.9.w_ref = bf16[1024,2048]{1,0:T(8,128)(2,1)} collective-permute-done((bf16[1024,2048]{1,0:T(8,128)(2,1)}, bf16[1024,2048]{1,0:T(8,128)(2,1)}, u32[]{:S(2)}, u32[]{:S(2)}) %collective-permute-start.9) | collective-permute-done | bytes 4194336 | tf_op jit(solution)/shard_map/ppermute | solution.py:671
  169.3 23.7 %mlp_first.1 = (bf16[1024,1024]{1,0:T(8,128)(2,1)}, bf16[1024,1024]{1,0:T(8,128)(2,1)}, bf16[256,2048]{1,0:T(8,128)(2,1)}, bf16[256,2048]{1,0:T(8,128)(2,1)}, bf...) custom-call(s32[16]{0:T(128)} %stack.67.order, ...), custom_call_target="tpu_custom_call" | custom-call | flops 12884901888 | bytes 20971520 | tf_op jit(solution)/shard_map/mlp_first/pallas_call | solution.py:403
  193.1 2.0 collective-permute-start.12
  195.1 24.6 %mlp_second.1 = (bf16[1024,1024]{1,0:T(8,128)(2,1)}, bf16[1024,1024]{1,0:T(8,128)(2,1)}, bf16[1024,2048]{1,0:T(8,128)(2,1)}, f32[1,1024]{1,0:T(1,128)}) custom-call(s32[16]{0:T(128)} %stack.67.order, bf16[1024,1024]{1,0:T(8,128)(2,1)} %get-tuple-element.106.n_ref, bf16[1024,1024]{1,0:T(8,128)(2,1)} %copy-done, bf16[1024,1024]{1,0:T(8,128)(2,1)} %get-tuple-element.108.nt_ref, ...), custom_call_target="tpu_custom_call" | custom-call | flops 12884901888 | bytes 20971520 | tf_op jit(solution)/shard_map/mlp_second/pallas_call | solution.py:403
  221.1 3.1 sums_one.2
  224.4 1.9 collective-permute-start.15
  226.3 2.0 collective-permute-done.13.other_ref
  229.6 9.1 %norm_two_back.1 = (f32[1024,1024]{1,0:T(8,128)}, bf16[1024,1024]{1,0:T(8,128)(2,1)}, bf16[1024,1024]{1,0:T(8,128)(2,1)}, f32[8,1024]{1,0:T(8,128)}) custom-call(f32[1024,1024]{1,0:T(8,128)} %get-tuple-element.105.hidden_ref, bf16[1024,1024]{1,0:T(8,128)(2,1)} %copy-done, bf16[1024,1024]{1,0:T(8,128)(2,1)} %get-tuple-element.126.refs_0_.own_ref, ...), custom_call_target="tpu_custom_call" | custom-call | flops 31457280 | bytes 16777216 | tf_op jit(solution)/shard_map/norm_two_back/pallas_call | solution.py:316
  239.6 3.7 sums_two_z.1.refs_8_
  243.2 1.9 collective-permute-start.16
  245.3 3.4 convolution_convert_fusion.1.refs_7_
  248.7 24.3 %attn_backward.1.grads_ref.order_only.refs_0_ = bf16[3,1024,512]{2,1,0:T(8,128)(2,1)} custom-call(s32[1024,1]{1,0:T(8,128)} %copy.37.seg_col.refs_0_, s32[1,1024]{1,0:T(1,128)} %bitcast.42, bf16[1024,1536]{1,0:T(8,128)(2,1)} %qkv_project.1.q_ref.k_ref.v_ref.refs_2_.refs_3_.refs_4_, bf16[1024,1536]{1,0:T(8,128)(2,1)} %qkv_project.1.q_ref.k_ref.v_ref.refs_2_.refs_3_.refs_4_, ...), custom_call_target="tpu_custom_call" | custom-call | flops 5368709120 | bytes 8388608 | tf_op jit(solution)/shard_map/attn_backward/pallas_call | solution.py:186
  273.0 10.1 %weight_grads.1 = (bf16[256,2048]{1,0:T(8,128)(2,1)}, bf16[256,2048]{1,0:T(8,128)(2,1)}, bf16[128,2048]{1,0:T(8,128)(2,1)}, bf16[128,2048]{1,0:T(8,128)(2,1)}, bf16[256,2048]{1,0:T(8,128)(2,1)}) custom-call(s32[16]{0:T(128)} %stack.67.order, bf16[1024,1024]{1,0:T(8,128)(2,1)} %get-tuple-element.138.nt_ref, ...), custom_call_target="tpu_custom_call" | custom-call | flops 4294967296 | bytes 12582912 | tf_op jit(solution)/shard_map/weight_grads/pallas_call | solution.py:502
  283.1 7.4 %qkv_back.1.refs_0_ = bf16[1024,1024]{1,0:T(8,128)(2,1)} custom-call(bf16[3,1024,512]{2,1,0:T(8,128)(2,1)} %attn_backward.1.grads_ref.order_only.refs_0_, bf16[1024,2048]{1,0:T(8,128)(2,1)} %collective-permute-done.7.w_ref.refs_1_, bf16[256,2048]{1,0:T(8,128)(2,1)} %get-tuple-element.140.refs_2_), custom_call_target="tpu_custom_call" | custom-call | flops 3221225472 | bytes 8388608 | tf_op jit(solution)/shard_map/qkv_back/pallas_call | solution.py:543
  292.2 2.5 collective-permute-start.18
  298.7 1.9 convert_reduce_fusion.2
  301.3 16.1 %collective-permute-done.19.refs_2_ = bf16[256,2048]{1,0:T(8,128)(2,1)S(1)} collective-permute-done((bf16[256,2048]{1,0:T(8,128)(2,1)}, bf16[256,2048]{1,0:T(8,128)(2,1)S(1)}, u32[]{:S(2)}, u32[]{:S(2)}) %collective-permute-start.19) | collective-permute-done | bytes 1048608 | tf_op jit(solution)/shard_map/ppermute | solution.py:687
  318.7 3.1 sums_one.3
  321.8 2.3 fusion.10
  324.4 3.8 add_convert_fusion
  328.2 1.7 collective-permute-start.20
  330.7 1.6 collective-permute-start.24
  332.3 16.8 %collective-permute-done.24 = f32[8,2048]{1,0:T(8,128)S(1)} collective-permute-done((f32[8,2048]{1,0:T(8,128)S(1)}, f32[8,2048]{1,0:T(8,128)S(1)}, u32[]{:S(2)}, u32[]{:S(2)}) %collective-permute-start.24) | collective-permute-done | bytes 65568 | tf_op jit(solution)/shard_map/ppermute | solution.py:687
  349.1 1.5 collective-permute-start.25
  350.7 3.1 fusion.9
  355.2 3.5 sums_two.1
  361.8 2.3 collective-permute-start.29
  365.2 29.0 %collective-permute-done.26 = bf16[1024,1024]{1,0:T(8,128)(2,1)S(1)} collective-permute-done((bf16[1024,1024]{1,0:T(8,128)(2,1)S(1)}, bf16[1024,1024]{1,0:T(8,128)(2,1)S(1)}, u32[]{:S(2)}, u32[]{:S(2)}) %collective-permute-start.26) | collective-permute-done | bytes 2097184 | tf_op jit(solution)/shard_map/ppermute | solution.py:671
  394.1 1.5 fusion.17
  395.6 2.1 units_last.1
  398.7 2.1 sums_last.1
  (173 shorter events, 26.9 us)
Async XLA Ops:
  7.2 57.3 %all-gather.4.cloned.1.call-start = ((), (), s32[]{:S(2)}) async-start(), calls=%async_computation.2 | async-start | bytes 4456448 | tf_op jit(solution)/shard_map/all_gather | solution.py:801
  8.9 111.5 %all-gather.6.cloned.1.call-start = ((), (), s32[]{:S(2)}) async-start(), calls=%async_computation.3 | async-start | bytes 4456448 | tf_op jit(solution)/shard_map/all_gather | solution.py:804
  10.8 182.2 %all-gather.8.cloned.1.call-start = ((), (), s32[]{:S(2)}) async-start(), calls=%async_computation.4 | async-start | bytes 4718592 | tf_op jit(solution)/shard_map/all_gather | solution.py:823
  10.9 15.9 %collective-permute-start = (bf16[512,1024]{1,0:T(8,128)(2,1)}, bf16[512,1024]{1,0:T(8,128)(2,1)S(1)}, u32[]{:S(2)}, u32[]{:S(2)}) collective-permute-start(bf16[512,1024]{1,0:T(8,128)(2,1)} %param.18), channel_id=1, source_target_pairs={{0,2},{1,0},{2,3},{3,1},{4,6},{5,4},{6,7},{7,5},{8,10},{9,8},{10,1... | collective-permute-start | bytes 3145736 | tf_op jit(solution)/shard_map/ppermute | solution.py:671
  11.3 26.7 %collective-permute-start.3 = (bf16[512,1024]{1,0:T(8,128)(2,1)}, bf16[512,1024]{1,0:T(8,128)(2,1)S(1)}, u32[]{:S(2)}, u32[]{:S(2)}) collective-permute-start(bf16[512,1024]{1,0:T(8,128)(2,1)} %param.35), channel_id=1, source_target_pairs={{0,2},{1,0},{2,3},{3,1},{4,6},{5,4},{6,7},{7,5},{8,10},{9,8},{10,1... | collective-permute-start | bytes 3145736 | tf_op jit(solution)/shard_map/ppermute | solution.py:671
  26.8 26.4 %collective-permute-start.1 = (bf16[512,1024]{1,0:T(8,128)(2,1)S(1)}, bf16[512,1024]{1,0:T(8,128)(2,1)S(1)}, u32[]{:S(2)}, u32[]{:S(2)}) collective-permute-start(bf16[512,1024]{1,0:T(8,128)(2,1)S(1)} %collective-permute-done), channel_id=1, source_target_pairs={{0,2},{2,0},{1,3},{3,1},{4,6},{6,4},{5,7},{7,5},{8,10},{10,8},{9,1... | collective-permute-start | bytes 3145736 | tf_op jit(solution)/shard_map/ppermute | solution.py:759
  38.1 17.5 %copy-start.6 = (bf16[512,1024]{1,0:T(8,128)(2,1)}, bf16[512,1024]{1,0:T(8,128)(2,1)S(1)}, u32[]{:S(2)}) copy-start(bf16[512,1024]{1,0:T(8,128)(2,1)S(1)} %collective-permute-done.3) | copy-start | bytes 3145732
  38.1 17.5 %collective-permute-start.4 = (bf16[512,1024]{1,0:T(8,128)(2,1)S(1)}, bf16[512,1024]{1,0:T(8,128)(2,1)}, u32[]{:S(2)}, u32[]{:S(2)}) collective-permute-start(bf16[512,1024]{1,0:T(8,128)(2,1)S(1)} %collective-permute-done.3), channel_id=1, source_target_pairs={{0,2},{2,0},{1,3},{3,1},{4,6},{6,4},{5,7},{7,5},{8,10},{10,8},{9,1... | collective-permute-start | bytes 3145736 | tf_op jit(solution)/shard_map/ppermute | solution.py:759
  38.1 6.6 %collective-permute-start.5 = (bf16[64,2048]{1,0:T(8,128)(2,1)}, bf16[64,2048]{1,0:T(8,128)(2,1)S(1)}, u32[]{:S(2)}, u32[]{:S(2)}) collective-permute-start(bf16[64,2048]{1,0:T(8,128)(2,1)} %get-tuple-element.98), channel_id=1, source_target_pairs={{0,2},{1,0},{2,3},{3,1},{4,6},{5,4},{6,7},{7,5},{8,10},{9,8},{10,1... | collective-permute-start | bytes 786440 | tf_op jit(solution)/shard_map/ppermute | solution.py:671
  44.7 6.6 %collective-permute-start.6 = (bf16[64,2048]{1,0:T(8,128)(2,1)S(1)}, bf16[64,2048]{1,0:T(8,128)(2,1)}, u32[]{:S(2)}, u32[]{:S(2)}) collective-permute-start(bf16[64,2048]{1,0:T(8,128)(2,1)S(1)} %collective-permute-done.5), channel_id=1, source_target_pairs={{0,1},{1,0},{2,3},{3,2},{4,5},{5,4},{6,7},{7,6},{8,9},{9,8},{10,11... | collective-permute-start | bytes 786440 | tf_op jit(solution)/shard_map/ppermute | solution.py:687
  44.7 19.8 %collective-permute-start.2 = (s32[1024]{0:T(1024)}, s32[1024]{0:T(1024)S(1)}, u32[]{:S(2)}, u32[]{:S(2)}) collective-permute-start(s32[1024]{0:T(1024)} %param.19), channel_id=1, source_target_pairs={{0,2},{1,0},{2,3},{3,1},{4,6},{5,4},{6,7},{7,5},{8,10},{9,8},{10,1... | collective-permute-start | bytes 12296 | tf_op jit(solution)/shard_map/ppermute | solution.py:671
  58.9 84.4 %copy-start = (bf16[1024,1024]{1,0:T(8,128)(2,1)}, bf16[1024,1024]{1,0:T(8,128)(2,1)S(1)}, u32[]{:S(2)}) copy-start(bf16[1024,1024]{1,0:T(8,128)(2,1)S(1)} %maximum_select_fusion.1.g_ref) | copy-start | bytes 6291460
  58.9 5.6 %copy-start.29 = (f32[1024]{0:T(1024)S(1)}, f32[1024]{0:T(1024)}, u32[]{:S(2)}) copy-start(f32[1024]{0:T(1024)} %param.25) | copy-start | bytes 12292
  58.9 5.7 %copy-start.30 = (f32[1024]{0:T(1024)S(1)}, f32[1024]{0:T(1024)}, u32[]{:S(2)}) copy-start(f32[1024]{0:T(1024)} %param.26) | copy-start | bytes 12292
  64.4 56.0 %copy-start.23 = (s32[1024]{0:T(1024)}, s32[1024]{0:T(1024)S(1)}, u32[]{:S(2)}) copy-start(s32[1024]{0:T(1024)S(1)} %collective-permute-done.2) | copy-start | bytes 12292
  64.5 48.8 %collective-permute-start.7 = (bf16[1024,2048]{1,0:T(8,128)(2,1)}, bf16[1024,2048]{1,0:T(8,128)(2,1)}, u32[]{:S(2)}, u32[]{:S(2)}) collective-permute-start(bf16[1024,2048]{1,0:T(8,128)(2,1)} %all-gather.4.cloned.1.call-done), channel_id=1, source_target_pairs={{0,2},{1,0},{2,3},{3,1},{4,6},{5,4},{6,7},{7,5},{8,10},{9,8},{10,1... | collective-permute-start | bytes 12582920 | tf_op jit(solution)/shard_map/ppermute | solution.py:671
  64.5 226.0 %reduce-scatter.3.cloned.1.call-start = ((), (), s32[]{:S(2)}) async-start(), calls=%async_computation.5 | async-start | bytes 1310720 | tf_op jit(solution)/shard_map/reduce_scatter | solution.py:856
  120.4 48.8 %collective-permute-start.9 = (bf16[1024,2048]{1,0:T(8,128)(2,1)}, bf16[1024,2048]{1,0:T(8,128)(2,1)}, u32[]{:S(2)}, u32[]{:S(2)}) collective-permute-start(bf16[1024,2048]{1,0:T(8,128)(2,1)} %all-gather.6.cloned.1.call-done), channel_id=1, source_target_pairs={{0,2},{1,0},{2,3},{3,1},{4,6},{5,4},{6,7},{7,5},{8,10},{9,8},{10,1... | collective-permute-start | bytes 12582920 | tf_op jit(solution)/shard_map/ppermute | solution.py:671
  142.0 4.5 %collective-permute-start.8 = (bf16[1024,1024]{1,0:T(8,128)(2,1)}, bf16[1024,1024]{1,0:T(8,128)(2,1)}, u32[]{:S(2)}, u32[]{:S(2)}) collective-permute-start(bf16[1024,1024]{1,0:T(8,128)(2,1)} %convolution_convert_fusion.refs_1_), channel_id=1, source_target_pairs={{0,2},{2,0},{1,3},{3,1},{4,6},{6,4},{5,7},{7,5},{8,10},{10,8},{9,1... | collective-permute-start | bytes 6291464 | tf_op jit(solution)/shard_map/ppermute | solution.py:759
  193.0 26.7 %collective-permute-start.11 = (bf16[256,2048]{1,0:T(8,128)(2,1)}, bf16[256,2048]{1,0:T(8,128)(2,1)S(1)}, u32[]{:S(2)}, u32[]{:S(2)}) collective-permute-start(bf16[256,2048]{1,0:T(8,128)(2,1)} %get-tuple-element.119), channel_id=1, source_target_pairs={{0,1},{1,0},{2,3},{3,2},{4,5},{5,4},{6,7},{7,6},{8,9},{9,8},{10,11... | collective-permute-start | bytes 3145736 | tf_op jit(solution)/shard_map/ppermute | solution.py:687
  193.1 26.6 %collective-permute-start.12 = (bf16[256,2048]{1,0:T(8,128)(2,1)}, bf16[256,2048]{1,0:T(8,128)(2,1)S(1)}, u32[]{:S(2)}, u32[]{:S(2)}) collective-permute-start(bf16[256,2048]{1,0:T(8,128)(2,1)} %get-tuple-element.120), channel_id=1, source_target_pairs={{0,4},{1,5},{2,6},{3,7},{4,0},{5,1},{6,2},{7,3},{8,12},{9,13},{10,... | collective-permute-start | bytes 3145736 | tf_op jit(solution)/shard_map/ppermute | solution.py:687
  224.2 4.2 %collective-permute-start.13 = (bf16[1024,1024]{1,0:T(8,128)(2,1)S(1)}, bf16[1024,1024]{1,0:T(8,128)(2,1)S(1)}, u32[]{:S(2)}, u32[]{:S(2)}) collective-permute-start(bf16[1024,1024]{1,0:T(8,128)(2,1)S(1)} %copy-done.3), channel_id=1, source_target_pairs={{0,2},{2,0},{1,3},{3,1},{4,6},{6,4},{5,7},{7,5},{8,10},{10,8},{9,1... | collective-permute-start | bytes 6291464 | tf_op jit(solution)/shard_map/ppermute | solution.py:759
  224.2 14.6 %collective-permute-start.14 = (bf16[128,2048]{1,0:T(8,128)(2,1)}, bf16[128,2048]{1,0:T(8,128)(2,1)S(1)}, u32[]{:S(2)}, u32[]{:S(2)}) collective-permute-start(bf16[128,2048]{1,0:T(8,128)(2,1)} %get-tuple-element.132), channel_id=1, source_target_pairs={{0,4},{1,5},{2,6},{3,7},{4,0},{5,1},{6,2},{7,3},{8,12},{9,13},{10,... | collective-permute-start | bytes 1572872 | tf_op jit(solution)/shard_map/ppermute | solution.py:687
  224.4 14.7 %collective-permute-start.15 = (bf16[128,2048]{1,0:T(8,128)(2,1)}, bf16[128,2048]{1,0:T(8,128)(2,1)}, u32[]{:S(2)}, u32[]{:S(2)}) collective-permute-start(bf16[128,2048]{1,0:T(8,128)(2,1)} %get-tuple-element.133), channel_id=1, source_target_pairs={{0,1},{1,0},{2,3},{3,2},{4,5},{5,4},{6,7},{7,6},{8,9},{9,8},{10,11... | collective-permute-start | bytes 1572872 | tf_op jit(solution)/shard_map/ppermute | solution.py:687
  239.6 5.7 %copy-start.14 = (bf16[1024,1024]{1,0:T(8,128)(2,1)S(1)}, bf16[1024,1024]{1,0:T(8,128)(2,1)}, u32[]{:S(2)}) copy-start(bf16[1024,1024]{1,0:T(8,128)(2,1)} %get-tuple-element.134.refs_6_) | copy-start | bytes 6291460
  243.2 48.3 %collective-permute-start.16 = (bf16[1024,2048]{1,0:T(8,128)(2,1)}, bf16[1024,2048]{1,0:T(8,128)(2,1)}, u32[]{:S(2)}, u32[]{:S(2)}) collective-permute-start(bf16[1024,2048]{1,0:T(8,128)(2,1)} %get-tuple-element.135), channel_id=1, source_target_pairs={{2,0},{0,1},{3,2},{1,3},{6,4},{4,5},{7,6},{5,7},{10,8},{8,9},{11,1... | collective-permute-start | bytes 12582920 | tf_op jit(solution)/shard_map/ppermute | solution.py:671
  245.2 150.4 %reduce-scatter.5.cloned.1.call-start = ((), (), s32[]{:S(2)}) async-start(), calls=%async_computation.6 | async-start | bytes 4456448 | tf_op jit(solution)/shard_map/reduce_scatter | solution.py:864
  291.6 5.3 %copy-start.7 = (bf16[512,1024]{1,0:T(8,128)(2,1)S(1)}, bf16[512,1024]{1,0:T(8,128)(2,1)}, u32[]{:S(2)}) copy-start(bf16[512,1024]{1,0:T(8,128)(2,1)} %copy-done.6) | copy-start | bytes 3145732
  291.8 5.3 %copy-start.13 = (bf16[1024,1024]{1,0:T(8,128)(2,1)S(1)}, bf16[1024,1024]{1,0:T(8,128)(2,1)}, u32[]{:S(2)}) copy-start(bf16[1024,1024]{1,0:T(8,128)(2,1)} %get-tuple-element.116) | copy-start | bytes 6291460
  292.2 25.1 %collective-permute-start.18 = (bf16[256,2048]{1,0:T(8,128)(2,1)}, bf16[256,2048]{1,0:T(8,128)(2,1)S(1)}, u32[]{:S(2)}, u32[]{:S(2)}) collective-permute-start(bf16[256,2048]{1,0:T(8,128)(2,1)} %get-tuple-element.140.refs_2_), channel_id=1, source_target_pairs={{0,1},{1,0},{2,3},{3,2},{4,5},{5,4},{6,7},{7,6},{8,9},{9,8},{10,11... | collective-permute-start | bytes 3145736 | tf_op jit(solution)/shard_map/ppermute | solution.py:687
  294.8 22.6 %collective-permute-start.19 = (bf16[256,2048]{1,0:T(8,128)(2,1)}, bf16[256,2048]{1,0:T(8,128)(2,1)S(1)}, u32[]{:S(2)}, u32[]{:S(2)}) collective-permute-start(bf16[256,2048]{1,0:T(8,128)(2,1)} %get-tuple-element.143), channel_id=1, source_target_pairs={{0,4},{1,5},{2,6},{3,7},{4,0},{5,1},{6,2},{7,3},{8,12},{9,13},{10,... | collective-permute-start | bytes 3145736 | tf_op jit(solution)/shard_map/ppermute | solution.py:687
  296.8 25.0 %collective-permute-start.17 = (bf16[512,1024]{1,0:T(8,128)(2,1)}, bf16[512,1024]{1,0:T(8,128)(2,1)}, u32[]{:S(2)}, u32[]{:S(2)}) collective-permute-start(bf16[512,1024]{1,0:T(8,128)(2,1)} %constant_dynamic-slice_fusion.1), channel_id=1, source_target_pairs={{0,2},{2,0},{1,3},{3,1},{4,6},{6,4},{5,7},{7,5},{8,10},{10,8},{9,1... | collective-permute-start | bytes 3145736 | tf_op jit(solution)/shard_map/ppermute | solution.py:759
  298.1 26.3 %collective-permute-start.10 = (bf16[512,1024]{1,0:T(8,128)(2,1)}, bf16[512,1024]{1,0:T(8,128)(2,1)}, u32[]{:S(2)}, u32[]{:S(2)}) collective-permute-start(bf16[512,1024]{1,0:T(8,128)(2,1)} %constant_dynamic-slice_fusion), channel_id=1, source_target_pairs={{0,2},{2,0},{1,3},{3,1},{4,6},{6,4},{5,7},{7,5},{8,10},{10,8},{9,1... | collective-permute-start | bytes 3145736 | tf_op jit(solution)/shard_map/ppermute | solution.py:759
  324.3 5.6 %copy-start.32 = (bf16[128,2048]{1,0:T(8,128)(2,1)S(1)}, bf16[128,2048]{1,0:T(8,128)(2,1)}, u32[]{:S(2)}) copy-start(bf16[128,2048]{1,0:T(8,128)(2,1)} %get-tuple-element.154) | copy-start | bytes 1572868
  324.3 6.1 %copy-start.31 = (bf16[128,2048]{1,0:T(8,128)(2,1)S(1)}, bf16[128,2048]{1,0:T(8,128)(2,1)}, u32[]{:S(2)}) copy-start(bf16[128,2048]{1,0:T(8,128)(2,1)} %get-tuple-element.155) | copy-start | bytes 1572868
  324.3 26.4 %copy-start.16 = (f32[1024,1024]{1,0:T(8,128)S(1)}, f32[1024,1024]{1,0:T(8,128)}, u32[]{:S(2)}) copy-start(f32[1024,1024]{1,0:T(8,128)} %get-tuple-element.127) | copy-start | bytes 12582916
  324.3 6.4 %collective-permute-start.23 = (f32[8,2048]{1,0:T(8,128)S(1)}, f32[8,2048]{1,0:T(8,128)S(1)}, u32[]{:S(2)}, u32[]{:S(2)}) collective-permute-start(f32[8,2048]{1,0:T(8,128)S(1)} %reshape.116), channel_id=1, source_target_pairs={{0,2},{2,0},{1,3},{3,1},{4,6},{6,4},{5,7},{7,5},{8,10},{10,8},{9,1... | collective-permute-start | bytes 196616 | tf_op jit(solution)/shard_map/ppermute | solution.py:731
  328.2 26.2 %collective-permute-start.20 = (bf16[64,2048]{1,0:T(8,128)(2,1)}, bf16[64,2048]{1,0:T(8,128)(2,1)S(1)}, u32[]{:S(2)}, u32[]{:S(2)}) collective-permute-start(bf16[64,2048]{1,0:T(8,128)(2,1)} %reduce-scatter.3.cloned.1.call-done), channel_id=1, source_target_pairs={{2,0},{0,1},{3,2},{1,3},{6,4},{4,5},{7,6},{5,7},{10,8},{8,9},{11,1... | collective-permute-start | bytes 786440 | tf_op jit(solution)/shard_map/ppermute | solution.py:671
  329.9 24.5 %collective-permute-start.21 = (bf16[128,2048]{1,0:T(8,128)(2,1)S(1)}, bf16[128,2048]{1,0:T(8,128)(2,1)}, u32[]{:S(2)}, u32[]{:S(2)}) collective-permute-start(bf16[128,2048]{1,0:T(8,128)(2,1)S(1)} %copy-done.32), channel_id=1, source_target_pairs={{0,4},{1,5},{2,6},{3,7},{4,0},{5,1},{6,2},{7,3},{8,12},{9,13},{10,... | collective-permute-start | bytes 1572872 | tf_op jit(solution)/shard_map/ppermute | solution.py:687
  330.4 24.1 %collective-permute-start.22 = (bf16[128,2048]{1,0:T(8,128)(2,1)S(1)}, bf16[128,2048]{1,0:T(8,128)(2,1)}, u32[]{:S(2)}, u32[]{:S(2)}) collective-permute-start(bf16[128,2048]{1,0:T(8,128)(2,1)S(1)} %copy-done.31), channel_id=1, source_target_pairs={{0,1},{1,0},{2,3},{3,2},{4,5},{5,4},{6,7},{7,6},{8,9},{9,8},{10,11... | collective-permute-start | bytes 1572872 | tf_op jit(solution)/shard_map/ppermute | solution.py:687
  330.7 18.4 %collective-permute-start.24 = (f32[8,2048]{1,0:T(8,128)S(1)}, f32[8,2048]{1,0:T(8,128)S(1)}, u32[]{:S(2)}, u32[]{:S(2)}) collective-permute-start(f32[8,2048]{1,0:T(8,128)S(1)} %add.144), channel_id=1, source_target_pairs={{0,4},{1,5},{2,6},{3,7},{4,0},{5,1},{6,2},{7,3},{8,12},{9,13},{10,... | collective-permute-start | bytes 196616 | tf_op jit(solution)/shard_map/ppermute | solution.py:687
  349.1 4.7 %collective-permute-start.25 = (f32[8,2048]{1,0:T(8,128)S(1)}, f32[8,2048]{1,0:T(8,128)S(1)}, u32[]{:S(2)}, u32[]{:S(2)}) collective-permute-start(f32[8,2048]{1,0:T(8,128)S(1)} %add.145), channel_id=1, source_target_pairs={{0,1},{1,0},{2,3},{3,2},{4,5},{5,4},{6,7},{7,6},{8,9},{9,8},{10,11... | collective-permute-start | bytes 196616 | tf_op jit(solution)/shard_map/ppermute | solution.py:687
  358.7 5.4 %copy-start.33 = (bf16[80,2048]{1,0:T(8,128)(2,1)S(1)}, bf16[80,2048]{1,0:T(8,128)(2,1)}, u32[]{:S(2)}) copy-start(bf16[80,2048]{1,0:T(8,128)(2,1)} %get-tuple-element.170) | copy-start | bytes 983044
  358.9 35.2 %collective-permute-start.26 = (bf16[1024,1024]{1,0:T(8,128)(2,1)S(1)}, bf16[1024,1024]{1,0:T(8,128)(2,1)S(1)}, u32[]{:S(2)}, u32[]{:S(2)}) collective-permute-start(bf16[1024,1024]{1,0:T(8,128)(2,1)S(1)} %pad_maximum_fusion), channel_id=1, source_target_pairs={{2,0},{0,1},{3,2},{1,3},{6,4},{4,5},{7,6},{5,7},{10,8},{8,9},{11,1... | collective-permute-start | bytes 6291464 | tf_op jit(solution)/shard_map/ppermute | solution.py:671
  360.0 37.6 %collective-permute-start.27 = (bf16[80,2048]{1,0:T(8,128)(2,1)S(1)}, bf16[80,2048]{1,0:T(8,128)(2,1)S(1)}, u32[]{:S(2)}, u32[]{:S(2)}) collective-permute-start(bf16[80,2048]{1,0:T(8,128)(2,1)S(1)} %copy-done.36), channel_id=1, source_target_pairs={{2,0},{0,1},{3,2},{1,3},{6,4},{4,5},{7,6},{5,7},{10,8},{8,9},{11,1... | collective-permute-start | bytes 983048 | tf_op jit(solution)/shard_map/ppermute | solution.py:679
  360.8 36.9 %collective-permute-start.28 = (bf16[80,2048]{1,0:T(8,128)(2,1)S(1)}, bf16[80,2048]{1,0:T(8,128)(2,1)S(1)}, u32[]{:S(2)}, u32[]{:S(2)}) collective-permute-start(bf16[80,2048]{1,0:T(8,128)(2,1)S(1)} %copy-done.35), channel_id=1, source_target_pairs={{10,0},{8,1},{11,2},{9,3},{14,4},{12,5},{15,6},{13,7},{2,8},{0,9},... | collective-permute-start | bytes 983048 | tf_op jit(solution)/shard_map/ppermute | solution.py:679
  361.8 35.9 %collective-permute-start.29 = (bf16[80,2048]{1,0:T(8,128)(2,1)S(1)}, bf16[80,2048]{1,0:T(8,128)(2,1)S(1)}, u32[]{:S(2)}, u32[]{:S(2)}) collective-permute-start(bf16[80,2048]{1,0:T(8,128)(2,1)S(1)} %copy-done.34), channel_id=1, source_target_pairs={{18,0},{16,1},{19,2},{17,3},{22,4},{20,5},{23,6},{21,7},{26,8},{24... | collective-permute-start | bytes 983048 | tf_op jit(solution)/shard_map/ppermute | solution.py:679
  364.1 33.6 %collective-permute-start.30 = (bf16[80,2048]{1,0:T(8,128)(2,1)S(1)}, bf16[80,2048]{1,0:T(8,128)(2,1)S(1)}, u32[]{:S(2)}, u32[]{:S(2)}) collective-permute-start(bf16[80,2048]{1,0:T(8,128)(2,1)S(1)} %copy-done.33), channel_id=1, source_target_pairs={{26,0},{24,1},{27,2},{25,3},{30,4},{28,5},{31,6},{29,7},{18,8},{16... | collective-permute-start | bytes 983048 | tf_op jit(solution)/shard_map/ppermute | solution.py:679
  (25 other events, 52.4 us)
Sparse Core Ops, SparseCore 0:
  10.8 53.2 all-gather.3
  66.8 49.0 all-gather.5
  118.6 71.9 all-gather.7
  245.3 26.9 reduce-scatter.2
  291.7 86.9 reduce-scatter.4

commit v7 on v6

--- a/solution.py
+++ b/solution.py
@@ -833,42 +833,30 @@
 
     out_part, gn_part, first_grads, bias_first = mlp(
         order, normed_two, grad_rows, normed_two_t, grad_rows_t, full_first,
-        bias_up[:half_units], (), True,
-    )
+        bias_up[:half_units], (), False,
+    )
+    first_grads = swap(first_grads[0], inverse=True)
     full_second, gn_part = lax.optimization_barrier((full_second, gn_part))
     out_part, gn_part, second_grads, bias_second = mlp(
         order, normed_two, grad_rows, normed_two_t, grad_rows_t, full_second,
-        bias_up[half_units:], (out_part, gn_part), False,
-    )
-    first_state = scatter_near(first_grads, gn_part)
-    gn_part, second_grads, first_state = lax.optimization_barrier(
-        (gn_part, second_grads[0], first_state)
+        bias_up[half_units:], (out_part, gn_part), True,
     )
     own_output = (own(hidden) + tp_scatter(out_part) + b_down).astype(BF16)
 
     grad_hidden, grad_attended, grad_attended_t, sums_two = norm_back_rows(
         hidden, grad_rows, tp_terms(gn_part), ln2_gain
     )
-    first_sums = z_sums(first_state, grad_attended)
-    second_grads, first_sums = lax.optimization_barrier((second_grads, first_sums))
-    second_grads = swap(second_grads, inverse=True)
+    first_grads, grad_attended = lax.optimization_barrier((first_grads, grad_attended))
+    first_mlp = lax.psum_scatter(first_grads, ("z", "y", "c"), scatter_dimension=0, tiled=True)
     grad_mixed = dot_nn(grad_attended, full_out).astype(BF16)
-    first_mlp = lax.psum_scatter(first_sums, "z", scatter_dimension=0, tiled=True)
-    grads = attn_backward(segments, qkv, mixed, lse, grad_mixed, head_width, first_sums)
+    grads = attn_backward(segments, qkv, mixed, lse, grad_mixed, head_width, grad_mixed)
     block_rows = w_query.shape[0]
-    pieces = weight_grads(order, normed_t, grads, grad_attended_t, mixed, grads)
-    grad_normed_part = qkv_back(grads, full_attn, pieces[0])
-    second_grads, first_mlp, grad_normed_part = lax.optimization_barrier(
-        (second_grads, first_mlp, grad_normed_part)
-    )
-    second_mlp = lax.psum_scatter(second_grads, ("z", "y", "c"), scatter_dimension=0, tiled=True)
-    state = scatter_near(pieces, grad_normed_part)
-    grad_normed_own, grad_normed_other = tp_scatter_terms(grad_normed_part)
-    first_mlp, grad_normed_other, state = lax.optimization_barrier(
-        (first_mlp, grad_normed_other, state)
-    )
-    first_mlp = swap(first_mlp, inverse=True)
-    grad_normed = grad_normed_own.astype(F32) + grad_normed_other.astype(F32)
+    second_state = scatter_near(second_grads, grads)
+    grad_normed_part = qkv_back(grads, full_attn, second_state[3])
+    pieces = weight_grads(order, normed_t, grads, grad_attended_t, mixed, grad_normed_part)
+    second_sums = z_sums(second_state, pieces[0])
+    second_mlp = lax.psum_scatter(second_sums, "z", scatter_dimension=0, tiled=True)
+    grad_normed = tp_scatter(grad_normed_part)
     own_scaled, own_inverse = normalize(own_input.astype(F32))
     grad_own = own(grad_hidden) + norm_back(grad_normed, own_scaled, own_inverse, ln1_gain)
     grad_own = grad_own.astype(BF16)
@@ -893,8 +881,12 @@
     filled = sums.shape[0]
     sums = jnp.pad(sums, (0, -filled % (8 * columns))).reshape(-1, columns)
     sums = near_sum(sums)
-    last_sums = far_sums(state, [sums], first_mlp)
-    own_output, grad_own, *last_sums = lax.optimization_barrier((own_output, grad_own, *last_sums))
+    state = scatter_near(pieces, sums)
+    last_sums = far_sums(state, [sums], None)
+    own_output, grad_own, second_mlp, *last_sums = lax.optimization_barrier(
+        (own_output, grad_own, second_mlp, *last_sums)
+    )
+    second_mlp = swap(second_mlp, inverse=True)
     leaving = swap(jnp.concatenate([own_output, grad_own], axis=0), inverse=True)
     output, grad_input = leaving[:own_rows], leaving[own_rows:]
     shard = jax.ShapeDtypeStruct((block_rows, unit_width), F32)

time: 419 us -> 455 us (1.086)
  waiting for transfers between devices: 167 us -> 204 us
    reduce_scatter x2, waiting for transfers between devices: 0.01 us -> 23.1 us  [the longest x1 23.1 us: per_device(): lax.psum_scatter(first_grads, ('z', 'y', 'c'), scatter_dimension=0, tiled...]
    ppermute x9, waiting for transfers between devices: 124 us -> 144 us  [swap(): return lax.ppermute(values, SWAP, pairs)]
    ppermute x11, waiting for transfers between devices: 39.8 us -> 32.9 us  [hop(): return lax.ppermute(values, ('z', 'y', 'c', 'h'), pairs)]
  transfers between devices with their start and end apart: 36 -> 36, of which waited for: 13 -> 16; matrix products, arithmetic and copies ran while one was open for 9% -> 9% of each run, Pallas kernels for 36% -> 33%
where the time goes in v7:
time: 455 us; the launch traced here: 447 us
  waiting for transfers between devices  204 us (45%)
  Pallas kernels  155 us (34%)
  starting transfers between devices  23.7 us (5%)
  other arithmetic  22.9 us (5%)
  local copies, waits for them, and re-layouts  18.1 us (4%)
  between operations  14.6 us (3%)
  matrix products  8.29 us (2%)
    ppermute x9, waiting for transfers between devices, swap(): return lax.ppermute(values, SWAP, pairs)  144 us
    pallas_call x2, Pallas kernels, mlp(): pl.pallas_call(functools.partial(mlp_kernel, block=min(ROWS, length), wit...  48.8 us
    ppermute x11, waiting for transfers between devices, hop(): return lax.ppermute(values, ('z', 'y', 'c', 'h'), pairs)  32.9 us
    pallas_call x1, Pallas kernels, attn_backward(): pl.pallas_call(without(functools.partial(attn_backward_kernel, block=bloc...  24.3 us
    reduce_scatter x1, waiting for transfers between devices, per_device(): lax.psum_scatter(first_grads, ('z', 'y', 'c'), scatter_dimension=0, tiled...  23.1 us
    pallas_call x1, Pallas kernels, attn_forward(): pl.pallas_call(functools.partial(attn_forward_kernel, block=block), grid=...  16.4 us
    pallas_call x6, Pallas kernels, sums_call(): pl.pallas_call(body, in_specs=([pl.BlockSpec(memory_space=pl.ANY)] if aft...  15.5 us
    pallas_call x2, Pallas kernels, norm_rows(): pl.pallas_call(functools.partial(norm_kernel, residual=residual), grid=(l...  12.9 us
  transfers between devices with their start and end apart: 36, of which 16 were waited for; matrix products, arithmetic and copies ran while one was open for 9% of the time, Pallas kernels for 33%

profile of v7, /device:TPU:0, one launch (start us, length us, event | category | flops | bytes accessed | tf_op | source)
XLA Modules:
  0.0 447.1 jit_solution(5852382458435884392)
XLA Ops:
  9.0 1.8 mlp_shards.1
  11.3 2.0 collective-permute-start.3
  13.4 13.4 %collective-permute-done = bf16[512,1024]{1,0:T(8,128)(2,1)S(1)} collective-permute-done((bf16[512,1024]{1,0:T(8,128)(2,1)}, bf16[512,1024]{1,0:T(8,128)(2,1)S(1)}, u32[]{:S(2)}, u32[]{:S(2)}) %collective-permute-start) | collective-permute-done | bytes 1048608 | tf_op jit(solution)/shard_map/ppermute | solution.py:671
  26.8 11.2 %collective-permute-done.3 = bf16[512,1024]{1,0:T(8,128)(2,1)S(1)} collective-permute-done((bf16[512,1024]{1,0:T(8,128)(2,1)}, bf16[512,1024]{1,0:T(8,128)(2,1)S(1)}, u32[]{:S(2)}, u32[]{:S(2)}) %collective-permute-start.3) | collective-permute-done | bytes 1048608 | tf_op jit(solution)/shard_map/ppermute | solution.py:671
  38.6 6.1 %collective-permute-done.5 = bf16[64,2048]{1,0:T(8,128)(2,1)S(1)} collective-permute-done((bf16[64,2048]{1,0:T(8,128)(2,1)}, bf16[64,2048]{1,0:T(8,128)(2,1)S(1)}, u32[]{:S(2)}, u32[]{:S(2)}) %collective-permute-start.5) | collective-permute-done | bytes 262176 | tf_op jit(solution)/shard_map/ppermute | solution.py:671
  44.7 6.6 %collective-permute-done.6 = bf16[64,2048]{1,0:T(8,128)(2,1)} collective-permute-done((bf16[64,2048]{1,0:T(8,128)(2,1)S(1)}, bf16[64,2048]{1,0:T(8,128)(2,1)}, u32[]{:S(2)}, u32[]{:S(2)}) %collective-permute-start.6) | collective-permute-done | bytes 262176 | tf_op jit(solution)/shard_map/ppermute | solution.py:687
  51.3 2.0 maximum_select_fusion.2
  53.3 2.3 maximum_select_fusion.refs_0_
  55.6 3.3 maximum_select_fusion.1.g_ref
  58.9 5.5 %norm_one.1 = (bf16[1024,1024]{1,0:T(8,128)(2,1)}, bf16[1024,1024]{1,0:T(8,128)(2,1)}) custom-call(bf16[1024,1024]{1,0:T(8,128)(2,1)} %maximum_select_fusion.refs_0_, f32[1,1024]{1,0:T(1,128)} %bitcast.39, f32[1,1024]{1,0:T(1,128)} %bitcast.46), custom_call_target="tpu_custom_call" | custom-call | flops 20971520 | bytes 14680064 | tf_op jit(solution)/shard_map/norm_one/pallas_call | solution.py:276
  65.4 47.9 %collective-permute-done.7.w_ref.refs_1_ = bf16[1024,2048]{1,0:T(8,128)(2,1)} collective-permute-done((bf16[1024,2048]{1,0:T(8,128)(2,1)}, bf16[1024,2048]{1,0:T(8,128)(2,1)}, u32[]{:S(2)}, u32[]{:S(2)}) %collective-permute-start.7) | collective-permute-done | bytes 4194336 | tf_op jit(solution)/shard_map/ppermute | solution.py:671
  113.3 7.2 %qkv_project.1.q_ref.k_ref.v_ref.refs_2_.refs_3_.refs_4_ = bf16[1024,1536]{1,0:T(8,128)(2,1)} custom-call(bf16[1024,1024]{1,0:T(8,128)(2,1)} %get-tuple-element.85.n_ref, f32[1,1536]{1,0:T(1,128)} %reshape.108.b_ref, bf16[1024,2048]{1,0:T(8,128)(2,1)} %collective-permute-done.7.w_ref.refs_1_), custom_call_target="tpu_custom_call" | custom-call | flops 3221225472 | bytes 8388608 | tf_op jit(solution)/shard_map/qkv_project/pallas_call | solution.py:457
  121.6 16.4 %attn_forward.1 = (bf16[1024,512]{1,0:T(8,128)(2,1)}, f32[4,8,1024]{2,1,0:T(8,128)}) custom-call(s32[1024,1]{1,0:T(8,128)} %copy.37.seg_col.refs_0_, s32[1,1024]{1,0:T(1,128)} %bitcast.41, bf16[1024,1536]{1,0:T(8,128)(2,1)} %qkv_project.1.q_ref.k_ref.v_ref.refs_2_.refs_3_.refs_4_, bf16[1024,1536]{1,0:T(8,128)(2,1)} %qkv_project.1.q_ref.k_ref.v_ref.refs_2_.refs_3_.refs_4_, ...), custom_call_target="tpu_custom_call" | custom-call | flops 2147483648 | bytes 4194304 | tf_op jit(solution)/shard_map/attn_forward/pallas_call | solution.py:157
  137.9 4.2 convolution_convert_fusion.refs_1_
  143.5 2.5 copy.39.gt_ref
  146.6 7.4 %norm_two.1 = (bf16[1024,1024]{1,0:T(8,128)(2,1)}, bf16[1024,1024]{1,0:T(8,128)(2,1)}, f32[1024,1024]{1,0:T(8,128)}) custom-call(bf16[1024,1024]{1,0:T(8,128)(2,1)} %maximum_select_fusion.refs_0_, bf16[1024,1024]{1,0:T(8,128)(2,1)} %convolution_convert_fusion.refs_1_, bf16[1024,1024]{1,0:T(8,128)(2,1)} %collective-permute-done.8.refs_2_, ...), custom_call_target="tpu_custom_call" | custom-call | flops 20971520 | bytes 14680064 | tf_op jit(solution)/shard_map/norm_two/pallas_call | solution.py:276
  154.0 15.3 %collective-permute-done.9.w_ref = bf16[1024,2048]{1,0:T(8,128)(2,1)} collective-permute-done((bf16[1024,2048]{1,0:T(8,128)(2,1)}, bf16[1024,2048]{1,0:T(8,128)(2,1)}, u32[]{:S(2)}, u32[]{:S(2)}) %collective-permute-start.9) | collective-permute-done | bytes 4194336 | tf_op jit(solution)/shard_map/ppermute | solution.py:671
  169.3 23.8 %mlp_first.1 = (bf16[1024,1024]{1,0:T(8,128)(2,1)}, bf16[1024,1024]{1,0:T(8,128)(2,1)}, bf16[1024,2048]{1,0:T(8,128)(2,1)}, f32[1,1024]{1,0:T(1,128)}) custom-call(s32[16]{0:T(128)} %stack.67.order, bf16[1024,1024]{1,0:T(8,128)(2,1)} %get-tuple-element.90.n_ref, bf16[1024,1024]{1,0:T(8,128)(2,1)} %copy-done, bf16[1024,1024]{1,0:T(8,128)(2,1)} %get-tuple-element.92.nt_ref, ...), custom_call_target="tpu_custom_call" | custom-call | flops 12884901888 | bytes 20971520 | tf_op jit(solution)/shard_map/mlp_first/pallas_call | solution.py:403
  193.2 25.0 %mlp_second.1 = (bf16[1024,1024]{1,0:T(8,128)(2,1)}, bf16[1024,1024]{1,0:T(8,128)(2,1)}, bf16[256,2048]{1,0:T(8,128)(2,1)}, bf16[256,2048]{1,0:T(8,128)(2,1)}, b...) custom-call(s32[16]{0:T(128)} %stack.67.order, ...), custom_call_target="tpu_custom_call" | custom-call | flops 12884901888 | bytes 20971520 | tf_op jit(solution)/shard_map/mlp_second/pallas_call | solution.py:403
  218.7 2.0 collective-permute-start.14
  220.7 2.2 collective-permute-done.11.other_ref
  222.8 9.1 %norm_two_back.1 = (f32[1024,1024]{1,0:T(8,128)}, bf16[1024,1024]{1,0:T(8,128)(2,1)}, bf16[1024,1024]{1,0:T(8,128)(2,1)}, f32[8,1024]{1,0:T(8,128)}) custom-call(f32[1024,1024]{1,0:T(8,128)} %get-tuple-element.89.hidden_ref, bf16[1024,1024]{1,0:T(8,128)(2,1)} %copy-done, bf16[1024,1024]{1,0:T(8,128)(2,1)} %get-tuple-element.101.own_ref, ...), custom_call_target="tpu_custom_call" | custom-call | flops 31457280 | bytes 16777216 | tf_op jit(solution)/shard_map/norm_two_back/pallas_call | solution.py:316
  231.9 18.8 %collective-permute-done.12 = bf16[1024,2048]{1,0:T(8,128)(2,1)} collective-permute-done((bf16[1024,2048]{1,0:T(8,128)(2,1)}, bf16[1024,2048]{1,0:T(8,128)(2,1)}, u32[]{:S(2)}, u32[]{:S(2)}) %collective-permute-start.12) | collective-permute-done | bytes 4194336 | tf_op jit(solution)/shard_map/ppermute | solution.py:671
  250.7 4.1 convolution_convert_fusion.1.refs_7_.refs_8_
  254.8 24.3 %attn_backward.1.refs_0_.grads_ref = bf16[3,1024,512]{2,1,0:T(8,128)(2,1)} custom-call(s32[1024,1]{1,0:T(8,128)} %copy.37.seg_col.refs_0_, s32[1,1024]{1,0:T(1,128)} %bitcast.42, bf16[1024,1536]{1,0:T(8,128)(2,1)} %qkv_project.1.q_ref.k_ref.v_ref.refs_2_.refs_3_.refs_4_, bf16[1024,1536]{1,0:T(8,128)(2,1)} %qkv_project.1.q_ref.k_ref.v_ref.refs_2_.refs_3_.refs_4_, ...), custom_call_target="tpu_custom_call" | custom-call | flops 5368709120 | bytes 8388608 | tf_op jit(solution)/shard_map/attn_backward/pallas_call | solution.py:186
  280.5 2.9 sums_one.2
  283.4 2.5 collective-permute-start.17
  285.9 1.9 collective-permute-start.16
  287.8 7.4 %qkv_back.1.order_only = bf16[1024,1024]{1,0:T(8,128)(2,1)} custom-call(bf16[3,1024,512]{2,1,0:T(8,128)(2,1)} %attn_backward.1.refs_0_.grads_ref, bf16[1024,2048]{1,0:T(8,128)(2,1)} %collective-permute-done.7.w_ref.refs_1_, bf16[128,2048]{1,0:T(8,128)(2,1)} %get-tuple-element.111.refs_2_), custom_call_target="tpu_custom_call" | custom-call | flops 3221225472 | bytes 8388608 | tf_op jit(solution)/shard_map/qkv_back/pallas_call | solution.py:543
  295.2 10.2 %weight_grads.1 = (bf16[256,2048]{1,0:T(8,128)(2,1)}, bf16[256,2048]{1,0:T(8,128)(2,1)}, bf16[128,2048]{1,0:T(8,128)(2,1)}, bf16[128,2048]{1,0:T(8,128)(2,1)}, bf16[256,2048]{1,0:T(8,128)(2,1)}) custom-call(s32[16]{0:T(128)} %stack.67.order, bf16[1024,1024]{1,0:T(8,128)(2,1)} %get-tuple-element.114.nt_ref, ...), custom_call_target="tpu_custom_call" | custom-call | flops 4294967296 | bytes 12582912 | tf_op jit(solution)/shard_map/weight_grads/pallas_call | solution.py:502
  306.3 3.5 sums_two_z.1
  315.1 1.9 convert_reduce_fusion.2
  317.8 2.3 fusion.10
  321.6 2.0 collective-permute-start.21
  323.6 18.2 %collective-permute-done.21 = f32[8,2048]{1,0:T(8,128)S(1)} collective-permute-done((f32[8,2048]{1,0:T(8,128)S(1)}, f32[8,2048]{1,0:T(8,128)S(1)}, u32[]{:S(2)}, u32[]{:S(2)}) %collective-permute-start.21) | collective-permute-done | bytes 65568 | tf_op jit(solution)/shard_map/ppermute | solution.py:687
  341.8 1.7 collective-permute-start.22
  343.5 3.9 add_convert_fusion
  348.0 3.1 sums_one.3
  351.8 3.9 fusion.9
  355.7 7.9 %collective-permute-done.23.from_y2 = bf16[128,2048]{1,0:T(8,128)(2,1)S(1)} collective-permute-done((bf16[128,2048]{1,0:T(8,128)(2,1)}, bf16[128,2048]{1,0:T(8,128)(2,1)S(1)}, u32[]{:S(2)}, u32[]{:S(2)}) %collective-permute-start.23) | collective-permute-done | bytes 524320 | tf_op jit(solution)/shard_map/ppermute | solution.py:687
  364.6 3.6 sums_two.1
  370.9 3.1 collective-permute-start.29
  374.4 25.3 %collective-permute-done.25 = bf16[1024,1024]{1,0:T(8,128)(2,1)S(1)} collective-permute-done((bf16[1024,1024]{1,0:T(8,128)(2,1)S(1)}, bf16[1024,1024]{1,0:T(8,128)(2,1)S(1)}, u32[]{:S(2)}, u32[]{:S(2)}) %collective-permute-start.25) | collective-permute-done | bytes 2097184 | tf_op jit(solution)/shard_map/ppermute | solution.py:671
  399.7 2.5 collective-permute-start.26
  403.6 5.5 %collective-permute-done.26.second_ref = bf16[64,2048]{1,0:T(8,128)(2,1)S(1)} collective-permute-done((bf16[64,2048]{1,0:T(8,128)(2,1)S(1)}, bf16[64,2048]{1,0:T(8,128)(2,1)S(1)}, u32[]{:S(2)}, u32[]{:S(2)}) %collective-permute-start.26) | collective-permute-done | bytes 262176 | tf_op jit(solution)/shard_map/ppermute | solution.py:671
  409.1 23.1 %reduce-scatter.5.cloned.1.call-done.first_ref = bf16[64,2048]{1,0:T(8,128)(2,1)} async-done(((bf16[1024,2048]{1,0:T(8,128)(2,1)}), bf16[64,2048]{1,0:T(8,128)(2,1)}) %reduce-scatter.5.cloned.1.call-update) | async-done | bytes 262160 | tf_op jit(solution)/shard_map/reduce_scatter | solution.py:850
  432.2 2.1 units_last.1
  435.3 2.1 sums_last.1
  (163 shorter events, 27.7 us)
Async XLA Ops:
  7.2 57.3 %all-gather.4.cloned.1.call-start = ((), (), s32[]{:S(2)}) async-start(), calls=%async_computation.2 | async-start | bytes 4456448 | tf_op jit(solution)/shard_map/all_gather | solution.py:801
  8.9 111.6 %all-gather.6.cloned.1.call-start = ((), (), s32[]{:S(2)}) async-start(), calls=%async_computation.3 | async-start | bytes 4456448 | tf_op jit(solution)/shard_map/all_gather | solution.py:804
  10.8 182.4 %all-gather.8.cloned.1.call-start = ((), (), s32[]{:S(2)}) async-start(), calls=%async_computation.4 | async-start | bytes 4718592 | tf_op jit(solution)/shard_map/all_gather | solution.py:823
  10.9 15.9 %collective-permute-start = (bf16[512,1024]{1,0:T(8,128)(2,1)}, bf16[512,1024]{1,0:T(8,128)(2,1)S(1)}, u32[]{:S(2)}, u32[]{:S(2)}) collective-permute-start(bf16[512,1024]{1,0:T(8,128)(2,1)} %param.18), channel_id=1, source_target_pairs={{0,2},{1,0},{2,3},{3,1},{4,6},{5,4},{6,7},{7,5},{8,10},{9,8},{10,1... | collective-permute-start | bytes 3145736 | tf_op jit(solution)/shard_map/ppermute | solution.py:671
  11.3 26.7 %collective-permute-start.3 = (bf16[512,1024]{1,0:T(8,128)(2,1)}, bf16[512,1024]{1,0:T(8,128)(2,1)S(1)}, u32[]{:S(2)}, u32[]{:S(2)}) collective-permute-start(bf16[512,1024]{1,0:T(8,128)(2,1)} %param.35), channel_id=1, source_target_pairs={{0,2},{1,0},{2,3},{3,1},{4,6},{5,4},{6,7},{7,5},{8,10},{9,8},{10,1... | collective-permute-start | bytes 3145736 | tf_op jit(solution)/shard_map/ppermute | solution.py:671
  26.8 26.4 %collective-permute-start.1 = (bf16[512,1024]{1,0:T(8,128)(2,1)S(1)}, bf16[512,1024]{1,0:T(8,128)(2,1)S(1)}, u32[]{:S(2)}, u32[]{:S(2)}) collective-permute-start(bf16[512,1024]{1,0:T(8,128)(2,1)S(1)} %collective-permute-done), channel_id=1, source_target_pairs={{0,2},{2,0},{1,3},{3,1},{4,6},{6,4},{5,7},{7,5},{8,10},{10,8},{9,1... | collective-permute-start | bytes 3145736 | tf_op jit(solution)/shard_map/ppermute | solution.py:759
  38.1 17.5 %copy-start.2 = (bf16[512,1024]{1,0:T(8,128)(2,1)}, bf16[512,1024]{1,0:T(8,128)(2,1)S(1)}, u32[]{:S(2)}) copy-start(bf16[512,1024]{1,0:T(8,128)(2,1)S(1)} %collective-permute-done.3) | copy-start | bytes 3145732
  38.1 17.5 %collective-permute-start.4 = (bf16[512,1024]{1,0:T(8,128)(2,1)S(1)}, bf16[512,1024]{1,0:T(8,128)(2,1)}, u32[]{:S(2)}, u32[]{:S(2)}) collective-permute-start(bf16[512,1024]{1,0:T(8,128)(2,1)S(1)} %collective-permute-done.3), channel_id=1, source_target_pairs={{0,2},{2,0},{1,3},{3,1},{4,6},{6,4},{5,7},{7,5},{8,10},{10,8},{9,1... | collective-permute-start | bytes 3145736 | tf_op jit(solution)/shard_map/ppermute | solution.py:759
  38.1 6.6 %collective-permute-start.5 = (bf16[64,2048]{1,0:T(8,128)(2,1)}, bf16[64,2048]{1,0:T(8,128)(2,1)S(1)}, u32[]{:S(2)}, u32[]{:S(2)}) collective-permute-start(bf16[64,2048]{1,0:T(8,128)(2,1)} %get-tuple-element.82), channel_id=1, source_target_pairs={{0,2},{1,0},{2,3},{3,1},{4,6},{5,4},{6,7},{7,5},{8,10},{9,8},{10,1... | collective-permute-start | bytes 786440 | tf_op jit(solution)/shard_map/ppermute | solution.py:671
  44.7 6.6 %collective-permute-start.6 = (bf16[64,2048]{1,0:T(8,128)(2,1)S(1)}, bf16[64,2048]{1,0:T(8,128)(2,1)}, u32[]{:S(2)}, u32[]{:S(2)}) collective-permute-start(bf16[64,2048]{1,0:T(8,128)(2,1)S(1)} %collective-permute-done.5), channel_id=1, source_target_pairs={{0,1},{1,0},{2,3},{3,2},{4,5},{5,4},{6,7},{7,6},{8,9},{9,8},{10,11... | collective-permute-start | bytes 786440 | tf_op jit(solution)/shard_map/ppermute | solution.py:687
  44.7 19.8 %collective-permute-start.2 = (s32[1024]{0:T(1024)}, s32[1024]{0:T(1024)S(1)}, u32[]{:S(2)}, u32[]{:S(2)}) collective-permute-start(s32[1024]{0:T(1024)} %param.19), channel_id=1, source_target_pairs={{0,2},{1,0},{2,3},{3,1},{4,6},{5,4},{6,7},{7,5},{8,10},{9,8},{10,1... | collective-permute-start | bytes 12296 | tf_op jit(solution)/shard_map/ppermute | solution.py:671
  58.9 84.6 %copy-start = (bf16[1024,1024]{1,0:T(8,128)(2,1)}, bf16[1024,1024]{1,0:T(8,128)(2,1)S(1)}, u32[]{:S(2)}) copy-start(bf16[1024,1024]{1,0:T(8,128)(2,1)S(1)} %maximum_select_fusion.1.g_ref) | copy-start | bytes 6291460
  58.9 5.7 %copy-start.25 = (f32[1024]{0:T(1024)S(1)}, f32[1024]{0:T(1024)}, u32[]{:S(2)}) copy-start(f32[1024]{0:T(1024)} %param.25) | copy-start | bytes 12292
  58.9 5.8 %copy-start.26 = (f32[1024]{0:T(1024)S(1)}, f32[1024]{0:T(1024)}, u32[]{:S(2)}) copy-start(f32[1024]{0:T(1024)} %param.26) | copy-start | bytes 12292
  64.4 56.1 %copy-start.19 = (s32[1024]{0:T(1024)}, s32[1024]{0:T(1024)S(1)}, u32[]{:S(2)}) copy-start(s32[1024]{0:T(1024)S(1)} %collective-permute-done.2) | copy-start | bytes 12292
  64.5 48.8 %collective-permute-start.7 = (bf16[1024,2048]{1,0:T(8,128)(2,1)}, bf16[1024,2048]{1,0:T(8,128)(2,1)}, u32[]{:S(2)}, u32[]{:S(2)}) collective-permute-start(bf16[1024,2048]{1,0:T(8,128)(2,1)} %all-gather.4.cloned.1.call-done), channel_id=1, source_target_pairs={{0,2},{1,0},{2,3},{3,1},{4,6},{5,4},{6,7},{7,5},{8,10},{9,8},{10,1... | collective-permute-start | bytes 12582920 | tf_op jit(solution)/shard_map/ppermute | solution.py:671
  64.5 303.6 %reduce-scatter.3.cloned.1.call-start = ((), (), s32[]{:S(2)}) async-start(), calls=%async_computation.5 | async-start | bytes 1310720 | tf_op jit(solution)/shard_map/reduce_scatter | solution.py:858
  120.5 48.8 %collective-permute-start.9 = (bf16[1024,2048]{1,0:T(8,128)(2,1)}, bf16[1024,2048]{1,0:T(8,128)(2,1)}, u32[]{:S(2)}, u32[]{:S(2)}) collective-permute-start(bf16[1024,2048]{1,0:T(8,128)(2,1)} %all-gather.6.cloned.1.call-done), channel_id=1, source_target_pairs={{0,2},{1,0},{2,3},{3,1},{4,6},{5,4},{6,7},{7,5},{8,10},{9,8},{10,1... | collective-permute-start | bytes 12582920 | tf_op jit(solution)/shard_map/ppermute | solution.py:671
  137.9 4.9 %copy-start.22 = (f32[4096]{0:T(1024)S(1)}, f32[4096]{0:T(1024)}, u32[]{:S(2)}) copy-start(f32[4096]{0:T(1024)} %param.32) | copy-start | bytes 49156
  142.1 4.5 %collective-permute-start.8 = (bf16[1024,1024]{1,0:T(8,128)(2,1)}, bf16[1024,1024]{1,0:T(8,128)(2,1)}, u32[]{:S(2)}, u32[]{:S(2)}) collective-permute-start(bf16[1024,1024]{1,0:T(8,128)(2,1)} %convolution_convert_fusion.refs_1_), channel_id=1, source_target_pairs={{0,2},{2,0},{1,3},{3,1},{4,6},{6,4},{5,7},{7,5},{8,10},{10,8},{9,1... | collective-permute-start | bytes 6291464 | tf_op jit(solution)/shard_map/ppermute | solution.py:759
  193.2 57.6 %collective-permute-start.12 = (bf16[1024,2048]{1,0:T(8,128)(2,1)}, bf16[1024,2048]{1,0:T(8,128)(2,1)}, u32[]{:S(2)}, u32[]{:S(2)}) collective-permute-start(bf16[1024,2048]{1,0:T(8,128)(2,1)} %get-tuple-element.104), channel_id=1, source_target_pairs={{2,0},{0,1},{3,2},{1,3},{6,4},{4,5},{7,6},{5,7},{10,8},{8,9},{11,1... | collective-permute-start | bytes 12582920 | tf_op jit(solution)/shard_map/ppermute | solution.py:671
  218.2 4.7 %collective-permute-start.11 = (bf16[1024,1024]{1,0:T(8,128)(2,1)}, bf16[1024,1024]{1,0:T(8,128)(2,1)}, u32[]{:S(2)}, u32[]{:S(2)}) collective-permute-start(bf16[1024,1024]{1,0:T(8,128)(2,1)} %get-tuple-element.101.own_ref), channel_id=1, source_target_pairs={{0,2},{2,0},{1,3},{3,1},{4,6},{6,4},{5,7},{7,5},{8,10},{10,8},{9,1... | collective-permute-start | bytes 6291464 | tf_op jit(solution)/shard_map/ppermute | solution.py:759
  218.7 60.4 %collective-permute-start.13 = (bf16[256,2048]{1,0:T(8,128)(2,1)}, bf16[256,2048]{1,0:T(8,128)(2,1)S(1)}, u32[]{:S(2)}, u32[]{:S(2)}) collective-permute-start(bf16[256,2048]{1,0:T(8,128)(2,1)} %get-tuple-element.107), channel_id=1, source_target_pairs={{0,1},{1,0},{2,3},{3,2},{4,5},{5,4},{6,7},{7,6},{8,9},{9,8},{10,11... | collective-permute-start | bytes 3145736 | tf_op jit(solution)/shard_map/ppermute | solution.py:687
  218.7 60.5 %collective-permute-start.14 = (bf16[256,2048]{1,0:T(8,128)(2,1)}, bf16[256,2048]{1,0:T(8,128)(2,1)S(1)}, u32[]{:S(2)}, u32[]{:S(2)}) collective-permute-start(bf16[256,2048]{1,0:T(8,128)(2,1)} %get-tuple-element.108), channel_id=1, source_target_pairs={{0,4},{1,5},{2,6},{3,7},{4,0},{5,1},{6,2},{7,3},{8,12},{9,13},{10,... | collective-permute-start | bytes 3145736 | tf_op jit(solution)/shard_map/ppermute | solution.py:687
  283.4 21.9 %collective-permute-start.17 = (bf16[128,2048]{1,0:T(8,128)(2,1)}, bf16[128,2048]{1,0:T(8,128)(2,1)S(1)}, u32[]{:S(2)}, u32[]{:S(2)}) collective-permute-start(bf16[128,2048]{1,0:T(8,128)(2,1)} %get-tuple-element.113), channel_id=1, source_target_pairs={{0,1},{1,0},{2,3},{3,2},{4,5},{5,4},{6,7},{7,6},{8,9},{9,8},{10,11... | collective-permute-start | bytes 1572872 | tf_op jit(solution)/shard_map/ppermute | solution.py:687
  285.9 19.5 %collective-permute-start.16 = (bf16[128,2048]{1,0:T(8,128)(2,1)}, bf16[128,2048]{1,0:T(8,128)(2,1)S(1)}, u32[]{:S(2)}, u32[]{:S(2)}) collective-permute-start(bf16[128,2048]{1,0:T(8,128)(2,1)} %get-tuple-element.111.refs_2_), channel_id=1, source_target_pairs={{0,4},{1,5},{2,6},{3,7},{4,0},{5,1},{6,2},{7,3},{8,12},{9,13},{10,... | collective-permute-start | bytes 1572872 | tf_op jit(solution)/shard_map/ppermute | solution.py:687
  309.8 122.3 %reduce-scatter.5.cloned.1.call-start = ((), (), s32[]{:S(2)}) async-start(), calls=%async_computation.6 | async-start | bytes 4456448 | tf_op jit(solution)/shard_map/reduce_scatter | solution.py:850
  313.1 4.7 %collective-permute-start.15 = (bf16[512,1024]{1,0:T(8,128)(2,1)}, bf16[512,1024]{1,0:T(8,128)(2,1)}, u32[]{:S(2)}, u32[]{:S(2)}) collective-permute-start(bf16[512,1024]{1,0:T(8,128)(2,1)} %constant_dynamic-slice_fusion.1), channel_id=1, source_target_pairs={{0,2},{2,0},{1,3},{3,1},{4,6},{6,4},{5,7},{7,5},{8,10},{10,8},{9,1... | collective-permute-start | bytes 3145736 | tf_op jit(solution)/shard_map/ppermute | solution.py:759
  313.3 4.5 %copy-start.18 = (f32[1024]{0:T(1024)S(1)}, f32[1024]{0:T(1024)}, u32[]{:S(2)}) copy-start(f32[1024]{0:T(1024)} %param.20) | copy-start | bytes 12292
  314.4 29.1 %collective-permute-start.10 = (bf16[512,1024]{1,0:T(8,128)(2,1)}, bf16[512,1024]{1,0:T(8,128)(2,1)}, u32[]{:S(2)}, u32[]{:S(2)}) collective-permute-start(bf16[512,1024]{1,0:T(8,128)(2,1)} %constant_dynamic-slice_fusion), channel_id=1, source_target_pairs={{0,2},{2,0},{1,3},{3,1},{4,6},{6,4},{5,7},{7,5},{8,10},{10,8},{9,1... | collective-permute-start | bytes 3145736 | tf_op jit(solution)/shard_map/ppermute | solution.py:759
  314.9 33.1 %collective-permute-start.18 = (bf16[256,2048]{1,0:T(8,128)(2,1)}, bf16[256,2048]{1,0:T(8,128)(2,1)}, u32[]{:S(2)}, u32[]{:S(2)}) collective-permute-start(bf16[256,2048]{1,0:T(8,128)(2,1)} %get-tuple-element.116.refs_6_), channel_id=1, source_target_pairs={{0,1},{1,0},{2,3},{3,2},{4,5},{5,4},{6,7},{7,6},{8,9},{9,8},{10,11... | collective-permute-start | bytes 3145736 | tf_op jit(solution)/shard_map/ppermute | solution.py:687
  315.0 33.0 %collective-permute-start.19 = (bf16[256,2048]{1,0:T(8,128)(2,1)}, bf16[256,2048]{1,0:T(8,128)(2,1)}, u32[]{:S(2)}, u32[]{:S(2)}) collective-permute-start(bf16[256,2048]{1,0:T(8,128)(2,1)} %get-tuple-element.117), channel_id=1, source_target_pairs={{0,4},{1,5},{2,6},{3,7},{4,0},{5,1},{6,2},{7,3},{8,12},{9,13},{10,... | collective-permute-start | bytes 3145736 | tf_op jit(solution)/shard_map/ppermute | solution.py:687
  317.0 26.5 %copy-start.21 = (f32[1024]{0:T(1024)S(1)}, f32[1024]{0:T(1024)}, u32[]{:S(2)}) copy-start(f32[1024]{0:T(1024)} %param.34) | copy-start | bytes 12292
  320.2 1.3 collective-permute-start.20
  321.6 20.2 %collective-permute-start.21 = (f32[8,2048]{1,0:T(8,128)S(1)}, f32[8,2048]{1,0:T(8,128)S(1)}, u32[]{:S(2)}, u32[]{:S(2)}) collective-permute-start(f32[8,2048]{1,0:T(8,128)S(1)} %add.144), channel_id=1, source_target_pairs={{0,4},{1,5},{2,6},{3,7},{4,0},{5,1},{6,2},{7,3},{8,12},{9,13},{10,... | collective-permute-start | bytes 196616 | tf_op jit(solution)/shard_map/ppermute | solution.py:687
  341.8 5.6 %collective-permute-start.22 = (f32[8,2048]{1,0:T(8,128)S(1)}, f32[8,2048]{1,0:T(8,128)S(1)}, u32[]{:S(2)}, u32[]{:S(2)}) collective-permute-start(f32[8,2048]{1,0:T(8,128)S(1)} %add.145), channel_id=1, source_target_pairs={{0,1},{1,0},{2,3},{3,2},{4,5},{5,4},{6,7},{7,6},{8,9},{9,8},{10,11... | collective-permute-start | bytes 196616 | tf_op jit(solution)/shard_map/ppermute | solution.py:687
  351.1 12.5 %collective-permute-start.23 = (bf16[128,2048]{1,0:T(8,128)(2,1)}, bf16[128,2048]{1,0:T(8,128)(2,1)S(1)}, u32[]{:S(2)}, u32[]{:S(2)}) collective-permute-start(bf16[128,2048]{1,0:T(8,128)(2,1)} %get-tuple-element.124), channel_id=1, source_target_pairs={{0,4},{1,5},{2,6},{3,7},{4,0},{5,1},{6,2},{7,3},{8,12},{9,13},{10,... | collective-permute-start | bytes 1572872 | tf_op jit(solution)/shard_map/ppermute | solution.py:687
  351.2 12.6 %collective-permute-start.24 = (bf16[128,2048]{1,0:T(8,128)(2,1)}, bf16[128,2048]{1,0:T(8,128)(2,1)S(1)}, u32[]{:S(2)}, u32[]{:S(2)}) collective-permute-start(bf16[128,2048]{1,0:T(8,128)(2,1)} %get-tuple-element.125), channel_id=1, source_target_pairs={{0,1},{1,0},{2,3},{3,2},{4,5},{5,4},{6,7},{7,6},{8,9},{9,8},{10,11... | collective-permute-start | bytes 1572872 | tf_op jit(solution)/shard_map/ppermute | solution.py:687
  364.6 3.6 copy-start.7
  368.2 5.8 %copy-start.27 = (bf16[80,2048]{1,0:T(8,128)(2,1)S(1)}, bf16[80,2048]{1,0:T(8,128)(2,1)}, u32[]{:S(2)}) copy-start(bf16[80,2048]{1,0:T(8,128)(2,1)} %get-tuple-element.138) | copy-start | bytes 983044
  368.2 31.5 %copy-start.31 = (bf16[64,2048]{1,0:T(8,128)(2,1)S(1)}, bf16[64,2048]{1,0:T(8,128)(2,1)}, u32[]{:S(2)}) copy-start(bf16[64,2048]{1,0:T(8,128)(2,1)} %reduce-scatter.3.cloned.1.call-done) | copy-start | bytes 786436
  368.4 31.3 %collective-permute-start.25 = (bf16[1024,1024]{1,0:T(8,128)(2,1)S(1)}, bf16[1024,1024]{1,0:T(8,128)(2,1)S(1)}, u32[]{:S(2)}, u32[]{:S(2)}) collective-permute-start(bf16[1024,1024]{1,0:T(8,128)(2,1)S(1)} %pad_maximum_fusion), channel_id=1, source_target_pairs={{2,0},{0,1},{3,2},{1,3},{6,4},{4,5},{7,6},{5,7},{10,8},{8,9},{11,1... | collective-permute-start | bytes 6291464 | tf_op jit(solution)/shard_map/ppermute | solution.py:671
  369.3 65.0 %collective-permute-start.27 = (bf16[80,2048]{1,0:T(8,128)(2,1)S(1)}, bf16[80,2048]{1,0:T(8,128)(2,1)S(1)}, u32[]{:S(2)}, u32[]{:S(2)}) collective-permute-start(bf16[80,2048]{1,0:T(8,128)(2,1)S(1)} %copy-done.30), channel_id=1, source_target_pairs={{2,0},{0,1},{3,2},{1,3},{6,4},{4,5},{7,6},{5,7},{10,8},{8,9},{11,1... | collective-permute-start | bytes 983048 | tf_op jit(solution)/shard_map/ppermute | solution.py:679
  369.8 64.4 %collective-permute-start.28 = (bf16[80,2048]{1,0:T(8,128)(2,1)S(1)}, bf16[80,2048]{1,0:T(8,128)(2,1)S(1)}, u32[]{:S(2)}, u32[]{:S(2)}) collective-permute-start(bf16[80,2048]{1,0:T(8,128)(2,1)S(1)} %copy-done.29), channel_id=1, source_target_pairs={{10,0},{8,1},{11,2},{9,3},{14,4},{12,5},{15,6},{13,7},{2,8},{0,9},... | collective-permute-start | bytes 983048 | tf_op jit(solution)/shard_map/ppermute | solution.py:679
  370.9 63.3 %collective-permute-start.29 = (bf16[80,2048]{1,0:T(8,128)(2,1)S(1)}, bf16[80,2048]{1,0:T(8,128)(2,1)S(1)}, u32[]{:S(2)}, u32[]{:S(2)}) collective-permute-start(bf16[80,2048]{1,0:T(8,128)(2,1)S(1)} %copy-done.28), channel_id=1, source_target_pairs={{18,0},{16,1},{19,2},{17,3},{22,4},{20,5},{23,6},{21,7},{26,8},{24... | collective-permute-start | bytes 983048 | tf_op jit(solution)/shard_map/ppermute | solution.py:679
  374.0 60.3 %collective-permute-start.30 = (bf16[80,2048]{1,0:T(8,128)(2,1)S(1)}, bf16[80,2048]{1,0:T(8,128)(2,1)S(1)}, u32[]{:S(2)}, u32[]{:S(2)}) collective-permute-start(bf16[80,2048]{1,0:T(8,128)(2,1)S(1)} %copy-done.27), channel_id=1, source_target_pairs={{26,0},{24,1},{27,2},{25,3},{30,4},{28,5},{31,6},{29,7},{18,8},{16... | collective-permute-start | bytes 983048 | tf_op jit(solution)/shard_map/ppermute | solution.py:679
  399.7 9.4 %collective-permute-start.26 = (bf16[64,2048]{1,0:T(8,128)(2,1)S(1)}, bf16[64,2048]{1,0:T(8,128)(2,1)S(1)}, u32[]{:S(2)}, u32[]{:S(2)}) collective-permute-start(bf16[64,2048]{1,0:T(8,128)(2,1)S(1)} %copy-done.31), channel_id=1, source_target_pairs={{2,0},{0,1},{3,2},{1,3},{6,4},{4,5},{7,6},{5,7},{10,8},{8,9},{11,1... | collective-permute-start | bytes 786440 | tf_op jit(solution)/shard_map/ppermute | solution.py:671
  409.1 23.1 %copy-start.17 = (bf16[64,2048]{1,0:T(8,128)(2,1)}, bf16[64,2048]{1,0:T(8,128)(2,1)S(1)}, u32[]{:S(2)}) copy-start(bf16[64,2048]{1,0:T(8,128)(2,1)S(1)} %collective-permute-done.26.second_ref) | copy-start | bytes 786436
  (20 other events, 30.6 us)
Sparse Core Ops, SparseCore 0:
  10.8 53.2 all-gather.3
  66.8 49.0 all-gather.5
  118.6 71.8 all-gather.7
  310.0 26.5 reduce-scatter.2
  340.7 91.3 reduce-scatter.4

commit v8 on v6

--- a/solution.py
+++ b/solution.py
@@ -567,10 +567,24 @@
     return total.astype(BF16)
 
 
-def first_sums_kernel(from_x, from_y, keep_y, keep_x, y_ref, x_ref):
+def high_low(values):
+    high = values.astype(BF16).astype(F32)
+    return jnp.concatenate([high, values - high], axis=0).astype(BF16)
+
+
+def from_high_low(rows):
+    rows = rows.astype(F32)
+    half = rows.shape[0] // 2
+    return rows[:half, :] + rows[half:, :]
+
+
+def first_sums_kernel(from_x, from_y, keep_y, keep_x, *refs):
+    small, (y_ref, x_ref) = refs[:-2], refs[-2:]
     half = y_ref.shape[0]
     y_ref[...] = added(keep_y[...], from_x[:half, :])
-    x_ref[...] = added(keep_x[...], from_y[:half, :])
+    x_ref[:half, :] = added(keep_x[...], from_y[:half, :])
+    for values in small:
+        x_ref[half:, :] = high_low(values[...])
 
 
 def second_sums_kernel(from_x, from_y, near, from_y2, from_x2, *outs, with_small):
@@ -580,9 +594,7 @@
     half = from_y2.shape[0]
     rows = half * 2 // far
     if with_small:
-        values = small[...]
-        high = values.astype(BF16).astype(F32)
-        extra = jnp.concatenate([high, values - high], axis=0).astype(BF16)
+        extra = high_low(small[...] + from_high_low(from_x2[half:, :]))
     for i, out in enumerate(outs):
         first, second, place = (from_x, from_y2, i) if i < far // 2 else (from_y, from_x2, i - far // 2)
         out[:rows, :] = added(
@@ -615,8 +627,7 @@
     rows, columns = outs[0].shape
     for k, out in enumerate(outs):
         out[...] = total[:rows, k * columns : (k + 1) * columns]
-    extra = small.shape[0]
-    small[...] = total[rows : rows + extra, :] + total[rows + extra :, :]
+    small[...] = from_high_low(total[rows:, :])
 
 
 def units_last_kernel(first_ref, second_ref, up_ref, down_ref, *, tile):
@@ -686,13 +697,18 @@
                     pairs.append(((a * 2 + c) * 2 + h, ((a ^ a_mask) * 2 + c) * 2 + (h ^ h_mask)))
         return lax.ppermute(values, ("z", "y", "c", "h"), pairs)
 
-    def scatter_near(pieces, after):
+    def scatter_near(pieces, after, small=()):
         from_x, from_y = hop(pieces[0], 0, 1), hop(pieces[1], 1, 0)
         half, columns = pieces[2].shape
         y_sum, x_sum = sums_call(
             first_sums_kernel,
-            [from_x, from_y, pieces[2], pieces[3]],
-            [jax.ShapeDtypeStruct((half, columns), BF16)] * 2,
+            [from_x, from_y, pieces[2], pieces[3], *small],
+            [
+                jax.ShapeDtypeStruct((half, columns), BF16),
+                jax.ShapeDtypeStruct(
+                    (half + sum(2 * values.shape[0] for values in small), columns), BF16
+                ),
+            ],
             after,
             "sums_one",
         )
@@ -727,10 +743,8 @@
     def far_parts(sums):
         return [swap_hop(sums[i], 2 * i, inverse=True) for i in range(far)]
 
-    def near_sum(values):
+    def core_sum(values):
         values = values + lax.ppermute(values, "c", [(0, 1), (1, 0)])
-        values = values + hop(values, 1, 0)
-        values = values + hop(values, 0, 1)
         return lax.psum(values, "l") if inner > 1 else values
 
     a, h = lax.axis_index(("z", "y")), lax.axis_index("h")
@@ -738,7 +752,7 @@
     for a_low, h_mask in ((0, 0), (1, 0), (0, 1), (1, 1)):
         for i in range(far):
             order.append((a ^ (2 * i + a_low)) * 2 + (h ^ h_mask))
-    return swap, hop, scatter_near, far_sums, z_sums, far_parts, near_sum, jnp.stack(order).astype(jnp.int32)
+    return swap, hop, scatter_near, far_sums, z_sums, far_parts, core_sum, jnp.stack(order).astype(jnp.int32)
 
 
 def per_device(sizes, *arguments):
@@ -753,7 +767,7 @@
     unit_width = w_up.shape[1]
     half_units = unit_width // 2
     tile = min(TILE, half_units)
-    swap, hop, scatter_near, far_sums, z_sums, far_parts, near_sum, order = moves(sizes)
+    swap, hop, scatter_near, far_sums, z_sums, far_parts, core_sum, order = moves(sizes)
 
     def partner(values):
         return lax.ppermute(values, "c", [(0, 1), (1, 0)])
@@ -862,13 +876,7 @@
         (second_grads, first_mlp, grad_normed_part)
     )
     second_mlp = lax.psum_scatter(second_grads, ("z", "y", "c"), scatter_dimension=0, tiled=True)
-    state = scatter_near(pieces, grad_normed_part)
-    grad_normed_own, grad_normed_other = tp_scatter_terms(grad_normed_part)
-    first_mlp, grad_normed_other, state = lax.optimization_barrier(
-        (first_mlp, grad_normed_other, state)
-    )
-    first_mlp = swap(first_mlp, inverse=True)
-    grad_normed = grad_normed_own.astype(F32) + grad_normed_other.astype(F32)
+    grad_normed = tp_scatter(grad_normed_part)
     own_scaled, own_inverse = normalize(own_input.astype(F32))
     grad_own = own(grad_hidden) + norm_back(grad_normed, own_scaled, own_inverse, ln1_gain)
     grad_own = grad_own.astype(BF16)
@@ -892,7 +900,10 @@
     columns = pieces[0].shape[1]
     filled = sums.shape[0]
     sums = jnp.pad(sums, (0, -filled % (8 * columns))).reshape(-1, columns)
-    sums = near_sum(sums)
+    sums = core_sum(sums)
+    state = scatter_near(pieces, None, [sums])
+    first_mlp, state = lax.optimization_barrier((first_mlp, state))
+    first_mlp = swap(first_mlp, inverse=True)
     last_sums = far_sums(state, [sums], first_mlp)
     own_output, grad_own, *last_sums = lax.optimization_barrier((own_output, grad_own, *last_sums))
     leaving = swap(jnp.concatenate([own_output, grad_own], axis=0), inverse=True)
@@ -913,7 +924,7 @@
         grad_w_up,
         "sums_last",
     )
-    sums = sums.reshape(-1)
+    sums = (sums + hop(sums, 1, 0)).reshape(-1)
     small = [sums[i * width : (i + 1) * width] for i in range(8)]
     return (
         output, grad_input, small[0], small[1],

time: 419 us -> 416 us (level)
    reduce_scatter x1, waiting for transfers between devices: 0.01 us -> 29.2 us  [per_device(): lax.psum_scatter(second_grads, ('z', 'y', 'c'), scatter_dimension=0, tile...]
    ppermute x9, waiting for transfers between devices: 124 us -> 100 us  [swap(): return lax.ppermute(values, SWAP, pairs)]
    ppermute x11 -> x10, waiting for transfers between devices: 39.8 us -> 31 us  [hop(): return lax.ppermute(values, ('z', 'y', 'c', 'h'), pairs)]
    unnamed x83 -> x71, local copies, waits for them, and re-layouts: 8.71 us -> 5.91 us
    ppermute x11 -> x10, starting transfers between devices: 11.7 us -> 10.7 us  [hop(): return lax.ppermute(values, ('z', 'y', 'c', 'h'), pairs)]
  transfers between devices with their start and end apart: 36 -> 35, of which waited for: 13 -> 17; matrix products, arithmetic and copies ran while one was open for 9% -> 10% of each run, Pallas kernels for 36% -> 36%
where the time goes in v8:
time: 416 us; the launch traced here: 408 us
  waiting for transfers between devices  166 us (40%)
  Pallas kernels  155 us (37%)
  starting transfers between devices  24.2 us (6%)
  other arithmetic  23.9 us (6%)
  local copies, waits for them, and re-layouts  16.5 us (4%)
  between operations  14.7 us (4%)
  matrix products  7.62 us (2%)
    ppermute x9, waiting for transfers between devices, swap(): return lax.ppermute(values, SWAP, pairs)  100 us
    pallas_call x2, Pallas kernels, mlp(): pl.pallas_call(functools.partial(mlp_kernel, block=min(ROWS, length), wit...  48.4 us
    ppermute x10, waiting for transfers between devices, hop(): return lax.ppermute(values, ('z', 'y', 'c', 'h'), pairs)  31 us
    reduce_scatter x1, waiting for transfers between devices, per_device(): lax.psum_scatter(second_grads, ('z', 'y', 'c'), scatter_dimension=0, tile...  29.2 us
    pallas_call x1, Pallas kernels, attn_backward(): pl.pallas_call(without(functools.partial(attn_backward_kernel, block=bloc...  24.3 us
    pallas_call x1, Pallas kernels, attn_forward(): pl.pallas_call(functools.partial(attn_forward_kernel, block=block), grid=...  16.4 us
    pallas_call x6, Pallas kernels, sums_call(): pl.pallas_call(body, in_specs=([pl.BlockSpec(memory_space=pl.ANY)] if aft...  15.5 us
    pallas_call x2, Pallas kernels, norm_rows(): pl.pallas_call(functools.partial(norm_kernel, residual=residual), grid=(l...  13 us
  transfers between devices with their start and end apart: 35, of which 17 were waited for; matrix products, arithmetic and copies ran while one was open for 10% of the time, Pallas kernels for 36%

profile of v8, /device:TPU:0, one launch (start us, length us, event | category | flops | bytes accessed | tf_op | source)
XLA Modules:
  0.0 408.0 jit_solution(1015885821719261559)
XLA Ops:
  7.2 1.7 pad_maximum_fusion.1
  9.0 1.8 mlp_shards.1
  11.3 2.0 collective-permute-start.3
  13.4 13.4 %collective-permute-done = bf16[512,1024]{1,0:T(8,128)(2,1)S(1)} collective-permute-done((bf16[512,1024]{1,0:T(8,128)(2,1)}, bf16[512,1024]{1,0:T(8,128)(2,1)S(1)}, u32[]{:S(2)}, u32[]{:S(2)}) %collective-permute-start) | collective-permute-done | bytes 1048608 | tf_op jit(solution)/shard_map/ppermute | solution.py:682
  26.8 11.2 %collective-permute-done.3 = bf16[512,1024]{1,0:T(8,128)(2,1)S(1)} collective-permute-done((bf16[512,1024]{1,0:T(8,128)(2,1)}, bf16[512,1024]{1,0:T(8,128)(2,1)S(1)}, u32[]{:S(2)}, u32[]{:S(2)}) %collective-permute-start.3) | collective-permute-done | bytes 1048608 | tf_op jit(solution)/shard_map/ppermute | solution.py:682
  38.6 6.1 %collective-permute-done.5 = bf16[64,2048]{1,0:T(8,128)(2,1)S(1)} collective-permute-done((bf16[64,2048]{1,0:T(8,128)(2,1)}, bf16[64,2048]{1,0:T(8,128)(2,1)S(1)}, u32[]{:S(2)}, u32[]{:S(2)}) %collective-permute-start.5) | collective-permute-done | bytes 262176 | tf_op jit(solution)/shard_map/ppermute | solution.py:682
  44.7 6.6 %collective-permute-done.6 = bf16[64,2048]{1,0:T(8,128)(2,1)} collective-permute-done((bf16[64,2048]{1,0:T(8,128)(2,1)S(1)}, bf16[64,2048]{1,0:T(8,128)(2,1)}, u32[]{:S(2)}, u32[]{:S(2)}) %collective-permute-start.6) | collective-permute-done | bytes 262176 | tf_op jit(solution)/shard_map/ppermute | solution.py:698
  51.3 2.0 maximum_select_fusion.2
  53.2 2.3 maximum_select_fusion.refs_0_
  55.6 3.3 maximum_select_fusion.1.g_ref
  58.9 5.5 %norm_one.1 = (bf16[1024,1024]{1,0:T(8,128)(2,1)}, bf16[1024,1024]{1,0:T(8,128)(2,1)}) custom-call(bf16[1024,1024]{1,0:T(8,128)(2,1)} %maximum_select_fusion.refs_0_, f32[1,1024]{1,0:T(1,128)} %bitcast.39, f32[1,1024]{1,0:T(1,128)} %bitcast.46), custom_call_target="tpu_custom_call" | custom-call | flops 20971520 | bytes 14680064 | tf_op jit(solution)/shard_map/norm_one/pallas_call | solution.py:276
  65.3 47.9 %collective-permute-done.7.w_ref.refs_1_ = bf16[1024,2048]{1,0:T(8,128)(2,1)} collective-permute-done((bf16[1024,2048]{1,0:T(8,128)(2,1)}, bf16[1024,2048]{1,0:T(8,128)(2,1)}, u32[]{:S(2)}, u32[]{:S(2)}) %collective-permute-start.7) | collective-permute-done | bytes 4194336 | tf_op jit(solution)/shard_map/ppermute | solution.py:682
  113.3 7.2 %qkv_project.1.q_ref.k_ref.v_ref.refs_2_.refs_3_.refs_4_ = bf16[1024,1536]{1,0:T(8,128)(2,1)} custom-call(bf16[1024,1024]{1,0:T(8,128)(2,1)} %get-tuple-element.100.n_ref, f32[1,1536]{1,0:T(1,128)} %reshape.108.b_ref, bf16[1024,2048]{1,0:T(8,128)(2,1)} %collective-permute-done.7.w_ref.refs_1_), custom_call_target="tpu_custom_call" | custom-call | flops 3221225472 | bytes 8388608 | tf_op jit(solution)/shard_map/qkv_project/pallas_call | solution.py:457
  121.6 16.4 %attn_forward.1 = (bf16[1024,512]{1,0:T(8,128)(2,1)}, f32[4,8,1024]{2,1,0:T(8,128)}) custom-call(s32[1024,1]{1,0:T(8,128)} %copy.37.seg_col.refs_0_, s32[1,1024]{1,0:T(1,128)} %bitcast.41, bf16[1024,1536]{1,0:T(8,128)(2,1)} %qkv_project.1.q_ref.k_ref.v_ref.refs_2_.refs_3_.refs_4_, bf16[1024,1536]{1,0:T(8,128)(2,1)} %qkv_project.1.q_ref.k_ref.v_ref.refs_2_.refs_3_.refs_4_, ...), custom_call_target="tpu_custom_call" | custom-call | flops 2147483648 | bytes 4194304 | tf_op jit(solution)/shard_map/attn_forward/pallas_call | solution.py:157
  137.9 4.2 %convolution_convert_fusion.refs_1_ = bf16[1024,1024]{1,0:T(8,128)(2,1)} fusion(bf16[1024,512]{1,0:T(8,128)(2,1)} %get-tuple-element.103.refs_5_.mixed_ref, bf16[1024,2048]{1,0:T(8,128)(2,1)} %collective-permute-done.7.w_ref.refs_1_), kind=kOutput, calls=%fused_computation.22 | convolution fusion | flops 1074790400 | bytes 4194304 | tf_op jit(solution)/shard_map/dot_general | solution.py:45
  143.4 2.6 copy.39.gt_ref
  146.6 7.5 %norm_two.1 = (bf16[1024,1024]{1,0:T(8,128)(2,1)}, bf16[1024,1024]{1,0:T(8,128)(2,1)}, f32[1024,1024]{1,0:T(8,128)}) custom-call(bf16[1024,1024]{1,0:T(8,128)(2,1)} %maximum_select_fusion.refs_0_, bf16[1024,1024]{1,0:T(8,128)(2,1)} %convolution_convert_fusion.refs_1_, bf16[1024,1024]{1,0:T(8,128)(2,1)} %collective-permute-done.8.refs_2_, ...), custom_call_target="tpu_custom_call" | custom-call | flops 20971520 | bytes 14680064 | tf_op jit(solution)/shard_map/norm_two/pallas_call | solution.py:276
  154.1 15.2 %collective-permute-done.9.w_ref = bf16[1024,2048]{1,0:T(8,128)(2,1)} collective-permute-done((bf16[1024,2048]{1,0:T(8,128)(2,1)}, bf16[1024,2048]{1,0:T(8,128)(2,1)}, u32[]{:S(2)}, u32[]{:S(2)}) %collective-permute-start.9) | collective-permute-done | bytes 4194336 | tf_op jit(solution)/shard_map/ppermute | solution.py:682
  169.3 23.7 %mlp_first.1 = (bf16[1024,1024]{1,0:T(8,128)(2,1)}, bf16[1024,1024]{1,0:T(8,128)(2,1)}, bf16[256,2048]{1,0:T(8,128)(2,1)}, bf16[256,2048]{1,0:T(8,128)(2,1)}, bf...) custom-call(s32[16]{0:T(128)} %stack.67.order, ...), custom_call_target="tpu_custom_call" | custom-call | flops 12884901888 | bytes 20971520 | tf_op jit(solution)/shard_map/mlp_first/pallas_call | solution.py:403
  193.2 2.0 collective-permute-start.12
  195.2 24.7 %mlp_second.1 = (bf16[1024,1024]{1,0:T(8,128)(2,1)}, bf16[1024,1024]{1,0:T(8,128)(2,1)}, bf16[1024,2048]{1,0:T(8,128)(2,1)}, f32[1,1024]{1,0:T(1,128)}) custom-call(s32[16]{0:T(128)} %stack.67.order, bf16[1024,1024]{1,0:T(8,128)(2,1)} %get-tuple-element.105.n_ref, bf16[1024,1024]{1,0:T(8,128)(2,1)} %copy-done, bf16[1024,1024]{1,0:T(8,128)(2,1)} %get-tuple-element.107.nt_ref, ...), custom_call_target="tpu_custom_call" | custom-call | flops 12884901888 | bytes 20971520 | tf_op jit(solution)/shard_map/mlp_second/pallas_call | solution.py:403
  221.3 3.1 sums_one.2
  224.5 1.9 collective-permute-start.15
  226.5 2.0 collective-permute-done.13.other_ref
  229.8 9.1 %norm_two_back.1 = (f32[1024,1024]{1,0:T(8,128)}, bf16[1024,1024]{1,0:T(8,128)(2,1)}, bf16[1024,1024]{1,0:T(8,128)(2,1)}, f32[8,1024]{1,0:T(8,128)}) custom-call(f32[1024,1024]{1,0:T(8,128)} %get-tuple-element.104.hidden_ref, bf16[1024,1024]{1,0:T(8,128)(2,1)} %copy-done, bf16[1024,1024]{1,0:T(8,128)(2,1)} %get-tuple-element.125.refs_0_.own_ref, ...), custom_call_target="tpu_custom_call" | custom-call | flops 31457280 | bytes 16777216 | tf_op jit(solution)/shard_map/norm_two_back/pallas_call | solution.py:316
  239.7 3.7 sums_two_z.1.refs_8_
  243.4 1.9 collective-permute-start.16
  245.4 3.5 convolution_convert_fusion.1.refs_7_
  248.9 24.3 %attn_backward.1.grads_ref.order_only.refs_0_ = bf16[3,1024,512]{2,1,0:T(8,128)(2,1)} custom-call(s32[1024,1]{1,0:T(8,128)} %copy.37.seg_col.refs_0_, s32[1,1024]{1,0:T(1,128)} %bitcast.42, bf16[1024,1536]{1,0:T(8,128)(2,1)} %qkv_project.1.q_ref.k_ref.v_ref.refs_2_.refs_3_.refs_4_, bf16[1024,1536]{1,0:T(8,128)(2,1)} %qkv_project.1.q_ref.k_ref.v_ref.refs_2_.refs_3_.refs_4_, ...), custom_call_target="tpu_custom_call" | custom-call | flops 5368709120 | bytes 8388608 | tf_op jit(solution)/shard_map/attn_backward/pallas_call | solution.py:186
  273.2 10.1 %weight_grads.1 = (bf16[256,2048]{1,0:T(8,128)(2,1)}, bf16[256,2048]{1,0:T(8,128)(2,1)}, bf16[128,2048]{1,0:T(8,128)(2,1)}, bf16[128,2048]{1,0:T(8,128)(2,1)}, bf16[256,2048]{1,0:T(8,128)(2,1)}) custom-call(s32[16]{0:T(128)} %stack.67.order, bf16[1024,1024]{1,0:T(8,128)(2,1)} %get-tuple-element.137.nt_ref, ...), custom_call_target="tpu_custom_call" | custom-call | flops 4294967296 | bytes 12582912 | tf_op jit(solution)/shard_map/weight_grads/pallas_call | solution.py:502
  283.3 7.4 %qkv_back.1 = bf16[1024,1024]{1,0:T(8,128)(2,1)} custom-call(bf16[3,1024,512]{2,1,0:T(8,128)(2,1)} %attn_backward.1.grads_ref.order_only.refs_0_, bf16[1024,2048]{1,0:T(8,128)(2,1)} %collective-permute-done.7.w_ref.refs_1_, bf16[256,2048]{1,0:T(8,128)(2,1)} %get-tuple-element.139.refs_2_), custom_call_target="tpu_custom_call" | custom-call | flops 3221225472 | bytes 8388608 | tf_op jit(solution)/shard_map/qkv_back/pallas_call | solution.py:543
  296.1 2.5 collective-permute-start.18
  299.8 2.0 convert_reduce_fusion.2
  302.6 2.4 fusion.10
  307.1 16.8 %collective-permute-done.19.from_y.refs_2_ = bf16[256,2048]{1,0:T(8,128)(2,1)} collective-permute-done((bf16[256,2048]{1,0:T(8,128)(2,1)}, bf16[256,2048]{1,0:T(8,128)(2,1)}, u32[]{:S(2)}, u32[]{:S(2)}) %collective-permute-start.19) | collective-permute-done | bytes 1048608 | tf_op jit(solution)/shard_map/ppermute | solution.py:698
  323.9 3.0 sums_one.3
  327.7 4.1 %add_convert_fusion = bf16[512,1024]{1,0:T(8,128)(2,1)} fusion(bf16[512,1024]{1,0:T(8,128)(2,1)} %collective-permute-done.10, f32[1024,1024]{1,0:T(8,128)} %get-tuple-element.104.hidden_ref, s32[]{:T(128)S(6)} %select_n.43, f32[1024]{0:T(1024)S(1)} %copy-done.23, bf16[1024,1024]{1,0:T(8,128)(2,1)} %get-tuple-element.115), kind=kLoop, calls=%fused_computation.21 | loop fusion | flops 3145728 | bytes 5246980 | tf_op jit(solution)/shard_map/convert_element_type | solution.py:861
  334.0 3.1 fusion.9
  337.1 5.3 %collective-permute-done.21.refs_0_.first_ref = bf16[64,2048]{1,0:T(8,128)(2,1)S(1)} collective-permute-done((bf16[64,2048]{1,0:T(8,128)(2,1)S(1)}, bf16[64,2048]{1,0:T(8,128)(2,1)S(1)}, u32[]{:S(2)}, u32[]{:S(2)}) %collective-permute-start.21) | collective-permute-done | bytes 262176 | tf_op jit(solution)/shard_map/ppermute | solution.py:682
  342.4 5.3 %collective-permute-done.22.refs_4_ = bf16[128,2048]{1,0:T(8,128)(2,1)} collective-permute-done((bf16[128,2048]{1,0:T(8,128)(2,1)S(1)}, bf16[128,2048]{1,0:T(8,128)(2,1)}, u32[]{:S(2)}, u32[]{:S(2)}) %collective-permute-start.22) | collective-permute-done | bytes 524320 | tf_op jit(solution)/shard_map/ppermute | solution.py:698
  347.7 3.5 sums_two.1
  351.1 1.5 pad_maximum_fusion
  355.1 2.8 collective-permute-start.27
  359.3 29.2 %reduce-scatter.5.cloned.1.call-done.second_ref = bf16[64,2048]{1,0:T(8,128)(2,1)} async-done(((bf16[1024,2048]{1,0:T(8,128)(2,1)}), bf16[64,2048]{1,0:T(8,128)(2,1)}) %reduce-scatter.5.cloned.1.call-update) | async-done | bytes 262160 | tf_op jit(solution)/shard_map/reduce_scatter | solution.py:878
  388.4 2.1 units_last.1
  390.5 1.6 collective-permute-done.25.refs_1_
  393.1 2.1 sums_last.1
  397.7 2.0 collective-permute-done.29
  (158 shorter events, 29.6 us)
Async XLA Ops:
  7.2 57.3 %all-gather.4.cloned.1.call-start = ((), (), s32[]{:S(2)}) async-start(), calls=%async_computation.2 | async-start | bytes 4456448 | tf_op jit(solution)/shard_map/all_gather | solution.py:815
  8.9 111.6 %all-gather.6.cloned.1.call-start = ((), (), s32[]{:S(2)}) async-start(), calls=%async_computation.3 | async-start | bytes 4456448 | tf_op jit(solution)/shard_map/all_gather | solution.py:818
  10.8 182.3 %all-gather.8.cloned.1.call-start = ((), (), s32[]{:S(2)}) async-start(), calls=%async_computation.4 | async-start | bytes 4718592 | tf_op jit(solution)/shard_map/all_gather | solution.py:837
  10.9 15.9 %collective-permute-start = (bf16[512,1024]{1,0:T(8,128)(2,1)}, bf16[512,1024]{1,0:T(8,128)(2,1)S(1)}, u32[]{:S(2)}, u32[]{:S(2)}) collective-permute-start(bf16[512,1024]{1,0:T(8,128)(2,1)} %param.18), channel_id=1, source_target_pairs={{0,2},{1,0},{2,3},{3,1},{4,6},{5,4},{6,7},{7,5},{8,10},{9,8},{10,1... | collective-permute-start | bytes 3145736 | tf_op jit(solution)/shard_map/ppermute | solution.py:682
  11.3 26.7 %collective-permute-start.3 = (bf16[512,1024]{1,0:T(8,128)(2,1)}, bf16[512,1024]{1,0:T(8,128)(2,1)S(1)}, u32[]{:S(2)}, u32[]{:S(2)}) collective-permute-start(bf16[512,1024]{1,0:T(8,128)(2,1)} %param.35), channel_id=1, source_target_pairs={{0,2},{1,0},{2,3},{3,1},{4,6},{5,4},{6,7},{7,5},{8,10},{9,8},{10,1... | collective-permute-start | bytes 3145736 | tf_op jit(solution)/shard_map/ppermute | solution.py:682
  26.8 26.4 %collective-permute-start.1 = (bf16[512,1024]{1,0:T(8,128)(2,1)S(1)}, bf16[512,1024]{1,0:T(8,128)(2,1)S(1)}, u32[]{:S(2)}, u32[]{:S(2)}) collective-permute-start(bf16[512,1024]{1,0:T(8,128)(2,1)S(1)} %collective-permute-done), channel_id=1, source_target_pairs={{0,2},{2,0},{1,3},{3,1},{4,6},{6,4},{5,7},{7,5},{8,10},{10,8},{9,1... | collective-permute-start | bytes 3145736 | tf_op jit(solution)/shard_map/ppermute | solution.py:773
  38.1 17.5 %copy-start.3 = (bf16[512,1024]{1,0:T(8,128)(2,1)}, bf16[512,1024]{1,0:T(8,128)(2,1)S(1)}, u32[]{:S(2)}) copy-start(bf16[512,1024]{1,0:T(8,128)(2,1)S(1)} %collective-permute-done.3) | copy-start | bytes 3145732
  38.1 17.5 %collective-permute-start.4 = (bf16[512,1024]{1,0:T(8,128)(2,1)S(1)}, bf16[512,1024]{1,0:T(8,128)(2,1)}, u32[]{:S(2)}, u32[]{:S(2)}) collective-permute-start(bf16[512,1024]{1,0:T(8,128)(2,1)S(1)} %collective-permute-done.3), channel_id=1, source_target_pairs={{0,2},{2,0},{1,3},{3,1},{4,6},{6,4},{5,7},{7,5},{8,10},{10,8},{9,1... | collective-permute-start | bytes 3145736 | tf_op jit(solution)/shard_map/ppermute | solution.py:773
  38.1 6.6 %collective-permute-start.5 = (bf16[64,2048]{1,0:T(8,128)(2,1)}, bf16[64,2048]{1,0:T(8,128)(2,1)S(1)}, u32[]{:S(2)}, u32[]{:S(2)}) collective-permute-start(bf16[64,2048]{1,0:T(8,128)(2,1)} %get-tuple-element.97), channel_id=1, source_target_pairs={{0,2},{1,0},{2,3},{3,1},{4,6},{5,4},{6,7},{7,5},{8,10},{9,8},{10,1... | collective-permute-start | bytes 786440 | tf_op jit(solution)/shard_map/ppermute | solution.py:682
  44.7 6.6 %collective-permute-start.6 = (bf16[64,2048]{1,0:T(8,128)(2,1)S(1)}, bf16[64,2048]{1,0:T(8,128)(2,1)}, u32[]{:S(2)}, u32[]{:S(2)}) collective-permute-start(bf16[64,2048]{1,0:T(8,128)(2,1)S(1)} %collective-permute-done.5), channel_id=1, source_target_pairs={{0,1},{1,0},{2,3},{3,2},{4,5},{5,4},{6,7},{7,6},{8,9},{9,8},{10,11... | collective-permute-start | bytes 786440 | tf_op jit(solution)/shard_map/ppermute | solution.py:698
  44.7 19.8 %collective-permute-start.2 = (s32[1024]{0:T(1024)}, s32[1024]{0:T(1024)S(1)}, u32[]{:S(2)}, u32[]{:S(2)}) collective-permute-start(s32[1024]{0:T(1024)} %param.19), channel_id=1, source_target_pairs={{0,2},{1,0},{2,3},{3,1},{4,6},{5,4},{6,7},{7,5},{8,10},{9,8},{10,1... | collective-permute-start | bytes 12296 | tf_op jit(solution)/shard_map/ppermute | solution.py:682
  58.9 84.5 %copy-start = (bf16[1024,1024]{1,0:T(8,128)(2,1)}, bf16[1024,1024]{1,0:T(8,128)(2,1)S(1)}, u32[]{:S(2)}) copy-start(bf16[1024,1024]{1,0:T(8,128)(2,1)S(1)} %maximum_select_fusion.1.g_ref) | copy-start | bytes 6291460
  58.9 5.7 %copy-start.27 = (f32[1024]{0:T(1024)S(1)}, f32[1024]{0:T(1024)}, u32[]{:S(2)}) copy-start(f32[1024]{0:T(1024)} %param.25) | copy-start | bytes 12292
  58.9 5.7 %copy-start.28 = (f32[1024]{0:T(1024)S(1)}, f32[1024]{0:T(1024)}, u32[]{:S(2)}) copy-start(f32[1024]{0:T(1024)} %param.26) | copy-start | bytes 12292
  64.4 56.1 %copy-start.21 = (s32[1024]{0:T(1024)}, s32[1024]{0:T(1024)S(1)}, u32[]{:S(2)}) copy-start(s32[1024]{0:T(1024)S(1)} %collective-permute-done.2) | copy-start | bytes 12292
  64.5 48.8 %collective-permute-start.7 = (bf16[1024,2048]{1,0:T(8,128)(2,1)}, bf16[1024,2048]{1,0:T(8,128)(2,1)}, u32[]{:S(2)}, u32[]{:S(2)}) collective-permute-start(bf16[1024,2048]{1,0:T(8,128)(2,1)} %all-gather.4.cloned.1.call-done), channel_id=1, source_target_pairs={{0,2},{1,0},{2,3},{3,1},{4,6},{5,4},{6,7},{7,5},{8,10},{9,8},{10,1... | collective-permute-start | bytes 12582920 | tf_op jit(solution)/shard_map/ppermute | solution.py:682
  64.5 226.1 %reduce-scatter.3.cloned.1.call-start = ((), (), s32[]{:S(2)}) async-start(), calls=%async_computation.5 | async-start | bytes 1310720 | tf_op jit(solution)/shard_map/reduce_scatter | solution.py:870
  120.5 48.8 %collective-permute-start.9 = (bf16[1024,2048]{1,0:T(8,128)(2,1)}, bf16[1024,2048]{1,0:T(8,128)(2,1)}, u32[]{:S(2)}, u32[]{:S(2)}) collective-permute-start(bf16[1024,2048]{1,0:T(8,128)(2,1)} %all-gather.6.cloned.1.call-done), channel_id=1, source_target_pairs={{0,2},{1,0},{2,3},{3,1},{4,6},{5,4},{6,7},{7,5},{8,10},{9,8},{10,1... | collective-permute-start | bytes 12582920 | tf_op jit(solution)/shard_map/ppermute | solution.py:682
  142.1 4.5 %collective-permute-start.8 = (bf16[1024,1024]{1,0:T(8,128)(2,1)}, bf16[1024,1024]{1,0:T(8,128)(2,1)}, u32[]{:S(2)}, u32[]{:S(2)}) collective-permute-start(bf16[1024,1024]{1,0:T(8,128)(2,1)} %convolution_convert_fusion.refs_1_), channel_id=1, source_target_pairs={{0,2},{2,0},{1,3},{3,1},{4,6},{6,4},{5,7},{7,5},{8,10},{10,8},{9,1... | collective-permute-start | bytes 6291464 | tf_op jit(solution)/shard_map/ppermute | solution.py:773
  193.1 26.8 %collective-permute-start.11 = (bf16[256,2048]{1,0:T(8,128)(2,1)}, bf16[256,2048]{1,0:T(8,128)(2,1)S(1)}, u32[]{:S(2)}, u32[]{:S(2)}) collective-permute-start(bf16[256,2048]{1,0:T(8,128)(2,1)} %get-tuple-element.118), channel_id=1, source_target_pairs={{0,1},{1,0},{2,3},{3,2},{4,5},{5,4},{6,7},{7,6},{8,9},{9,8},{10,11... | collective-permute-start | bytes 3145736 | tf_op jit(solution)/shard_map/ppermute | solution.py:698
  193.2 26.7 %collective-permute-start.12 = (bf16[256,2048]{1,0:T(8,128)(2,1)}, bf16[256,2048]{1,0:T(8,128)(2,1)S(1)}, u32[]{:S(2)}, u32[]{:S(2)}) collective-permute-start(bf16[256,2048]{1,0:T(8,128)(2,1)} %get-tuple-element.119), channel_id=1, source_target_pairs={{0,4},{1,5},{2,6},{3,7},{4,0},{5,1},{6,2},{7,3},{8,12},{9,13},{10,... | collective-permute-start | bytes 3145736 | tf_op jit(solution)/shard_map/ppermute | solution.py:698
  224.3 4.2 %collective-permute-start.13 = (bf16[1024,1024]{1,0:T(8,128)(2,1)S(1)}, bf16[1024,1024]{1,0:T(8,128)(2,1)S(1)}, u32[]{:S(2)}, u32[]{:S(2)}) collective-permute-start(bf16[1024,1024]{1,0:T(8,128)(2,1)S(1)} %copy-done.1), channel_id=1, source_target_pairs={{0,2},{2,0},{1,3},{3,1},{4,6},{6,4},{5,7},{7,5},{8,10},{10,8},{9,1... | collective-permute-start | bytes 6291464 | tf_op jit(solution)/shard_map/ppermute | solution.py:773
  224.3 14.6 %collective-permute-start.14 = (bf16[128,2048]{1,0:T(8,128)(2,1)}, bf16[128,2048]{1,0:T(8,128)(2,1)S(1)}, u32[]{:S(2)}, u32[]{:S(2)}) collective-permute-start(bf16[128,2048]{1,0:T(8,128)(2,1)} %get-tuple-element.131), channel_id=1, source_target_pairs={{0,4},{1,5},{2,6},{3,7},{4,0},{5,1},{6,2},{7,3},{8,12},{9,13},{10,... | collective-permute-start | bytes 1572872 | tf_op jit(solution)/shard_map/ppermute | solution.py:698
  224.5 14.7 %collective-permute-start.15 = (bf16[128,2048]{1,0:T(8,128)(2,1)}, bf16[128,2048]{1,0:T(8,128)(2,1)}, u32[]{:S(2)}, u32[]{:S(2)}) collective-permute-start(bf16[128,2048]{1,0:T(8,128)(2,1)} %get-tuple-element.132), channel_id=1, source_target_pairs={{0,1},{1,0},{2,3},{3,2},{4,5},{5,4},{6,7},{7,6},{8,9},{9,8},{10,11... | collective-permute-start | bytes 1572872 | tf_op jit(solution)/shard_map/ppermute | solution.py:698
  239.7 5.7 %copy-start.11 = (bf16[1024,1024]{1,0:T(8,128)(2,1)S(1)}, bf16[1024,1024]{1,0:T(8,128)(2,1)}, u32[]{:S(2)}) copy-start(bf16[1024,1024]{1,0:T(8,128)(2,1)} %get-tuple-element.133.refs_6_) | copy-start | bytes 6291460
  243.4 48.3 %collective-permute-start.16 = (bf16[1024,2048]{1,0:T(8,128)(2,1)}, bf16[1024,2048]{1,0:T(8,128)(2,1)}, u32[]{:S(2)}, u32[]{:S(2)}) collective-permute-start(bf16[1024,2048]{1,0:T(8,128)(2,1)} %get-tuple-element.134), channel_id=1, source_target_pairs={{2,0},{0,1},{3,2},{1,3},{6,4},{4,5},{7,6},{5,7},{10,8},{8,9},{11,1... | collective-permute-start | bytes 12582920 | tf_op jit(solution)/shard_map/ppermute | solution.py:682
  245.4 143.1 %reduce-scatter.5.cloned.1.call-start = ((), (), s32[]{:S(2)}) async-start(), calls=%async_computation.6 | async-start | bytes 4456448 | tf_op jit(solution)/shard_map/reduce_scatter | solution.py:878
  294.3 8.2 %collective-permute-start.17 = (bf16[512,1024]{1,0:T(8,128)(2,1)}, bf16[512,1024]{1,0:T(8,128)(2,1)}, u32[]{:S(2)}, u32[]{:S(2)}) collective-permute-start(bf16[512,1024]{1,0:T(8,128)(2,1)} %constant_dynamic-slice_fusion.1), channel_id=1, source_target_pairs={{0,2},{2,0},{1,3},{3,1},{4,6},{6,4},{5,7},{7,5},{8,10},{10,8},{9,1... | collective-permute-start | bytes 3145736 | tf_op jit(solution)/shard_map/ppermute | solution.py:773
  294.6 8.0 %copy-start.20 = (f32[1024]{0:T(1024)S(1)}, f32[1024]{0:T(1024)}, u32[]{:S(2)}) copy-start(f32[1024]{0:T(1024)} %param.20) | copy-start | bytes 12292
  295.6 32.1 %collective-permute-start.10 = (bf16[512,1024]{1,0:T(8,128)(2,1)}, bf16[512,1024]{1,0:T(8,128)(2,1)}, u32[]{:S(2)}, u32[]{:S(2)}) collective-permute-start(bf16[512,1024]{1,0:T(8,128)(2,1)} %constant_dynamic-slice_fusion), channel_id=1, source_target_pairs={{0,2},{2,0},{1,3},{3,1},{4,6},{6,4},{5,7},{7,5},{8,10},{10,8},{9,1... | collective-permute-start | bytes 3145736 | tf_op jit(solution)/shard_map/ppermute | solution.py:773
  296.1 27.8 %collective-permute-start.18 = (bf16[256,2048]{1,0:T(8,128)(2,1)}, bf16[256,2048]{1,0:T(8,128)(2,1)}, u32[]{:S(2)}, u32[]{:S(2)}) collective-permute-start(bf16[256,2048]{1,0:T(8,128)(2,1)} %get-tuple-element.139.refs_2_), channel_id=1, source_target_pairs={{0,1},{1,0},{2,3},{3,2},{4,5},{5,4},{6,7},{7,6},{8,9},{9,8},{10,11... | collective-permute-start | bytes 3145736 | tf_op jit(solution)/shard_map/ppermute | solution.py:698
  298.7 25.2 %collective-permute-start.19 = (bf16[256,2048]{1,0:T(8,128)(2,1)}, bf16[256,2048]{1,0:T(8,128)(2,1)}, u32[]{:S(2)}, u32[]{:S(2)}) collective-permute-start(bf16[256,2048]{1,0:T(8,128)(2,1)} %get-tuple-element.142), channel_id=1, source_target_pairs={{0,4},{1,5},{2,6},{3,7},{4,0},{5,1},{6,2},{7,3},{8,12},{9,13},{10,... | collective-permute-start | bytes 3145736 | tf_op jit(solution)/shard_map/ppermute | solution.py:698
  305.0 22.7 %copy-start.23 = (f32[1024]{0:T(1024)S(1)}, f32[1024]{0:T(1024)}, u32[]{:S(2)}) copy-start(f32[1024]{0:T(1024)} %param.34) | copy-start | bytes 12292
  305.1 1.3 collective-permute-start.20
  326.9 6.1 %copy-start.30 = (bf16[64,2048]{1,0:T(8,128)(2,1)S(1)}, bf16[64,2048]{1,0:T(8,128)(2,1)}, u32[]{:S(2)}) copy-start(bf16[64,2048]{1,0:T(8,128)(2,1)} %reduce-scatter.3.cloned.1.call-done) | copy-start | bytes 786436
  326.9 7.1 %copy-start.13 = (f32[1024,1024]{1,0:T(8,128)S(1)}, f32[1024,1024]{1,0:T(8,128)}, u32[]{:S(2)}) copy-start(f32[1024,1024]{1,0:T(8,128)} %get-tuple-element.126) | copy-start | bytes 12582916
  326.9 20.8 %collective-permute-start.23 = (bf16[144,2048]{1,0:T(8,128)(2,1)}, bf16[144,2048]{1,0:T(8,128)(2,1)}, u32[]{:S(2)}, u32[]{:S(2)}) collective-permute-start(bf16[144,2048]{1,0:T(8,128)(2,1)} %get-tuple-element.156), channel_id=1, source_target_pairs={{0,1},{1,0},{2,3},{3,2},{4,5},{5,4},{6,7},{7,6},{8,9},{9,8},{10,11... | collective-permute-start | bytes 1769480 | tf_op jit(solution)/shard_map/ppermute | solution.py:698
  331.8 15.9 %collective-permute-start.22 = (bf16[128,2048]{1,0:T(8,128)(2,1)S(1)}, bf16[128,2048]{1,0:T(8,128)(2,1)}, u32[]{:S(2)}, u32[]{:S(2)}) collective-permute-start(bf16[128,2048]{1,0:T(8,128)(2,1)S(1)} %copy-done.29), channel_id=1, source_target_pairs={{0,4},{1,5},{2,6},{3,7},{4,0},{5,1},{6,2},{7,3},{8,12},{9,13},{10,... | collective-permute-start | bytes 1572872 | tf_op jit(solution)/shard_map/ppermute | solution.py:698
  333.0 9.4 %collective-permute-start.21 = (bf16[64,2048]{1,0:T(8,128)(2,1)S(1)}, bf16[64,2048]{1,0:T(8,128)(2,1)S(1)}, u32[]{:S(2)}, u32[]{:S(2)}) collective-permute-start(bf16[64,2048]{1,0:T(8,128)(2,1)S(1)} %copy-done.30), channel_id=1, source_target_pairs={{2,0},{0,1},{3,2},{1,3},{6,4},{4,5},{7,6},{5,7},{10,8},{8,9},{11,1... | collective-permute-start | bytes 786440 | tf_op jit(solution)/shard_map/ppermute | solution.py:682
  337.1 14.1 %copy-start.7 = (bf16[512,1024]{1,0:T(8,128)(2,1)S(1)}, bf16[512,1024]{1,0:T(8,128)(2,1)}, u32[]{:S(2)}) copy-start(bf16[512,1024]{1,0:T(8,128)(2,1)} %add_convert_fusion) | copy-start | bytes 3145732
  337.1 14.1 %copy-start.8 = (bf16[512,1024]{1,0:T(8,128)(2,1)S(1)}, bf16[512,1024]{1,0:T(8,128)(2,1)}, u32[]{:S(2)}) copy-start(bf16[512,1024]{1,0:T(8,128)(2,1)} %fusion.9) | copy-start | bytes 3145732
  342.4 5.3 %copy-start.12 = (bf16[64,2048]{1,0:T(8,128)(2,1)}, bf16[64,2048]{1,0:T(8,128)(2,1)S(1)}, u32[]{:S(2)}) copy-start(bf16[64,2048]{1,0:T(8,128)(2,1)S(1)} %collective-permute-done.21.refs_0_.first_ref) | copy-start | bytes 786436
  352.7 43.5 %collective-permute-start.24 = (bf16[1024,1024]{1,0:T(8,128)(2,1)}, bf16[1024,1024]{1,0:T(8,128)(2,1)S(1)}, u32[]{:S(2)}, u32[]{:S(2)}) collective-permute-start(bf16[1024,1024]{1,0:T(8,128)(2,1)} %pad_maximum_fusion), channel_id=1, source_target_pairs={{2,0},{0,1},{3,2},{1,3},{6,4},{4,5},{7,6},{5,7},{10,8},{8,9},{11,1... | collective-permute-start | bytes 6291464 | tf_op jit(solution)/shard_map/ppermute | solution.py:682
  354.1 37.9 %collective-permute-start.25 = (bf16[80,2048]{1,0:T(8,128)(2,1)}, bf16[80,2048]{1,0:T(8,128)(2,1)S(1)}, u32[]{:S(2)}, u32[]{:S(2)}) collective-permute-start(bf16[80,2048]{1,0:T(8,128)(2,1)} %get-tuple-element.165), channel_id=1, source_target_pairs={{2,0},{0,1},{3,2},{1,3},{6,4},{4,5},{7,6},{5,7},{10,8},{8,9},{11,1... | collective-permute-start | bytes 983048 | tf_op jit(solution)/shard_map/ppermute | solution.py:690
  354.2 37.9 %collective-permute-start.26 = (bf16[80,2048]{1,0:T(8,128)(2,1)}, bf16[80,2048]{1,0:T(8,128)(2,1)S(1)}, u32[]{:S(2)}, u32[]{:S(2)}) collective-permute-start(bf16[80,2048]{1,0:T(8,128)(2,1)} %get-tuple-element.166), channel_id=1, source_target_pairs={{10,0},{8,1},{11,2},{9,3},{14,4},{12,5},{15,6},{13,7},{2,8},{0,9},... | collective-permute-start | bytes 983048 | tf_op jit(solution)/shard_map/ppermute | solution.py:690
  355.1 37.0 %collective-permute-start.27 = (bf16[80,2048]{1,0:T(8,128)(2,1)}, bf16[80,2048]{1,0:T(8,128)(2,1)S(1)}, u32[]{:S(2)}, u32[]{:S(2)}) collective-permute-start(bf16[80,2048]{1,0:T(8,128)(2,1)} %get-tuple-element.167), channel_id=1, source_target_pairs={{18,0},{16,1},{19,2},{17,3},{22,4},{20,5},{23,6},{21,7},{26,8},{24... | collective-permute-start | bytes 983048 | tf_op jit(solution)/shard_map/ppermute | solution.py:690
  357.9 34.2 %collective-permute-start.28 = (bf16[80,2048]{1,0:T(8,128)(2,1)}, bf16[80,2048]{1,0:T(8,128)(2,1)S(1)}, u32[]{:S(2)}, u32[]{:S(2)}) collective-permute-start(bf16[80,2048]{1,0:T(8,128)(2,1)} %get-tuple-element.168), channel_id=1, source_target_pairs={{26,0},{24,1},{27,2},{25,3},{30,4},{28,5},{31,6},{29,7},{18,8},{16... | collective-permute-start | bytes 983048 | tf_op jit(solution)/shard_map/ppermute | solution.py:690
  395.2 4.5 %collective-permute-start.29 = (f32[8,2048]{1,0:T(8,128)}, f32[8,2048]{1,0:T(8,128)S(1)}, u32[]{:S(2)}, u32[]{:S(2)}) collective-permute-start(f32[8,2048]{1,0:T(8,128)} %get-tuple-element.169), channel_id=1, source_target_pairs={{0,4},{1,5},{2,6},{3,7},{4,0},{5,1},{6,2},{7,3},{8,12},{9,13},{10,... | collective-permute-start | bytes 196616 | tf_op jit(solution)/shard_map/ppermute | solution.py:698
  (18 other events, 40.1 us)
Sparse Core Ops, SparseCore 0:
  10.8 53.2 all-gather.3
  66.8 49.0 all-gather.5
  118.6 71.8 all-gather.7
  245.5 26.9 reduce-scatter.2
  291.8 96.5 reduce-scatter.4

commit v9 on v8

--- a/solution.py
+++ b/solution.py
@@ -901,7 +901,7 @@
     filled = sums.shape[0]
     sums = jnp.pad(sums, (0, -filled % (8 * columns))).reshape(-1, columns)
     sums = core_sum(sums)
-    state = scatter_near(pieces, None, [sums])
+    state = scatter_near(pieces, own_output, [sums])
     first_mlp, state = lax.optimization_barrier((first_mlp, state))
     first_mlp = swap(first_mlp, inverse=True)
     last_sums = far_sums(state, [sums], first_mlp)

time: 416 us -> 417 us (level)
  the two profiles are of different devices: /device:TPU:0 before, /device:TPU:10 now
where the time goes in v9:
time: 417 us; the launch traced here: 409 us
  waiting for transfers between devices  168 us (40%)
  Pallas kernels  155 us (37%)
  other arithmetic  24.3 us (6%)
  starting transfers between devices  23.1 us (6%)
  local copies, waits for them, and re-layouts  16.1 us (4%)
  between operations  14.7 us (4%)
  matrix products  7.61 us (2%)
    ppermute x9, waiting for transfers between devices, swap(): return lax.ppermute(values, SWAP, pairs)  100 us
    pallas_call x2, Pallas kernels, mlp(): pl.pallas_call(functools.partial(mlp_kernel, block=min(ROWS, length), wit...  48.4 us
    reduce_scatter x1, waiting for transfers between devices, per_device(): lax.psum_scatter(second_grads, ('z', 'y', 'c'), scatter_dimension=0, tile...  30.4 us
    ppermute x10, waiting for transfers between devices, hop(): return lax.ppermute(values, ('z', 'y', 'c', 'h'), pairs)  27.7 us
    pallas_call x1, Pallas kernels, attn_backward(): pl.pallas_call(without(functools.partial(attn_backward_kernel, block=bloc...  24.3 us
    pallas_call x1, Pallas kernels, attn_forward(): pl.pallas_call(functools.partial(attn_forward_kernel, block=block), grid=...  16.4 us
    pallas_call x6, Pallas kernels, sums_call(): pl.pallas_call(body, in_specs=([pl.BlockSpec(memory_space=pl.ANY)] if aft...  15.9 us
    pallas_call x2, Pallas kernels, norm_rows(): pl.pallas_call(functools.partial(norm_kernel, residual=residual), grid=(l...  12.9 us
  transfers between devices with their start and end apart: 35, of which 17 were waited for; matrix products, arithmetic and copies ran while one was open for 10% of the time, Pallas kernels for 36%

profile of v9, /device:TPU:10, one launch (start us, length us, event | category | flops | bytes accessed | tf_op | source)
XLA Modules:
  0.0 408.8 jit_solution(1643682759137207135)
XLA Ops:
  7.2 1.7 pad_maximum_fusion.1
  9.0 1.8 mlp_shards.1
  11.5 12.6 %collective-permute-done = bf16[512,1024]{1,0:T(8,128)(2,1)S(1)} collective-permute-done((bf16[512,1024]{1,0:T(8,128)(2,1)}, bf16[512,1024]{1,0:T(8,128)(2,1)S(1)}, u32[]{:S(2)}, u32[]{:S(2)}) %collective-permute-start) | collective-permute-done | bytes 1048608 | tf_op jit(solution)/shard_map/ppermute | solution.py:682
  25.0 10.3 %collective-permute-done.3 = bf16[512,1024]{1,0:T(8,128)(2,1)S(1)} collective-permute-done((bf16[512,1024]{1,0:T(8,128)(2,1)}, bf16[512,1024]{1,0:T(8,128)(2,1)S(1)}, u32[]{:S(2)}, u32[]{:S(2)}) %collective-permute-start.3) | collective-permute-done | bytes 1048608 | tf_op jit(solution)/shard_map/ppermute | solution.py:682
  35.8 1.9 collective-permute-start.5
  37.7 4.2 %collective-permute-done.5 = bf16[64,2048]{1,0:T(8,128)(2,1)S(1)} collective-permute-done((bf16[64,2048]{1,0:T(8,128)(2,1)}, bf16[64,2048]{1,0:T(8,128)(2,1)S(1)}, u32[]{:S(2)}, u32[]{:S(2)}) %collective-permute-start.5) | collective-permute-done | bytes 262176 | tf_op jit(solution)/shard_map/ppermute | solution.py:682
  41.9 2.4 collective-permute-start.6
  44.3 6.3 %collective-permute-done.6 = bf16[64,2048]{1,0:T(8,128)(2,1)} collective-permute-done((bf16[64,2048]{1,0:T(8,128)(2,1)S(1)}, bf16[64,2048]{1,0:T(8,128)(2,1)}, u32[]{:S(2)}, u32[]{:S(2)}) %collective-permute-start.6) | collective-permute-done | bytes 262176 | tf_op jit(solution)/shard_map/ppermute | solution.py:698
  50.6 1.9 maximum_select_fusion.2
  52.6 2.3 maximum_select_fusion.refs_0_
  54.9 3.3 maximum_select_fusion.1.g_ref
  58.2 5.5 %norm_one.1 = (bf16[1024,1024]{1,0:T(8,128)(2,1)}, bf16[1024,1024]{1,0:T(8,128)(2,1)}) custom-call(bf16[1024,1024]{1,0:T(8,128)(2,1)} %maximum_select_fusion.refs_0_, f32[1,1024]{1,0:T(1,128)} %bitcast.39, f32[1,1024]{1,0:T(1,128)} %bitcast.46), custom_call_target="tpu_custom_call" | custom-call | flops 20971520 | bytes 14680064 | tf_op jit(solution)/shard_map/norm_one/pallas_call | solution.py:276
  64.8 45.5 %collective-permute-done.7.w_ref.refs_1_ = bf16[1024,2048]{1,0:T(8,128)(2,1)} collective-permute-done((bf16[1024,2048]{1,0:T(8,128)(2,1)}, bf16[1024,2048]{1,0:T(8,128)(2,1)}, u32[]{:S(2)}, u32[]{:S(2)}) %collective-permute-start.7) | collective-permute-done | bytes 4194336 | tf_op jit(solution)/shard_map/ppermute | solution.py:682
  110.3 7.2 %qkv_project.1.q_ref.k_ref.v_ref.refs_2_.refs_3_.refs_4_ = bf16[1024,1536]{1,0:T(8,128)(2,1)} custom-call(bf16[1024,1024]{1,0:T(8,128)(2,1)} %get-tuple-element.100.n_ref, f32[1,1536]{1,0:T(1,128)} %reshape.108.b_ref, bf16[1024,2048]{1,0:T(8,128)(2,1)} %collective-permute-done.7.w_ref.refs_1_), custom_call_target="tpu_custom_call" | custom-call | flops 3221225472 | bytes 8388608 | tf_op jit(solution)/shard_map/qkv_project/pallas_call | solution.py:457
  117.5 2.5 collective-permute-start.9
  121.0 16.4 %attn_forward.1 = (bf16[1024,512]{1,0:T(8,128)(2,1)}, f32[4,8,1024]{2,1,0:T(8,128)}) custom-call(s32[1024,1]{1,0:T(8,128)} %copy.37.seg_col.refs_0_, s32[1,1024]{1,0:T(1,128)} %bitcast.41, bf16[1024,1536]{1,0:T(8,128)(2,1)} %qkv_project.1.q_ref.k_ref.v_ref.refs_2_.refs_3_.refs_4_, bf16[1024,1536]{1,0:T(8,128)(2,1)} %qkv_project.1.q_ref.k_ref.v_ref.refs_2_.refs_3_.refs_4_, ...), custom_call_target="tpu_custom_call" | custom-call | flops 2147483648 | bytes 4194304 | tf_op jit(solution)/shard_map/attn_forward/pallas_call | solution.py:157
  137.4 4.2 %convolution_convert_fusion.refs_1_ = bf16[1024,1024]{1,0:T(8,128)(2,1)} fusion(bf16[1024,512]{1,0:T(8,128)(2,1)} %get-tuple-element.103.refs_5_.mixed_ref, bf16[1024,2048]{1,0:T(8,128)(2,1)} %collective-permute-done.7.w_ref.refs_1_), kind=kOutput, calls=%fused_computation.22 | convolution fusion | flops 1074790400 | bytes 4194304 | tf_op jit(solution)/shard_map/dot_general | solution.py:45
  142.8 2.5 copy.39.gt_ref
  146.0 7.4 %norm_two.1 = (bf16[1024,1024]{1,0:T(8,128)(2,1)}, bf16[1024,1024]{1,0:T(8,128)(2,1)}, f32[1024,1024]{1,0:T(8,128)}) custom-call(bf16[1024,1024]{1,0:T(8,128)(2,1)} %maximum_select_fusion.refs_0_, bf16[1024,1024]{1,0:T(8,128)(2,1)} %convolution_convert_fusion.refs_1_, bf16[1024,1024]{1,0:T(8,128)(2,1)} %collective-permute-done.8.refs_2_, ...), custom_call_target="tpu_custom_call" | custom-call | flops 20971520 | bytes 14680064 | tf_op jit(solution)/shard_map/norm_two/pallas_call | solution.py:276
  153.4 12.9 %collective-permute-done.9.w_ref = bf16[1024,2048]{1,0:T(8,128)(2,1)} collective-permute-done((bf16[1024,2048]{1,0:T(8,128)(2,1)}, bf16[1024,2048]{1,0:T(8,128)(2,1)}, u32[]{:S(2)}, u32[]{:S(2)}) %collective-permute-start.9) | collective-permute-done | bytes 4194336 | tf_op jit(solution)/shard_map/ppermute | solution.py:682
  166.3 23.7 %mlp_first.1 = (bf16[1024,1024]{1,0:T(8,128)(2,1)}, bf16[1024,1024]{1,0:T(8,128)(2,1)}, bf16[256,2048]{1,0:T(8,128)(2,1)}, bf16[256,2048]{1,0:T(8,128)(2,1)}, bf...) custom-call(s32[16]{0:T(128)} %stack.67.order, ...), custom_call_target="tpu_custom_call" | custom-call | flops 12884901888 | bytes 20971520 | tf_op jit(solution)/shard_map/mlp_first/pallas_call | solution.py:403
  190.1 2.5 collective-permute-start.11
  194.1 24.7 %mlp_second.1 = (bf16[1024,1024]{1,0:T(8,128)(2,1)}, bf16[1024,1024]{1,0:T(8,128)(2,1)}, bf16[1024,2048]{1,0:T(8,128)(2,1)}, f32[1,1024]{1,0:T(1,128)}) custom-call(s32[16]{0:T(128)} %stack.67.order, bf16[1024,1024]{1,0:T(8,128)(2,1)} %get-tuple-element.105.n_ref, bf16[1024,1024]{1,0:T(8,128)(2,1)} %copy-done, bf16[1024,1024]{1,0:T(8,128)(2,1)} %get-tuple-element.107.nt_ref, ...), custom_call_target="tpu_custom_call" | custom-call | flops 12884901888 | bytes 20971520 | tf_op jit(solution)/shard_map/mlp_second/pallas_call | solution.py:403
  220.1 3.1 sums_one.2
  223.9 3.5 collective-permute-done.13.other_ref
  228.7 9.1 %norm_two_back.1 = (f32[1024,1024]{1,0:T(8,128)}, bf16[1024,1024]{1,0:T(8,128)(2,1)}, bf16[1024,1024]{1,0:T(8,128)(2,1)}, f32[8,1024]{1,0:T(8,128)}) custom-call(f32[1024,1024]{1,0:T(8,128)} %get-tuple-element.104.hidden_ref, bf16[1024,1024]{1,0:T(8,128)(2,1)} %copy-done, bf16[1024,1024]{1,0:T(8,128)(2,1)} %get-tuple-element.125.refs_0_.own_ref, ...), custom_call_target="tpu_custom_call" | custom-call | flops 31457280 | bytes 16777216 | tf_op jit(solution)/shard_map/norm_two_back/pallas_call | solution.py:316
  238.6 3.7 sums_two_z.1.refs_8_
  242.5 3.4 convolution_convert_fusion.1.refs_7_
  245.9 24.3 %attn_backward.1.grads_ref.order_only.refs_0_ = bf16[3,1024,512]{2,1,0:T(8,128)(2,1)} custom-call(s32[1024,1]{1,0:T(8,128)} %copy.37.seg_col.refs_0_, s32[1,1024]{1,0:T(1,128)} %bitcast.42, bf16[1024,1536]{1,0:T(8,128)(2,1)} %qkv_project.1.q_ref.k_ref.v_ref.refs_2_.refs_3_.refs_4_, bf16[1024,1536]{1,0:T(8,128)(2,1)} %qkv_project.1.q_ref.k_ref.v_ref.refs_2_.refs_3_.refs_4_, ...), custom_call_target="tpu_custom_call" | custom-call | flops 5368709120 | bytes 8388608 | tf_op jit(solution)/shard_map/attn_backward/pallas_call | solution.py:186
  270.2 10.2 %weight_grads.1 = (bf16[256,2048]{1,0:T(8,128)(2,1)}, bf16[256,2048]{1,0:T(8,128)(2,1)}, bf16[128,2048]{1,0:T(8,128)(2,1)}, bf16[128,2048]{1,0:T(8,128)(2,1)}, bf16[256,2048]{1,0:T(8,128)(2,1)}) custom-call(s32[16]{0:T(128)} %stack.67.order, bf16[1024,1024]{1,0:T(8,128)(2,1)} %get-tuple-element.137.nt_ref, ...), custom_call_target="tpu_custom_call" | custom-call | flops 4294967296 | bytes 12582912 | tf_op jit(solution)/shard_map/weight_grads/pallas_call | solution.py:502
  280.3 7.4 %qkv_back.1 = bf16[1024,1024]{1,0:T(8,128)(2,1)} custom-call(bf16[3,1024,512]{2,1,0:T(8,128)(2,1)} %attn_backward.1.grads_ref.order_only.refs_0_, bf16[1024,2048]{1,0:T(8,128)(2,1)} %collective-permute-done.7.w_ref.refs_1_, bf16[256,2048]{1,0:T(8,128)(2,1)} %get-tuple-element.139.refs_2_), custom_call_target="tpu_custom_call" | custom-call | flops 3221225472 | bytes 8388608 | tf_op jit(solution)/shard_map/qkv_back/pallas_call | solution.py:543
  287.7 3.4 collective-permute-done.16
  296.8 2.0 convert_reduce_fusion.2
  299.6 2.4 fusion.10
  302.2 3.9 add_convert_fusion.refs_0_
  306.7 14.4 %collective-permute-done.19.refs_2_ = bf16[256,2048]{1,0:T(8,128)(2,1)} collective-permute-done((bf16[256,2048]{1,0:T(8,128)(2,1)}, bf16[256,2048]{1,0:T(8,128)(2,1)}, u32[]{:S(2)}, u32[]{:S(2)}) %collective-permute-start.19) | collective-permute-done | bytes 1048608 | tf_op jit(solution)/shard_map/ppermute | solution.py:698
  321.1 3.4 sums_one.3
  326.9 3.8 fusion.9
  330.7 11.1 %collective-permute-done.21.refs_0_.first_ref = bf16[64,2048]{1,0:T(8,128)(2,1)S(1)} collective-permute-done((bf16[64,2048]{1,0:T(8,128)(2,1)}, bf16[64,2048]{1,0:T(8,128)(2,1)S(1)}, u32[]{:S(2)}, u32[]{:S(2)}) %collective-permute-start.21) | collective-permute-done | bytes 262176 | tf_op jit(solution)/shard_map/ppermute | solution.py:682
  341.8 4.2 %collective-permute-done.22.refs_4_ = bf16[128,2048]{1,0:T(8,128)(2,1)} collective-permute-done((bf16[128,2048]{1,0:T(8,128)(2,1)}, bf16[128,2048]{1,0:T(8,128)(2,1)}, u32[]{:S(2)}, u32[]{:S(2)}) %collective-permute-start.22) | collective-permute-done | bytes 524320 | tf_op jit(solution)/shard_map/ppermute | solution.py:698
  346.0 3.5 sums_two.1
  349.5 1.5 pad_maximum_fusion
  351.9 3.4 collective-permute-start.27
  355.4 30.4 %reduce-scatter.5.cloned.1.call-done.second_ref = bf16[64,2048]{1,0:T(8,128)(2,1)} async-done(((bf16[1024,2048]{1,0:T(8,128)(2,1)}), bf16[64,2048]{1,0:T(8,128)(2,1)}) %reduce-scatter.5.cloned.1.call-update) | async-done | bytes 262160 | tf_op jit(solution)/shard_map/reduce_scatter | solution.py:878
  385.8 2.1 units_last.1
  388.5 4.7 %collective-permute-done.28.refs_4_ = bf16[80,2048]{1,0:T(8,128)(2,1)S(1)} collective-permute-done((bf16[80,2048]{1,0:T(8,128)(2,1)}, bf16[80,2048]{1,0:T(8,128)(2,1)S(1)}, u32[]{:S(2)}, u32[]{:S(2)}) %collective-permute-start.28) | collective-permute-done | bytes 327712 | tf_op jit(solution)/shard_map/ppermute | solution.py:690
  393.9 2.1 sums_last.1
  398.1 2.4 collective-permute-done.29
  (152 shorter events, 27.4 us)
Async XLA Ops:
  7.2 56.6 %all-gather.4.cloned.1.call-start = ((), (), s32[]{:S(2)}) async-start(), calls=%async_computation.2 | async-start | bytes 4456448 | tf_op jit(solution)/shard_map/all_gather | solution.py:815
  8.9 108.6 %all-gather.6.cloned.1.call-start = ((), (), s32[]{:S(2)}) async-start(), calls=%async_computation.3 | async-start | bytes 4456448 | tf_op jit(solution)/shard_map/all_gather | solution.py:818
  10.8 179.2 %all-gather.8.cloned.1.call-start = ((), (), s32[]{:S(2)}) async-start(), calls=%async_computation.4 | async-start | bytes 4718592 | tf_op jit(solution)/shard_map/all_gather | solution.py:837
  10.9 13.2 %collective-permute-start = (bf16[512,1024]{1,0:T(8,128)(2,1)}, bf16[512,1024]{1,0:T(8,128)(2,1)S(1)}, u32[]{:S(2)}, u32[]{:S(2)}) collective-permute-start(bf16[512,1024]{1,0:T(8,128)(2,1)} %param.18), channel_id=1, source_target_pairs={{0,2},{1,0},{2,3},{3,1},{4,6},{5,4},{6,7},{7,5},{8,10},{9,8},{10,1... | collective-permute-start | bytes 3145736 | tf_op jit(solution)/shard_map/ppermute | solution.py:682
  11.4 23.9 %collective-permute-start.3 = (bf16[512,1024]{1,0:T(8,128)(2,1)}, bf16[512,1024]{1,0:T(8,128)(2,1)S(1)}, u32[]{:S(2)}, u32[]{:S(2)}) collective-permute-start(bf16[512,1024]{1,0:T(8,128)(2,1)} %param.35), channel_id=1, source_target_pairs={{0,2},{1,0},{2,3},{3,1},{4,6},{5,4},{6,7},{7,5},{8,10},{9,8},{10,1... | collective-permute-start | bytes 3145736 | tf_op jit(solution)/shard_map/ppermute | solution.py:682
  24.1 28.5 %collective-permute-start.1 = (bf16[512,1024]{1,0:T(8,128)(2,1)S(1)}, bf16[512,1024]{1,0:T(8,128)(2,1)S(1)}, u32[]{:S(2)}, u32[]{:S(2)}) collective-permute-start(bf16[512,1024]{1,0:T(8,128)(2,1)S(1)} %collective-permute-done), channel_id=1, source_target_pairs={{0,2},{2,0},{1,3},{3,1},{4,6},{6,4},{5,7},{7,5},{8,10},{10,8},{9,1... | collective-permute-start | bytes 3145736 | tf_op jit(solution)/shard_map/ppermute | solution.py:773
  35.3 19.6 %copy-start.4 = (bf16[512,1024]{1,0:T(8,128)(2,1)}, bf16[512,1024]{1,0:T(8,128)(2,1)S(1)}, u32[]{:S(2)}) copy-start(bf16[512,1024]{1,0:T(8,128)(2,1)S(1)} %collective-permute-done.3) | copy-start | bytes 3145732
  35.3 19.6 %collective-permute-start.4 = (bf16[512,1024]{1,0:T(8,128)(2,1)S(1)}, bf16[512,1024]{1,0:T(8,128)(2,1)}, u32[]{:S(2)}, u32[]{:S(2)}) collective-permute-start(bf16[512,1024]{1,0:T(8,128)(2,1)S(1)} %collective-permute-done.3), channel_id=1, source_target_pairs={{0,2},{2,0},{1,3},{3,1},{4,6},{6,4},{5,7},{7,5},{8,10},{10,8},{9,1... | collective-permute-start | bytes 3145736 | tf_op jit(solution)/shard_map/ppermute | solution.py:773
  35.8 6.1 %collective-permute-start.5 = (bf16[64,2048]{1,0:T(8,128)(2,1)}, bf16[64,2048]{1,0:T(8,128)(2,1)S(1)}, u32[]{:S(2)}, u32[]{:S(2)}) collective-permute-start(bf16[64,2048]{1,0:T(8,128)(2,1)} %get-tuple-element.97), channel_id=1, source_target_pairs={{0,2},{1,0},{2,3},{3,1},{4,6},{5,4},{6,7},{7,5},{8,10},{9,8},{10,1... | collective-permute-start | bytes 786440 | tf_op jit(solution)/shard_map/ppermute | solution.py:682
  41.9 8.8 %collective-permute-start.6 = (bf16[64,2048]{1,0:T(8,128)(2,1)S(1)}, bf16[64,2048]{1,0:T(8,128)(2,1)}, u32[]{:S(2)}, u32[]{:S(2)}) collective-permute-start(bf16[64,2048]{1,0:T(8,128)(2,1)S(1)} %collective-permute-done.5), channel_id=1, source_target_pairs={{0,1},{1,0},{2,3},{3,2},{4,5},{5,4},{6,7},{7,6},{8,9},{9,8},{10,11... | collective-permute-start | bytes 786440 | tf_op jit(solution)/shard_map/ppermute | solution.py:698
  44.3 19.5 %collective-permute-start.2 = (s32[1024]{0:T(1024)}, s32[1024]{0:T(1024)S(1)}, u32[]{:S(2)}, u32[]{:S(2)}) collective-permute-start(s32[1024]{0:T(1024)} %param.19), channel_id=1, source_target_pairs={{0,2},{1,0},{2,3},{3,1},{4,6},{5,4},{6,7},{7,5},{8,10},{9,8},{10,1... | collective-permute-start | bytes 12296 | tf_op jit(solution)/shard_map/ppermute | solution.py:682
  58.2 84.6 %copy-start = (bf16[1024,1024]{1,0:T(8,128)(2,1)}, bf16[1024,1024]{1,0:T(8,128)(2,1)S(1)}, u32[]{:S(2)}) copy-start(bf16[1024,1024]{1,0:T(8,128)(2,1)S(1)} %maximum_select_fusion.1.g_ref) | copy-start | bytes 6291460
  58.2 5.8 %copy-start.26 = (f32[1024]{0:T(1024)S(1)}, f32[1024]{0:T(1024)}, u32[]{:S(2)}) copy-start(f32[1024]{0:T(1024)} %param.25) | copy-start | bytes 12292
  58.2 5.9 %copy-start.27 = (f32[1024]{0:T(1024)S(1)}, f32[1024]{0:T(1024)}, u32[]{:S(2)}) copy-start(f32[1024]{0:T(1024)} %param.26) | copy-start | bytes 12292
  63.7 56.2 %copy-start.20 = (s32[1024]{0:T(1024)}, s32[1024]{0:T(1024)S(1)}, u32[]{:S(2)}) copy-start(s32[1024]{0:T(1024)S(1)} %collective-permute-done.2) | copy-start | bytes 12292
  63.8 46.5 %collective-permute-start.7 = (bf16[1024,2048]{1,0:T(8,128)(2,1)}, bf16[1024,2048]{1,0:T(8,128)(2,1)}, u32[]{:S(2)}, u32[]{:S(2)}) collective-permute-start(bf16[1024,2048]{1,0:T(8,128)(2,1)} %all-gather.4.cloned.1.call-done), channel_id=1, source_target_pairs={{0,2},{1,0},{2,3},{3,1},{4,6},{5,4},{6,7},{7,5},{8,10},{9,8},{10,1... | collective-permute-start | bytes 12582920 | tf_op jit(solution)/shard_map/ppermute | solution.py:682
  64.0 223.8 %reduce-scatter.3.cloned.1.call-start = ((), (), s32[]{:S(2)}) async-start(), calls=%async_computation.5 | async-start | bytes 1310720 | tf_op jit(solution)/shard_map/reduce_scatter | solution.py:870
  117.5 48.8 %collective-permute-start.9 = (bf16[1024,2048]{1,0:T(8,128)(2,1)}, bf16[1024,2048]{1,0:T(8,128)(2,1)}, u32[]{:S(2)}, u32[]{:S(2)}) collective-permute-start(bf16[1024,2048]{1,0:T(8,128)(2,1)} %all-gather.6.cloned.1.call-done), channel_id=1, source_target_pairs={{0,2},{1,0},{2,3},{3,1},{4,6},{5,4},{6,7},{7,5},{8,10},{9,8},{10,1... | collective-permute-start | bytes 12582920 | tf_op jit(solution)/shard_map/ppermute | solution.py:682
  137.4 4.8 %copy-start.23 = (f32[4096]{0:T(1024)S(1)}, f32[4096]{0:T(1024)}, u32[]{:S(2)}) copy-start(f32[4096]{0:T(1024)} %param.32) | copy-start | bytes 49156
  141.5 4.5 %collective-permute-start.8 = (bf16[1024,1024]{1,0:T(8,128)(2,1)}, bf16[1024,1024]{1,0:T(8,128)(2,1)}, u32[]{:S(2)}, u32[]{:S(2)}) collective-permute-start(bf16[1024,1024]{1,0:T(8,128)(2,1)} %convolution_convert_fusion.refs_1_), channel_id=1, source_target_pairs={{0,2},{2,0},{1,3},{3,1},{4,6},{6,4},{5,7},{7,5},{8,10},{10,8},{9,1... | collective-permute-start | bytes 6291464 | tf_op jit(solution)/shard_map/ppermute | solution.py:773
  190.1 28.7 %collective-permute-start.11 = (bf16[256,2048]{1,0:T(8,128)(2,1)}, bf16[256,2048]{1,0:T(8,128)(2,1)S(1)}, u32[]{:S(2)}, u32[]{:S(2)}) collective-permute-start(bf16[256,2048]{1,0:T(8,128)(2,1)} %get-tuple-element.118), channel_id=1, source_target_pairs={{0,1},{1,0},{2,3},{3,2},{4,5},{5,4},{6,7},{7,6},{8,9},{9,8},{10,11... | collective-permute-start | bytes 3145736 | tf_op jit(solution)/shard_map/ppermute | solution.py:698
  192.6 26.1 %collective-permute-start.12 = (bf16[256,2048]{1,0:T(8,128)(2,1)}, bf16[256,2048]{1,0:T(8,128)(2,1)S(1)}, u32[]{:S(2)}, u32[]{:S(2)}) collective-permute-start(bf16[256,2048]{1,0:T(8,128)(2,1)} %get-tuple-element.119), channel_id=1, source_target_pairs={{0,4},{1,5},{2,6},{3,7},{4,0},{5,1},{6,2},{7,3},{8,12},{9,13},{10,... | collective-permute-start | bytes 3145736 | tf_op jit(solution)/shard_map/ppermute | solution.py:698
  223.2 4.2 %collective-permute-start.13 = (bf16[1024,1024]{1,0:T(8,128)(2,1)S(1)}, bf16[1024,1024]{1,0:T(8,128)(2,1)S(1)}, u32[]{:S(2)}, u32[]{:S(2)}) collective-permute-start(bf16[1024,1024]{1,0:T(8,128)(2,1)S(1)} %copy-done.2), channel_id=1, source_target_pairs={{0,2},{2,0},{1,3},{3,1},{4,6},{6,4},{5,7},{7,5},{8,10},{10,8},{9,1... | collective-permute-start | bytes 6291464 | tf_op jit(solution)/shard_map/ppermute | solution.py:773
  223.2 14.6 %collective-permute-start.14 = (bf16[128,2048]{1,0:T(8,128)(2,1)}, bf16[128,2048]{1,0:T(8,128)(2,1)S(1)}, u32[]{:S(2)}, u32[]{:S(2)}) collective-permute-start(bf16[128,2048]{1,0:T(8,128)(2,1)} %get-tuple-element.131), channel_id=1, source_target_pairs={{0,4},{1,5},{2,6},{3,7},{4,0},{5,1},{6,2},{7,3},{8,12},{9,13},{10,... | collective-permute-start | bytes 1572872 | tf_op jit(solution)/shard_map/ppermute | solution.py:698
  223.8 14.3 %collective-permute-start.15 = (bf16[128,2048]{1,0:T(8,128)(2,1)}, bf16[128,2048]{1,0:T(8,128)(2,1)}, u32[]{:S(2)}, u32[]{:S(2)}) collective-permute-start(bf16[128,2048]{1,0:T(8,128)(2,1)} %get-tuple-element.132), channel_id=1, source_target_pairs={{0,1},{1,0},{2,3},{3,2},{4,5},{5,4},{6,7},{7,6},{8,9},{9,8},{10,11... | collective-permute-start | bytes 1572872 | tf_op jit(solution)/shard_map/ppermute | solution.py:698
  242.3 48.8 %collective-permute-start.16 = (bf16[1024,2048]{1,0:T(8,128)(2,1)}, bf16[1024,2048]{1,0:T(8,128)(2,1)}, u32[]{:S(2)}, u32[]{:S(2)}) collective-permute-start(bf16[1024,2048]{1,0:T(8,128)(2,1)} %get-tuple-element.134), channel_id=1, source_target_pairs={{2,0},{0,1},{3,2},{1,3},{6,4},{4,5},{7,6},{5,7},{10,8},{8,9},{11,1... | collective-permute-start | bytes 12582920 | tf_op jit(solution)/shard_map/ppermute | solution.py:682
  242.4 143.4 %reduce-scatter.5.cloned.1.call-start = ((), (), s32[]{:S(2)}) async-start(), calls=%async_computation.6 | async-start | bytes 4456448 | tf_op jit(solution)/shard_map/reduce_scatter | solution.py:878
  293.7 5.8 %collective-permute-start.17 = (bf16[512,1024]{1,0:T(8,128)(2,1)}, bf16[512,1024]{1,0:T(8,128)(2,1)}, u32[]{:S(2)}, u32[]{:S(2)}) collective-permute-start(bf16[512,1024]{1,0:T(8,128)(2,1)} %constant_dynamic-slice_fusion.1), channel_id=1, source_target_pairs={{0,2},{2,0},{1,3},{3,1},{4,6},{6,4},{5,7},{7,5},{8,10},{10,8},{9,1... | collective-permute-start | bytes 3145736 | tf_op jit(solution)/shard_map/ppermute | solution.py:773
  294.0 5.6 %copy-start.19 = (f32[1024]{0:T(1024)S(1)}, f32[1024]{0:T(1024)}, u32[]{:S(2)}) copy-start(f32[1024]{0:T(1024)} %param.20) | copy-start | bytes 12292
  295.0 7.2 %collective-permute-start.10 = (bf16[512,1024]{1,0:T(8,128)(2,1)}, bf16[512,1024]{1,0:T(8,128)(2,1)}, u32[]{:S(2)}, u32[]{:S(2)}) collective-permute-start(bf16[512,1024]{1,0:T(8,128)(2,1)} %constant_dynamic-slice_fusion), channel_id=1, source_target_pairs={{0,2},{2,0},{1,3},{3,1},{4,6},{6,4},{5,7},{7,5},{8,10},{10,8},{9,1... | collective-permute-start | bytes 3145736 | tf_op jit(solution)/shard_map/ppermute | solution.py:773
  295.5 25.6 %collective-permute-start.18 = (bf16[256,2048]{1,0:T(8,128)(2,1)}, bf16[256,2048]{1,0:T(8,128)(2,1)}, u32[]{:S(2)}, u32[]{:S(2)}) collective-permute-start(bf16[256,2048]{1,0:T(8,128)(2,1)} %get-tuple-element.139.refs_2_), channel_id=1, source_target_pairs={{0,1},{1,0},{2,3},{3,2},{4,5},{5,4},{6,7},{7,6},{8,9},{9,8},{10,11... | collective-permute-start | bytes 3145736 | tf_op jit(solution)/shard_map/ppermute | solution.py:698
  295.6 25.5 %collective-permute-start.19 = (bf16[256,2048]{1,0:T(8,128)(2,1)}, bf16[256,2048]{1,0:T(8,128)(2,1)}, u32[]{:S(2)}, u32[]{:S(2)}) collective-permute-start(bf16[256,2048]{1,0:T(8,128)(2,1)} %get-tuple-element.142), channel_id=1, source_target_pairs={{0,4},{1,5},{2,6},{3,7},{4,0},{5,1},{6,2},{7,3},{8,12},{9,13},{10,... | collective-permute-start | bytes 3145736 | tf_op jit(solution)/shard_map/ppermute | solution.py:698
  302.1 4.0 collective-permute-start.20
  324.5 21.5 %collective-permute-start.23 = (bf16[144,2048]{1,0:T(8,128)(2,1)}, bf16[144,2048]{1,0:T(8,128)(2,1)}, u32[]{:S(2)}, u32[]{:S(2)}) collective-permute-start(bf16[144,2048]{1,0:T(8,128)(2,1)} %get-tuple-element.156), channel_id=1, source_target_pairs={{0,1},{1,0},{2,3},{3,2},{4,5},{5,4},{6,7},{7,6},{8,9},{9,8},{10,11... | collective-permute-start | bytes 1769480 | tf_op jit(solution)/shard_map/ppermute | solution.py:698
  325.8 20.1 %collective-permute-start.22 = (bf16[128,2048]{1,0:T(8,128)(2,1)}, bf16[128,2048]{1,0:T(8,128)(2,1)}, u32[]{:S(2)}, u32[]{:S(2)}) collective-permute-start(bf16[128,2048]{1,0:T(8,128)(2,1)} %get-tuple-element.155), channel_id=1, source_target_pairs={{0,4},{1,5},{2,6},{3,7},{4,0},{5,1},{6,2},{7,3},{8,12},{9,13},{10,... | collective-permute-start | bytes 1572872 | tf_op jit(solution)/shard_map/ppermute | solution.py:698
  326.9 14.9 %collective-permute-start.21 = (bf16[64,2048]{1,0:T(8,128)(2,1)}, bf16[64,2048]{1,0:T(8,128)(2,1)S(1)}, u32[]{:S(2)}, u32[]{:S(2)}) collective-permute-start(bf16[64,2048]{1,0:T(8,128)(2,1)} %reduce-scatter.3.cloned.1.call-done), channel_id=1, source_target_pairs={{2,0},{0,1},{3,2},{1,3},{6,4},{4,5},{7,6},{5,7},{10,8},{8,9},{11,1... | collective-permute-start | bytes 786440 | tf_op jit(solution)/shard_map/ppermute | solution.py:682
  330.7 18.8 %copy-start.1 = (bf16[512,1024]{1,0:T(8,128)(2,1)S(1)}, bf16[512,1024]{1,0:T(8,128)(2,1)}, u32[]{:S(2)}) copy-start(bf16[512,1024]{1,0:T(8,128)(2,1)} %add_convert_fusion.refs_0_) | copy-start | bytes 3145732
  330.7 18.8 %copy-start.8 = (bf16[512,1024]{1,0:T(8,128)(2,1)S(1)}, bf16[512,1024]{1,0:T(8,128)(2,1)}, u32[]{:S(2)}) copy-start(bf16[512,1024]{1,0:T(8,128)(2,1)} %fusion.9) | copy-start | bytes 3145732
  351.0 45.6 %collective-permute-start.24 = (bf16[1024,1024]{1,0:T(8,128)(2,1)}, bf16[1024,1024]{1,0:T(8,128)(2,1)S(1)}, u32[]{:S(2)}, u32[]{:S(2)}) collective-permute-start(bf16[1024,1024]{1,0:T(8,128)(2,1)} %pad_maximum_fusion), channel_id=1, source_target_pairs={{2,0},{0,1},{3,2},{1,3},{6,4},{4,5},{7,6},{5,7},{10,8},{8,9},{11,1... | collective-permute-start | bytes 6291464 | tf_op jit(solution)/shard_map/ppermute | solution.py:682
  351.0 37.5 %collective-permute-start.25 = (bf16[80,2048]{1,0:T(8,128)(2,1)}, bf16[80,2048]{1,0:T(8,128)(2,1)S(1)}, u32[]{:S(2)}, u32[]{:S(2)}) collective-permute-start(bf16[80,2048]{1,0:T(8,128)(2,1)} %get-tuple-element.165), channel_id=1, source_target_pairs={{2,0},{0,1},{3,2},{1,3},{6,4},{4,5},{7,6},{5,7},{10,8},{8,9},{11,1... | collective-permute-start | bytes 983048 | tf_op jit(solution)/shard_map/ppermute | solution.py:690
  351.0 37.5 %collective-permute-start.26 = (bf16[80,2048]{1,0:T(8,128)(2,1)}, bf16[80,2048]{1,0:T(8,128)(2,1)S(1)}, u32[]{:S(2)}, u32[]{:S(2)}) collective-permute-start(bf16[80,2048]{1,0:T(8,128)(2,1)} %get-tuple-element.166), channel_id=1, source_target_pairs={{10,0},{8,1},{11,2},{9,3},{14,4},{12,5},{15,6},{13,7},{2,8},{0,9},... | collective-permute-start | bytes 983048 | tf_op jit(solution)/shard_map/ppermute | solution.py:690
  351.9 36.6 %collective-permute-start.27 = (bf16[80,2048]{1,0:T(8,128)(2,1)}, bf16[80,2048]{1,0:T(8,128)(2,1)S(1)}, u32[]{:S(2)}, u32[]{:S(2)}) collective-permute-start(bf16[80,2048]{1,0:T(8,128)(2,1)} %get-tuple-element.167), channel_id=1, source_target_pairs={{18,0},{16,1},{19,2},{17,3},{22,4},{20,5},{23,6},{21,7},{26,8},{24... | collective-permute-start | bytes 983048 | tf_op jit(solution)/shard_map/ppermute | solution.py:690
  355.3 37.9 %collective-permute-start.28 = (bf16[80,2048]{1,0:T(8,128)(2,1)}, bf16[80,2048]{1,0:T(8,128)(2,1)S(1)}, u32[]{:S(2)}, u32[]{:S(2)}) collective-permute-start(bf16[80,2048]{1,0:T(8,128)(2,1)} %get-tuple-element.168), channel_id=1, source_target_pairs={{26,0},{24,1},{27,2},{25,3},{30,4},{28,5},{31,6},{29,7},{18,8},{16... | collective-permute-start | bytes 983048 | tf_op jit(solution)/shard_map/ppermute | solution.py:690
  388.5 4.7 %copy-start.14 = (bf16[80,2048]{1,0:T(8,128)(2,1)}, bf16[80,2048]{1,0:T(8,128)(2,1)S(1)}, u32[]{:S(2)}) copy-start(bf16[80,2048]{1,0:T(8,128)(2,1)S(1)} %collective-permute-done.25.refs_1_) | copy-start | bytes 983044
  388.5 4.7 %copy-start.15 = (bf16[80,2048]{1,0:T(8,128)(2,1)}, bf16[80,2048]{1,0:T(8,128)(2,1)S(1)}, u32[]{:S(2)}) copy-start(bf16[80,2048]{1,0:T(8,128)(2,1)S(1)} %collective-permute-done.26.refs_2_) | copy-start | bytes 983044
  388.5 4.7 %copy-start.16 = (bf16[80,2048]{1,0:T(8,128)(2,1)}, bf16[80,2048]{1,0:T(8,128)(2,1)S(1)}, u32[]{:S(2)}) copy-start(bf16[80,2048]{1,0:T(8,128)(2,1)S(1)} %collective-permute-done.27.refs_3_) | copy-start | bytes 983044
  396.0 4.5 %copy-start.18 = (f32[8,2048]{1,0:T(8,128)S(1)}, f32[8,2048]{1,0:T(8,128)}, u32[]{:S(2)}) copy-start(f32[8,2048]{1,0:T(8,128)} %get-tuple-element.169) | copy-start | bytes 196612
  396.0 4.5 %collective-permute-start.29 = (f32[8,2048]{1,0:T(8,128)}, f32[8,2048]{1,0:T(8,128)S(1)}, u32[]{:S(2)}, u32[]{:S(2)}) collective-permute-start(f32[8,2048]{1,0:T(8,128)} %get-tuple-element.169), channel_id=1, source_target_pairs={{0,4},{1,5},{2,6},{3,7},{4,0},{5,1},{6,2},{7,3},{8,12},{9,13},{10,... | collective-permute-start | bytes 196616 | tf_op jit(solution)/shard_map/ppermute | solution.py:698
  (15 other events, 32.0 us)
Sparse Core Ops, SparseCore 0:
  10.8 51.6 all-gather.3
  65.2 49.0 all-gather.5
  117.0 71.2 all-gather.7
  242.5 26.1 reduce-scatter.2
  291.2 94.5 reduce-scatter.4
